TPU v7x, 32 devices: a whole 2x2x4 slice. The times are simulated.
32 devices in a mesh: seq: 8 (over z, y), head: 4 (over x, core).
Axes of the slice: x: 2, y: 2, z: 4, core: 2. Of those that a mesh axis runs over, the one named last changes fastest.
Arguments:
- queries: bfloat16 [4096, 8192], P('seq', 'head'), may hold values from -4 to 4
- key_vecs: bfloat16 [4096, 8192], P('seq', 'head'), may hold values from -4 to 4
- value_vecs: bfloat16 [4096, 8192], P('seq', 'head'), may hold values from -6 to 6
- log_decay: float32 [4096, 64], P('seq', 'head'), may hold values from -3 to 0, as said below
- norm_gain: float32 [8192], P('head'), may hold values from 0.1 to 1.9
- cotangent: bfloat16 [4096, 8192], P('seq', 'head'), may hold values from -6 to 6
Outputs:
- attended: bfloat16 [4096, 8192], P('seq', 'head')
- grad_queries: bfloat16 [4096, 8192], P('seq', 'head')
- grad_keys: bfloat16 [4096, 8192], P('seq', 'head')
- grad_values: bfloat16 [4096, 8192], P('seq', 'head')
Inputs may be any that keep to these rules, and one draw needn't show every extreme that they name: `log_decay`: every entry is negative.
All inputs are finite; a program needn't handle non-finite values.
Results may differ from a plain program's by a relative error of at most 0.0051.
Values sent between devices are 32-bit elements; how exact they have to be, the bound alone decides.
No kernel may reach another device: no remote copies, remote signals or barrier semaphores. Data moves between devices by JAX's collectives and lax.ppermute only.
A program may use at most 128 MiB of HBM per device.

v0:
```python
import functools

import jax
import jax.numpy as jnp
from jax import lax
from jax.experimental import pallas as pl
from jax.experimental.pallas import tpu as pltpu
from jax.sharding import PartitionSpec as P

HEAD_DIM = 128
BLOCK = 512
FORWARD_CHUNKS = 2
BACKWARD_CHUNKS = 2
TILE = 256
epsilon = 1e-06
f32 = jnp.float32
bf16 = jnp.bfloat16

NN = (((1,), (0,)), ((), ()))
NT = (((1,), (1,)), ((), ()))
TN = (((0,), (0,)), ((), ()))


def dot(a, b, dims=NN):
    return lax.dot_general(a, b, dims, preferred_element_type=f32)


def halves(x):
    high = x.astype(bf16)
    return high, (x - high.astype(f32)).astype(bf16)


def column(row):
    return jnp.transpose(jnp.broadcast_to(row, (HEAD_DIM, row.shape[1])))


def wide(col, width):
    return jnp.concatenate([col] * (width // HEAD_DIM), axis=1)


def cumulative(decay):
    length = decay.shape[1]
    first = decay.astype(bf16)
    rest = decay - first.astype(f32)
    second = rest.astype(bf16)
    third = (rest - second.astype(f32)).astype(bf16)
    upto = lax.broadcasted_iota(jnp.int32, (length, length), 0) <= lax.broadcasted_iota(
        jnp.int32, (length, length), 1
    )
    upto = jnp.where(upto, 1.0, 0.0).astype(bf16)
    return dot(first, upto) + dot(second, upto) + dot(third, upto)


def trail_row(row):
    return jnp.exp(row[:, -1:] - row)


def outer_sum(left, scale_row, right):
    scaled = jnp.transpose(left.astype(f32)) * scale_row
    high, low = halves(scaled)
    return dot(high, right) + dot(low, right)


def cols(j):
    return slice(j * HEAD_DIM, (j + 1) * HEAD_DIM)


class Part:
    def __init__(self, first, count, slot, group_heads):
        self.first, self.count, self.slot, self.group_heads = first, count, slot, group_heads
        self.steps = 2 if count % 4 == 0 else 1
        self.per_step = count // self.steps

    def group(self, info):
        return info[0][0] if self.slot == "mine" else 1 - info[0][0]

    def head(self, info, o):
        return self.group(info) * self.group_heads + self.first + o

    def row(self, cumul_ref, info, o):
        return cumul_ref[pl.ds(self.head(info, o), 1), :]

    def wide_cols(self, info, o):
        return pl.ds(pl.multiple_of(self.head(info, o) * HEAD_DIM, HEAD_DIM), HEAD_DIM)

    def each(self, body):
        for j in range(self.per_step):
            body(pl.program_id(0) * self.per_step + j if self.steps > 1 else j, j)


def at_head(o):
    if isinstance(o, int):
        return cols(o)
    return pl.ds(pl.multiple_of(o * HEAD_DIM, HEAD_DIM), HEAD_DIM)


def chosen(part, values, o, j):
    read, refs = values
    if len(refs) == 1:
        return read(refs[0], at_head(o))
    found = read(refs[0], cols(j))
    for step in range(1, part.steps):
        found = jnp.where(pl.program_id(0) == step, read(refs[step], cols(j)), found)
    return found


def store_decay(part, info, cumul_ref, o, out_ref):
    row = part.row(cumul_ref, info, o)
    out_ref[pl.ds(part.count * HEAD_DIM + o, 1), :] = jnp.broadcast_to(
        jnp.exp(row[:, -1:]), (1, HEAD_DIM)
    )


def pieces_kernel(part, info, key_ref, value_ref, cumul_ref, out_ref):
    def head(o, j):
        at = part.wide_cols(info, o)
        out_ref[at_head(o), :] = outer_sum(
            key_ref[:, at], trail_row(part.row(cumul_ref, info, o)), value_ref[:, at]
        )
        store_decay(part, info, cumul_ref, o, out_ref)

    part.each(head)


def first_pieces_kernel(part, info, key_ref, value_ref, decay_ref, out_ref, cumul_ref):
    @pl.when(pl.program_id(0) == 0)
    def _():
        cumul_ref[...] = cumulative(decay_ref[...])

    def head(o, j):
        out_ref[at_head(o), :] = outer_sum(
            key_ref[:, cols(j)], trail_row(part.row(cumul_ref, info, o)), value_ref[:, cols(j)]
        )
        store_decay(part, info, cumul_ref, o, out_ref)

    part.each(head)


def inner_kernel(part, info, query_ref, key_ref, value_ref, cumul_ref, out_ref):
    def head(o, j):
        row = part.row(cumul_ref, info, o)
        col = column(row)
        at = part.wide_cols(info, o)
        query, key, value = query_ref[:, at], key_ref[:, at], value_ref[:, at]
        for top in range(0, BLOCK, TILE):
            end = top + TILE
            scores = dot(query[top:end], key[:end], NT)
            spread = wide(col[top:end], end) - row[:, :end]
            causal = lax.broadcasted_iota(jnp.int32, (TILE, end), 0) + top >= (
                lax.broadcasted_iota(jnp.int32, (TILE, end), 1)
            )
            weights = (scores * jnp.exp(jnp.where(causal, spread, -1e30))).astype(bf16)
            out_ref[top:end, at_head(o)] = dot(weights, value[:end])

    part.each(head)


def output_kernel(
    part, offset, info, inner_ref, query_ref, cot_ref, gain_ref, cumul_ref, state_ref, before_ref,
    out_ref, sums_ref, square_ref, product_ref,
):
    @pl.when(pl.program_id(0) == 0)
    def _():
        square_ref[...] = jnp.zeros_like(square_ref)
        product_ref[...] = jnp.zeros_like(product_ref)

    def head(o, j):
        lead = jnp.exp(column(part.row(cumul_ref, info, o)))
        high, low = halves(state_ref[at_head(o), :])
        at = part.wide_cols(info, o)
        query = query_ref[:, at]
        out = inner_ref[:, at_head(offset + o)] + lead * (dot(query, high) + dot(query, low))
        out_ref[:, at_head(o)] = out
        square_ref[...] += out * out
        product_ref[...] += cot_ref[:, at].astype(f32) * gain_ref[:, at] * out

    part.each(head)

    @pl.when(pl.program_id(0) == part.steps - 1)
    def _():
        rows = lax.broadcasted_iota(jnp.int32, (8, HEAD_DIM), 0)
        total = before_ref[...]
        for place, ref in ((0, square_ref), (1, product_ref)):
            pick = jnp.where(rows == place, 1.0, 0.0).astype(bf16)
            high, low = halves(ref[...])
            total += dot(pick, high, NT) + dot(pick, low, NT)
        sums_ref[...] = total


def grad_kernel(features, part, held, info, *refs):
    outs, (cot_ref, gain_ref, query_ref, cumul_ref, *refs) = refs[:held], refs[held:]
    shares, (attended_ref, grad_ref, piece_ref) = refs[:-3], refs[-3:]
    sums = shares[0][...]
    for share in shares[1:]:
        sums = sums + share[...]
    inverse = lax.rsqrt(sums[0:1] / features + epsilon)
    mean_term = inverse * sums[1:2] / features
    inverse_col, mean_col = column(inverse), column(mean_term)

    def head(o, j):
        at = part.wide_cols(info, o)
        gain = gain_ref[:, at]
        normed = chosen(part, (lambda ref, at: ref[:, at], outs), o, j) * inverse_col
        attended_ref[:, cols(j)] = (normed * gain).astype(bf16)
        scaled_grad = cot_ref[:, at].astype(f32) * gain
        grad = (inverse_col * (scaled_grad - normed * mean_col)).astype(bf16)
        grad_ref[:, at_head(o)] = grad
        lead = jnp.exp(part.row(cumul_ref, info, o))
        piece_ref[at_head(o), :] = outer_sum(query_ref[:, at], lead, grad)
        store_decay(part, info, cumul_ref, o, piece_ref)

    part.each(head)


def backward_kernel(part, info, query_ref, key_ref, value_ref, grad_ref, cumul_ref, *refs):
    states, (grad_query_ref, inner_key_ref, inner_value_ref) = refs[:-3], refs[-3:]

    def head(o, j):
        row = part.row(cumul_ref, info, o)
        col = column(row)
        at = part.wide_cols(info, o)
        query, key = query_ref[:, at], key_ref[:, at]
        value, grad = value_ref[:, at], grad_ref[:, at_head(o)]
        high, low = halves(chosen(part, (lambda ref, at: ref[at, :], states), o, j))
        outer = jnp.exp(col) * (dot(grad, high, NT) + dot(grad, low, NT))
        for top in range(0, BLOCK, TILE):
            end = top + TILE
            scores = dot(key[top:end], query[top:], NT)
            grad_scores = dot(value[top:end], grad[top:], NT)
            spread = row[:, top:] - wide(col[top:end], BLOCK - top)
            causal = lax.broadcasted_iota(jnp.int32, spread.shape, 0) <= (
                lax.broadcasted_iota(jnp.int32, spread.shape, 1)
            )
            decays = jnp.exp(jnp.where(causal, spread, -1e30))
            weights = (scores * decays).astype(bf16)
            grad_weights = (grad_scores * decays).astype(bf16)
            inner_value_ref[top:end, at_head(o)] = dot(weights, grad[top:])
            inner_key_ref[top:end, at_head(o)] = dot(grad_weights, query[top:])
            inner_query = dot(grad_weights, key[top:end], TN)
            outer = inner_query + outer if top == 0 else jnp.concatenate(
                [outer[:top], outer[top:] + inner_query], axis=0
            )
        grad_query_ref[:, cols(j)] = outer.astype(bf16)

    part.each(head)


def final_kernel(
    part, info, inner_key_ref, inner_value_ref, key_ref, value_ref, cumul_ref, state_ref,
    grad_key_ref, grad_value_ref,
):
    def head(o, j):
        trail = column(trail_row(part.row(cumul_ref, info, o)))
        high, low = halves(state_ref[at_head(o), :])
        at = part.wide_cols(info, o)
        key, value = key_ref[:, at], value_ref[:, at]
        grad_key_ref[:, cols(j)] = (
            inner_key_ref[:, at_head(o)] + trail * (dot(value, high, NT) + dot(value, low, NT))
        ).astype(bf16)
        grad_value_ref[:, cols(j)] = (
            inner_value_ref[:, at_head(o)] + trail * (dot(key, high) + dot(key, low))
        ).astype(bf16)

    part.each(head)


def ordered(is_first, half, j, keep_ref, got_ref):
    rows = slice(j * HEAD_DIM, (j + 1) * HEAD_DIM)
    place = slice(half * HEAD_DIM + j, half * HEAD_DIM + j + 1)
    keep, got = keep_ref[rows, :], got_ref[rows, :]
    keep_decay, got_decay = keep_ref[place, :], got_ref[place, :]
    return (
        jnp.where(is_first, keep, got),
        jnp.where(is_first, got, keep),
        jnp.where(is_first, keep_decay, got_decay),
        jnp.where(is_first, got_decay, keep_decay),
    )


def scan_position(places, forward, info):
    member, pair = info[0][0], info[1][0]
    if forward:
        return member == 0, pair
    return member == 1, places - 1 - pair


def copy_kernel(info, in_ref, out_ref):
    out_ref[...] = in_ref[...]


def hop_kernel(half, p, position, info, keep_ref, got_ref, *refs):
    arrived, out_ref = refs[:-1], refs[-1]
    is_first, place = position(info)

    @pl.when(place == p)
    def _():
        for j in range(half):
            first, second, first_decay, second_decay = ordered(is_first, half, j, keep_ref, got_ref)
            value = second_decay * first + second
            for arrived_ref in arrived:
                value += (first_decay * second_decay) * arrived_ref[cols(j), :]
            out_ref[cols(j), :] = value


def last_kernel(half, position, info, keep_ref, got_ref, *refs):
    arrived, (mine_ref, send_ref) = refs[:-2], refs[-2:]
    is_first, place = position(info)
    for p in range(len(arrived) + 1):

        @pl.when(place == p)
        def _():
            for j in range(half):
                first, _, first_decay, _ = ordered(is_first, half, j, keep_ref, got_ref)
                if p == 0:
                    before, after = jnp.zeros_like(first), first
                else:
                    before = arrived[p - 1][cols(j), :]
                    after = first_decay * before + first
                mine_ref[cols(j), :] = jnp.where(is_first, before, after)
                send_ref[cols(j), :] = jnp.where(is_first, after, before)


def on_device(queries, key_vecs, value_vecs, log_decay, norm_gain, cotangent):
    tokens, width = queries.shape
    assert tokens == BLOCK
    heads = width // HEAD_DIM
    group_heads = heads // 2
    head_count = lax.axis_size("head")
    features = width * head_count
    places = lax.axis_size("seq") // 2
    my_index = lax.axis_index("seq")
    member, pair = my_index % 2, my_index // 2
    gain = norm_gain.reshape(1, width)
    info = (member.astype(jnp.int32).reshape(1), pair.astype(jnp.int32).reshape(1))

    any_spec = pl.BlockSpec(memory_space=pl.ANY)
    whole = jax.ShapeDtypeStruct((tokens, width), bf16)
    sums_shape = jax.ShapeDtypeStruct((8, tokens), f32)

    def states_of(count, extra=0):
        return jax.ShapeDtypeStruct((count * HEAD_DIM + extra, HEAD_DIM), f32)

    def local_of(count, dtype=f32):
        return jax.ShapeDtypeStruct((tokens, count * HEAD_DIM), dtype)

    def run(kernel, grid, ins, outs, scratch=(), after=(), aliases=None, cost=1.0, limit=24):
        used = len(ins)
        after = [x for i, x in enumerate(after) if not any(x is y for y in after[:i])]

        def body(member_ref, pair_ref, *refs):
            kernel((member_ref, pair_ref), *refs[:used], *refs[used + len(after):])

        return pl.pallas_call(
            body,
            out_shape=[shape for shape, _ in outs],
            grid_spec=pltpu.PrefetchScalarGridSpec(
                num_scalar_prefetch=2,
                grid=(grid,),
                in_specs=[spec for _, spec in ins] + [any_spec] * len(after),
                out_specs=[spec for _, spec in outs],
                scratch_shapes=list(scratch),
            ),
            input_output_aliases=aliases or {},
            compiler_params=pltpu.CompilerParams(vmem_limit_bytes=limit * 1024 * 1024),
            cost_estimate=pl.CostEstimate(
                flops=int(cost * 1e9), bytes_accessed=int(cost * 2.5e6), transcendentals=0
            ),
        )(*info, *[array for array, _ in ins], *after)

    def fixed(shape):
        return pl.BlockSpec(shape, lambda i, *info: (0,) * len(shape))

    def plain(array):
        return array, fixed(array.shape)

    def give(shape):
        return shape, fixed(shape.shape)

    class Calls(Part):
        def full_spec(self):
            width = self.per_step
            return pl.BlockSpec(
                (tokens, width * HEAD_DIM),
                lambda i, *info: (
                    0, (self.group(info) * self.group_heads + self.first) // width + i
                ),
            )

        def call(self, kernel, ins, outs, **options):
            return run(functools.partial(kernel, self), self.steps, ins, outs, **options)

    def parts_of(chunks, slot):
        count = group_heads // chunks
        return [Calls(c * count, count, slot, group_heads) for c in range(chunks)]

    swap = [(2 * p + m, 2 * p + 1 - m) for p in range(places) for m in (0, 1)]

    def chain(chunks, make_piece, forward, filler, on_mine, on_theirs):
        position = functools.partial(scan_position, places, forward)
        my_parts, their_parts = parts_of(chunks, "mine"), parts_of(chunks, "theirs")
        count = group_heads // chunks
        state, wide_state = states_of(count), states_of(count, 8)

        def device(place, m):
            return 2 * (place if forward else places - 1 - place) + m

        sends, keeps, received, last = [], [], [], ()

        def exchange(last):
            c = len(received)
            if c == 0 or c >= chunks:
                if c == 0:
                    received.append(lax.ppermute(sends[0], "seq", swap))
                return last
            sent, = run(copy_kernel, 1, [plain(sends[c])], [give(wide_state)], after=last, cost=0.02)
            received.append(lax.ppermute(sent, "seq", swap))
            return (sent,)

        for part in their_parts:
            sends.append(make_piece(part, last))
            last = () if forward and len(sends) == 1 else (sends[-1],)
        last = exchange(last)
        if forward:
            last = exchange(last)
        rest = [functools.partial(make_piece, part) for part in my_parts]
        for make in rest[:1] if forward else rest:
            keeps.append(make(last))
            last = (keeps[-1],)
        if not forward:
            last = exchange(last)
        arrived, mine, theirs, late = {}, [], [], []
        for step in range(chunks + places - 1):
            for p in range(places - 1):
                c = step - p
                if not 0 <= c < chunks:
                    continue
                ins = [plain(keeps[c]), plain(received[c])]
                if p > 0:
                    ins.append(plain(arrived[c, p]))
                value, = run(
                    functools.partial(hop_kernel, count, p, position), 1, ins, [give(state)],
                    after=last, cost=0.3,
                )
                pairs = [(device(p, m), device(p + 1, m)) for m in (0, 1)]
                arrived[c, p + 1] = lax.ppermute(value, "seq", pairs)
                last = (value,)
            last = exchange(last)
            while len(keeps) < chunks:
                keeps.append(rest[len(keeps)](last))
                last = (keeps[-1],)
            c = step + 1 - places
            if c >= 0:
                ins = [plain(keeps[c]), plain(received[c])]
                ins += [plain(arrived[c, p]) for p in range(1, places)]
                own, send = run(
                    functools.partial(last_kernel, count, position), 1, ins, [give(state)] * 2,
                    after=last, cost=0.3,
                )
                theirs.append(lax.ppermute(send, "seq", swap))
                mine.append(own)
                last = (send,)
                filler.append(functools.partial(on_mine, c, own))
                late.append(functools.partial(on_theirs, c, theirs[c]))
                if c >= 2:
                    filler.append(late.pop(0))
                if forward and c >= chunks - 2 and filler:
                    last = (filler.pop(0)(last),)
            if filler:
                last = (filler.pop(0)(last),)
        for work in filler + late:
            last = (work(last),)
        return mine, theirs

    inner, outs = {}, {}
    held_cumul, held_sums = [], [jnp.zeros(sums_shape.shape, f32)]
    back_count = group_heads // BACKWARD_CHUNKS
    front_count = group_heads // FORWARD_CHUNKS
    per_back = back_count // front_count
    back_parts = {slot: parts_of(BACKWARD_CHUNKS, slot) for slot in ("mine", "theirs")}
    front_parts = {slot: parts_of(FORWARD_CHUNKS, slot) for slot in ("mine", "theirs")}

    def cumul_in():
        return plain(held_cumul[0])

    def forward_piece(part, after):
        if not held_cumul:
            piece, cumul = part.call(
                first_pieces_kernel,
                [(key_vecs, part.full_spec()), (value_vecs, part.full_spec()), plain(log_decay.T)],
                [give(states_of(part.count, 8)), give(jax.ShapeDtypeStruct((heads, tokens), f32))],
                cost=0.05, limit=60,
            )
            held_cumul.append(cumul)
            return piece
        return part.call(
            pieces_kernel, [plain(key_vecs), plain(value_vecs), cumul_in()],
            [give(states_of(part.count, 8))], after=after, cost=0.05,
        )[0]

    def inner_work(slot, c, after):
        part = back_parts[slot][c]
        inner[slot, c], = part.call(
            inner_kernel, [plain(queries), plain(key_vecs), plain(value_vecs), cumul_in()],
            [give(local_of(part.count))], after=after, cost=2.2 if inner else 0.1,
        )
        return inner[slot, c]

    def output_work(slot, c, before, after):
        part = front_parts[slot][c]
        outs[slot, c], held_sums[0] = run(
            functools.partial(output_kernel, part, c % per_back * front_count), part.steps,
            [plain(inner[slot, c // per_back]), plain(queries), plain(cotangent), plain(gain),
             cumul_in(), plain(before), plain(held_sums[0])],
            [give(local_of(part.count)), give(sums_shape)],
            scratch=[pltpu.VMEM((tokens, HEAD_DIM), f32)] * 2, after=after, cost=0.8,
        )
        return held_sums[0]

    works = [
        functools.partial(inner_work, slot, c)
        for c in range(BACKWARD_CHUNKS) for slot in ("mine", "theirs")
    ]
    mine, theirs = chain(
        FORWARD_CHUNKS, forward_piece, True, works,
        functools.partial(output_work, "mine"), functools.partial(output_work, "theirs"),
    )
    states = {"mine": mine, "theirs": theirs}

    sums = held_sums[0]
    shares = [sums] + [
        lax.ppermute(sums, "head", [(i, (i + k) % head_count) for i in range(head_count)])
        for k in range(1, head_count)
    ]

    attended, grad_queries, grad_keys, grad_values = [], [], [], []
    grads, inner_grads = {}, {}

    def target(held):
        return tuple(held[-1:])

    def covered(c):
        return range(c * per_back, (c + 1) * per_back)

    def backward_piece(part, after):
        before = target(attended)
        c = part.first // part.count
        ins = [plain(outs[part.slot, i]) for i in covered(c)]
        ins += [plain(cotangent), plain(gain), plain(queries), cumul_in()]
        ins += [plain(share) for share in shares]
        whole_out, grads[part.slot, c], piece = run(
            functools.partial(grad_kernel, features, part, per_back), part.steps, ins,
            [(whole, part.full_spec()), give(local_of(part.count, bf16)),
             give(states_of(part.count, 8))],
            after=before + tuple(after), aliases={2 + len(ins): 0} if before else None, cost=2.0,
        )
        attended.append(whole_out)
        return piece

    def backward_work(slot, c, after):
        part, held = back_parts[slot][c], target(grad_queries)
        ins = [plain(queries), plain(key_vecs), plain(value_vecs), plain(grads[slot, c]), cumul_in()]
        ins += [plain(states[slot][i]) for i in covered(c)]
        whole_out, *inner_grads[slot, c] = part.call(
            backward_kernel, ins,
            [(whole, part.full_spec()), give(local_of(part.count)), give(local_of(part.count))],
            after=held + tuple(after), aliases={2 + len(ins): 0} if held else None, cost=4.3,
        )
        grad_queries.append(whole_out)
        return inner_grads[slot, c][0]

    def final_work(slot, c, before, after):
        part, held = back_parts[slot][c], target(grad_keys) + target(grad_values)
        ins = [plain(array) for array in (*inner_grads[slot, c], key_vecs, value_vecs)]
        ins += [cumul_in(), plain(before)]
        whole_key, whole_value = part.call(
            final_kernel, ins, [(whole, part.full_spec())] * 2, after=held + tuple(after),
            aliases={2 + len(ins): 0, 3 + len(ins): 1} if held else None, cost=2.0,
        )
        grad_keys.append(whole_key)
        grad_values.append(whole_value)
        return whole_key

    works = [
        functools.partial(backward_work, slot, c)
        for c in range(BACKWARD_CHUNKS) for slot in ("mine", "theirs")
    ]
    chain(
        BACKWARD_CHUNKS, backward_piece, False, works,
        functools.partial(final_work, "mine"), functools.partial(final_work, "theirs"),
    )
    return attended[-1], grad_queries[-1], grad_keys[-1], grad_values[-1]


def solution(mesh):
    return jax.shard_map(
        on_device,
        mesh=mesh,
        in_specs=(
            P("seq", "head"),
            P("seq", "head"),
            P("seq", "head"),
            P("seq", "head"),
            P("head"),
            P("seq", "head"),
        ),
        out_specs=(P("seq", "head"), P("seq", "head"), P("seq", "head"), P("seq", "head")),
        check_vma=False,
    )
```

profile of v0, /device:TPU:0, one launch (start us, length us, event | category | flops | bytes accessed | tf_op | source)
XLA Modules:
  0.0 103.6 jit_solution(8740737687458492498)
XLA Ops:
  0.7 3.0 %shard_map.93 = (f32[520,128]{1,0:T(8,128)}, f32[16,512]{1,0:T(8,128)}) custom-call(s32[1]{0:T(128)} %bitcast.member_ref, s32[1]{0:T(128)} %bitcast.1.pair_ref, bf16[512,2048]{1,0:T(8,128)(2,1)} %refs_2_.31, bf16[512,2048]{1,0:T(8,128)(2,1)} %refs_3_.15, f32[16,512]{1,0:T(8,128)} %bitcast.12), custom_call_target="tpu_custom_call" | custom-call | flops 50000000 | bytes 125000 | tf_op jit(solution)/shard_map/pallas_call | solution.py:353
  3.6 3.0 %collective-permute-start = (f32[520,128]{1,0:T(8,128)}, f32[520,128]{1,0:T(8,128)S(1)}, u32[]{:S(2)}, u32[]{:S(2)}) collective-permute-start(f32[520,128]{1,0:T(8,128)} %get-tuple-element.55), channel_id=1, source_target_pairs={{0,4},{4,0},{8,12},{12,8},{16,20},{20,16},{24,28},{28,24},{1,5},{5... | collective-permute-start | bytes 798728 | tf_op jit(solution)/shard_map/ppermute | solution.py:413
  6.6 1.6 %copy-done.2 = bf16[512,2048]{1,0:T(8,128)(2,1)S(1)} copy-done((bf16[512,2048]{1,0:T(8,128)(2,1)S(1)}, bf16[512,2048]{1,0:T(8,128)(2,1)}, u32[]{:S(2)}) %copy-start.2) | copy-done | bytes 2097176
  11.4 2.7 %collective-permute-done.refs_1_ = f32[520,128]{1,0:T(8,128)S(1)} collective-permute-done((f32[520,128]{1,0:T(8,128)}, f32[520,128]{1,0:T(8,128)S(1)}, u32[]{:S(2)}, u32[]{:S(2)}) %collective-permute-start) | collective-permute-done | bytes 266272 | tf_op jit(solution)/shard_map/ppermute | solution.py:413
  14.1 4.1 %collective-permute-start.1 = (f32[512,128]{1,0:T(8,128)S(1)}, f32[512,128]{1,0:T(8,128)S(1)}, u32[]{:S(2)}, u32[]{:S(2)}) collective-permute-start(f32[512,128]{1,0:T(8,128)S(1)} %shard_map.97.refs_3_), channel_id=1, source_target_pairs={{0,8},{4,12},{1,9},{5,13},{2,10},{6,14},{3,11},{7,15}} | collective-permute-start | bytes 786440 | tf_op jit(solution)/shard_map/ppermute | solution.py:445
  19.1 1.9 %shard_map.99.refs_2_.refs_0_ = f32[512,512]{1,0:T(8,128)S(1)} custom-call(s32[1]{0:T(128)} %bitcast.member_ref, s32[1]{0:T(128)} %bitcast.1.pair_ref, bf16[512,2048]{1,0:T(8,128)(2,1)S(1)} %copy-done, bf16[512,2048]{1,0:T(8,128)(2,1)S(1)} %copy-done.1, bf16[512,2048]{1,0:T(8,128)(2,1)S(1)} %copy-done.3, f32[16,512]{1,0:T(8,128)S(1)} %copy-done.5, ...), custom_call_target="tpu_custom_call" | custom-call | flops 100000000 | bytes 250000 | tf_op jit(solution)/shard_map/pallas_call | solution.py:353
  21.0 1.6 %collective-permute-start.4 = (f32[512,128]{1,0:T(8,128)S(1)}, f32[512,128]{1,0:T(8,128)S(1)}, u32[]{:S(2)}, u32[]{:S(2)}) collective-permute-start(f32[512,128]{1,0:T(8,128)S(1)} %shard_map.100.refs_3_), channel_id=1, source_target_pairs={{0,8},{4,12},{1,9},{5,13},{2,10},{6,14},{3,11},{7,15}} | collective-permute-start | bytes 786440 | tf_op jit(solution)/shard_map/ppermute | solution.py:445
  23.3 1.9 %shard_map.102.refs_3_.refs_0_ = f32[512,512]{1,0:T(8,128)S(1)} custom-call(s32[1]{0:T(128)} %bitcast.member_ref, s32[1]{0:T(128)} %bitcast.1.pair_ref, bf16[512,2048]{1,0:T(8,128)(2,1)S(1)} %copy-done, bf16[512,2048]{1,0:T(8,128)(2,1)S(1)} %copy-done.1, bf16[512,2048]{1,0:T(8,128)(2,1)S(1)} %copy-done.3, f32[16,512]{1,0:T(8,128)S(1)} %copy-done.5, ...), custom_call_target="tpu_custom_call" | custom-call | flops 2200000000 | bytes 5500000 | tf_op jit(solution)/shard_map/pallas_call | solution.py:353
  25.3 2.4 %collective-permute-done.4.refs_2_ = f32[512,128]{1,0:T(8,128)S(1)} collective-permute-done((f32[512,128]{1,0:T(8,128)S(1)}, f32[512,128]{1,0:T(8,128)S(1)}, u32[]{:S(2)}, u32[]{:S(2)}) %collective-permute-start.4) | collective-permute-done | bytes 262176 | tf_op jit(solution)/shard_map/ppermute | solution.py:445
  29.1 1.9 %shard_map.105.refs_3_.refs_0_ = f32[512,512]{1,0:T(8,128)S(1)} custom-call(s32[1]{0:T(128)} %bitcast.member_ref, s32[1]{0:T(128)} %bitcast.1.pair_ref, bf16[512,2048]{1,0:T(8,128)(2,1)S(1)} %copy-done, bf16[512,2048]{1,0:T(8,128)(2,1)S(1)} %copy-done.1, bf16[512,2048]{1,0:T(8,128)(2,1)S(1)} %copy-done.3, f32[16,512]{1,0:T(8,128)S(1)} %copy-done.6, ...), custom_call_target="tpu_custom_call" | custom-call | flops 2200000000 | bytes 5500000 | tf_op jit(solution)/shard_map/pallas_call | solution.py:353
  31.9 1.6 %collective-permute-start.9 = (f32[512,128]{1,0:T(8,128)S(1)}, f32[512,128]{1,0:T(8,128)S(1)}, u32[]{:S(2)}, u32[]{:S(2)}) collective-permute-start(f32[512,128]{1,0:T(8,128)S(1)} %get-tuple-element.57.refs_4_), channel_id=1, source_target_pairs={{0,4},{4,0},{8,12},{12,8},{16,20},{20,16},{24,28},{28,24},{1,5},{5... | collective-permute-start | bytes 786440 | tf_op jit(solution)/shard_map/ppermute | solution.py:459
  33.4 1.9 %shard_map.108.refs_7_.refs_0_ = f32[512,512]{1,0:T(8,128)S(1)} custom-call(s32[1]{0:T(128)} %bitcast.member_ref, s32[1]{0:T(128)} %bitcast.1.pair_ref, bf16[512,2048]{1,0:T(8,128)(2,1)S(1)} %copy-done, bf16[512,2048]{1,0:T(8,128)(2,1)S(1)} %copy-done.1, bf16[512,2048]{1,0:T(8,128)(2,1)S(1)} %copy-done.3, f32[16,512]{1,0:T(8,128)S(1)} %copy-done.6, ...), custom_call_target="tpu_custom_call" | custom-call | flops 2200000000 | bytes 5500000 | tf_op jit(solution)/shard_map/pallas_call | solution.py:353
  38.3 1.5 %collective-permute-done.9.refs_5_ = f32[512,128]{1,0:T(8,128)S(1)} collective-permute-done((f32[512,128]{1,0:T(8,128)S(1)}, f32[512,128]{1,0:T(8,128)S(1)}, u32[]{:S(2)}, u32[]{:S(2)}) %collective-permute-start.9) | collective-permute-done | bytes 262176 | tf_op jit(solution)/shard_map/ppermute | solution.py:459
  40.9 3.3 %collective-permute-done.8.refs_5_ = f32[512,128]{1,0:T(8,128)S(1)} collective-permute-done((f32[512,128]{1,0:T(8,128)S(1)}, f32[512,128]{1,0:T(8,128)S(1)}, u32[]{:S(2)}, u32[]{:S(2)}) %collective-permute-start.8) | collective-permute-done | bytes 262176 | tf_op jit(solution)/shard_map/ppermute | solution.py:459
  45.3 1.6 %collective-permute-start.11 = (f32[8,512]{1,0:T(8,128)S(1)}, f32[8,512]{1,0:T(8,128)S(1)}, u32[]{:S(2)}, u32[]{:S(2)}) collective-permute-start(f32[8,512]{1,0:T(8,128)S(1)} %get-tuple-element.64.refs_5_), channel_id=1, source_target_pairs={{0,2},{1,3},{2,0},{3,1},{4,6},{5,7},{6,4},{7,5},{8,10},{9,11},{10,... | collective-permute-start | bytes 49160 | tf_op jit(solution)/shard_map/ppermute | solution.py:531
  47.1 2.0 %collective-permute-done.11.refs_7_ = f32[8,512]{1,0:T(8,128)S(1)} collective-permute-done((f32[8,512]{1,0:T(8,128)S(1)}, f32[8,512]{1,0:T(8,128)S(1)}, u32[]{:S(2)}, u32[]{:S(2)}) %collective-permute-start.11) | collective-permute-done | bytes 16416 | tf_op jit(solution)/shard_map/ppermute | solution.py:531
  50.0 1.7 %shard_map.114 = (bf16[512,2048]{1,0:T(8,128)(2,1)}, bf16[512,512]{1,0:T(8,128)(2,1)S(1)}, f32[520,128]{1,0:T(8,128)S(1)}) custom-call(s32[1]{0:T(128)} %bitcast.member_ref, s32[1]{0:T(128)} %bitcast.1.pair_ref, f32[512,512]{1,0:T(8,128)S(1)} %get-tuple-element.67.refs_0_, bf16[512,2048]{1,0:T(8,128)(2,1)S(1)} %copy-done.4, f32[1,2048]{1,0:T(1,128)S(1)} %bitcast.8, ...), custom_call_target="tpu_custom_call" | custom-call | flops 2000000000 | bytes 5000000 | tf_op jit(solution)/shard_map/pallas_call | solution.py:353
  51.7 1.5 %collective-permute-start.13 = (f32[520,128]{1,0:T(8,128)S(1)}, f32[520,128]{1,0:T(8,128)S(1)}, u32[]{:S(2)}, u32[]{:S(2)}) collective-permute-start(f32[520,128]{1,0:T(8,128)S(1)} %get-tuple-element.69.refs_10_), channel_id=1, source_target_pairs={{0,4},{4,0},{8,12},{12,8},{16,20},{20,16},{24,28},{28,24},{1,5},{5... | collective-permute-start | bytes 798728 | tf_op jit(solution)/shard_map/ppermute | solution.py:413
  53.2 1.7 %shard_map.115 = (bf16[512,2048]{1,0:T(8,128)(2,1)}, bf16[512,512]{1,0:T(8,128)(2,1)S(1)}, f32[520,128]{1,0:T(8,128)S(1)}) custom-call(s32[1]{0:T(128)} %bitcast.member_ref, s32[1]{0:T(128)} %bitcast.1.pair_ref, f32[512,512]{1,0:T(8,128)S(1)} %get-tuple-element.66.refs_0_, bf16[512,2048]{1,0:T(8,128)(2,1)S(1)} %copy-done.4, ...), custom_call_target="tpu_custom_call", output_to_operand_aliasing={{0}: (11, {})} | custom-call | flops 2000000000 | bytes 5000000 | tf_op jit(solution)/shard_map/pallas_call | solution.py:353
  55.0 1.7 %shard_map.116 = (bf16[512,2048]{1,0:T(8,128)(2,1)}, bf16[512,512]{1,0:T(8,128)(2,1)S(1)}, f32[520,128]{1,0:T(8,128)S(1)}) custom-call(s32[1]{0:T(128)} %bitcast.member_ref, s32[1]{0:T(128)} %bitcast.1.pair_ref, f32[512,512]{1,0:T(8,128)S(1)} %get-tuple-element.65.refs_0_, bf16[512,2048]{1,0:T(8,128)(2,1)S(1)} %copy-done.4, ...), custom_call_target="tpu_custom_call", output_to_operand_aliasing={{0}: (11, {})} | custom-call | flops 2000000000 | bytes 5000000 | tf_op jit(solution)/shard_map/pallas_call | solution.py:353
  56.7 1.7 %shard_map.117 = (bf16[512,2048]{1,0:T(8,128)(2,1)}, bf16[512,512]{1,0:T(8,128)(2,1)S(1)}, f32[520,128]{1,0:T(8,128)S(1)}) custom-call(s32[1]{0:T(128)} %bitcast.member_ref, s32[1]{0:T(128)} %bitcast.1.pair_ref, f32[512,512]{1,0:T(8,128)S(1)} %get-tuple-element.61.refs_0_, bf16[512,2048]{1,0:T(8,128)(2,1)S(1)} %copy-done.4, ...), custom_call_target="tpu_custom_call", output_to_operand_aliasing={{0}: (11, {})} | custom-call | flops 2000000000 | bytes 5000000 | tf_op jit(solution)/shard_map/pallas_call | solution.py:353
  59.9 4.0 %shard_map.120 = (bf16[512,2048]{1,0:T(8,128)(2,1)}, f32[512,512]{1,0:T(8,128)S(1)}, f32[512,512]{1,0:T(8,128)S(1)}) custom-call(s32[1]{0:T(128)} %bitcast.member_ref, s32[1]{0:T(128)} %bitcast.1.pair_ref, bf16[512,2048]{1,0:T(8,128)(2,1)S(1)} %copy-done, bf16[512,2048]{1,0:T(8,128)(2,1)S(1)} %copy-done.1, bf16[512,2048]{1,0:T(8,128)(2,1)S(1)} %copy-done.3, ...), custom_call_target="tpu_custom_call" | custom-call | flops 4300000256 | bytes 10750000 | tf_op jit(solution)/shard_map/pallas_call | solution.py:353
  66.4 4.0 %shard_map.123 = (bf16[512,2048]{1,0:T(8,128)(2,1)}, f32[512,512]{1,0:T(8,128)S(1)}, f32[512,512]{1,0:T(8,128)S(1)}) custom-call(s32[1]{0:T(128)} %bitcast.member_ref, s32[1]{0:T(128)} %bitcast.1.pair_ref, bf16[512,2048]{1,0:T(8,128)(2,1)S(1)} %copy-done, bf16[512,2048]{1,0:T(8,128)(2,1)S(1)} %copy-done.1, ...), custom_call_target="tpu_custom_call", output_to_operand_aliasing={{0}: (8, {})} | custom-call | flops 4300000256 | bytes 10750000 | tf_op jit(solution)/shard_map/pallas_call | solution.py:353
  71.1 1.3 %collective-permute-start.18 = (f32[512,128]{1,0:T(8,128)S(1)}, f32[512,128]{1,0:T(8,128)S(1)}, u32[]{:S(2)}, u32[]{:S(2)}) collective-permute-start(f32[512,128]{1,0:T(8,128)S(1)} %shard_map.125.refs_7_), channel_id=1, source_target_pairs={{8,0},{12,4},{9,1},{13,5},{10,2},{14,6},{11,3},{15,7}} | collective-permute-start | bytes 786440 | tf_op jit(solution)/shard_map/ppermute | solution.py:445
  72.4 4.0 %shard_map.126 = (bf16[512,2048]{1,0:T(8,128)(2,1)}, f32[512,512]{1,0:T(8,128)S(1)}, f32[512,512]{1,0:T(8,128)S(1)}) custom-call(s32[1]{0:T(128)} %bitcast.member_ref, s32[1]{0:T(128)} %bitcast.1.pair_ref, bf16[512,2048]{1,0:T(8,128)(2,1)S(1)} %copy-done, bf16[512,2048]{1,0:T(8,128)(2,1)S(1)} %copy-done.1, ...), custom_call_target="tpu_custom_call", output_to_operand_aliasing={{0}: (8, {})} | custom-call | flops 4300000256 | bytes 10750000 | tf_op jit(solution)/shard_map/pallas_call | solution.py:353
  77.6 12.1 %collective-permute-done.18.refs_4_ = f32[512,128]{1,0:T(8,128)S(1)} collective-permute-done((f32[512,128]{1,0:T(8,128)S(1)}, f32[512,128]{1,0:T(8,128)S(1)}, u32[]{:S(2)}, u32[]{:S(2)}) %collective-permute-start.18) | collective-permute-done | bytes 262176 | tf_op jit(solution)/shard_map/ppermute | solution.py:445
  90.1 3.9 %shard_map.129 = (bf16[512,2048]{1,0:T(8,128)(2,1)}, f32[512,512]{1,0:T(8,128)S(1)}, f32[512,512]{1,0:T(8,128)S(1)}) custom-call(s32[1]{0:T(128)} %bitcast.member_ref, s32[1]{0:T(128)} %bitcast.1.pair_ref, bf16[512,2048]{1,0:T(8,128)(2,1)S(1)} %copy-done, bf16[512,2048]{1,0:T(8,128)(2,1)S(1)} %copy-done.1, ...), custom_call_target="tpu_custom_call", output_to_operand_aliasing={{0}: (8, {})} | custom-call | flops 4300000256 | bytes 10750000 | tf_op jit(solution)/shard_map/pallas_call | solution.py:353
  94.2 1.8 %collective-permute-start.21 = (f32[512,128]{1,0:T(8,128)S(1)}, f32[512,128]{1,0:T(8,128)S(1)}, u32[]{:S(2)}, u32[]{:S(2)}) collective-permute-start(f32[512,128]{1,0:T(8,128)S(1)} %get-tuple-element.90.refs_6_), channel_id=1, source_target_pairs={{0,4},{4,0},{8,12},{12,8},{16,20},{20,16},{24,28},{28,24},{1,5},{5... | collective-permute-start | bytes 786440 | tf_op jit(solution)/shard_map/ppermute | solution.py:459
  96.0 1.8 %shard_map.131 = (bf16[512,2048]{1,0:T(8,128)(2,1)}, bf16[512,2048]{1,0:T(8,128)(2,1)}) custom-call(s32[1]{0:T(128)} %bitcast.member_ref, s32[1]{0:T(128)} %bitcast.1.pair_ref, f32[512,512]{1,0:T(8,128)S(1)} %get-tuple-element.81.refs_2_.refs_0_, f32[512,512]{1,0:T(8,128)S(1)} %get-tuple-element.94.refs_1_, bf16[512,2048]{1,0:T(8,128)(2,1)S(1)} %copy-done.1, ...), custom_call_target="tpu_custom_call" | custom-call | flops 2000000000 | bytes 5000000 | tf_op jit(solution)/shard_map/pallas_call | solution.py:353
  97.7 1.7 %shard_map.132 = (bf16[512,2048]{1,0:T(8,128)(2,1)}, bf16[512,2048]{1,0:T(8,128)(2,1)}) custom-call(s32[1]{0:T(128)} %bitcast.member_ref, s32[1]{0:T(128)} %bitcast.1.pair_ref, f32[512,512]{1,0:T(8,128)S(1)} %get-tuple-element.85.refs_3_.refs_0_, f32[512,512]{1,0:T(8,128)S(1)} %get-tuple-element.92.refs_1_, ...), custom_call_target="tpu_custom_call", output_to_operand_aliasing={{0}: (8, {}), {1}: (9, {})} | custom-call | flops 2000000000 | bytes 5000000 | tf_op jit(solution)/shard_map/pallas_call | solution.py:353
  99.5 1.7 %shard_map.133 = (bf16[512,2048]{1,0:T(8,128)(2,1)}, bf16[512,2048]{1,0:T(8,128)(2,1)}) custom-call(s32[1]{0:T(128)} %bitcast.member_ref, s32[1]{0:T(128)} %bitcast.1.pair_ref, f32[512,512]{1,0:T(8,128)S(1)} %get-tuple-element.83.refs_3_.refs_0_, f32[512,512]{1,0:T(8,128)S(1)} %get-tuple-element.91.refs_1_, ...), custom_call_target="tpu_custom_call", output_to_operand_aliasing={{0}: (8, {}), {1}: (9, {})} | custom-call | flops 2000000000 | bytes 5000000 | tf_op jit(solution)/shard_map/pallas_call | solution.py:353
  101.9 1.7 %shard_map.134 = (bf16[512,2048]{1,0:T(8,128)(2,1)}, bf16[512,2048]{1,0:T(8,128)(2,1)}) custom-call(s32[1]{0:T(128)} %bitcast.member_ref, s32[1]{0:T(128)} %bitcast.1.pair_ref, f32[512,512]{1,0:T(8,128)S(1)} %get-tuple-element.88.refs_5_.refs_0_, f32[512,512]{1,0:T(8,128)S(1)} %get-tuple-element.89.refs_1_, ...), custom_call_target="tpu_custom_call", output_to_operand_aliasing={{0}: (8, {}), {1}: (9, {})} | custom-call | flops 2000000000 | bytes 5000000 | tf_op jit(solution)/shard_map/pallas_call | solution.py:353
  (73 shorter events, 20.4 us)
Async XLA Ops:
  0.7 5.9 %copy-start.1 = (bf16[512,2048]{1,0:T(8,128)(2,1)S(1)}, bf16[512,2048]{1,0:T(8,128)(2,1)}, u32[]{:S(2)}) copy-start(bf16[512,2048]{1,0:T(8,128)(2,1)} %refs_2_.31) | copy-start | bytes 6291460
  3.6 10.4 %collective-permute-start = (f32[520,128]{1,0:T(8,128)}, f32[520,128]{1,0:T(8,128)S(1)}, u32[]{:S(2)}, u32[]{:S(2)}) collective-permute-start(f32[520,128]{1,0:T(8,128)} %get-tuple-element.55), channel_id=1, source_target_pairs={{0,4},{4,0},{8,12},{12,8},{16,20},{20,16},{24,28},{28,24},{1,5},{5... | collective-permute-start | bytes 798728 | tf_op jit(solution)/shard_map/ppermute | solution.py:413
  6.6 1.6 %copy-start.2 = (bf16[512,2048]{1,0:T(8,128)(2,1)S(1)}, bf16[512,2048]{1,0:T(8,128)(2,1)}, u32[]{:S(2)}) copy-start(bf16[512,2048]{1,0:T(8,128)(2,1)} %refs_3_.15) | copy-start | bytes 6291460
  8.2 0.8 copy-start.5
  8.9 1.6 %copy-start.3 = (bf16[512,2048]{1,0:T(8,128)(2,1)S(1)}, bf16[512,2048]{1,0:T(8,128)(2,1)}, u32[]{:S(2)}) copy-start(bf16[512,2048]{1,0:T(8,128)(2,1)} %refs_3_.15) | copy-start | bytes 6291460
  9.8 11.2 %collective-permute-start.2 = (f32[520,128]{1,0:T(8,128)S(1)}, f32[520,128]{1,0:T(8,128)S(1)}, u32[]{:S(2)}, u32[]{:S(2)}) collective-permute-start(f32[520,128]{1,0:T(8,128)S(1)} %shard_map.95.refs_3_), channel_id=1, source_target_pairs={{0,4},{4,0},{8,12},{12,8},{16,20},{20,16},{24,28},{28,24},{1,5},{5... | collective-permute-start | bytes 798728 | tf_op jit(solution)/shard_map/ppermute | solution.py:416
  14.1 5.0 %copy-start = (bf16[512,2048]{1,0:T(8,128)(2,1)S(1)}, bf16[512,2048]{1,0:T(8,128)(2,1)}, u32[]{:S(2)}) copy-start(bf16[512,2048]{1,0:T(8,128)(2,1)} %refs_0_.23) | copy-start | bytes 6291460
  14.1 8.5 %collective-permute-start.1 = (f32[512,128]{1,0:T(8,128)S(1)}, f32[512,128]{1,0:T(8,128)S(1)}, u32[]{:S(2)}, u32[]{:S(2)}) collective-permute-start(f32[512,128]{1,0:T(8,128)S(1)} %shard_map.97.refs_3_), channel_id=1, source_target_pairs={{0,8},{4,12},{1,9},{5,13},{2,10},{6,14},{3,11},{7,15}} | collective-permute-start | bytes 786440 | tf_op jit(solution)/shard_map/ppermute | solution.py:445
  21.0 6.6 %collective-permute-start.4 = (f32[512,128]{1,0:T(8,128)S(1)}, f32[512,128]{1,0:T(8,128)S(1)}, u32[]{:S(2)}, u32[]{:S(2)}) collective-permute-start(f32[512,128]{1,0:T(8,128)S(1)} %shard_map.100.refs_3_), channel_id=1, source_target_pairs={{0,8},{4,12},{1,9},{5,13},{2,10},{6,14},{3,11},{7,15}} | collective-permute-start | bytes 786440 | tf_op jit(solution)/shard_map/ppermute | solution.py:445
  22.6 5.7 %collective-permute-start.3 = (f32[512,128]{1,0:T(8,128)S(1)}, f32[512,128]{1,0:T(8,128)S(1)}, u32[]{:S(2)}, u32[]{:S(2)}) collective-permute-start(f32[512,128]{1,0:T(8,128)S(1)} %shard_map.101.refs_4_), channel_id=1, source_target_pairs={{8,16},{12,20},{9,17},{13,21},{10,18},{14,22},{11,19},{15,23}} | collective-permute-start | bytes 786440 | tf_op jit(solution)/shard_map/ppermute | solution.py:445
  25.3 3.8 %copy-start.6 = (f32[16,512]{1,0:T(8,128)S(1)}, f32[16,512]{1,0:T(8,128)}, u32[]{:S(2)}) copy-start(f32[16,512]{1,0:T(8,128)} %get-tuple-element.54.refs_2_.refs_3_.refs_4_) | copy-start | bytes 98308
  27.7 3.3 %collective-permute-start.5 = (f32[512,128]{1,0:T(8,128)S(1)}, f32[512,128]{1,0:T(8,128)S(1)}, u32[]{:S(2)}, u32[]{:S(2)}) collective-permute-start(f32[512,128]{1,0:T(8,128)S(1)} %shard_map.103.refs_3_), channel_id=1, source_target_pairs={{8,16},{12,20},{9,17},{13,21},{10,18},{14,22},{11,19},{15,23}} | collective-permute-start | bytes 786440 | tf_op jit(solution)/shard_map/ppermute | solution.py:445
  28.4 3.4 %collective-permute-start.7 = (f32[512,128]{1,0:T(8,128)S(1)}, f32[512,128]{1,0:T(8,128)S(1)}, u32[]{:S(2)}, u32[]{:S(2)}) collective-permute-start(f32[512,128]{1,0:T(8,128)S(1)} %shard_map.104.refs_4_), channel_id=1, source_target_pairs={{16,24},{20,28},{17,25},{21,29},{18,26},{22,30},{19,27},{23,31}} | collective-permute-start | bytes 786440 | tf_op jit(solution)/shard_map/ppermute | solution.py:445
  31.0 5.5 %collective-permute-start.6 = (f32[512,128]{1,0:T(8,128)S(1)}, f32[512,128]{1,0:T(8,128)S(1)}, u32[]{:S(2)}, u32[]{:S(2)}) collective-permute-start(f32[512,128]{1,0:T(8,128)S(1)} %shard_map.106.refs_5_), channel_id=1, source_target_pairs={{16,24},{20,28},{17,25},{21,29},{18,26},{22,30},{19,27},{23,31}} | collective-permute-start | bytes 786440 | tf_op jit(solution)/shard_map/ppermute | solution.py:445
  31.8 3.5 %copy-start.4 = (bf16[512,2048]{1,0:T(8,128)(2,1)S(1)}, bf16[512,2048]{1,0:T(8,128)(2,1)}, u32[]{:S(2)}) copy-start(bf16[512,2048]{1,0:T(8,128)(2,1)} %refs_1_.35) | copy-start | bytes 6291460
  31.8 3.5 %copy-start.7 = (f32[2048]{0:T(1024)S(1)}, f32[2048]{0:T(1024)}, u32[]{:S(2)}) copy-start(f32[2048]{0:T(1024)} %param.10) | copy-start | bytes 24580
  31.9 7.9 %collective-permute-start.9 = (f32[512,128]{1,0:T(8,128)S(1)}, f32[512,128]{1,0:T(8,128)S(1)}, u32[]{:S(2)}, u32[]{:S(2)}) collective-permute-start(f32[512,128]{1,0:T(8,128)S(1)} %get-tuple-element.57.refs_4_), channel_id=1, source_target_pairs={{0,4},{4,0},{8,12},{12,8},{16,20},{20,16},{24,28},{28,24},{1,5},{5... | collective-permute-start | bytes 786440 | tf_op jit(solution)/shard_map/ppermute | solution.py:459
  36.6 7.6 %collective-permute-start.8 = (f32[512,128]{1,0:T(8,128)S(1)}, f32[512,128]{1,0:T(8,128)S(1)}, u32[]{:S(2)}, u32[]{:S(2)}) collective-permute-start(f32[512,128]{1,0:T(8,128)S(1)} %get-tuple-element.60.refs_7_), channel_id=1, source_target_pairs={{0,4},{4,0},{8,12},{12,8},{16,20},{20,16},{24,28},{28,24},{1,5},{5... | collective-permute-start | bytes 786440 | tf_op jit(solution)/shard_map/ppermute | solution.py:459
  45.3 1.8 %collective-permute-start.12 = (f32[8,512]{1,0:T(8,128)S(1)}, f32[8,512]{1,0:T(8,128)S(1)}, u32[]{:S(2)}, u32[]{:S(2)}) collective-permute-start(f32[8,512]{1,0:T(8,128)S(1)} %get-tuple-element.64.refs_5_), channel_id=1, source_target_pairs={{0,3},{1,0},{2,1},{3,2},{4,7},{5,4},{6,5},{7,6},{8,11},{9,8},{10,9... | collective-permute-start | bytes 49160 | tf_op jit(solution)/shard_map/ppermute | solution.py:531
  45.3 3.8 %collective-permute-start.11 = (f32[8,512]{1,0:T(8,128)S(1)}, f32[8,512]{1,0:T(8,128)S(1)}, u32[]{:S(2)}, u32[]{:S(2)}) collective-permute-start(f32[8,512]{1,0:T(8,128)S(1)} %get-tuple-element.64.refs_5_), channel_id=1, source_target_pairs={{0,2},{1,3},{2,0},{3,1},{4,6},{5,7},{6,4},{7,5},{8,10},{9,11},{10,... | collective-permute-start | bytes 49160 | tf_op jit(solution)/shard_map/ppermute | solution.py:531
  46.9 3.2 %collective-permute-start.10 = (f32[8,512]{1,0:T(8,128)S(1)}, f32[8,512]{1,0:T(8,128)S(1)}, u32[]{:S(2)}, u32[]{:S(2)}) collective-permute-start(f32[8,512]{1,0:T(8,128)S(1)} %get-tuple-element.64.refs_5_), channel_id=1, source_target_pairs={{0,1},{1,2},{2,3},{3,0},{4,5},{5,6},{6,7},{7,4},{8,9},{9,10},{10,1... | collective-permute-start | bytes 49160 | tf_op jit(solution)/shard_map/ppermute | solution.py:531
  51.7 7.3 %collective-permute-start.13 = (f32[520,128]{1,0:T(8,128)S(1)}, f32[520,128]{1,0:T(8,128)S(1)}, u32[]{:S(2)}, u32[]{:S(2)}) collective-permute-start(f32[520,128]{1,0:T(8,128)S(1)} %get-tuple-element.69.refs_10_), channel_id=1, source_target_pairs={{0,4},{4,0},{8,12},{12,8},{16,20},{20,16},{24,28},{28,24},{1,5},{5... | collective-permute-start | bytes 798728 | tf_op jit(solution)/shard_map/ppermute | solution.py:413
  58.4 6.6 %collective-permute-start.15 = (f32[520,128]{1,0:T(8,128)S(1)}, f32[520,128]{1,0:T(8,128)S(1)}, u32[]{:S(2)}, u32[]{:S(2)}) collective-permute-start(f32[520,128]{1,0:T(8,128)S(1)} %shard_map.118.refs_2_), channel_id=1, source_target_pairs={{0,4},{4,0},{8,12},{12,8},{16,20},{20,16},{24,28},{28,24},{1,5},{5... | collective-permute-start | bytes 798728 | tf_op jit(solution)/shard_map/ppermute | solution.py:416
  59.0 6.7 %collective-permute-start.14 = (f32[512,128]{1,0:T(8,128)S(1)}, f32[512,128]{1,0:T(8,128)S(1)}, u32[]{:S(2)}, u32[]{:S(2)}) collective-permute-start(f32[512,128]{1,0:T(8,128)S(1)} %shard_map.119.refs_6_), channel_id=1, source_target_pairs={{24,16},{28,20},{25,17},{29,21},{26,18},{30,22},{27,19},{31,23}} | collective-permute-start | bytes 786440 | tf_op jit(solution)/shard_map/ppermute | solution.py:445
  65.0 5.4 %collective-permute-start.17 = (f32[512,128]{1,0:T(8,128)S(1)}, f32[512,128]{1,0:T(8,128)S(1)}, u32[]{:S(2)}, u32[]{:S(2)}) collective-permute-start(f32[512,128]{1,0:T(8,128)S(1)} %shard_map.121.refs_3_), channel_id=1, source_target_pairs={{24,16},{28,20},{25,17},{29,21},{26,18},{30,22},{27,19},{31,23}} | collective-permute-start | bytes 786440 | tf_op jit(solution)/shard_map/ppermute | solution.py:445
  65.7 5.3 %collective-permute-start.16 = (f32[512,128]{1,0:T(8,128)S(1)}, f32[512,128]{1,0:T(8,128)S(1)}, u32[]{:S(2)}, u32[]{:S(2)}) collective-permute-start(f32[512,128]{1,0:T(8,128)S(1)} %shard_map.122.refs_7_), channel_id=1, source_target_pairs={{16,8},{20,12},{17,9},{21,13},{18,10},{22,14},{19,11},{23,15}} | collective-permute-start | bytes 786440 | tf_op jit(solution)/shard_map/ppermute | solution.py:445
  70.4 6.0 %collective-permute-start.19 = (f32[512,128]{1,0:T(8,128)S(1)}, f32[512,128]{1,0:T(8,128)S(1)}, u32[]{:S(2)}, u32[]{:S(2)}) collective-permute-start(f32[512,128]{1,0:T(8,128)S(1)} %shard_map.124.refs_3_), channel_id=1, source_target_pairs={{16,8},{20,12},{17,9},{21,13},{18,10},{22,14},{19,11},{23,15}} | collective-permute-start | bytes 786440 | tf_op jit(solution)/shard_map/ppermute | solution.py:445
  71.1 18.6 %collective-permute-start.18 = (f32[512,128]{1,0:T(8,128)S(1)}, f32[512,128]{1,0:T(8,128)S(1)}, u32[]{:S(2)}, u32[]{:S(2)}) collective-permute-start(f32[512,128]{1,0:T(8,128)S(1)} %shard_map.125.refs_7_), channel_id=1, source_target_pairs={{8,0},{12,4},{9,1},{13,5},{10,2},{14,6},{11,3},{15,7}} | collective-permute-start | bytes 786440 | tf_op jit(solution)/shard_map/ppermute | solution.py:445
  76.3 17.7 %collective-permute-start.20 = (f32[512,128]{1,0:T(8,128)S(1)}, f32[512,128]{1,0:T(8,128)S(1)}, u32[]{:S(2)}, u32[]{:S(2)}) collective-permute-start(f32[512,128]{1,0:T(8,128)S(1)} %shard_map.127.refs_5_), channel_id=1, source_target_pairs={{8,0},{12,4},{9,1},{13,5},{10,2},{14,6},{11,3},{15,7}} | collective-permute-start | bytes 786440 | tf_op jit(solution)/shard_map/ppermute | solution.py:445
  89.8 9.7 %collective-permute-start.22 = (f32[512,128]{1,0:T(8,128)S(1)}, f32[512,128]{1,0:T(8,128)S(1)}, u32[]{:S(2)}, u32[]{:S(2)}) collective-permute-start(f32[512,128]{1,0:T(8,128)S(1)} %get-tuple-element.86.refs_7_), channel_id=1, source_target_pairs={{0,4},{4,0},{8,12},{12,8},{16,20},{20,16},{24,28},{28,24},{1,5},{5... | collective-permute-start | bytes 786440 | tf_op jit(solution)/shard_map/ppermute | solution.py:459
  94.2 7.7 %collective-permute-start.21 = (f32[512,128]{1,0:T(8,128)S(1)}, f32[512,128]{1,0:T(8,128)S(1)}, u32[]{:S(2)}, u32[]{:S(2)}) collective-permute-start(f32[512,128]{1,0:T(8,128)S(1)} %get-tuple-element.90.refs_6_), channel_id=1, source_target_pairs={{0,4},{4,0},{8,12},{12,8},{16,20},{20,16},{24,28},{28,24},{1,5},{5... | collective-permute-start | bytes 786440 | tf_op jit(solution)/shard_map/ppermute | solution.py:459
where the time goes:
time: 104 us
  Pallas kernels  47.8 us (46%)
  waiting for transfers between devices  26.7 us (26%)
  starting transfers between devices  25 us (24%)
  local copies, waits for them, and re-layouts  3.02 us (3%)
  between operations  1.06 us (1%)
    pallas_call x42, Pallas kernels, run(): pl.pallas_call(body, out_shape=[shape for shape, _ in outs], grid_spec=pl...  47.8 us
    ppermute x12, waiting for transfers between devices, chain(): arrived[c, p + 1] = lax.ppermute(value, 'seq', pairs)  14.5 us
    ppermute x12, starting transfers between devices, chain(): arrived[c, p + 1] = lax.ppermute(value, 'seq', pairs)  13.8 us
    ppermute x4, waiting for transfers between devices, chain(): theirs.append(lax.ppermute(send, 'seq', swap))  5.42 us
    ppermute x2, starting transfers between devices, exchange(): received.append(lax.ppermute(sends[0], 'seq', swap))  4.46 us
    ppermute x4, starting transfers between devices, chain(): theirs.append(lax.ppermute(send, 'seq', swap))  4.32 us
    unnamed x16, local copies, waits for them, and re-layouts  3.02 us
    ppermute x3, waiting for transfers between devices, on_device(): lax.ppermute(sums, 'head', [(i, (i + k) % head_count) for i in range(head...  2.96 us
  transfers between devices with their start and end apart: 23, of which 9 were waited for; matrix products, arithmetic and copies ran while one was open for 0% of the time, Pallas kernels for 39%

commit v1 on v0

--- a/solution.py
+++ b/solution.py
@@ -56,9 +56,8 @@
 
 
 def outer_sum(left, scale_row, right):
-    scaled = jnp.transpose(left.astype(f32)) * scale_row
-    high, low = halves(scaled)
-    return dot(high, right) + dot(low, right)
+    scaled = jnp.transpose(left).astype(f32) * scale_row
+    return dot(scaled.astype(bf16), right)
 
 
 def cols(j):
@@ -66,10 +65,10 @@
 
 
 class Part:
-    def __init__(self, first, count, slot, group_heads):
+    def __init__(self, first, count, slot, group_heads, per_step=2):
         self.first, self.count, self.slot, self.group_heads = first, count, slot, group_heads
-        self.steps = 2 if count % 4 == 0 else 1
-        self.per_step = count // self.steps
+        self.per_step = per_step if count % per_step == 0 else 1
+        self.steps = count // self.per_step
 
     def group(self, info):
         return info[0][0] if self.slot == "mine" else 1 - info[0][0]
@@ -98,9 +97,12 @@
     read, refs = values
     if len(refs) == 1:
         return read(refs[0], at_head(o))
-    found = read(refs[0], cols(j))
-    for step in range(1, part.steps):
-        found = jnp.where(pl.program_id(0) == step, read(refs[step], cols(j)), found)
+    size = part.count // len(refs)
+    found = None
+    for step in range(part.steps):
+        index = step * part.per_step + j
+        here = read(refs[index // size], cols(index % size))
+        found = here if found is None else jnp.where(pl.program_id(0) == step, here, found)
     return found
 
 
@@ -166,10 +168,9 @@
 
     def head(o, j):
         lead = jnp.exp(column(part.row(cumul_ref, info, o)))
-        high, low = halves(state_ref[at_head(o), :])
         at = part.wide_cols(info, o)
-        query = query_ref[:, at]
-        out = inner_ref[:, at_head(offset + o)] + lead * (dot(query, high) + dot(query, low))
+        state = state_ref[at_head(o), :].astype(bf16)
+        out = inner_ref[:, at_head(offset + o)] + lead * dot(query_ref[:, at], state)
         out_ref[:, at_head(o)] = out
         square_ref[...] += out * out
         product_ref[...] += cot_ref[:, at].astype(f32) * gain_ref[:, at] * out
@@ -212,17 +213,18 @@
     part.each(head)
 
 
-def backward_kernel(part, info, query_ref, key_ref, value_ref, grad_ref, cumul_ref, *refs):
-    states, (grad_query_ref, inner_key_ref, inner_value_ref) = refs[:-3], refs[-3:]
-
+def backward_kernel(
+    part, offset, state_offset, info, query_ref, key_ref, value_ref, grad_ref, cumul_ref, state_ref,
+    grad_query_ref, inner_key_ref, inner_value_ref,
+):
     def head(o, j):
         row = part.row(cumul_ref, info, o)
         col = column(row)
         at = part.wide_cols(info, o)
         query, key = query_ref[:, at], key_ref[:, at]
-        value, grad = value_ref[:, at], grad_ref[:, at_head(o)]
-        high, low = halves(chosen(part, (lambda ref, at: ref[at, :], states), o, j))
-        outer = jnp.exp(col) * (dot(grad, high, NT) + dot(grad, low, NT))
+        value, grad = value_ref[:, at], grad_ref[:, at_head(offset + o)]
+        state = state_ref[at_head(state_offset + o), :].astype(bf16)
+        outer = jnp.exp(col) * dot(grad, state, NT)
         for top in range(0, BLOCK, TILE):
             end = top + TILE
             scores = dot(key[top:end], query[top:], NT)
@@ -234,8 +236,8 @@
             decays = jnp.exp(jnp.where(causal, spread, -1e30))
             weights = (scores * decays).astype(bf16)
             grad_weights = (grad_scores * decays).astype(bf16)
-            inner_value_ref[top:end, at_head(o)] = dot(weights, grad[top:])
-            inner_key_ref[top:end, at_head(o)] = dot(grad_weights, query[top:])
+            inner_value_ref[top:end, at_head(o)] = dot(weights, grad[top:]).astype(bf16)
+            inner_key_ref[top:end, at_head(o)] = dot(grad_weights, query[top:]).astype(bf16)
             inner_query = dot(grad_weights, key[top:end], TN)
             outer = inner_query + outer if top == 0 else jnp.concatenate(
                 [outer[:top], outer[top:] + inner_query], axis=0
@@ -245,21 +247,20 @@
     part.each(head)
 
 
-def final_kernel(
-    part, info, inner_key_ref, inner_value_ref, key_ref, value_ref, cumul_ref, state_ref,
-    grad_key_ref, grad_value_ref,
-):
+def final_kernel(part, held, info, *refs):
+    inner_keys, inner_values, refs = refs[:held], refs[held:2 * held], refs[2 * held:]
+    key_ref, value_ref, cumul_ref, state_ref, grad_key_ref, grad_value_ref = refs
+
     def head(o, j):
         trail = column(trail_row(part.row(cumul_ref, info, o)))
-        high, low = halves(state_ref[at_head(o), :])
+        state = state_ref[at_head(o), :].astype(bf16)
         at = part.wide_cols(info, o)
-        key, value = key_ref[:, at], value_ref[:, at]
+        inner_key = chosen(part, (lambda ref, at: ref[:, at], inner_keys), o, j).astype(f32)
+        inner_value = chosen(part, (lambda ref, at: ref[:, at], inner_values), o, j).astype(f32)
         grad_key_ref[:, cols(j)] = (
-            inner_key_ref[:, at_head(o)] + trail * (dot(value, high, NT) + dot(value, low, NT))
+            inner_key + trail * dot(value_ref[:, at], state, NT)
         ).astype(bf16)
-        grad_value_ref[:, cols(j)] = (
-            inner_value_ref[:, at_head(o)] + trail * (dot(key, high) + dot(key, low))
-        ).astype(bf16)
+        grad_value_ref[:, cols(j)] = (inner_value + trail * dot(key_ref[:, at], state)).astype(bf16)
 
     part.each(head)
 
@@ -389,13 +390,13 @@
         def call(self, kernel, ins, outs, **options):
             return run(functools.partial(kernel, self), self.steps, ins, outs, **options)
 
-    def parts_of(chunks, slot):
+    def parts_of(chunks, slot, per_step=2):
         count = group_heads // chunks
-        return [Calls(c * count, count, slot, group_heads) for c in range(chunks)]
+        return [Calls(c * count, count, slot, group_heads, per_step) for c in range(chunks)]
 
     swap = [(2 * p + m, 2 * p + 1 - m) for p in range(places) for m in (0, 1)]
 
-    def chain(chunks, make_piece, forward, filler, on_mine, on_theirs):
+    def chain(chunks, make_piece, forward, filler, plan, on_mine, on_theirs):
         position = functools.partial(scan_position, places, forward)
         my_parts, their_parts = parts_of(chunks, "mine"), parts_of(chunks, "theirs")
         count = group_heads // chunks
@@ -420,14 +421,18 @@
             sends.append(make_piece(part, last))
             last = () if forward and len(sends) == 1 else (sends[-1],)
         last = exchange(last)
-        if forward:
-            last = exchange(last)
-        rest = [functools.partial(make_piece, part) for part in my_parts]
-        for make in rest[:1] if forward else rest:
-            keeps.append(make(last))
+        for part in my_parts:
+            keeps.append(make_piece(part, last))
             last = (keeps[-1],)
-        if not forward:
-            last = exchange(last)
+        last = exchange(last)
+
+        def fill(slot, last):
+            for _ in range(plan[slot] if slot < len(plan) else 1):
+                if filler:
+                    last = (filler.pop(0)(last),)
+            return last
+
+        last = fill(0, last)
         arrived, mine, theirs, late = {}, [], [], []
         for step in range(chunks + places - 1):
             for p in range(places - 1):
@@ -445,9 +450,6 @@
                 arrived[c, p + 1] = lax.ppermute(value, "seq", pairs)
                 last = (value,)
             last = exchange(last)
-            while len(keeps) < chunks:
-                keeps.append(rest[len(keeps)](last))
-                last = (keeps[-1],)
             c = step + 1 - places
             if c >= 0:
                 ins = [plain(keeps[c]), plain(received[c])]
@@ -463,10 +465,7 @@
                 late.append(functools.partial(on_theirs, c, theirs[c]))
                 if c >= 2:
                     filler.append(late.pop(0))
-                if forward and c >= chunks - 2 and filler:
-                    last = (filler.pop(0)(last),)
-            if filler:
-                last = (filler.pop(0)(last),)
+            last = fill(step + 1, last)
         for work in filler + late:
             last = (work(last),)
         return mine, theirs
@@ -477,6 +476,9 @@
     front_count = group_heads // FORWARD_CHUNKS
     per_back = back_count // front_count
     back_parts = {slot: parts_of(BACKWARD_CHUNKS, slot) for slot in ("mine", "theirs")}
+    thin = min(2 * BACKWARD_CHUNKS, group_heads)
+    per_thin = thin // BACKWARD_CHUNKS
+    thin_parts = {slot: parts_of(thin, slot, 1) for slot in ("mine", "theirs")}
     front_parts = {slot: parts_of(FORWARD_CHUNKS, slot) for slot in ("mine", "theirs")}
 
     def cumul_in():
@@ -521,7 +523,7 @@
         for c in range(BACKWARD_CHUNKS) for slot in ("mine", "theirs")
     ]
     mine, theirs = chain(
-        FORWARD_CHUNKS, forward_piece, True, works,
+        FORWARD_CHUNKS, forward_piece, True, works, (1, 0, 1, 1, 2),
         functools.partial(output_work, "mine"), functools.partial(output_work, "theirs"),
     )
     states = {"mine": mine, "theirs": theirs}
@@ -557,23 +559,26 @@
         return piece
 
     def backward_work(slot, c, after):
-        part, held = back_parts[slot][c], target(grad_queries)
-        ins = [plain(queries), plain(key_vecs), plain(value_vecs), plain(grads[slot, c]), cumul_in()]
-        ins += [plain(states[slot][i]) for i in covered(c)]
-        whole_out, *inner_grads[slot, c] = part.call(
-            backward_kernel, ins,
-            [(whole, part.full_spec()), give(local_of(part.count)), give(local_of(part.count))],
-            after=held + tuple(after), aliases={2 + len(ins): 0} if held else None, cost=4.3,
+        part, held = thin_parts[slot][c], target(grad_queries)
+        chunk, offset = c // per_thin, part.first % back_count
+        ins = [plain(queries), plain(key_vecs), plain(value_vecs), plain(grads[slot, chunk])]
+        ins += [cumul_in(), plain(states[slot][part.first // front_count])]
+        whole_out, *inner_grads[slot, c] = run(
+            functools.partial(backward_kernel, part, offset, part.first % front_count), part.steps, ins,
+            [(whole, part.full_spec())] + [give(local_of(part.count, bf16))] * 2,
+            after=held + tuple(after), aliases={2 + len(ins): 0} if held else None, cost=2.2,
         )
         grad_queries.append(whole_out)
         return inner_grads[slot, c][0]
 
     def final_work(slot, c, before, after):
         part, held = back_parts[slot][c], target(grad_keys) + target(grad_values)
-        ins = [plain(array) for array in (*inner_grads[slot, c], key_vecs, value_vecs)]
-        ins += [cumul_in(), plain(before)]
-        whole_key, whole_value = part.call(
-            final_kernel, ins, [(whole, part.full_spec())] * 2, after=held + tuple(after),
+        thins = [inner_grads[slot, i] for i in range(c * per_thin, (c + 1) * per_thin)]
+        ins = [plain(pair[0]) for pair in thins] + [plain(pair[1]) for pair in thins]
+        ins += [plain(key_vecs), plain(value_vecs), cumul_in(), plain(before)]
+        whole_key, whole_value = run(
+            functools.partial(final_kernel, part, per_thin), part.steps, ins,
+            [(whole, part.full_spec())] * 2, after=held + tuple(after),
             aliases={2 + len(ins): 0, 3 + len(ins): 1} if held else None, cost=2.0,
         )
         grad_keys.append(whole_key)
@@ -582,10 +587,10 @@
 
     works = [
         functools.partial(backward_work, slot, c)
-        for c in range(BACKWARD_CHUNKS) for slot in ("mine", "theirs")
+        for c in range(thin) for slot in ("mine", "theirs")
     ]
     chain(
-        BACKWARD_CHUNKS, backward_piece, False, works,
+        BACKWARD_CHUNKS, backward_piece, False, works, (1, 1, 2, 2, 1, 9),
         functools.partial(final_work, "mine"), functools.partial(final_work, "theirs"),
     )
     return attended[-1], grad_queries[-1], grad_keys[-1], grad_values[-1]

time: 104 us -> 111 us (1.067)
  waiting for transfers between devices: 26.7 us -> 30.6 us
  Pallas kernels: 47.8 us -> 49.9 us
    ppermute x12, waiting for transfers between devices: 14.5 us -> 21.3 us  [chain(): arrived[c, p + 1] = lax.ppermute(value, 'seq', pairs)]
    ppermute x2, waiting for transfers between devices: 2.67 us -> 0.01 us  [exchange(): received.append(lax.ppermute(sends[0], 'seq', swap))]
    pallas_call x42 -> x46, Pallas kernels: 47.8 us -> 49.9 us  [run(): pl.pallas_call(body, out_shape=[shape for shape, _ in outs], grid_spec=pl...]
    ppermute x12, starting transfers between devices: 13.8 us -> 15.2 us  [chain(): arrived[c, p + 1] = lax.ppermute(value, 'seq', pairs)]
    ppermute x4, starting transfers between devices: 4.32 us -> 2.92 us  [chain(): theirs.append(lax.ppermute(send, 'seq', swap))]
where the time goes in v1:
time: 111 us; the launch traced here: 110 us
  Pallas kernels  49.9 us (45%)
  waiting for transfers between devices  30.6 us (28%)
  starting transfers between devices  25 us (23%)
  local copies, waits for them, and re-layouts  3.81 us (3%)
    pallas_call x46, Pallas kernels, run(): pl.pallas_call(body, out_shape=[shape for shape, _ in outs], grid_spec=pl...  49.9 us
    ppermute x12, waiting for transfers between devices, chain(): arrived[c, p + 1] = lax.ppermute(value, 'seq', pairs)  21.3 us
    ppermute x12, starting transfers between devices, chain(): arrived[c, p + 1] = lax.ppermute(value, 'seq', pairs)  15.2 us
    ppermute x4, waiting for transfers between devices, chain(): theirs.append(lax.ppermute(send, 'seq', swap))  5.35 us
    unnamed x16, local copies, waits for them, and re-layouts  3.81 us
    ppermute x2, starting transfers between devices, exchange(): received.append(lax.ppermute(sends[0], 'seq', swap))  3.37 us
    ppermute x3, waiting for transfers between devices, on_device(): lax.ppermute(sums, 'head', [(i, (i + k) % head_count) for i in range(head...  2.96 us
    ppermute x4, starting transfers between devices, chain(): theirs.append(lax.ppermute(send, 'seq', swap))  2.92 us
  transfers between devices with their start and end apart: 23, of which 9 were waited for; matrix products, arithmetic and copies ran while one was open for 0% of the time, Pallas kernels for 39%

profile of v1, /device:TPU:0, one launch (start us, length us, event | category | flops | bytes accessed | tf_op | source)
XLA Modules:
  0.0 110.5 jit_solution(2554659361338628515)
XLA Ops:
  0.7 2.8 %shard_map.93 = (f32[520,128]{1,0:T(8,128)}, f32[16,512]{1,0:T(8,128)}) custom-call(s32[1]{0:T(128)} %bitcast.member_ref, s32[1]{0:T(128)} %bitcast.1.pair_ref, bf16[512,2048]{1,0:T(8,128)(2,1)} %refs_4_.7, bf16[512,2048]{1,0:T(8,128)(2,1)} %refs_5_.7, f32[16,512]{1,0:T(8,128)} %bitcast.12), custom_call_target="tpu_custom_call" | custom-call | flops 50000000 | bytes 125000 | tf_op jit(solution)/shard_map/pallas_call | solution.py:354
  3.5 3.0 %collective-permute-start = (f32[520,128]{1,0:T(8,128)}, f32[520,128]{1,0:T(8,128)S(1)}, u32[]{:S(2)}, u32[]{:S(2)}) collective-permute-start(f32[520,128]{1,0:T(8,128)} %get-tuple-element.67), channel_id=1, source_target_pairs={{0,4},{4,0},{8,12},{12,8},{16,20},{20,16},{24,28},{28,24},{1,5},{5... | collective-permute-start | bytes 798728 | tf_op jit(solution)/shard_map/ppermute | solution.py:414
  6.5 1.6 %copy-done.2 = bf16[512,2048]{1,0:T(8,128)(2,1)S(1)} copy-done((bf16[512,2048]{1,0:T(8,128)(2,1)S(1)}, bf16[512,2048]{1,0:T(8,128)(2,1)}, u32[]{:S(2)}) %copy-start.2) | copy-done | bytes 2097176
  12.3 1.9 %shard_map.98.refs_2_.refs_0_ = f32[512,512]{1,0:T(8,128)S(1)} custom-call(s32[1]{0:T(128)} %bitcast.member_ref, s32[1]{0:T(128)} %bitcast.1.pair_ref, bf16[512,2048]{1,0:T(8,128)(2,1)S(1)} %copy-done, bf16[512,2048]{1,0:T(8,128)(2,1)S(1)} %copy-done.1, bf16[512,2048]{1,0:T(8,128)(2,1)S(1)} %copy-done.3, f32[16,512]{1,0:T(8,128)S(1)} %copy-done.5, ...), custom_call_target="tpu_custom_call" | custom-call | flops 100000000 | bytes 250000 | tf_op jit(solution)/shard_map/pallas_call | solution.py:354
  14.3 3.5 %collective-permute-start.1 = (f32[512,128]{1,0:T(8,128)S(1)}, f32[512,128]{1,0:T(8,128)S(1)}, u32[]{:S(2)}, u32[]{:S(2)}) collective-permute-start(f32[512,128]{1,0:T(8,128)S(1)} %shard_map.99.refs_2_), channel_id=1, source_target_pairs={{0,8},{4,12},{1,9},{5,13},{2,10},{6,14},{3,11},{7,15}} | collective-permute-start | bytes 786440 | tf_op jit(solution)/shard_map/ppermute | solution.py:450
  18.8 3.6 %collective-permute-start.4 = (f32[512,128]{1,0:T(8,128)S(1)}, f32[512,128]{1,0:T(8,128)S(1)}, u32[]{:S(2)}, u32[]{:S(2)}) collective-permute-start(f32[512,128]{1,0:T(8,128)S(1)} %shard_map.100.refs_3_), channel_id=1, source_target_pairs={{0,8},{4,12},{1,9},{5,13},{2,10},{6,14},{3,11},{7,15}} | collective-permute-start | bytes 786440 | tf_op jit(solution)/shard_map/ppermute | solution.py:450
  22.5 2.0 %collective-permute-done.1.refs_2_ = f32[512,128]{1,0:T(8,128)S(1)} collective-permute-done((f32[512,128]{1,0:T(8,128)S(1)}, f32[512,128]{1,0:T(8,128)S(1)}, u32[]{:S(2)}, u32[]{:S(2)}) %collective-permute-start.1) | collective-permute-done | bytes 262176 | tf_op jit(solution)/shard_map/ppermute | solution.py:450
  25.2 1.9 %shard_map.102.refs_3_.refs_0_ = f32[512,512]{1,0:T(8,128)S(1)} custom-call(s32[1]{0:T(128)} %bitcast.member_ref, s32[1]{0:T(128)} %bitcast.1.pair_ref, bf16[512,2048]{1,0:T(8,128)(2,1)S(1)} %copy-done, bf16[512,2048]{1,0:T(8,128)(2,1)S(1)} %copy-done.1, bf16[512,2048]{1,0:T(8,128)(2,1)S(1)} %copy-done.3, f32[16,512]{1,0:T(8,128)S(1)} %copy-done.5, ...), custom_call_target="tpu_custom_call" | custom-call | flops 2200000000 | bytes 5500000 | tf_op jit(solution)/shard_map/pallas_call | solution.py:354
  30.0 1.9 %shard_map.105.refs_3_.refs_0_ = f32[512,512]{1,0:T(8,128)S(1)} custom-call(s32[1]{0:T(128)} %bitcast.member_ref, s32[1]{0:T(128)} %bitcast.1.pair_ref, bf16[512,2048]{1,0:T(8,128)(2,1)S(1)} %copy-done, bf16[512,2048]{1,0:T(8,128)(2,1)S(1)} %copy-done.1, bf16[512,2048]{1,0:T(8,128)(2,1)S(1)} %copy-done.3, f32[16,512]{1,0:T(8,128)S(1)} %copy-done.6, ...), custom_call_target="tpu_custom_call" | custom-call | flops 2200000000 | bytes 5500000 | tf_op jit(solution)/shard_map/pallas_call | solution.py:354
  33.4 1.9 %shard_map.108.refs_7_.refs_0_ = f32[512,512]{1,0:T(8,128)S(1)} custom-call(s32[1]{0:T(128)} %bitcast.member_ref, s32[1]{0:T(128)} %bitcast.1.pair_ref, bf16[512,2048]{1,0:T(8,128)(2,1)S(1)} %copy-done, bf16[512,2048]{1,0:T(8,128)(2,1)S(1)} %copy-done.1, bf16[512,2048]{1,0:T(8,128)(2,1)S(1)} %copy-done.3, f32[16,512]{1,0:T(8,128)S(1)} %copy-done.6, ...), custom_call_target="tpu_custom_call" | custom-call | flops 2200000000 | bytes 5500000 | tf_op jit(solution)/shard_map/pallas_call | solution.py:354
  36.4 1.6 %collective-permute-start.8 = (f32[512,128]{1,0:T(8,128)S(1)}, f32[512,128]{1,0:T(8,128)S(1)}, u32[]{:S(2)}, u32[]{:S(2)}) collective-permute-start(f32[512,128]{1,0:T(8,128)S(1)} %get-tuple-element.72.refs_7_), channel_id=1, source_target_pairs={{0,4},{4,0},{8,12},{12,8},{16,20},{20,16},{24,28},{28,24},{1,5},{5... | collective-permute-start | bytes 786440 | tf_op jit(solution)/shard_map/ppermute | solution.py:461
  39.0 3.1 %collective-permute-done.9.refs_5_ = f32[512,128]{1,0:T(8,128)S(1)} collective-permute-done((f32[512,128]{1,0:T(8,128)S(1)}, f32[512,128]{1,0:T(8,128)S(1)}, u32[]{:S(2)}, u32[]{:S(2)}) %collective-permute-start.9) | collective-permute-done | bytes 262176 | tf_op jit(solution)/shard_map/ppermute | solution.py:461
  43.1 2.2 %collective-permute-done.8.refs_5_ = f32[512,128]{1,0:T(8,128)S(1)} collective-permute-done((f32[512,128]{1,0:T(8,128)S(1)}, f32[512,128]{1,0:T(8,128)S(1)}, u32[]{:S(2)}, u32[]{:S(2)}) %collective-permute-start.8) | collective-permute-done | bytes 262176 | tf_op jit(solution)/shard_map/ppermute | solution.py:461
  48.1 2.0 %collective-permute-done.11.refs_7_ = f32[8,512]{1,0:T(8,128)S(1)} collective-permute-done((f32[8,512]{1,0:T(8,128)S(1)}, f32[8,512]{1,0:T(8,128)S(1)}, u32[]{:S(2)}, u32[]{:S(2)}) %collective-permute-start.11) | collective-permute-done | bytes 16416 | tf_op jit(solution)/shard_map/ppermute | solution.py:533
  51.1 1.7 %shard_map.114 = (bf16[512,2048]{1,0:T(8,128)(2,1)}, bf16[512,512]{1,0:T(8,128)(2,1)S(1)}, f32[520,128]{1,0:T(8,128)S(1)}) custom-call(s32[1]{0:T(128)} %bitcast.member_ref, s32[1]{0:T(128)} %bitcast.1.pair_ref, f32[512,512]{1,0:T(8,128)S(1)} %get-tuple-element.79.refs_0_, bf16[512,2048]{1,0:T(8,128)(2,1)S(1)} %copy-done.4, f32[1,2048]{1,0:T(1,128)S(1)} %bitcast.8, ...), custom_call_target="tpu_custom_call" | custom-call | flops 2000000000 | bytes 5000000 | tf_op jit(solution)/shard_map/pallas_call | solution.py:354
  53.1 1.7 %shard_map.115 = (bf16[512,2048]{1,0:T(8,128)(2,1)}, bf16[512,512]{1,0:T(8,128)(2,1)S(1)}, f32[520,128]{1,0:T(8,128)S(1)}) custom-call(s32[1]{0:T(128)} %bitcast.member_ref, s32[1]{0:T(128)} %bitcast.1.pair_ref, f32[512,512]{1,0:T(8,128)S(1)} %get-tuple-element.78.refs_0_, bf16[512,2048]{1,0:T(8,128)(2,1)S(1)} %copy-done.4, ...), custom_call_target="tpu_custom_call", output_to_operand_aliasing={{0}: (11, {})} | custom-call | flops 2000000000 | bytes 5000000 | tf_op jit(solution)/shard_map/pallas_call | solution.py:354
  54.8 1.7 %shard_map.116 = (bf16[512,2048]{1,0:T(8,128)(2,1)}, bf16[512,512]{1,0:T(8,128)(2,1)S(1)}, f32[520,128]{1,0:T(8,128)S(1)}) custom-call(s32[1]{0:T(128)} %bitcast.member_ref, s32[1]{0:T(128)} %bitcast.1.pair_ref, f32[512,512]{1,0:T(8,128)S(1)} %get-tuple-element.77.refs_0_, bf16[512,2048]{1,0:T(8,128)(2,1)S(1)} %copy-done.4, ...), custom_call_target="tpu_custom_call", output_to_operand_aliasing={{0}: (11, {})} | custom-call | flops 2000000000 | bytes 5000000 | tf_op jit(solution)/shard_map/pallas_call | solution.py:354
  56.5 1.7 %shard_map.117 = (bf16[512,2048]{1,0:T(8,128)(2,1)}, bf16[512,512]{1,0:T(8,128)(2,1)S(1)}, f32[520,128]{1,0:T(8,128)S(1)}) custom-call(s32[1]{0:T(128)} %bitcast.member_ref, s32[1]{0:T(128)} %bitcast.1.pair_ref, f32[512,512]{1,0:T(8,128)S(1)} %get-tuple-element.73.refs_0_, bf16[512,2048]{1,0:T(8,128)(2,1)S(1)} %copy-done.4, ...), custom_call_target="tpu_custom_call", output_to_operand_aliasing={{0}: (11, {})} | custom-call | flops 2000000000 | bytes 5000000 | tf_op jit(solution)/shard_map/pallas_call | solution.py:354
  58.2 1.7 %collective-permute-start.15 = (f32[520,128]{1,0:T(8,128)S(1)}, f32[520,128]{1,0:T(8,128)S(1)}, u32[]{:S(2)}, u32[]{:S(2)}) collective-permute-start(f32[520,128]{1,0:T(8,128)S(1)} %shard_map.118.refs_6_), channel_id=1, source_target_pairs={{0,4},{4,0},{8,12},{12,8},{16,20},{20,16},{24,28},{28,24},{1,5},{5... | collective-permute-start | bytes 798728 | tf_op jit(solution)/shard_map/ppermute | solution.py:417
  59.9 2.4 %shard_map.119 = (bf16[512,2048]{1,0:T(8,128)(2,1)}, bf16[512,256]{1,0:T(8,128)(2,1)S(1)}, bf16[512,256]{1,0:T(8,128)(2,1)S(1)}) custom-call(s32[1]{0:T(128)} %bitcast.member_ref, s32[1]{0:T(128)} %bitcast.1.pair_ref, bf16[512,2048]{1,0:T(8,128)(2,1)S(1)} %copy-done, bf16[512,2048]{1,0:T(8,128)(2,1)S(1)} %copy-done.1, bf16[512,2048]{1,0:T(8,128)(2,1)S(1)} %copy-done.3, ...), custom_call_target="tpu_custom_call" | custom-call | flops 2200000000 | bytes 5500000 | tf_op jit(solution)/shard_map/pallas_call | solution.py:354
  63.2 2.5 %shard_map.121 = (bf16[512,2048]{1,0:T(8,128)(2,1)}, bf16[512,256]{1,0:T(8,128)(2,1)S(1)}, bf16[512,256]{1,0:T(8,128)(2,1)S(1)}) custom-call(s32[1]{0:T(128)} %bitcast.member_ref, s32[1]{0:T(128)} %bitcast.1.pair_ref, bf16[512,2048]{1,0:T(8,128)(2,1)S(1)} %copy-done, bf16[512,2048]{1,0:T(8,128)(2,1)S(1)} %copy-done.1, ...), custom_call_target="tpu_custom_call", output_to_operand_aliasing={{0}: (8, {})} | custom-call | flops 2200000000 | bytes 5500000 | tf_op jit(solution)/shard_map/pallas_call | solution.py:354
  67.0 2.5 %shard_map.124 = (bf16[512,2048]{1,0:T(8,128)(2,1)}, bf16[512,256]{1,0:T(8,128)(2,1)S(1)}, bf16[512,256]{1,0:T(8,128)(2,1)S(1)}) custom-call(s32[1]{0:T(128)} %bitcast.member_ref, s32[1]{0:T(128)} %bitcast.1.pair_ref, bf16[512,2048]{1,0:T(8,128)(2,1)S(1)} %copy-done, bf16[512,2048]{1,0:T(8,128)(2,1)S(1)} %copy-done.1, ...), custom_call_target="tpu_custom_call", output_to_operand_aliasing={{0}: (8, {})} | custom-call | flops 2200000000 | bytes 5500000 | tf_op jit(solution)/shard_map/pallas_call | solution.py:354
  69.5 2.4 %shard_map.125 = (bf16[512,2048]{1,0:T(8,128)(2,1)}, bf16[512,256]{1,0:T(8,128)(2,1)S(1)}, bf16[512,256]{1,0:T(8,128)(2,1)S(1)}) custom-call(s32[1]{0:T(128)} %bitcast.member_ref, s32[1]{0:T(128)} %bitcast.1.pair_ref, bf16[512,2048]{1,0:T(8,128)(2,1)S(1)} %copy-done, bf16[512,2048]{1,0:T(8,128)(2,1)S(1)} %copy-done.1, ...), custom_call_target="tpu_custom_call", output_to_operand_aliasing={{0}: (8, {})} | custom-call | flops 2200000000 | bytes 5500000 | tf_op jit(solution)/shard_map/pallas_call | solution.py:354
  73.9 2.5 %shard_map.128 = (bf16[512,2048]{1,0:T(8,128)(2,1)}, bf16[512,256]{1,0:T(8,128)(2,1)S(1)}, bf16[512,256]{1,0:T(8,128)(2,1)S(1)}) custom-call(s32[1]{0:T(128)} %bitcast.member_ref, s32[1]{0:T(128)} %bitcast.1.pair_ref, bf16[512,2048]{1,0:T(8,128)(2,1)S(1)} %copy-done, bf16[512,2048]{1,0:T(8,128)(2,1)S(1)} %copy-done.1, ...), custom_call_target="tpu_custom_call", output_to_operand_aliasing={{0}: (8, {})} | custom-call | flops 2200000000 | bytes 5500000 | tf_op jit(solution)/shard_map/pallas_call | solution.py:354
  76.4 2.4 %shard_map.129 = (bf16[512,2048]{1,0:T(8,128)(2,1)}, bf16[512,256]{1,0:T(8,128)(2,1)S(1)}, bf16[512,256]{1,0:T(8,128)(2,1)S(1)}) custom-call(s32[1]{0:T(128)} %bitcast.member_ref, s32[1]{0:T(128)} %bitcast.1.pair_ref, bf16[512,2048]{1,0:T(8,128)(2,1)S(1)} %copy-done, bf16[512,2048]{1,0:T(8,128)(2,1)S(1)} %copy-done.1, ...), custom_call_target="tpu_custom_call", output_to_operand_aliasing={{0}: (8, {})} | custom-call | flops 2200000000 | bytes 5500000 | tf_op jit(solution)/shard_map/pallas_call | solution.py:354
  80.1 16.4 %collective-permute-done.18.refs_4_ = f32[512,128]{1,0:T(8,128)S(1)} collective-permute-done((f32[512,128]{1,0:T(8,128)S(1)}, f32[512,128]{1,0:T(8,128)S(1)}, u32[]{:S(2)}, u32[]{:S(2)}) %collective-permute-start.18) | collective-permute-done | bytes 262176 | tf_op jit(solution)/shard_map/ppermute | solution.py:450
  96.7 2.5 %shard_map.132 = (bf16[512,2048]{1,0:T(8,128)(2,1)}, bf16[512,256]{1,0:T(8,128)(2,1)S(1)}, bf16[512,256]{1,0:T(8,128)(2,1)S(1)}) custom-call(s32[1]{0:T(128)} %bitcast.member_ref, s32[1]{0:T(128)} %bitcast.1.pair_ref, bf16[512,2048]{1,0:T(8,128)(2,1)S(1)} %copy-done, bf16[512,2048]{1,0:T(8,128)(2,1)S(1)} %copy-done.1, ...), custom_call_target="tpu_custom_call", output_to_operand_aliasing={{0}: (8, {})} | custom-call | flops 2200000000 | bytes 5500000 | tf_op jit(solution)/shard_map/pallas_call | solution.py:354
  101.3 2.4 %shard_map.134 = (bf16[512,2048]{1,0:T(8,128)(2,1)}, bf16[512,256]{1,0:T(8,128)(2,1)S(1)}, bf16[512,256]{1,0:T(8,128)(2,1)S(1)}) custom-call(s32[1]{0:T(128)} %bitcast.member_ref, s32[1]{0:T(128)} %bitcast.1.pair_ref, bf16[512,2048]{1,0:T(8,128)(2,1)S(1)} %copy-done, bf16[512,2048]{1,0:T(8,128)(2,1)S(1)} %copy-done.1, ...), custom_call_target="tpu_custom_call", output_to_operand_aliasing={{0}: (8, {})} | custom-call | flops 2200000000 | bytes 5500000 | tf_op jit(solution)/shard_map/pallas_call | solution.py:354
  103.7 1.7 %shard_map.135 = (bf16[512,2048]{1,0:T(8,128)(2,1)}, bf16[512,2048]{1,0:T(8,128)(2,1)}) custom-call(s32[1]{0:T(128)} %bitcast.member_ref, s32[1]{0:T(128)} %bitcast.1.pair_ref, bf16[512,256]{1,0:T(8,128)(2,1)S(1)} %get-tuple-element.93.refs_2_.refs_0_, bf16[512,256]{1,0:T(8,128)(2,1)S(1)} %get-tuple-element.97.refs_7_.refs_1_, ...), custom_call_target="tpu_custom_call" | custom-call | flops 2000000000 | bytes 5000000 | tf_op jit(solution)/shard_map/pallas_call | solution.py:354
  105.4 1.6 %shard_map.136 = (bf16[512,2048]{1,0:T(8,128)(2,1)}, bf16[512,2048]{1,0:T(8,128)(2,1)}) custom-call(s32[1]{0:T(128)} %bitcast.member_ref, s32[1]{0:T(128)} %bitcast.1.pair_ref, bf16[512,256]{1,0:T(8,128)(2,1)S(1)} %get-tuple-element.101.refs_7_.refs_0_, ...), custom_call_target="tpu_custom_call", output_to_operand_aliasing={{0}: (10, {}), {1}: (11, {})} | custom-call | flops 2000000000 | bytes 5000000 | tf_op jit(solution)/shard_map/pallas_call | solution.py:354
  107.0 1.7 %shard_map.137 = (bf16[512,2048]{1,0:T(8,128)(2,1)}, bf16[512,2048]{1,0:T(8,128)(2,1)}) custom-call(s32[1]{0:T(128)} %bitcast.member_ref, s32[1]{0:T(128)} %bitcast.1.pair_ref, bf16[512,256]{1,0:T(8,128)(2,1)S(1)} %get-tuple-element.95.refs_2_.refs_0_, ...), custom_call_target="tpu_custom_call", output_to_operand_aliasing={{0}: (10, {}), {1}: (11, {})} | custom-call | flops 2000000000 | bytes 5000000 | tf_op jit(solution)/shard_map/pallas_call | solution.py:354
  108.8 1.7 %shard_map.138 = (bf16[512,2048]{1,0:T(8,128)(2,1)}, bf16[512,2048]{1,0:T(8,128)(2,1)}) custom-call(s32[1]{0:T(128)} %bitcast.member_ref, s32[1]{0:T(128)} %bitcast.1.pair_ref, bf16[512,256]{1,0:T(8,128)(2,1)S(1)} %get-tuple-element.103.refs_3_.refs_0_, ...), custom_call_target="tpu_custom_call", output_to_operand_aliasing={{0}: (10, {}), {1}: (11, {})} | custom-call | flops 2000000000 | bytes 5000000 | tf_op jit(solution)/shard_map/pallas_call | solution.py:354
  (77 shorter events, 25.2 us)
Async XLA Ops:
  0.7 5.8 %copy-start.1 = (bf16[512,2048]{1,0:T(8,128)(2,1)S(1)}, bf16[512,2048]{1,0:T(8,128)(2,1)}, u32[]{:S(2)}) copy-start(bf16[512,2048]{1,0:T(8,128)(2,1)} %refs_4_.7) | copy-start | bytes 6291460
  3.5 10.8 %collective-permute-start = (f32[520,128]{1,0:T(8,128)}, f32[520,128]{1,0:T(8,128)S(1)}, u32[]{:S(2)}, u32[]{:S(2)}) collective-permute-start(f32[520,128]{1,0:T(8,128)} %get-tuple-element.67), channel_id=1, source_target_pairs={{0,4},{4,0},{8,12},{12,8},{16,20},{20,16},{24,28},{28,24},{1,5},{5... | collective-permute-start | bytes 798728 | tf_op jit(solution)/shard_map/ppermute | solution.py:414
  6.5 1.6 %copy-start.2 = (bf16[512,2048]{1,0:T(8,128)(2,1)S(1)}, bf16[512,2048]{1,0:T(8,128)(2,1)}, u32[]{:S(2)}) copy-start(bf16[512,2048]{1,0:T(8,128)(2,1)} %refs_5_.7) | copy-start | bytes 6291460
  8.0 0.8 copy-start.5
  10.1 1.6 %copy-start = (bf16[512,2048]{1,0:T(8,128)(2,1)S(1)}, bf16[512,2048]{1,0:T(8,128)(2,1)}, u32[]{:S(2)}) copy-start(bf16[512,2048]{1,0:T(8,128)(2,1)} %refs_0_.31) | copy-start | bytes 6291460
  10.1 2.2 %copy-start.3 = (bf16[512,2048]{1,0:T(8,128)(2,1)S(1)}, bf16[512,2048]{1,0:T(8,128)(2,1)}, u32[]{:S(2)}) copy-start(bf16[512,2048]{1,0:T(8,128)(2,1)} %refs_5_.7) | copy-start | bytes 6291460
  10.8 7.9 %collective-permute-start.2 = (f32[520,128]{1,0:T(8,128)S(1)}, f32[520,128]{1,0:T(8,128)S(1)}, u32[]{:S(2)}, u32[]{:S(2)}) collective-permute-start(f32[520,128]{1,0:T(8,128)S(1)} %shard_map.97.refs_4_), channel_id=1, source_target_pairs={{0,4},{4,0},{8,12},{12,8},{16,20},{20,16},{24,28},{28,24},{1,5},{5... | collective-permute-start | bytes 798728 | tf_op jit(solution)/shard_map/ppermute | solution.py:417
  14.3 10.2 %collective-permute-start.1 = (f32[512,128]{1,0:T(8,128)S(1)}, f32[512,128]{1,0:T(8,128)S(1)}, u32[]{:S(2)}, u32[]{:S(2)}) collective-permute-start(f32[512,128]{1,0:T(8,128)S(1)} %shard_map.99.refs_2_), channel_id=1, source_target_pairs={{0,8},{4,12},{1,9},{5,13},{2,10},{6,14},{3,11},{7,15}} | collective-permute-start | bytes 786440 | tf_op jit(solution)/shard_map/ppermute | solution.py:450
  18.8 9.8 %collective-permute-start.4 = (f32[512,128]{1,0:T(8,128)S(1)}, f32[512,128]{1,0:T(8,128)S(1)}, u32[]{:S(2)}, u32[]{:S(2)}) collective-permute-start(f32[512,128]{1,0:T(8,128)S(1)} %shard_map.100.refs_3_), channel_id=1, source_target_pairs={{0,8},{4,12},{1,9},{5,13},{2,10},{6,14},{3,11},{7,15}} | collective-permute-start | bytes 786440 | tf_op jit(solution)/shard_map/ppermute | solution.py:450
  24.5 4.8 %collective-permute-start.3 = (f32[512,128]{1,0:T(8,128)S(1)}, f32[512,128]{1,0:T(8,128)S(1)}, u32[]{:S(2)}, u32[]{:S(2)}) collective-permute-start(f32[512,128]{1,0:T(8,128)S(1)} %shard_map.101.refs_4_), channel_id=1, source_target_pairs={{8,16},{12,20},{9,17},{13,21},{10,18},{14,22},{11,19},{15,23}} | collective-permute-start | bytes 786440 | tf_op jit(solution)/shard_map/ppermute | solution.py:450
  27.1 2.9 %copy-start.6 = (f32[16,512]{1,0:T(8,128)S(1)}, f32[16,512]{1,0:T(8,128)}, u32[]{:S(2)}) copy-start(f32[16,512]{1,0:T(8,128)} %get-tuple-element.66.refs_2_.refs_3_.refs_4_.refs_6_) | copy-start | bytes 98308
  28.6 3.3 %collective-permute-start.5 = (f32[512,128]{1,0:T(8,128)S(1)}, f32[512,128]{1,0:T(8,128)S(1)}, u32[]{:S(2)}, u32[]{:S(2)}) collective-permute-start(f32[512,128]{1,0:T(8,128)S(1)} %shard_map.103.refs_3_), channel_id=1, source_target_pairs={{8,16},{12,20},{9,17},{13,21},{10,18},{14,22},{11,19},{15,23}} | collective-permute-start | bytes 786440 | tf_op jit(solution)/shard_map/ppermute | solution.py:450
  29.3 3.4 %collective-permute-start.7 = (f32[512,128]{1,0:T(8,128)S(1)}, f32[512,128]{1,0:T(8,128)S(1)}, u32[]{:S(2)}, u32[]{:S(2)}) collective-permute-start(f32[512,128]{1,0:T(8,128)S(1)} %shard_map.104.refs_4_), channel_id=1, source_target_pairs={{16,24},{20,28},{17,25},{21,29},{18,26},{22,30},{19,27},{23,31}} | collective-permute-start | bytes 786440 | tf_op jit(solution)/shard_map/ppermute | solution.py:450
  32.0 4.3 %collective-permute-start.6 = (f32[512,128]{1,0:T(8,128)S(1)}, f32[512,128]{1,0:T(8,128)S(1)}, u32[]{:S(2)}, u32[]{:S(2)}) collective-permute-start(f32[512,128]{1,0:T(8,128)S(1)} %shard_map.106.refs_5_), channel_id=1, source_target_pairs={{16,24},{20,28},{17,25},{21,29},{18,26},{22,30},{19,27},{23,31}} | collective-permute-start | bytes 786440 | tf_op jit(solution)/shard_map/ppermute | solution.py:450
  32.8 2.5 %copy-start.4 = (bf16[512,2048]{1,0:T(8,128)(2,1)S(1)}, bf16[512,2048]{1,0:T(8,128)(2,1)}, u32[]{:S(2)}) copy-start(bf16[512,2048]{1,0:T(8,128)(2,1)} %refs_1_.39) | copy-start | bytes 6291460
  32.8 2.5 %copy-start.7 = (f32[2048]{0:T(1024)S(1)}, f32[2048]{0:T(1024)}, u32[]{:S(2)}) copy-start(f32[2048]{0:T(1024)} %param.10) | copy-start | bytes 24580
  32.8 9.3 %collective-permute-start.9 = (f32[512,128]{1,0:T(8,128)S(1)}, f32[512,128]{1,0:T(8,128)S(1)}, u32[]{:S(2)}, u32[]{:S(2)}) collective-permute-start(f32[512,128]{1,0:T(8,128)S(1)} %get-tuple-element.69.refs_4_), channel_id=1, source_target_pairs={{0,4},{4,0},{8,12},{12,8},{16,20},{20,16},{24,28},{28,24},{1,5},{5... | collective-permute-start | bytes 786440 | tf_op jit(solution)/shard_map/ppermute | solution.py:461
  36.4 8.9 %collective-permute-start.8 = (f32[512,128]{1,0:T(8,128)S(1)}, f32[512,128]{1,0:T(8,128)S(1)}, u32[]{:S(2)}, u32[]{:S(2)}) collective-permute-start(f32[512,128]{1,0:T(8,128)S(1)} %get-tuple-element.72.refs_7_), channel_id=1, source_target_pairs={{0,4},{4,0},{8,12},{12,8},{16,20},{20,16},{24,28},{28,24},{1,5},{5... | collective-permute-start | bytes 786440 | tf_op jit(solution)/shard_map/ppermute | solution.py:461
  46.4 1.8 %collective-permute-start.12 = (f32[8,512]{1,0:T(8,128)S(1)}, f32[8,512]{1,0:T(8,128)S(1)}, u32[]{:S(2)}, u32[]{:S(2)}) collective-permute-start(f32[8,512]{1,0:T(8,128)S(1)} %get-tuple-element.76.refs_5_), channel_id=1, source_target_pairs={{0,3},{1,0},{2,1},{3,2},{4,7},{5,4},{6,5},{7,6},{8,11},{9,8},{10,9... | collective-permute-start | bytes 49160 | tf_op jit(solution)/shard_map/ppermute | solution.py:533
  46.4 3.8 %collective-permute-start.11 = (f32[8,512]{1,0:T(8,128)S(1)}, f32[8,512]{1,0:T(8,128)S(1)}, u32[]{:S(2)}, u32[]{:S(2)}) collective-permute-start(f32[8,512]{1,0:T(8,128)S(1)} %get-tuple-element.76.refs_5_), channel_id=1, source_target_pairs={{0,2},{1,3},{2,0},{3,1},{4,6},{5,7},{6,4},{7,5},{8,10},{9,11},{10,... | collective-permute-start | bytes 49160 | tf_op jit(solution)/shard_map/ppermute | solution.py:533
  47.9 3.2 %collective-permute-start.10 = (f32[8,512]{1,0:T(8,128)S(1)}, f32[8,512]{1,0:T(8,128)S(1)}, u32[]{:S(2)}, u32[]{:S(2)}) collective-permute-start(f32[8,512]{1,0:T(8,128)S(1)} %get-tuple-element.76.refs_5_), channel_id=1, source_target_pairs={{0,1},{1,2},{2,3},{3,0},{4,5},{5,6},{6,7},{7,4},{8,9},{9,10},{10,1... | collective-permute-start | bytes 49160 | tf_op jit(solution)/shard_map/ppermute | solution.py:533
  52.7 9.6 %collective-permute-start.13 = (f32[520,128]{1,0:T(8,128)S(1)}, f32[520,128]{1,0:T(8,128)S(1)}, u32[]{:S(2)}, u32[]{:S(2)}) collective-permute-start(f32[520,128]{1,0:T(8,128)S(1)} %get-tuple-element.81.refs_10_), channel_id=1, source_target_pairs={{0,4},{4,0},{8,12},{12,8},{16,20},{20,16},{24,28},{28,24},{1,5},{5... | collective-permute-start | bytes 798728 | tf_op jit(solution)/shard_map/ppermute | solution.py:414
  58.2 7.5 %collective-permute-start.15 = (f32[520,128]{1,0:T(8,128)S(1)}, f32[520,128]{1,0:T(8,128)S(1)}, u32[]{:S(2)}, u32[]{:S(2)}) collective-permute-start(f32[520,128]{1,0:T(8,128)S(1)} %shard_map.118.refs_6_), channel_id=1, source_target_pairs={{0,4},{4,0},{8,12},{12,8},{16,20},{20,16},{24,28},{28,24},{1,5},{5... | collective-permute-start | bytes 798728 | tf_op jit(solution)/shard_map/ppermute | solution.py:417
  62.3 4.0 %collective-permute-start.14 = (f32[512,128]{1,0:T(8,128)S(1)}, f32[512,128]{1,0:T(8,128)S(1)}, u32[]{:S(2)}, u32[]{:S(2)}) collective-permute-start(f32[512,128]{1,0:T(8,128)S(1)} %shard_map.120.refs_7_), channel_id=1, source_target_pairs={{24,16},{28,20},{25,17},{29,21},{26,18},{30,22},{27,19},{31,23}} | collective-permute-start | bytes 786440 | tf_op jit(solution)/shard_map/ppermute | solution.py:450
  65.6 6.3 %collective-permute-start.17 = (f32[512,128]{1,0:T(8,128)S(1)}, f32[512,128]{1,0:T(8,128)S(1)}, u32[]{:S(2)}, u32[]{:S(2)}) collective-permute-start(f32[512,128]{1,0:T(8,128)S(1)} %shard_map.122.refs_3_), channel_id=1, source_target_pairs={{24,16},{28,20},{25,17},{29,21},{26,18},{30,22},{27,19},{31,23}} | collective-permute-start | bytes 786440 | tf_op jit(solution)/shard_map/ppermute | solution.py:450
  66.3 6.3 %collective-permute-start.16 = (f32[512,128]{1,0:T(8,128)S(1)}, f32[512,128]{1,0:T(8,128)S(1)}, u32[]{:S(2)}, u32[]{:S(2)}) collective-permute-start(f32[512,128]{1,0:T(8,128)S(1)} %shard_map.123.refs_7_), channel_id=1, source_target_pairs={{16,8},{20,12},{17,9},{21,13},{18,10},{22,14},{19,11},{23,15}} | collective-permute-start | bytes 786440 | tf_op jit(solution)/shard_map/ppermute | solution.py:450
  71.9 6.9 %collective-permute-start.19 = (f32[512,128]{1,0:T(8,128)S(1)}, f32[512,128]{1,0:T(8,128)S(1)}, u32[]{:S(2)}, u32[]{:S(2)}) collective-permute-start(f32[512,128]{1,0:T(8,128)S(1)} %shard_map.126.refs_3_), channel_id=1, source_target_pairs={{16,8},{20,12},{17,9},{21,13},{18,10},{22,14},{19,11},{23,15}} | collective-permute-start | bytes 786440 | tf_op jit(solution)/shard_map/ppermute | solution.py:450
  72.6 23.9 %collective-permute-start.18 = (f32[512,128]{1,0:T(8,128)S(1)}, f32[512,128]{1,0:T(8,128)S(1)}, u32[]{:S(2)}, u32[]{:S(2)}) collective-permute-start(f32[512,128]{1,0:T(8,128)S(1)} %shard_map.127.refs_7_), channel_id=1, source_target_pairs={{8,0},{12,4},{9,1},{13,5},{10,2},{14,6},{11,3},{15,7}} | collective-permute-start | bytes 786440 | tf_op jit(solution)/shard_map/ppermute | solution.py:450
  78.8 21.7 %collective-permute-start.20 = (f32[512,128]{1,0:T(8,128)S(1)}, f32[512,128]{1,0:T(8,128)S(1)}, u32[]{:S(2)}, u32[]{:S(2)}) collective-permute-start(f32[512,128]{1,0:T(8,128)S(1)} %shard_map.130.refs_5_), channel_id=1, source_target_pairs={{8,0},{12,4},{9,1},{13,5},{10,2},{14,6},{11,3},{15,7}} | collective-permute-start | bytes 786440 | tf_op jit(solution)/shard_map/ppermute | solution.py:450
  96.6 10.4 %collective-permute-start.22 = (f32[512,128]{1,0:T(8,128)S(1)}, f32[512,128]{1,0:T(8,128)S(1)}, u32[]{:S(2)}, u32[]{:S(2)}) collective-permute-start(f32[512,128]{1,0:T(8,128)S(1)} %get-tuple-element.104.refs_7_), channel_id=1, source_target_pairs={{0,4},{4,0},{8,12},{12,8},{16,20},{20,16},{24,28},{28,24},{1,5},{5... | collective-permute-start | bytes 786440 | tf_op jit(solution)/shard_map/ppermute | solution.py:461
  100.6 8.2 %collective-permute-start.21 = (f32[512,128]{1,0:T(8,128)S(1)}, f32[512,128]{1,0:T(8,128)S(1)}, u32[]{:S(2)}, u32[]{:S(2)}) collective-permute-start(f32[512,128]{1,0:T(8,128)S(1)} %get-tuple-element.107.refs_7_), channel_id=1, source_target_pairs={{0,4},{4,0},{8,12},{12,8},{16,20},{20,16},{24,28},{28,24},{1,5},{5... | collective-permute-start | bytes 786440 | tf_op jit(solution)/shard_map/ppermute | solution.py:461

commit v2 on v0

--- a/solution.py
+++ b/solution.py
@@ -247,8 +247,10 @@
 
 def final_kernel(
     part, info, inner_key_ref, inner_value_ref, key_ref, value_ref, cumul_ref, state_ref,
-    grad_key_ref, grad_value_ref,
+    grad_key_ref, grad_value_ref, token_ref,
 ):
+    token_ref[...] = jnp.zeros_like(token_ref)
+
     def head(o, j):
         trail = column(trail_row(part.row(cumul_ref, info, o)))
         high, low = halves(state_ref[at_head(o), :])
@@ -420,14 +422,10 @@
             sends.append(make_piece(part, last))
             last = () if forward and len(sends) == 1 else (sends[-1],)
         last = exchange(last)
-        if forward:
-            last = exchange(last)
-        rest = [functools.partial(make_piece, part) for part in my_parts]
-        for make in rest[:1] if forward else rest:
-            keeps.append(make(last))
+        for part in my_parts:
+            keeps.append(make_piece(part, last))
             last = (keeps[-1],)
-        if not forward:
-            last = exchange(last)
+        last = exchange(last + (received[0],) if forward else last)
         arrived, mine, theirs, late = {}, [], [], []
         for step in range(chunks + places - 1):
             for p in range(places - 1):
@@ -445,9 +443,8 @@
                 arrived[c, p + 1] = lax.ppermute(value, "seq", pairs)
                 last = (value,)
             last = exchange(last)
-            while len(keeps) < chunks:
-                keeps.append(rest[len(keeps)](last))
-                last = (keeps[-1],)
+            if filler:
+                last = (filler.pop(0)(last),)
             c = step + 1 - places
             if c >= 0:
                 ins = [plain(keeps[c]), plain(received[c])]
@@ -463,9 +460,6 @@
                 late.append(functools.partial(on_theirs, c, theirs[c]))
                 if c >= 2:
                     filler.append(late.pop(0))
-                if forward and c >= chunks - 2 and filler:
-                    last = (filler.pop(0)(last),)
-            if filler:
                 last = (filler.pop(0)(last),)
         for work in filler + late:
             last = (work(last),)
@@ -572,13 +566,15 @@
         part, held = back_parts[slot][c], target(grad_keys) + target(grad_values)
         ins = [plain(array) for array in (*inner_grads[slot, c], key_vecs, value_vecs)]
         ins += [cumul_in(), plain(before)]
-        whole_key, whole_value = part.call(
-            final_kernel, ins, [(whole, part.full_spec())] * 2, after=held + tuple(after),
+        whole_key, whole_value, token = part.call(
+            final_kernel, ins,
+            [(whole, part.full_spec())] * 2 + [give(jax.ShapeDtypeStruct((8, HEAD_DIM), f32))],
+            after=held + tuple(after),
             aliases={2 + len(ins): 0, 3 + len(ins): 1} if held else None, cost=2.0,
         )
         grad_keys.append(whole_key)
         grad_values.append(whole_value)
-        return whole_key
+        return token
 
     works = [
         functools.partial(backward_work, slot, c)

time: 104 us -> 106 us (1.019)
  starting transfers between devices: 25 us -> 27.2 us
    ppermute x4, waiting for transfers between devices: 5.42 us -> 9.21 us  [chain(): theirs.append(lax.ppermute(send, 'seq', swap))]
    ppermute x2, starting transfers between devices: 0.66 us -> 3.22 us  [exchange(): received.append(lax.ppermute(sent, 'seq', swap))]
    ppermute x12, waiting for transfers between devices: 14.5 us -> 12.3 us  [chain(): arrived[c, p + 1] = lax.ppermute(value, 'seq', pairs)]
    ppermute x12, starting transfers between devices: 13.8 us -> 14.9 us  [chain(): arrived[c, p + 1] = lax.ppermute(value, 'seq', pairs)]
  transfers between devices with their start and end apart: 23 -> 23, of which waited for: 9 -> 12; matrix products, arithmetic and copies ran while one was open for 0% -> 0% of each run, Pallas kernels for 39% -> 38%
where the time goes in v2:
time: 106 us
  Pallas kernels  47.9 us (45%)
  starting transfers between devices  27.2 us (26%)
  waiting for transfers between devices  27 us (25%)
  local copies, waits for them, and re-layouts  2.65 us (2%)
    pallas_call x42, Pallas kernels, run(): pl.pallas_call(body, out_shape=[shape for shape, _ in outs], grid_spec=pl...  47.9 us
    ppermute x12, starting transfers between devices, chain(): arrived[c, p + 1] = lax.ppermute(value, 'seq', pairs)  14.9 us
    ppermute x12, waiting for transfers between devices, chain(): arrived[c, p + 1] = lax.ppermute(value, 'seq', pairs)  12.3 us
    ppermute x4, waiting for transfers between devices, chain(): theirs.append(lax.ppermute(send, 'seq', swap))  9.21 us
    ppermute x4, starting transfers between devices, chain(): theirs.append(lax.ppermute(send, 'seq', swap))  3.66 us
    ppermute x2, starting transfers between devices, exchange(): received.append(lax.ppermute(sends[0], 'seq', swap))  3.64 us
    ppermute x2, starting transfers between devices, exchange(): received.append(lax.ppermute(sent, 'seq', swap))  3.22 us
    ppermute x3, waiting for transfers between devices, on_device(): lax.ppermute(sums, 'head', [(i, (i + k) % head_count) for i in range(head...  2.96 us
  transfers between devices with their start and end apart: 23, of which 12 were waited for; matrix products, arithmetic and copies ran while one was open for 0% of the time, Pallas kernels for 38%

profile of v2, /device:TPU:0, one launch (start us, length us, event | category | flops | bytes accessed | tf_op | source)
XLA Modules:
  0.0 105.8 jit_solution(13354810501092937215)
XLA Ops:
  0.7 3.0 %shard_map.93 = (f32[520,128]{1,0:T(8,128)}, f32[16,512]{1,0:T(8,128)}) custom-call(s32[1]{0:T(128)} %bitcast.member_ref, s32[1]{0:T(128)} %bitcast.1.pair_ref, bf16[512,2048]{1,0:T(8,128)(2,1)} %refs_2_.31, bf16[512,2048]{1,0:T(8,128)(2,1)} %refs_3_.15, f32[16,512]{1,0:T(8,128)} %bitcast.12), custom_call_target="tpu_custom_call" | custom-call | flops 50000000 | bytes 125000 | tf_op jit(solution)/shard_map/pallas_call | solution.py:355
  3.6 3.0 %collective-permute-start = (f32[520,128]{1,0:T(8,128)}, f32[520,128]{1,0:T(8,128)S(1)}, u32[]{:S(2)}, u32[]{:S(2)}) collective-permute-start(f32[520,128]{1,0:T(8,128)} %get-tuple-element.58), channel_id=1, source_target_pairs={{0,4},{4,0},{8,12},{12,8},{16,20},{20,16},{24,28},{28,24},{1,5},{5... | collective-permute-start | bytes 798728 | tf_op jit(solution)/shard_map/ppermute | solution.py:415
  6.6 1.6 %copy-done.2 = bf16[512,2048]{1,0:T(8,128)(2,1)S(1)} copy-done((bf16[512,2048]{1,0:T(8,128)(2,1)S(1)}, bf16[512,2048]{1,0:T(8,128)(2,1)}, u32[]{:S(2)}) %copy-start.2) | copy-done | bytes 2097176
  11.5 1.7 %collective-permute-done.refs_2_.refs_1_ = f32[520,128]{1,0:T(8,128)S(1)} collective-permute-done((f32[520,128]{1,0:T(8,128)}, f32[520,128]{1,0:T(8,128)S(1)}, u32[]{:S(2)}, u32[]{:S(2)}) %collective-permute-start) | collective-permute-done | bytes 266272 | tf_op jit(solution)/shard_map/ppermute | solution.py:415
  13.2 1.8 %collective-permute-start.2 = (f32[520,128]{1,0:T(8,128)S(1)}, f32[520,128]{1,0:T(8,128)S(1)}, u32[]{:S(2)}, u32[]{:S(2)}) collective-permute-start(f32[520,128]{1,0:T(8,128)S(1)} %shard_map.97.refs_2_), channel_id=1, source_target_pairs={{0,4},{4,0},{8,12},{12,8},{16,20},{20,16},{24,28},{28,24},{1,5},{5... | collective-permute-start | bytes 798728 | tf_op jit(solution)/shard_map/ppermute | solution.py:418
  15.1 3.4 %collective-permute-start.1 = (f32[512,128]{1,0:T(8,128)S(1)}, f32[512,128]{1,0:T(8,128)S(1)}, u32[]{:S(2)}, u32[]{:S(2)}) collective-permute-start(f32[512,128]{1,0:T(8,128)S(1)} %shard_map.98.refs_4_), channel_id=1, source_target_pairs={{0,8},{4,12},{1,9},{5,13},{2,10},{6,14},{3,11},{7,15}} | collective-permute-start | bytes 786440 | tf_op jit(solution)/shard_map/ppermute | solution.py:443
  18.5 1.9 %shard_map.99.refs_2_.refs_0_ = f32[512,512]{1,0:T(8,128)S(1)} custom-call(s32[1]{0:T(128)} %bitcast.member_ref, s32[1]{0:T(128)} %bitcast.1.pair_ref, bf16[512,2048]{1,0:T(8,128)(2,1)S(1)} %copy-done, bf16[512,2048]{1,0:T(8,128)(2,1)S(1)} %copy-done.1, bf16[512,2048]{1,0:T(8,128)(2,1)S(1)} %copy-done.3, f32[16,512]{1,0:T(8,128)S(1)} %copy-done.5, ...), custom_call_target="tpu_custom_call" | custom-call | flops 100000000 | bytes 250000 | tf_op jit(solution)/shard_map/pallas_call | solution.py:355
  20.9 3.3 %collective-permute-start.4 = (f32[512,128]{1,0:T(8,128)S(1)}, f32[512,128]{1,0:T(8,128)S(1)}, u32[]{:S(2)}, u32[]{:S(2)}) collective-permute-start(f32[512,128]{1,0:T(8,128)S(1)} %shard_map.100.refs_3_), channel_id=1, source_target_pairs={{0,8},{4,12},{1,9},{5,13},{2,10},{6,14},{3,11},{7,15}} | collective-permute-start | bytes 786440 | tf_op jit(solution)/shard_map/ppermute | solution.py:443
  25.0 1.9 %shard_map.102.refs_3_.refs_0_ = f32[512,512]{1,0:T(8,128)S(1)} custom-call(s32[1]{0:T(128)} %bitcast.member_ref, s32[1]{0:T(128)} %bitcast.1.pair_ref, bf16[512,2048]{1,0:T(8,128)(2,1)S(1)} %copy-done, bf16[512,2048]{1,0:T(8,128)(2,1)S(1)} %copy-done.1, bf16[512,2048]{1,0:T(8,128)(2,1)S(1)} %copy-done.3, f32[16,512]{1,0:T(8,128)S(1)} %copy-done.5, ...), custom_call_target="tpu_custom_call" | custom-call | flops 2200000000 | bytes 5500000 | tf_op jit(solution)/shard_map/pallas_call | solution.py:355
  26.9 1.6 %collective-permute-done.4.refs_2_ = f32[512,128]{1,0:T(8,128)S(1)} collective-permute-done((f32[512,128]{1,0:T(8,128)S(1)}, f32[512,128]{1,0:T(8,128)S(1)}, u32[]{:S(2)}, u32[]{:S(2)}) %collective-permute-start.4) | collective-permute-done | bytes 262176 | tf_op jit(solution)/shard_map/ppermute | solution.py:443
  29.9 1.9 %shard_map.105.refs_3_.refs_0_ = f32[512,512]{1,0:T(8,128)S(1)} custom-call(s32[1]{0:T(128)} %bitcast.member_ref, s32[1]{0:T(128)} %bitcast.1.pair_ref, bf16[512,2048]{1,0:T(8,128)(2,1)S(1)} %copy-done, bf16[512,2048]{1,0:T(8,128)(2,1)S(1)} %copy-done.1, bf16[512,2048]{1,0:T(8,128)(2,1)S(1)} %copy-done.3, f32[16,512]{1,0:T(8,128)S(1)} %copy-done.6, ...), custom_call_target="tpu_custom_call" | custom-call | flops 2200000000 | bytes 5500000 | tf_op jit(solution)/shard_map/pallas_call | solution.py:355
  32.6 1.9 %shard_map.107.refs_5_.refs_0_ = f32[512,512]{1,0:T(8,128)S(1)} custom-call(s32[1]{0:T(128)} %bitcast.member_ref, s32[1]{0:T(128)} %bitcast.1.pair_ref, bf16[512,2048]{1,0:T(8,128)(2,1)S(1)} %copy-done, bf16[512,2048]{1,0:T(8,128)(2,1)S(1)} %copy-done.1, bf16[512,2048]{1,0:T(8,128)(2,1)S(1)} %copy-done.3, f32[16,512]{1,0:T(8,128)S(1)} %copy-done.6, ...), custom_call_target="tpu_custom_call" | custom-call | flops 2200000000 | bytes 5500000 | tf_op jit(solution)/shard_map/pallas_call | solution.py:355
  39.6 3.7 %collective-permute-done.9.refs_5_ = f32[512,128]{1,0:T(8,128)S(1)} collective-permute-done((f32[512,128]{1,0:T(8,128)S(1)}, f32[512,128]{1,0:T(8,128)S(1)}, u32[]{:S(2)}, u32[]{:S(2)}) %collective-permute-start.9) | collective-permute-done | bytes 262176 | tf_op jit(solution)/shard_map/ppermute | solution.py:456
  44.5 1.7 %collective-permute-done.8.refs_5_ = f32[512,128]{1,0:T(8,128)S(1)} collective-permute-done((f32[512,128]{1,0:T(8,128)S(1)}, f32[512,128]{1,0:T(8,128)S(1)}, u32[]{:S(2)}, u32[]{:S(2)}) %collective-permute-start.8) | collective-permute-done | bytes 262176 | tf_op jit(solution)/shard_map/ppermute | solution.py:456
  47.3 1.5 %collective-permute-start.11 = (f32[8,512]{1,0:T(8,128)S(1)}, f32[8,512]{1,0:T(8,128)S(1)}, u32[]{:S(2)}, u32[]{:S(2)}) collective-permute-start(f32[8,512]{1,0:T(8,128)S(1)} %get-tuple-element.67.refs_5_), channel_id=1, source_target_pairs={{0,2},{1,3},{2,0},{3,1},{4,6},{5,7},{6,4},{7,5},{8,10},{9,11},{10,... | collective-permute-start | bytes 49160 | tf_op jit(solution)/shard_map/ppermute | solution.py:525
  49.0 2.0 %collective-permute-done.11.refs_7_ = f32[8,512]{1,0:T(8,128)S(1)} collective-permute-done((f32[8,512]{1,0:T(8,128)S(1)}, f32[8,512]{1,0:T(8,128)S(1)}, u32[]{:S(2)}, u32[]{:S(2)}) %collective-permute-start.11) | collective-permute-done | bytes 16416 | tf_op jit(solution)/shard_map/ppermute | solution.py:525
  52.0 1.7 %shard_map.114 = (bf16[512,2048]{1,0:T(8,128)(2,1)}, bf16[512,512]{1,0:T(8,128)(2,1)S(1)}, f32[520,128]{1,0:T(8,128)S(1)}) custom-call(s32[1]{0:T(128)} %bitcast.member_ref, s32[1]{0:T(128)} %bitcast.1.pair_ref, f32[512,512]{1,0:T(8,128)S(1)} %get-tuple-element.70.refs_0_, bf16[512,2048]{1,0:T(8,128)(2,1)S(1)} %copy-done.4, f32[1,2048]{1,0:T(1,128)S(1)} %bitcast.8, ...), custom_call_target="tpu_custom_call" | custom-call | flops 2000000000 | bytes 5000000 | tf_op jit(solution)/shard_map/pallas_call | solution.py:355
  54.4 1.7 %shard_map.115 = (bf16[512,2048]{1,0:T(8,128)(2,1)}, bf16[512,512]{1,0:T(8,128)(2,1)S(1)}, f32[520,128]{1,0:T(8,128)S(1)}) custom-call(s32[1]{0:T(128)} %bitcast.member_ref, s32[1]{0:T(128)} %bitcast.1.pair_ref, f32[512,512]{1,0:T(8,128)S(1)} %get-tuple-element.69.refs_0_, bf16[512,2048]{1,0:T(8,128)(2,1)S(1)} %copy-done.4, ...), custom_call_target="tpu_custom_call", output_to_operand_aliasing={{0}: (11, {})} | custom-call | flops 2000000000 | bytes 5000000 | tf_op jit(solution)/shard_map/pallas_call | solution.py:355
  56.1 1.7 %shard_map.116 = (bf16[512,2048]{1,0:T(8,128)(2,1)}, bf16[512,512]{1,0:T(8,128)(2,1)S(1)}, f32[520,128]{1,0:T(8,128)S(1)}) custom-call(s32[1]{0:T(128)} %bitcast.member_ref, s32[1]{0:T(128)} %bitcast.1.pair_ref, f32[512,512]{1,0:T(8,128)S(1)} %get-tuple-element.68.refs_0_, bf16[512,2048]{1,0:T(8,128)(2,1)S(1)} %copy-done.4, ...), custom_call_target="tpu_custom_call", output_to_operand_aliasing={{0}: (11, {})} | custom-call | flops 2000000000 | bytes 5000000 | tf_op jit(solution)/shard_map/pallas_call | solution.py:355
  57.8 1.7 %shard_map.117 = (bf16[512,2048]{1,0:T(8,128)(2,1)}, bf16[512,512]{1,0:T(8,128)(2,1)S(1)}, f32[520,128]{1,0:T(8,128)S(1)}) custom-call(s32[1]{0:T(128)} %bitcast.member_ref, s32[1]{0:T(128)} %bitcast.1.pair_ref, f32[512,512]{1,0:T(8,128)S(1)} %get-tuple-element.64.refs_0_, bf16[512,2048]{1,0:T(8,128)(2,1)S(1)} %copy-done.4, ...), custom_call_target="tpu_custom_call", output_to_operand_aliasing={{0}: (11, {})} | custom-call | flops 2000000000 | bytes 5000000 | tf_op jit(solution)/shard_map/pallas_call | solution.py:355
  59.5 1.4 %collective-permute-start.15 = (f32[520,128]{1,0:T(8,128)S(1)}, f32[520,128]{1,0:T(8,128)S(1)}, u32[]{:S(2)}, u32[]{:S(2)}) collective-permute-start(f32[520,128]{1,0:T(8,128)S(1)} %shard_map.118.refs_2_), channel_id=1, source_target_pairs={{0,4},{4,0},{8,12},{12,8},{16,20},{20,16},{24,28},{28,24},{1,5},{5... | collective-permute-start | bytes 798728 | tf_op jit(solution)/shard_map/ppermute | solution.py:418
  61.8 4.0 %shard_map.120 = (bf16[512,2048]{1,0:T(8,128)(2,1)}, f32[512,512]{1,0:T(8,128)S(1)}, f32[512,512]{1,0:T(8,128)S(1)}) custom-call(s32[1]{0:T(128)} %bitcast.member_ref, s32[1]{0:T(128)} %bitcast.1.pair_ref, bf16[512,2048]{1,0:T(8,128)(2,1)S(1)} %copy-done, bf16[512,2048]{1,0:T(8,128)(2,1)S(1)} %copy-done.1, bf16[512,2048]{1,0:T(8,128)(2,1)S(1)} %copy-done.3, ...), custom_call_target="tpu_custom_call" | custom-call | flops 4300000256 | bytes 10750000 | tf_op jit(solution)/shard_map/pallas_call | solution.py:355
  67.6 4.0 %shard_map.123 = (bf16[512,2048]{1,0:T(8,128)(2,1)}, f32[512,512]{1,0:T(8,128)S(1)}, f32[512,512]{1,0:T(8,128)S(1)}) custom-call(s32[1]{0:T(128)} %bitcast.member_ref, s32[1]{0:T(128)} %bitcast.1.pair_ref, bf16[512,2048]{1,0:T(8,128)(2,1)S(1)} %copy-done, bf16[512,2048]{1,0:T(8,128)(2,1)S(1)} %copy-done.1, ...), custom_call_target="tpu_custom_call", output_to_operand_aliasing={{0}: (8, {})} | custom-call | flops 4300000256 | bytes 10750000 | tf_op jit(solution)/shard_map/pallas_call | solution.py:355
  73.6 4.0 %shard_map.126 = (bf16[512,2048]{1,0:T(8,128)(2,1)}, f32[512,512]{1,0:T(8,128)S(1)}, f32[512,512]{1,0:T(8,128)S(1)}) custom-call(s32[1]{0:T(128)} %bitcast.member_ref, s32[1]{0:T(128)} %bitcast.1.pair_ref, bf16[512,2048]{1,0:T(8,128)(2,1)S(1)} %copy-done, bf16[512,2048]{1,0:T(8,128)(2,1)S(1)} %copy-done.1, ...), custom_call_target="tpu_custom_call", output_to_operand_aliasing={{0}: (8, {})} | custom-call | flops 4300000256 | bytes 10750000 | tf_op jit(solution)/shard_map/pallas_call | solution.py:355
  78.8 4.0 %shard_map.128 = (bf16[512,2048]{1,0:T(8,128)(2,1)}, f32[512,512]{1,0:T(8,128)S(1)}, f32[512,512]{1,0:T(8,128)S(1)}) custom-call(s32[1]{0:T(128)} %bitcast.member_ref, s32[1]{0:T(128)} %bitcast.1.pair_ref, bf16[512,2048]{1,0:T(8,128)(2,1)S(1)} %copy-done, bf16[512,2048]{1,0:T(8,128)(2,1)S(1)} %copy-done.1, ...), custom_call_target="tpu_custom_call", output_to_operand_aliasing={{0}: (8, {})} | custom-call | flops 4300000256 | bytes 10750000 | tf_op jit(solution)/shard_map/pallas_call | solution.py:355
  82.8 9.1 %collective-permute-done.20.refs_4_ = f32[512,128]{1,0:T(8,128)S(1)} collective-permute-done((f32[512,128]{1,0:T(8,128)S(1)}, f32[512,128]{1,0:T(8,128)S(1)}, u32[]{:S(2)}, u32[]{:S(2)}) %collective-permute-start.20) | collective-permute-done | bytes 262176 | tf_op jit(solution)/shard_map/ppermute | solution.py:443
  92.2 1.8 %shard_map.130 = (bf16[512,2048]{1,0:T(8,128)(2,1)}, bf16[512,2048]{1,0:T(8,128)(2,1)}, f32[8,128]{1,0:T(8,128)S(1)}) custom-call(s32[1]{0:T(128)} %bitcast.member_ref, s32[1]{0:T(128)} %bitcast.1.pair_ref, f32[512,512]{1,0:T(8,128)S(1)} %get-tuple-element.84.refs_2_.refs_0_, f32[512,512]{1,0:T(8,128)S(1)} %get-tuple-element.92.refs_1_, ...), custom_call_target="tpu_custom_call" | custom-call | flops 2000000000 | bytes 5000000 | tf_op jit(solution)/shard_map/pallas_call | solution.py:355
  93.9 1.6 %collective-permute-done.19.refs_4_ = f32[512,128]{1,0:T(8,128)S(1)} collective-permute-done((f32[512,128]{1,0:T(8,128)S(1)}, f32[512,128]{1,0:T(8,128)S(1)}, u32[]{:S(2)}, u32[]{:S(2)}) %collective-permute-start.19) | collective-permute-done | bytes 262176 | tf_op jit(solution)/shard_map/ppermute | solution.py:443
  96.7 1.7 %shard_map.132 = (bf16[512,2048]{1,0:T(8,128)(2,1)}, bf16[512,2048]{1,0:T(8,128)(2,1)}, f32[8,128]{1,0:T(8,128)S(1)}) custom-call(s32[1]{0:T(128)} %bitcast.member_ref, s32[1]{0:T(128)} %bitcast.1.pair_ref, f32[512,512]{1,0:T(8,128)S(1)} %get-tuple-element.88.refs_3_.refs_0_, ...), custom_call_target="tpu_custom_call", output_to_operand_aliasing={{0}: (8, {}), {1}: (9, {})} | custom-call | flops 2000000000 | bytes 5000000 | tf_op jit(solution)/shard_map/pallas_call | solution.py:355
  98.5 2.5 %collective-permute-done.22.refs_5_ = f32[512,128]{1,0:T(8,128)S(1)} collective-permute-done((f32[512,128]{1,0:T(8,128)S(1)}, f32[512,128]{1,0:T(8,128)S(1)}, u32[]{:S(2)}, u32[]{:S(2)}) %collective-permute-start.22) | collective-permute-done | bytes 262176 | tf_op jit(solution)/shard_map/ppermute | solution.py:456
  101.0 1.7 %shard_map.133 = (bf16[512,2048]{1,0:T(8,128)(2,1)}, bf16[512,2048]{1,0:T(8,128)(2,1)}, f32[8,128]{1,0:T(8,128)S(1)}) custom-call(s32[1]{0:T(128)} %bitcast.member_ref, s32[1]{0:T(128)} %bitcast.1.pair_ref, f32[512,512]{1,0:T(8,128)S(1)} %get-tuple-element.86.refs_3_.refs_0_, ...), custom_call_target="tpu_custom_call", output_to_operand_aliasing={{0}: (8, {}), {1}: (9, {})} | custom-call | flops 2000000000 | bytes 5000000 | tf_op jit(solution)/shard_map/pallas_call | solution.py:355
  104.0 1.7 %shard_map.134 = (bf16[512,2048]{1,0:T(8,128)(2,1)}, bf16[512,2048]{1,0:T(8,128)(2,1)}, f32[8,128]{1,0:T(8,128)}) custom-call(s32[1]{0:T(128)} %bitcast.member_ref, s32[1]{0:T(128)} %bitcast.1.pair_ref, f32[512,512]{1,0:T(8,128)S(1)} %get-tuple-element.90.refs_5_.refs_0_, ...), custom_call_target="tpu_custom_call", output_to_operand_aliasing={{0}: (8, {}), {1}: (9, {})} | custom-call | flops 2000000000 | bytes 5000000 | tf_op jit(solution)/shard_map/pallas_call | solution.py:355
  (73 shorter events, 24.3 us)
Async XLA Ops:
  0.7 5.9 %copy-start.1 = (bf16[512,2048]{1,0:T(8,128)(2,1)S(1)}, bf16[512,2048]{1,0:T(8,128)(2,1)}, u32[]{:S(2)}) copy-start(bf16[512,2048]{1,0:T(8,128)(2,1)} %refs_2_.31) | copy-start | bytes 6291460
  3.6 9.6 %collective-permute-start = (f32[520,128]{1,0:T(8,128)}, f32[520,128]{1,0:T(8,128)S(1)}, u32[]{:S(2)}, u32[]{:S(2)}) collective-permute-start(f32[520,128]{1,0:T(8,128)} %get-tuple-element.58), channel_id=1, source_target_pairs={{0,4},{4,0},{8,12},{12,8},{16,20},{20,16},{24,28},{28,24},{1,5},{5... | collective-permute-start | bytes 798728 | tf_op jit(solution)/shard_map/ppermute | solution.py:415
  6.6 1.6 %copy-start.2 = (bf16[512,2048]{1,0:T(8,128)(2,1)S(1)}, bf16[512,2048]{1,0:T(8,128)(2,1)}, u32[]{:S(2)}) copy-start(bf16[512,2048]{1,0:T(8,128)(2,1)} %refs_3_.15) | copy-start | bytes 6291460
  8.2 0.8 copy-start.5
  10.6 7.9 %copy-start.3 = (bf16[512,2048]{1,0:T(8,128)(2,1)S(1)}, bf16[512,2048]{1,0:T(8,128)(2,1)}, u32[]{:S(2)}) copy-start(bf16[512,2048]{1,0:T(8,128)(2,1)} %refs_3_.15) | copy-start | bytes 6291460
  11.5 7.0 %copy-start = (bf16[512,2048]{1,0:T(8,128)(2,1)S(1)}, bf16[512,2048]{1,0:T(8,128)(2,1)}, u32[]{:S(2)}) copy-start(bf16[512,2048]{1,0:T(8,128)(2,1)} %refs_0_.23) | copy-start | bytes 6291460
  13.2 7.6 %collective-permute-start.2 = (f32[520,128]{1,0:T(8,128)S(1)}, f32[520,128]{1,0:T(8,128)S(1)}, u32[]{:S(2)}, u32[]{:S(2)}) collective-permute-start(f32[520,128]{1,0:T(8,128)S(1)} %shard_map.97.refs_2_), channel_id=1, source_target_pairs={{0,4},{4,0},{8,12},{12,8},{16,20},{20,16},{24,28},{28,24},{1,5},{5... | collective-permute-start | bytes 798728 | tf_op jit(solution)/shard_map/ppermute | solution.py:418
  15.1 9.2 %collective-permute-start.1 = (f32[512,128]{1,0:T(8,128)S(1)}, f32[512,128]{1,0:T(8,128)S(1)}, u32[]{:S(2)}, u32[]{:S(2)}) collective-permute-start(f32[512,128]{1,0:T(8,128)S(1)} %shard_map.98.refs_4_), channel_id=1, source_target_pairs={{0,8},{4,12},{1,9},{5,13},{2,10},{6,14},{3,11},{7,15}} | collective-permute-start | bytes 786440 | tf_op jit(solution)/shard_map/ppermute | solution.py:443
  20.9 7.6 %collective-permute-start.4 = (f32[512,128]{1,0:T(8,128)S(1)}, f32[512,128]{1,0:T(8,128)S(1)}, u32[]{:S(2)}, u32[]{:S(2)}) collective-permute-start(f32[512,128]{1,0:T(8,128)S(1)} %shard_map.100.refs_3_), channel_id=1, source_target_pairs={{0,8},{4,12},{1,9},{5,13},{2,10},{6,14},{3,11},{7,15}} | collective-permute-start | bytes 786440 | tf_op jit(solution)/shard_map/ppermute | solution.py:443
  24.3 4.9 %collective-permute-start.3 = (f32[512,128]{1,0:T(8,128)S(1)}, f32[512,128]{1,0:T(8,128)S(1)}, u32[]{:S(2)}, u32[]{:S(2)}) collective-permute-start(f32[512,128]{1,0:T(8,128)S(1)} %shard_map.101.refs_4_), channel_id=1, source_target_pairs={{8,16},{12,20},{9,17},{13,21},{10,18},{14,22},{11,19},{15,23}} | collective-permute-start | bytes 786440 | tf_op jit(solution)/shard_map/ppermute | solution.py:443
  26.9 3.0 %copy-start.6 = (f32[16,512]{1,0:T(8,128)S(1)}, f32[16,512]{1,0:T(8,128)}, u32[]{:S(2)}) copy-start(f32[16,512]{1,0:T(8,128)} %get-tuple-element.57.refs_2_.refs_3_.refs_4_) | copy-start | bytes 98308
  28.5 3.3 %collective-permute-start.5 = (f32[512,128]{1,0:T(8,128)S(1)}, f32[512,128]{1,0:T(8,128)S(1)}, u32[]{:S(2)}, u32[]{:S(2)}) collective-permute-start(f32[512,128]{1,0:T(8,128)S(1)} %shard_map.103.refs_3_), channel_id=1, source_target_pairs={{8,16},{12,20},{9,17},{13,21},{10,18},{14,22},{11,19},{15,23}} | collective-permute-start | bytes 786440 | tf_op jit(solution)/shard_map/ppermute | solution.py:443
  29.2 5.3 %collective-permute-start.7 = (f32[512,128]{1,0:T(8,128)S(1)}, f32[512,128]{1,0:T(8,128)S(1)}, u32[]{:S(2)}, u32[]{:S(2)}) collective-permute-start(f32[512,128]{1,0:T(8,128)S(1)} %shard_map.104.refs_4_), channel_id=1, source_target_pairs={{16,24},{20,28},{17,25},{21,29},{18,26},{22,30},{19,27},{23,31}} | collective-permute-start | bytes 786440 | tf_op jit(solution)/shard_map/ppermute | solution.py:443
  31.9 5.3 %collective-permute-start.6 = (f32[512,128]{1,0:T(8,128)S(1)}, f32[512,128]{1,0:T(8,128)S(1)}, u32[]{:S(2)}, u32[]{:S(2)}) collective-permute-start(f32[512,128]{1,0:T(8,128)S(1)} %shard_map.106.refs_4_), channel_id=1, source_target_pairs={{16,24},{20,28},{17,25},{21,29},{18,26},{22,30},{19,27},{23,31}} | collective-permute-start | bytes 786440 | tf_op jit(solution)/shard_map/ppermute | solution.py:443
  34.5 1.6 %copy-start.4 = (bf16[512,2048]{1,0:T(8,128)(2,1)S(1)}, bf16[512,2048]{1,0:T(8,128)(2,1)}, u32[]{:S(2)}) copy-start(bf16[512,2048]{1,0:T(8,128)(2,1)} %refs_1_.35) | copy-start | bytes 6291460
  34.5 1.6 %copy-start.7 = (f32[2048]{0:T(1024)S(1)}, f32[2048]{0:T(1024)}, u32[]{:S(2)}) copy-start(f32[2048]{0:T(1024)} %param.10) | copy-start | bytes 24580
  34.6 8.7 %collective-permute-start.9 = (f32[512,128]{1,0:T(8,128)S(1)}, f32[512,128]{1,0:T(8,128)S(1)}, u32[]{:S(2)}, u32[]{:S(2)}) collective-permute-start(f32[512,128]{1,0:T(8,128)S(1)} %get-tuple-element.60.refs_7_), channel_id=1, source_target_pairs={{0,4},{4,0},{8,12},{12,8},{16,20},{20,16},{24,28},{28,24},{1,5},{5... | collective-permute-start | bytes 786440 | tf_op jit(solution)/shard_map/ppermute | solution.py:456
  37.3 8.8 %collective-permute-start.8 = (f32[512,128]{1,0:T(8,128)S(1)}, f32[512,128]{1,0:T(8,128)S(1)}, u32[]{:S(2)}, u32[]{:S(2)}) collective-permute-start(f32[512,128]{1,0:T(8,128)S(1)} %get-tuple-element.63.refs_7_), channel_id=1, source_target_pairs={{0,4},{4,0},{8,12},{12,8},{16,20},{20,16},{24,28},{28,24},{1,5},{5... | collective-permute-start | bytes 786440 | tf_op jit(solution)/shard_map/ppermute | solution.py:456
  47.3 1.7 %collective-permute-start.12 = (f32[8,512]{1,0:T(8,128)S(1)}, f32[8,512]{1,0:T(8,128)S(1)}, u32[]{:S(2)}, u32[]{:S(2)}) collective-permute-start(f32[8,512]{1,0:T(8,128)S(1)} %get-tuple-element.67.refs_5_), channel_id=1, source_target_pairs={{0,3},{1,0},{2,1},{3,2},{4,7},{5,4},{6,5},{7,6},{8,11},{9,8},{10,9... | collective-permute-start | bytes 49160 | tf_op jit(solution)/shard_map/ppermute | solution.py:525
  47.3 3.8 %collective-permute-start.11 = (f32[8,512]{1,0:T(8,128)S(1)}, f32[8,512]{1,0:T(8,128)S(1)}, u32[]{:S(2)}, u32[]{:S(2)}) collective-permute-start(f32[8,512]{1,0:T(8,128)S(1)} %get-tuple-element.67.refs_5_), channel_id=1, source_target_pairs={{0,2},{1,3},{2,0},{3,1},{4,6},{5,7},{6,4},{7,5},{8,10},{9,11},{10,... | collective-permute-start | bytes 49160 | tf_op jit(solution)/shard_map/ppermute | solution.py:525
  48.8 3.2 %collective-permute-start.10 = (f32[8,512]{1,0:T(8,128)S(1)}, f32[8,512]{1,0:T(8,128)S(1)}, u32[]{:S(2)}, u32[]{:S(2)}) collective-permute-start(f32[8,512]{1,0:T(8,128)S(1)} %get-tuple-element.67.refs_5_), channel_id=1, source_target_pairs={{0,1},{1,2},{2,3},{3,0},{4,5},{5,6},{6,7},{7,4},{8,9},{9,10},{10,1... | collective-permute-start | bytes 49160 | tf_op jit(solution)/shard_map/ppermute | solution.py:525
  53.7 7.3 %collective-permute-start.13 = (f32[520,128]{1,0:T(8,128)S(1)}, f32[520,128]{1,0:T(8,128)S(1)}, u32[]{:S(2)}, u32[]{:S(2)}) collective-permute-start(f32[520,128]{1,0:T(8,128)S(1)} %get-tuple-element.72.refs_10_), channel_id=1, source_target_pairs={{0,4},{4,0},{8,12},{12,8},{16,20},{20,16},{24,28},{28,24},{1,5},{5... | collective-permute-start | bytes 798728 | tf_op jit(solution)/shard_map/ppermute | solution.py:415
  59.5 6.7 %collective-permute-start.15 = (f32[520,128]{1,0:T(8,128)S(1)}, f32[520,128]{1,0:T(8,128)S(1)}, u32[]{:S(2)}, u32[]{:S(2)}) collective-permute-start(f32[520,128]{1,0:T(8,128)S(1)} %shard_map.118.refs_2_), channel_id=1, source_target_pairs={{0,4},{4,0},{8,12},{12,8},{16,20},{20,16},{24,28},{28,24},{1,5},{5... | collective-permute-start | bytes 798728 | tf_op jit(solution)/shard_map/ppermute | solution.py:418
  61.0 5.9 %collective-permute-start.14 = (f32[512,128]{1,0:T(8,128)S(1)}, f32[512,128]{1,0:T(8,128)S(1)}, u32[]{:S(2)}, u32[]{:S(2)}) collective-permute-start(f32[512,128]{1,0:T(8,128)S(1)} %shard_map.119.refs_6_), channel_id=1, source_target_pairs={{24,16},{28,20},{25,17},{29,21},{26,18},{30,22},{27,19},{31,23}} | collective-permute-start | bytes 786440 | tf_op jit(solution)/shard_map/ppermute | solution.py:443
  66.2 5.4 %collective-permute-start.17 = (f32[512,128]{1,0:T(8,128)S(1)}, f32[512,128]{1,0:T(8,128)S(1)}, u32[]{:S(2)}, u32[]{:S(2)}) collective-permute-start(f32[512,128]{1,0:T(8,128)S(1)} %shard_map.121.refs_3_), channel_id=1, source_target_pairs={{24,16},{28,20},{25,17},{29,21},{26,18},{30,22},{27,19},{31,23}} | collective-permute-start | bytes 786440 | tf_op jit(solution)/shard_map/ppermute | solution.py:443
  66.9 5.3 %collective-permute-start.16 = (f32[512,128]{1,0:T(8,128)S(1)}, f32[512,128]{1,0:T(8,128)S(1)}, u32[]{:S(2)}, u32[]{:S(2)}) collective-permute-start(f32[512,128]{1,0:T(8,128)S(1)} %shard_map.122.refs_7_), channel_id=1, source_target_pairs={{16,8},{20,12},{17,9},{21,13},{18,10},{22,14},{19,11},{23,15}} | collective-permute-start | bytes 786440 | tf_op jit(solution)/shard_map/ppermute | solution.py:443
  71.6 6.0 %collective-permute-start.18 = (f32[512,128]{1,0:T(8,128)S(1)}, f32[512,128]{1,0:T(8,128)S(1)}, u32[]{:S(2)}, u32[]{:S(2)}) collective-permute-start(f32[512,128]{1,0:T(8,128)S(1)} %shard_map.124.refs_3_), channel_id=1, source_target_pairs={{16,8},{20,12},{17,9},{21,13},{18,10},{22,14},{19,11},{23,15}} | collective-permute-start | bytes 786440 | tf_op jit(solution)/shard_map/ppermute | solution.py:443
  72.3 19.6 %collective-permute-start.20 = (f32[512,128]{1,0:T(8,128)S(1)}, f32[512,128]{1,0:T(8,128)S(1)}, u32[]{:S(2)}, u32[]{:S(2)}) collective-permute-start(f32[512,128]{1,0:T(8,128)S(1)} %shard_map.125.refs_7_), channel_id=1, source_target_pairs={{8,0},{12,4},{9,1},{13,5},{10,2},{14,6},{11,3},{15,7}} | collective-permute-start | bytes 786440 | tf_op jit(solution)/shard_map/ppermute | solution.py:443
  77.6 18.0 %collective-permute-start.19 = (f32[512,128]{1,0:T(8,128)S(1)}, f32[512,128]{1,0:T(8,128)S(1)}, u32[]{:S(2)}, u32[]{:S(2)}) collective-permute-start(f32[512,128]{1,0:T(8,128)S(1)} %shard_map.127.refs_7_), channel_id=1, source_target_pairs={{8,0},{12,4},{9,1},{13,5},{10,2},{14,6},{11,3},{15,7}} | collective-permute-start | bytes 786440 | tf_op jit(solution)/shard_map/ppermute | solution.py:443
  92.0 9.0 %collective-permute-start.22 = (f32[512,128]{1,0:T(8,128)S(1)}, f32[512,128]{1,0:T(8,128)S(1)}, u32[]{:S(2)}, u32[]{:S(2)}) collective-permute-start(f32[512,128]{1,0:T(8,128)S(1)} %get-tuple-element.94.refs_6_), channel_id=1, source_target_pairs={{0,4},{4,0},{8,12},{12,8},{16,20},{20,16},{24,28},{28,24},{1,5},{5... | collective-permute-start | bytes 786440 | tf_op jit(solution)/shard_map/ppermute | solution.py:456
  95.7 8.4 %collective-permute-start.21 = (f32[512,128]{1,0:T(8,128)S(1)}, f32[512,128]{1,0:T(8,128)S(1)}, u32[]{:S(2)}, u32[]{:S(2)}) collective-permute-start(f32[512,128]{1,0:T(8,128)S(1)} %get-tuple-element.96.refs_8_), channel_id=1, source_target_pairs={{0,4},{4,0},{8,12},{12,8},{16,20},{20,16},{24,28},{28,24},{1,5},{5... | collective-permute-start | bytes 786440 | tf_op jit(solution)/shard_map/ppermute | solution.py:456

commit v3 on v2

--- a/solution.py
+++ b/solution.py
@@ -304,7 +304,7 @@
             out_ref[cols(j), :] = value
 
 
-def last_kernel(half, position, info, keep_ref, got_ref, *refs):
+def last_kernel(half, position, info, keep_ref, front_ref, other_ref, *refs):
     arrived, (mine_ref, send_ref) = refs[:-2], refs[-2:]
     is_first, place = position(info)
     for p in range(len(arrived) + 1):
@@ -312,7 +312,9 @@
         @pl.when(place == p)
         def _():
             for j in range(half):
-                first, _, first_decay, _ = ordered(is_first, half, j, keep_ref, got_ref)
+                first, _, first_decay, _ = ordered(
+                    is_first, half, j, keep_ref, front_ref if p == 0 else other_ref
+                )
                 if p == 0:
                     before, after = jnp.zeros_like(first), first
                 else:
@@ -412,27 +414,34 @@
             c = len(received)
             if c == 0 or c >= chunks:
                 if c == 0:
-                    received.append(lax.ppermute(sends[0], "seq", swap))
+                    received.append([
+                        lax.ppermute(sends[0], "seq", [(device(p, m), device(p, 1 - m)) for p in ps for m in (0, 1)])
+                        for ps in ((0,), range(1, places))
+                    ])
                 return last
             sent, = run(copy_kernel, 1, [plain(sends[c])], [give(wide_state)], after=last, cost=0.02)
-            received.append(lax.ppermute(sent, "seq", swap))
+            received.append([lax.ppermute(sent, "seq", swap)])
             return (sent,)
 
         for part in their_parts:
             sends.append(make_piece(part, last))
             last = () if forward and len(sends) == 1 else (sends[-1],)
         last = exchange(last)
-        for part in my_parts:
-            keeps.append(make_piece(part, last))
+        if forward:
+            last = exchange(last)
+        rest = [functools.partial(make_piece, part) for part in my_parts]
+        for make in rest[:1] if forward else rest:
+            keeps.append(make(last))
             last = (keeps[-1],)
-        last = exchange(last + (received[0],) if forward else last)
+        if not forward:
+            last = exchange(last)
         arrived, mine, theirs, late = {}, [], [], []
         for step in range(chunks + places - 1):
             for p in range(places - 1):
                 c = step - p
                 if not 0 <= c < chunks:
                     continue
-                ins = [plain(keeps[c]), plain(received[c])]
+                ins = [plain(keeps[c]), plain(received[c][0 if p == 0 else -1])]
                 if p > 0:
                     ins.append(plain(arrived[c, p]))
                 value, = run(
@@ -443,11 +452,16 @@
                 arrived[c, p + 1] = lax.ppermute(value, "seq", pairs)
                 last = (value,)
             last = exchange(last)
+            while len(keeps) < chunks:
+                keeps.append(rest[len(keeps)](last))
+                last = (keeps[-1],)
+            if step == 0:
+                last += (received[0][-1],)
             if filler:
                 last = (filler.pop(0)(last),)
             c = step + 1 - places
             if c >= 0:
-                ins = [plain(keeps[c]), plain(received[c])]
+                ins = [plain(keeps[c]), plain(received[c][0]), plain(received[c][-1])]
                 ins += [plain(arrived[c, p]) for p in range(1, places)]
                 own, send = run(
                     functools.partial(last_kernel, count, position), 1, ins, [give(state)] * 2,

time: 106 us -> 110 us (1.038)
  starting transfers between devices: 27.2 us -> 30.6 us
    ppermute x4 -> x6, starting transfers between devices: 6.86 us -> 10.5 us  [the longest x4 9.83 us: exchange(): lax.ppermute(sends[0], 'seq', [(device(p, m), device(p, 1 - m)) for p in...]
    ppermute x4 -> x6, waiting for transfers between devices: 2.52 us -> 3.39 us  [the longest x2 1.75 us: exchange(): received.append([lax.ppermute(sent, 'seq', swap)])]
  transfers between devices with their start and end apart: 23 -> 25, of which waited for: 12 -> 12; matrix products, arithmetic and copies ran while one was open for 0% -> 0% of each run, Pallas kernels for 38% -> 37%
where the time goes in v3:
time: 110 us
  Pallas kernels  48 us (44%)
  starting transfers between devices  30.6 us (28%)
  waiting for transfers between devices  27.2 us (25%)
  local copies, waits for them, and re-layouts  3.02 us (3%)
    pallas_call x42, Pallas kernels, run(): pl.pallas_call(body, out_shape=[shape for shape, _ in outs], grid_spec=pl...  48 us
    ppermute x12, starting transfers between devices, chain(): arrived[c, p + 1] = lax.ppermute(value, 'seq', pairs)  14.2 us
    ppermute x12, waiting for transfers between devices, chain(): arrived[c, p + 1] = lax.ppermute(value, 'seq', pairs)  11.4 us
    ppermute x4, starting transfers between devices, exchange(): lax.ppermute(sends[0], 'seq', [(device(p, m), device(p, 1 - m)) for p in...  9.83 us
    ppermute x4, waiting for transfers between devices, chain(): theirs.append(lax.ppermute(send, 'seq', swap))  9.42 us
    ppermute x4, starting transfers between devices, chain(): theirs.append(lax.ppermute(send, 'seq', swap))  4.14 us
    unnamed x16, local copies, waits for them, and re-layouts  3.02 us
    ppermute x3, waiting for transfers between devices, on_device(): lax.ppermute(sums, 'head', [(i, (i + k) % head_count) for i in range(head...  2.96 us
  transfers between devices with their start and end apart: 25, of which 12 were waited for; matrix products, arithmetic and copies ran while one was open for 0% of the time, Pallas kernels for 37%

profile of v3, /device:TPU:0, one launch (start us, length us, event | category | flops | bytes accessed | tf_op | source)
XLA Modules:
  0.0 109.8 jit_solution(15926351565116827423)
XLA Ops:
  0.7 3.0 %shard_map.93 = (f32[520,128]{1,0:T(8,128)}, f32[16,512]{1,0:T(8,128)}) custom-call(s32[1]{0:T(128)} %bitcast.member_ref, s32[1]{0:T(128)} %bitcast.1.pair_ref, bf16[512,2048]{1,0:T(8,128)(2,1)} %refs_2_.31, bf16[512,2048]{1,0:T(8,128)(2,1)} %refs_3_.15, f32[16,512]{1,0:T(8,128)} %bitcast.12), custom_call_target="tpu_custom_call" | custom-call | flops 50000000 | bytes 125000 | tf_op jit(solution)/shard_map/pallas_call | solution.py:357
  3.6 4.9 %collective-permute-start.1 = (f32[520,128]{1,0:T(8,128)}, f32[520,128]{1,0:T(8,128)S(1)}, u32[]{:S(2)}, u32[]{:S(2)}) collective-permute-start(f32[520,128]{1,0:T(8,128)} %get-tuple-element.58), channel_id=1, source_target_pairs={{0,4},{4,0},{1,5},{5,1},{2,6},{6,2},{3,7},{7,3}} | collective-permute-start | bytes 798728 | tf_op jit(solution)/shard_map/ppermute | solution.py:418
  9.2 1.6 %copy-done.2 = bf16[512,2048]{1,0:T(8,128)(2,1)S(1)} copy-done((bf16[512,2048]{1,0:T(8,128)(2,1)S(1)}, bf16[512,2048]{1,0:T(8,128)(2,1)}, u32[]{:S(2)}) %copy-start.2) | copy-done | bytes 2097176
  14.0 1.6 %collective-permute-done.1.refs_1_ = f32[520,128]{1,0:T(8,128)S(1)} collective-permute-done((f32[520,128]{1,0:T(8,128)}, f32[520,128]{1,0:T(8,128)S(1)}, u32[]{:S(2)}, u32[]{:S(2)}) %collective-permute-start.1) | collective-permute-done | bytes 266272 | tf_op jit(solution)/shard_map/ppermute | solution.py:418
  15.7 2.0 %collective-permute-start.2 = (f32[512,128]{1,0:T(8,128)S(1)}, f32[512,128]{1,0:T(8,128)S(1)}, u32[]{:S(2)}, u32[]{:S(2)}) collective-permute-start(f32[512,128]{1,0:T(8,128)S(1)} %shard_map.97.refs_3_), channel_id=1, source_target_pairs={{0,8},{4,12},{1,9},{5,13},{2,10},{6,14},{3,11},{7,15}} | collective-permute-start | bytes 786440 | tf_op jit(solution)/shard_map/ppermute | solution.py:452
  18.5 1.9 %shard_map.99.refs_2_.refs_0_ = f32[512,512]{1,0:T(8,128)S(1)} custom-call(s32[1]{0:T(128)} %bitcast.member_ref, s32[1]{0:T(128)} %bitcast.1.pair_ref, bf16[512,2048]{1,0:T(8,128)(2,1)S(1)} %copy-done, bf16[512,2048]{1,0:T(8,128)(2,1)S(1)} %copy-done.1, bf16[512,2048]{1,0:T(8,128)(2,1)S(1)} %copy-done.3, f32[16,512]{1,0:T(8,128)S(1)} %copy-done.5, ...), custom_call_target="tpu_custom_call" | custom-call | flops 100000000 | bytes 250000 | tf_op jit(solution)/shard_map/pallas_call | solution.py:357
  20.8 4.3 %collective-permute-start.5 = (f32[512,128]{1,0:T(8,128)S(1)}, f32[512,128]{1,0:T(8,128)S(1)}, u32[]{:S(2)}, u32[]{:S(2)}) collective-permute-start(f32[512,128]{1,0:T(8,128)S(1)} %shard_map.100.refs_3_), channel_id=1, source_target_pairs={{0,8},{4,12},{1,9},{5,13},{2,10},{6,14},{3,11},{7,15}} | collective-permute-start | bytes 786440 | tf_op jit(solution)/shard_map/ppermute | solution.py:452
  25.9 1.9 %shard_map.102.refs_3_.refs_0_ = f32[512,512]{1,0:T(8,128)S(1)} custom-call(s32[1]{0:T(128)} %bitcast.member_ref, s32[1]{0:T(128)} %bitcast.1.pair_ref, bf16[512,2048]{1,0:T(8,128)(2,1)S(1)} %copy-done, bf16[512,2048]{1,0:T(8,128)(2,1)S(1)} %copy-done.1, bf16[512,2048]{1,0:T(8,128)(2,1)S(1)} %copy-done.3, f32[16,512]{1,0:T(8,128)S(1)} %copy-done.5, ...), custom_call_target="tpu_custom_call" | custom-call | flops 2200000000 | bytes 5500000 | tf_op jit(solution)/shard_map/pallas_call | solution.py:357
  27.8 2.0 %collective-permute-done.5.refs_2_.refs_3_ = f32[512,128]{1,0:T(8,128)S(1)} collective-permute-done((f32[512,128]{1,0:T(8,128)S(1)}, f32[512,128]{1,0:T(8,128)S(1)}, u32[]{:S(2)}, u32[]{:S(2)}) %collective-permute-start.5) | collective-permute-done | bytes 262176 | tf_op jit(solution)/shard_map/ppermute | solution.py:452
  31.2 1.9 %shard_map.105.refs_3_.refs_0_ = f32[512,512]{1,0:T(8,128)S(1)} custom-call(s32[1]{0:T(128)} %bitcast.member_ref, s32[1]{0:T(128)} %bitcast.1.pair_ref, bf16[512,2048]{1,0:T(8,128)(2,1)S(1)} %copy-done, bf16[512,2048]{1,0:T(8,128)(2,1)S(1)} %copy-done.1, bf16[512,2048]{1,0:T(8,128)(2,1)S(1)} %copy-done.3, f32[16,512]{1,0:T(8,128)S(1)} %copy-done.6, ...), custom_call_target="tpu_custom_call" | custom-call | flops 2200000000 | bytes 5500000 | tf_op jit(solution)/shard_map/pallas_call | solution.py:357
  33.9 1.9 %shard_map.107.refs_6_.refs_0_ = f32[512,512]{1,0:T(8,128)S(1)} custom-call(s32[1]{0:T(128)} %bitcast.member_ref, s32[1]{0:T(128)} %bitcast.1.pair_ref, bf16[512,2048]{1,0:T(8,128)(2,1)S(1)} %copy-done, bf16[512,2048]{1,0:T(8,128)(2,1)S(1)} %copy-done.1, bf16[512,2048]{1,0:T(8,128)(2,1)S(1)} %copy-done.3, f32[16,512]{1,0:T(8,128)S(1)} %copy-done.6, ...), custom_call_target="tpu_custom_call" | custom-call | flops 2200000000 | bytes 5500000 | tf_op jit(solution)/shard_map/pallas_call | solution.py:357
  35.9 1.6 %collective-permute-start.10 = (f32[512,128]{1,0:T(8,128)S(1)}, f32[512,128]{1,0:T(8,128)S(1)}, u32[]{:S(2)}, u32[]{:S(2)}) collective-permute-start(f32[512,128]{1,0:T(8,128)S(1)} %get-tuple-element.60.refs_7_), channel_id=1, source_target_pairs={{0,4},{4,0},{8,12},{12,8},{16,20},{20,16},{24,28},{28,24},{1,5},{5... | collective-permute-start | bytes 786440 | tf_op jit(solution)/shard_map/ppermute | solution.py:470
  41.3 3.7 %collective-permute-done.10.refs_5_ = f32[512,128]{1,0:T(8,128)S(1)} collective-permute-done((f32[512,128]{1,0:T(8,128)S(1)}, f32[512,128]{1,0:T(8,128)S(1)}, u32[]{:S(2)}, u32[]{:S(2)}) %collective-permute-start.10) | collective-permute-done | bytes 262176 | tf_op jit(solution)/shard_map/ppermute | solution.py:470
  46.2 1.7 %collective-permute-done.9.refs_5_ = f32[512,128]{1,0:T(8,128)S(1)} collective-permute-done((f32[512,128]{1,0:T(8,128)S(1)}, f32[512,128]{1,0:T(8,128)S(1)}, u32[]{:S(2)}, u32[]{:S(2)}) %collective-permute-start.9) | collective-permute-done | bytes 262176 | tf_op jit(solution)/shard_map/ppermute | solution.py:470
  49.0 1.5 %collective-permute-start.12 = (f32[8,512]{1,0:T(8,128)S(1)}, f32[8,512]{1,0:T(8,128)S(1)}, u32[]{:S(2)}, u32[]{:S(2)}) collective-permute-start(f32[8,512]{1,0:T(8,128)S(1)} %get-tuple-element.67.refs_5_), channel_id=1, source_target_pairs={{0,2},{1,3},{2,0},{3,1},{4,6},{5,7},{6,4},{7,5},{8,10},{9,11},{10,... | collective-permute-start | bytes 49160 | tf_op jit(solution)/shard_map/ppermute | solution.py:539
  50.7 2.1 %collective-permute-done.12.refs_7_ = f32[8,512]{1,0:T(8,128)S(1)} collective-permute-done((f32[8,512]{1,0:T(8,128)S(1)}, f32[8,512]{1,0:T(8,128)S(1)}, u32[]{:S(2)}, u32[]{:S(2)}) %collective-permute-start.12) | collective-permute-done | bytes 16416 | tf_op jit(solution)/shard_map/ppermute | solution.py:539
  53.7 1.7 %shard_map.114 = (bf16[512,2048]{1,0:T(8,128)(2,1)}, bf16[512,512]{1,0:T(8,128)(2,1)S(1)}, f32[520,128]{1,0:T(8,128)S(1)}) custom-call(s32[1]{0:T(128)} %bitcast.member_ref, s32[1]{0:T(128)} %bitcast.1.pair_ref, f32[512,512]{1,0:T(8,128)S(1)} %get-tuple-element.70.refs_0_, bf16[512,2048]{1,0:T(8,128)(2,1)S(1)} %copy-done.4, f32[1,2048]{1,0:T(1,128)S(1)} %bitcast.8, ...), custom_call_target="tpu_custom_call" | custom-call | flops 2000000000 | bytes 5000000 | tf_op jit(solution)/shard_map/pallas_call | solution.py:357
  55.4 3.4 %collective-permute-start.15 = (f32[520,128]{1,0:T(8,128)S(1)}, f32[520,128]{1,0:T(8,128)S(1)}, u32[]{:S(2)}, u32[]{:S(2)}) collective-permute-start(f32[520,128]{1,0:T(8,128)S(1)} %get-tuple-element.72.refs_10_), channel_id=1, source_target_pairs={{16,20},{20,16},{8,12},{12,8},{0,4},{4,0},{17,21},{21,17},{9,13},{... | collective-permute-start | bytes 798728 | tf_op jit(solution)/shard_map/ppermute | solution.py:418
  59.7 1.8 %shard_map.115 = (bf16[512,2048]{1,0:T(8,128)(2,1)}, bf16[512,512]{1,0:T(8,128)(2,1)S(1)}, f32[520,128]{1,0:T(8,128)S(1)}) custom-call(s32[1]{0:T(128)} %bitcast.member_ref, s32[1]{0:T(128)} %bitcast.1.pair_ref, f32[512,512]{1,0:T(8,128)S(1)} %get-tuple-element.69.refs_0_, bf16[512,2048]{1,0:T(8,128)(2,1)S(1)} %copy-done.4, ...), custom_call_target="tpu_custom_call", output_to_operand_aliasing={{0}: (11, {})} | custom-call | flops 2000000000 | bytes 5000000 | tf_op jit(solution)/shard_map/pallas_call | solution.py:357
  61.5 1.7 %shard_map.116 = (bf16[512,2048]{1,0:T(8,128)(2,1)}, bf16[512,512]{1,0:T(8,128)(2,1)S(1)}, f32[520,128]{1,0:T(8,128)S(1)}) custom-call(s32[1]{0:T(128)} %bitcast.member_ref, s32[1]{0:T(128)} %bitcast.1.pair_ref, f32[512,512]{1,0:T(8,128)S(1)} %get-tuple-element.68.refs_0_, bf16[512,2048]{1,0:T(8,128)(2,1)S(1)} %copy-done.4, ...), custom_call_target="tpu_custom_call", output_to_operand_aliasing={{0}: (11, {})} | custom-call | flops 2000000000 | bytes 5000000 | tf_op jit(solution)/shard_map/pallas_call | solution.py:357
  63.2 1.7 %shard_map.117 = (bf16[512,2048]{1,0:T(8,128)(2,1)}, bf16[512,512]{1,0:T(8,128)(2,1)S(1)}, f32[520,128]{1,0:T(8,128)S(1)}) custom-call(s32[1]{0:T(128)} %bitcast.member_ref, s32[1]{0:T(128)} %bitcast.1.pair_ref, f32[512,512]{1,0:T(8,128)S(1)} %get-tuple-element.64.refs_0_, bf16[512,2048]{1,0:T(8,128)(2,1)S(1)} %copy-done.4, ...), custom_call_target="tpu_custom_call", output_to_operand_aliasing={{0}: (11, {})} | custom-call | flops 2000000000 | bytes 5000000 | tf_op jit(solution)/shard_map/pallas_call | solution.py:357
  66.2 4.0 %shard_map.120 = (bf16[512,2048]{1,0:T(8,128)(2,1)}, f32[512,512]{1,0:T(8,128)S(1)}, f32[512,512]{1,0:T(8,128)S(1)}) custom-call(s32[1]{0:T(128)} %bitcast.member_ref, s32[1]{0:T(128)} %bitcast.1.pair_ref, bf16[512,2048]{1,0:T(8,128)(2,1)S(1)} %copy-done, bf16[512,2048]{1,0:T(8,128)(2,1)S(1)} %copy-done.1, bf16[512,2048]{1,0:T(8,128)(2,1)S(1)} %copy-done.3, ...), custom_call_target="tpu_custom_call" | custom-call | flops 4300000256 | bytes 10750000 | tf_op jit(solution)/shard_map/pallas_call | solution.py:357
  72.9 4.0 %shard_map.123 = (bf16[512,2048]{1,0:T(8,128)(2,1)}, f32[512,512]{1,0:T(8,128)S(1)}, f32[512,512]{1,0:T(8,128)S(1)}) custom-call(s32[1]{0:T(128)} %bitcast.member_ref, s32[1]{0:T(128)} %bitcast.1.pair_ref, bf16[512,2048]{1,0:T(8,128)(2,1)S(1)} %copy-done, bf16[512,2048]{1,0:T(8,128)(2,1)S(1)} %copy-done.1, ...), custom_call_target="tpu_custom_call", output_to_operand_aliasing={{0}: (8, {})} | custom-call | flops 4300000256 | bytes 10750000 | tf_op jit(solution)/shard_map/pallas_call | solution.py:357
  78.9 4.0 %shard_map.126 = (bf16[512,2048]{1,0:T(8,128)(2,1)}, f32[512,512]{1,0:T(8,128)S(1)}, f32[512,512]{1,0:T(8,128)S(1)}) custom-call(s32[1]{0:T(128)} %bitcast.member_ref, s32[1]{0:T(128)} %bitcast.1.pair_ref, bf16[512,2048]{1,0:T(8,128)(2,1)S(1)} %copy-done, bf16[512,2048]{1,0:T(8,128)(2,1)S(1)} %copy-done.1, ...), custom_call_target="tpu_custom_call", output_to_operand_aliasing={{0}: (8, {})} | custom-call | flops 4300000256 | bytes 10750000 | tf_op jit(solution)/shard_map/pallas_call | solution.py:357
  84.2 4.0 %shard_map.128 = (bf16[512,2048]{1,0:T(8,128)(2,1)}, f32[512,512]{1,0:T(8,128)S(1)}, f32[512,512]{1,0:T(8,128)S(1)}) custom-call(s32[1]{0:T(128)} %bitcast.member_ref, s32[1]{0:T(128)} %bitcast.1.pair_ref, bf16[512,2048]{1,0:T(8,128)(2,1)S(1)} %copy-done, bf16[512,2048]{1,0:T(8,128)(2,1)S(1)} %copy-done.1, ...), custom_call_target="tpu_custom_call", output_to_operand_aliasing={{0}: (8, {})} | custom-call | flops 4300000256 | bytes 10750000 | tf_op jit(solution)/shard_map/pallas_call | solution.py:357
  88.1 7.8 %collective-permute-done.22.refs_5_ = f32[512,128]{1,0:T(8,128)S(1)} collective-permute-done((f32[512,128]{1,0:T(8,128)S(1)}, f32[512,128]{1,0:T(8,128)S(1)}, u32[]{:S(2)}, u32[]{:S(2)}) %collective-permute-start.22) | collective-permute-done | bytes 262176 | tf_op jit(solution)/shard_map/ppermute | solution.py:452
  96.1 1.8 %shard_map.130 = (bf16[512,2048]{1,0:T(8,128)(2,1)}, bf16[512,2048]{1,0:T(8,128)(2,1)}, f32[8,128]{1,0:T(8,128)S(1)}) custom-call(s32[1]{0:T(128)} %bitcast.member_ref, s32[1]{0:T(128)} %bitcast.1.pair_ref, f32[512,512]{1,0:T(8,128)S(1)} %get-tuple-element.84.refs_2_.refs_0_, f32[512,512]{1,0:T(8,128)S(1)} %get-tuple-element.92.refs_1_, ...), custom_call_target="tpu_custom_call" | custom-call | flops 2000000000 | bytes 5000000 | tf_op jit(solution)/shard_map/pallas_call | solution.py:357
  98.0 1.5 %collective-permute-done.21.refs_5_ = f32[512,128]{1,0:T(8,128)S(1)} collective-permute-done((f32[512,128]{1,0:T(8,128)S(1)}, f32[512,128]{1,0:T(8,128)S(1)}, u32[]{:S(2)}, u32[]{:S(2)}) %collective-permute-start.21) | collective-permute-done | bytes 262176 | tf_op jit(solution)/shard_map/ppermute | solution.py:452
  100.6 1.7 %shard_map.132 = (bf16[512,2048]{1,0:T(8,128)(2,1)}, bf16[512,2048]{1,0:T(8,128)(2,1)}, f32[8,128]{1,0:T(8,128)S(1)}) custom-call(s32[1]{0:T(128)} %bitcast.member_ref, s32[1]{0:T(128)} %bitcast.1.pair_ref, f32[512,512]{1,0:T(8,128)S(1)} %get-tuple-element.88.refs_3_.refs_0_, ...), custom_call_target="tpu_custom_call", output_to_operand_aliasing={{0}: (8, {}), {1}: (9, {})} | custom-call | flops 2000000000 | bytes 5000000 | tf_op jit(solution)/shard_map/pallas_call | solution.py:357
  102.4 2.9 %collective-permute-done.24.refs_5_ = f32[512,128]{1,0:T(8,128)S(1)} collective-permute-done((f32[512,128]{1,0:T(8,128)S(1)}, f32[512,128]{1,0:T(8,128)S(1)}, u32[]{:S(2)}, u32[]{:S(2)}) %collective-permute-start.24) | collective-permute-done | bytes 262176 | tf_op jit(solution)/shard_map/ppermute | solution.py:470
  105.2 1.7 %shard_map.133 = (bf16[512,2048]{1,0:T(8,128)(2,1)}, bf16[512,2048]{1,0:T(8,128)(2,1)}, f32[8,128]{1,0:T(8,128)S(1)}) custom-call(s32[1]{0:T(128)} %bitcast.member_ref, s32[1]{0:T(128)} %bitcast.1.pair_ref, f32[512,512]{1,0:T(8,128)S(1)} %get-tuple-element.86.refs_3_.refs_0_, ...), custom_call_target="tpu_custom_call", output_to_operand_aliasing={{0}: (8, {}), {1}: (9, {})} | custom-call | flops 2000000000 | bytes 5000000 | tf_op jit(solution)/shard_map/pallas_call | solution.py:357
  108.1 1.7 %shard_map.134 = (bf16[512,2048]{1,0:T(8,128)(2,1)}, bf16[512,2048]{1,0:T(8,128)(2,1)}, f32[8,128]{1,0:T(8,128)}) custom-call(s32[1]{0:T(128)} %bitcast.member_ref, s32[1]{0:T(128)} %bitcast.1.pair_ref, f32[512,512]{1,0:T(8,128)S(1)} %get-tuple-element.90.refs_6_.refs_0_, ...), custom_call_target="tpu_custom_call", output_to_operand_aliasing={{0}: (8, {}), {1}: (9, {})} | custom-call | flops 2000000000 | bytes 5000000 | tf_op jit(solution)/shard_map/pallas_call | solution.py:357
  (77 shorter events, 25.7 us)
Async XLA Ops:
  0.7 8.5 %copy-start.1 = (bf16[512,2048]{1,0:T(8,128)(2,1)S(1)}, bf16[512,2048]{1,0:T(8,128)(2,1)}, u32[]{:S(2)}) copy-start(bf16[512,2048]{1,0:T(8,128)(2,1)} %refs_2_.31) | copy-start | bytes 6291460
  3.6 12.0 %collective-permute-start.1 = (f32[520,128]{1,0:T(8,128)}, f32[520,128]{1,0:T(8,128)S(1)}, u32[]{:S(2)}, u32[]{:S(2)}) collective-permute-start(f32[520,128]{1,0:T(8,128)} %get-tuple-element.58), channel_id=1, source_target_pairs={{0,4},{4,0},{1,5},{5,1},{2,6},{6,2},{3,7},{7,3}} | collective-permute-start | bytes 798728 | tf_op jit(solution)/shard_map/ppermute | solution.py:418
  8.5 10.0 %collective-permute-start = (f32[520,128]{1,0:T(8,128)}, f32[520,128]{1,0:T(8,128)S(1)}, u32[]{:S(2)}, u32[]{:S(2)}) collective-permute-start(f32[520,128]{1,0:T(8,128)} %get-tuple-element.58), channel_id=1, source_target_pairs={{8,12},{12,8},{16,20},{20,16},{24,28},{28,24},{9,13},{13,9},{17,21... | collective-permute-start | bytes 798728 | tf_op jit(solution)/shard_map/ppermute | solution.py:418
  9.2 1.6 %copy-start.2 = (bf16[512,2048]{1,0:T(8,128)(2,1)S(1)}, bf16[512,2048]{1,0:T(8,128)(2,1)}, u32[]{:S(2)}) copy-start(bf16[512,2048]{1,0:T(8,128)(2,1)} %refs_3_.15) | copy-start | bytes 6291460
  11.5 1.6 %copy-start.3 = (bf16[512,2048]{1,0:T(8,128)(2,1)S(1)}, bf16[512,2048]{1,0:T(8,128)(2,1)}, u32[]{:S(2)}) copy-start(bf16[512,2048]{1,0:T(8,128)(2,1)} %refs_3_.15) | copy-start | bytes 6291460
  12.4 8.4 %collective-permute-start.3 = (f32[520,128]{1,0:T(8,128)S(1)}, f32[520,128]{1,0:T(8,128)S(1)}, u32[]{:S(2)}, u32[]{:S(2)}) collective-permute-start(f32[520,128]{1,0:T(8,128)S(1)} %shard_map.95.refs_3_), channel_id=1, source_target_pairs={{0,4},{4,0},{8,12},{12,8},{16,20},{20,16},{24,28},{28,24},{1,5},{5... | collective-permute-start | bytes 798728 | tf_op jit(solution)/shard_map/ppermute | solution.py:423
  15.7 2.8 %copy-start = (bf16[512,2048]{1,0:T(8,128)(2,1)S(1)}, bf16[512,2048]{1,0:T(8,128)(2,1)}, u32[]{:S(2)}) copy-start(bf16[512,2048]{1,0:T(8,128)(2,1)} %refs_0_.23) | copy-start | bytes 6291460
  15.7 9.5 %collective-permute-start.2 = (f32[512,128]{1,0:T(8,128)S(1)}, f32[512,128]{1,0:T(8,128)S(1)}, u32[]{:S(2)}, u32[]{:S(2)}) collective-permute-start(f32[512,128]{1,0:T(8,128)S(1)} %shard_map.97.refs_3_), channel_id=1, source_target_pairs={{0,8},{4,12},{1,9},{5,13},{2,10},{6,14},{3,11},{7,15}} | collective-permute-start | bytes 786440 | tf_op jit(solution)/shard_map/ppermute | solution.py:452
  20.8 9.0 %collective-permute-start.5 = (f32[512,128]{1,0:T(8,128)S(1)}, f32[512,128]{1,0:T(8,128)S(1)}, u32[]{:S(2)}, u32[]{:S(2)}) collective-permute-start(f32[512,128]{1,0:T(8,128)S(1)} %shard_map.100.refs_3_), channel_id=1, source_target_pairs={{0,8},{4,12},{1,9},{5,13},{2,10},{6,14},{3,11},{7,15}} | collective-permute-start | bytes 786440 | tf_op jit(solution)/shard_map/ppermute | solution.py:452
  25.2 5.3 %collective-permute-start.4 = (f32[512,128]{1,0:T(8,128)S(1)}, f32[512,128]{1,0:T(8,128)S(1)}, u32[]{:S(2)}, u32[]{:S(2)}) collective-permute-start(f32[512,128]{1,0:T(8,128)S(1)} %shard_map.101.refs_4_), channel_id=1, source_target_pairs={{8,16},{12,20},{9,17},{13,21},{10,18},{14,22},{11,19},{15,23}} | collective-permute-start | bytes 786440 | tf_op jit(solution)/shard_map/ppermute | solution.py:452
  27.8 3.4 %copy-start.6 = (f32[16,512]{1,0:T(8,128)S(1)}, f32[16,512]{1,0:T(8,128)}, u32[]{:S(2)}) copy-start(f32[16,512]{1,0:T(8,128)} %get-tuple-element.57.refs_2_.refs_3_.refs_4_) | copy-start | bytes 98308
  29.8 3.3 %collective-permute-start.6 = (f32[512,128]{1,0:T(8,128)S(1)}, f32[512,128]{1,0:T(8,128)S(1)}, u32[]{:S(2)}, u32[]{:S(2)}) collective-permute-start(f32[512,128]{1,0:T(8,128)S(1)} %shard_map.103.refs_3_), channel_id=1, source_target_pairs={{8,16},{12,20},{9,17},{13,21},{10,18},{14,22},{11,19},{15,23}} | collective-permute-start | bytes 786440 | tf_op jit(solution)/shard_map/ppermute | solution.py:452
  30.5 5.3 %collective-permute-start.8 = (f32[512,128]{1,0:T(8,128)S(1)}, f32[512,128]{1,0:T(8,128)S(1)}, u32[]{:S(2)}, u32[]{:S(2)}) collective-permute-start(f32[512,128]{1,0:T(8,128)S(1)} %shard_map.104.refs_4_), channel_id=1, source_target_pairs={{16,24},{20,28},{17,25},{21,29},{18,26},{22,30},{19,27},{23,31}} | collective-permute-start | bytes 786440 | tf_op jit(solution)/shard_map/ppermute | solution.py:452
  33.2 5.5 %collective-permute-start.7 = (f32[512,128]{1,0:T(8,128)S(1)}, f32[512,128]{1,0:T(8,128)S(1)}, u32[]{:S(2)}, u32[]{:S(2)}) collective-permute-start(f32[512,128]{1,0:T(8,128)S(1)} %shard_map.106.refs_4_), channel_id=1, source_target_pairs={{16,24},{20,28},{17,25},{21,29},{18,26},{22,30},{19,27},{23,31}} | collective-permute-start | bytes 786440 | tf_op jit(solution)/shard_map/ppermute | solution.py:452
  35.8 1.7 %copy-start.4 = (bf16[512,2048]{1,0:T(8,128)(2,1)S(1)}, bf16[512,2048]{1,0:T(8,128)(2,1)}, u32[]{:S(2)}) copy-start(bf16[512,2048]{1,0:T(8,128)(2,1)} %refs_1_.35) | copy-start | bytes 6291460
  35.8 1.7 %copy-start.7 = (f32[2048]{0:T(1024)S(1)}, f32[2048]{0:T(1024)}, u32[]{:S(2)}) copy-start(f32[2048]{0:T(1024)} %param.10) | copy-start | bytes 24580
  35.9 9.1 %collective-permute-start.10 = (f32[512,128]{1,0:T(8,128)S(1)}, f32[512,128]{1,0:T(8,128)S(1)}, u32[]{:S(2)}, u32[]{:S(2)}) collective-permute-start(f32[512,128]{1,0:T(8,128)S(1)} %get-tuple-element.60.refs_7_), channel_id=1, source_target_pairs={{0,4},{4,0},{8,12},{12,8},{16,20},{20,16},{24,28},{28,24},{1,5},{5... | collective-permute-start | bytes 786440 | tf_op jit(solution)/shard_map/ppermute | solution.py:470
  38.8 9.1 %collective-permute-start.9 = (f32[512,128]{1,0:T(8,128)S(1)}, f32[512,128]{1,0:T(8,128)S(1)}, u32[]{:S(2)}, u32[]{:S(2)}) collective-permute-start(f32[512,128]{1,0:T(8,128)S(1)} %get-tuple-element.63.refs_7_), channel_id=1, source_target_pairs={{0,4},{4,0},{8,12},{12,8},{16,20},{20,16},{24,28},{28,24},{1,5},{5... | collective-permute-start | bytes 786440 | tf_op jit(solution)/shard_map/ppermute | solution.py:470
  49.0 1.7 %collective-permute-start.13 = (f32[8,512]{1,0:T(8,128)S(1)}, f32[8,512]{1,0:T(8,128)S(1)}, u32[]{:S(2)}, u32[]{:S(2)}) collective-permute-start(f32[8,512]{1,0:T(8,128)S(1)} %get-tuple-element.67.refs_5_), channel_id=1, source_target_pairs={{0,3},{1,0},{2,1},{3,2},{4,7},{5,4},{6,5},{7,6},{8,11},{9,8},{10,9... | collective-permute-start | bytes 49160 | tf_op jit(solution)/shard_map/ppermute | solution.py:539
  49.0 3.8 %collective-permute-start.12 = (f32[8,512]{1,0:T(8,128)S(1)}, f32[8,512]{1,0:T(8,128)S(1)}, u32[]{:S(2)}, u32[]{:S(2)}) collective-permute-start(f32[8,512]{1,0:T(8,128)S(1)} %get-tuple-element.67.refs_5_), channel_id=1, source_target_pairs={{0,2},{1,3},{2,0},{3,1},{4,6},{5,7},{6,4},{7,5},{8,10},{9,11},{10,... | collective-permute-start | bytes 49160 | tf_op jit(solution)/shard_map/ppermute | solution.py:539
  50.5 3.2 %collective-permute-start.11 = (f32[8,512]{1,0:T(8,128)S(1)}, f32[8,512]{1,0:T(8,128)S(1)}, u32[]{:S(2)}, u32[]{:S(2)}) collective-permute-start(f32[8,512]{1,0:T(8,128)S(1)} %get-tuple-element.67.refs_5_), channel_id=1, source_target_pairs={{0,1},{1,2},{2,3},{3,0},{4,5},{5,6},{6,7},{7,4},{8,9},{9,10},{10,1... | collective-permute-start | bytes 49160 | tf_op jit(solution)/shard_map/ppermute | solution.py:539
  55.4 10.8 %collective-permute-start.15 = (f32[520,128]{1,0:T(8,128)S(1)}, f32[520,128]{1,0:T(8,128)S(1)}, u32[]{:S(2)}, u32[]{:S(2)}) collective-permute-start(f32[520,128]{1,0:T(8,128)S(1)} %get-tuple-element.72.refs_10_), channel_id=1, source_target_pairs={{16,20},{20,16},{8,12},{12,8},{0,4},{4,0},{17,21},{21,17},{9,13},{... | collective-permute-start | bytes 798728 | tf_op jit(solution)/shard_map/ppermute | solution.py:418
  58.8 6.6 %collective-permute-start.14 = (f32[520,128]{1,0:T(8,128)S(1)}, f32[520,128]{1,0:T(8,128)S(1)}, u32[]{:S(2)}, u32[]{:S(2)}) collective-permute-start(f32[520,128]{1,0:T(8,128)S(1)} %get-tuple-element.72.refs_10_), channel_id=1, source_target_pairs={{24,28},{28,24},{25,29},{29,25},{26,30},{30,26},{27,31},{31,27}} | collective-permute-start | bytes 798728 | tf_op jit(solution)/shard_map/ppermute | solution.py:418
  64.9 6.6 %collective-permute-start.17 = (f32[520,128]{1,0:T(8,128)S(1)}, f32[520,128]{1,0:T(8,128)S(1)}, u32[]{:S(2)}, u32[]{:S(2)}) collective-permute-start(f32[520,128]{1,0:T(8,128)S(1)} %shard_map.118.refs_2_), channel_id=1, source_target_pairs={{0,4},{4,0},{8,12},{12,8},{16,20},{20,16},{24,28},{28,24},{1,5},{5... | collective-permute-start | bytes 798728 | tf_op jit(solution)/shard_map/ppermute | solution.py:423
  65.5 6.7 %collective-permute-start.16 = (f32[512,128]{1,0:T(8,128)S(1)}, f32[512,128]{1,0:T(8,128)S(1)}, u32[]{:S(2)}, u32[]{:S(2)}) collective-permute-start(f32[512,128]{1,0:T(8,128)S(1)} %shard_map.119.refs_6_), channel_id=1, source_target_pairs={{24,16},{28,20},{25,17},{29,21},{26,18},{30,22},{27,19},{31,23}} | collective-permute-start | bytes 786440 | tf_op jit(solution)/shard_map/ppermute | solution.py:452
  71.5 5.4 %collective-permute-start.19 = (f32[512,128]{1,0:T(8,128)S(1)}, f32[512,128]{1,0:T(8,128)S(1)}, u32[]{:S(2)}, u32[]{:S(2)}) collective-permute-start(f32[512,128]{1,0:T(8,128)S(1)} %shard_map.121.refs_3_), channel_id=1, source_target_pairs={{24,16},{28,20},{25,17},{29,21},{26,18},{30,22},{27,19},{31,23}} | collective-permute-start | bytes 786440 | tf_op jit(solution)/shard_map/ppermute | solution.py:452
  72.2 5.3 %collective-permute-start.18 = (f32[512,128]{1,0:T(8,128)S(1)}, f32[512,128]{1,0:T(8,128)S(1)}, u32[]{:S(2)}, u32[]{:S(2)}) collective-permute-start(f32[512,128]{1,0:T(8,128)S(1)} %shard_map.122.refs_7_), channel_id=1, source_target_pairs={{16,8},{20,12},{17,9},{21,13},{18,10},{22,14},{19,11},{23,15}} | collective-permute-start | bytes 786440 | tf_op jit(solution)/shard_map/ppermute | solution.py:452
  76.9 6.0 %collective-permute-start.20 = (f32[512,128]{1,0:T(8,128)S(1)}, f32[512,128]{1,0:T(8,128)S(1)}, u32[]{:S(2)}, u32[]{:S(2)}) collective-permute-start(f32[512,128]{1,0:T(8,128)S(1)} %shard_map.124.refs_3_), channel_id=1, source_target_pairs={{16,8},{20,12},{17,9},{21,13},{18,10},{22,14},{19,11},{23,15}} | collective-permute-start | bytes 786440 | tf_op jit(solution)/shard_map/ppermute | solution.py:452
  77.6 18.4 %collective-permute-start.22 = (f32[512,128]{1,0:T(8,128)S(1)}, f32[512,128]{1,0:T(8,128)S(1)}, u32[]{:S(2)}, u32[]{:S(2)}) collective-permute-start(f32[512,128]{1,0:T(8,128)S(1)} %shard_map.125.refs_7_), channel_id=1, source_target_pairs={{8,0},{12,4},{9,1},{13,5},{10,2},{14,6},{11,3},{15,7}} | collective-permute-start | bytes 786440 | tf_op jit(solution)/shard_map/ppermute | solution.py:452
  82.9 16.6 %collective-permute-start.21 = (f32[512,128]{1,0:T(8,128)S(1)}, f32[512,128]{1,0:T(8,128)S(1)}, u32[]{:S(2)}, u32[]{:S(2)}) collective-permute-start(f32[512,128]{1,0:T(8,128)S(1)} %shard_map.127.refs_7_), channel_id=1, source_target_pairs={{8,0},{12,4},{9,1},{13,5},{10,2},{14,6},{11,3},{15,7}} | collective-permute-start | bytes 786440 | tf_op jit(solution)/shard_map/ppermute | solution.py:452
  96.0 9.2 %collective-permute-start.24 = (f32[512,128]{1,0:T(8,128)S(1)}, f32[512,128]{1,0:T(8,128)S(1)}, u32[]{:S(2)}, u32[]{:S(2)}) collective-permute-start(f32[512,128]{1,0:T(8,128)S(1)} %get-tuple-element.94.refs_6_), channel_id=1, source_target_pairs={{0,4},{4,0},{8,12},{12,8},{16,20},{20,16},{24,28},{28,24},{1,5},{5... | collective-permute-start | bytes 786440 | tf_op jit(solution)/shard_map/ppermute | solution.py:470
  99.6 8.5 %collective-permute-start.23 = (f32[512,128]{1,0:T(8,128)S(1)}, f32[512,128]{1,0:T(8,128)S(1)}, u32[]{:S(2)}, u32[]{:S(2)}) collective-permute-start(f32[512,128]{1,0:T(8,128)S(1)} %get-tuple-element.96.refs_8_), channel_id=1, source_target_pairs={{0,4},{4,0},{8,12},{12,8},{16,20},{20,16},{24,28},{28,24},{1,5},{5... | collective-permute-start | bytes 786440 | tf_op jit(solution)/shard_map/ppermute | solution.py:470
  (1 other events, 0.8 us)

commit v4 on v2

--- a/solution.py
+++ b/solution.py
@@ -422,10 +422,14 @@
             sends.append(make_piece(part, last))
             last = () if forward and len(sends) == 1 else (sends[-1],)
         last = exchange(last)
-        for part in my_parts:
-            keeps.append(make_piece(part, last))
+        if forward:
+            last = exchange(last)
+        rest = [functools.partial(make_piece, part) for part in my_parts]
+        for make in rest[:1] if forward else rest:
+            keeps.append(make(last))
             last = (keeps[-1],)
-        last = exchange(last + (received[0],) if forward else last)
+        if not forward:
+            last = exchange(last)
         arrived, mine, theirs, late = {}, [], [], []
         for step in range(chunks + places - 1):
             for p in range(places - 1):
@@ -439,10 +443,16 @@
                     functools.partial(hop_kernel, count, p, position), 1, ins, [give(state)],
                     after=last, cost=0.3,
                 )
-                pairs = [(device(p, m), device(p + 1, m)) for m in (0, 1)]
+                other = {p: p + 1, p + 1: p}
+                pairs = [
+                    (device(q, m), device(other.get(q, q), m)) for q in range(places) for m in (0, 1)
+                ]
                 arrived[c, p + 1] = lax.ppermute(value, "seq", pairs)
                 last = (value,)
             last = exchange(last)
+            while len(keeps) < chunks:
+                keeps.append(rest[len(keeps)](last))
+                last = (keeps[-1],)
             if filler:
                 last = (filler.pop(0)(last),)
             c = step + 1 - places

time: 106 us -> 115 us (1.085)
  starting transfers between devices: 27.2 us -> 44.5 us
  waiting for transfers between devices: 27 us -> 17.7 us
    ppermute x12, starting transfers between devices: 14.9 us -> 32.5 us  [chain(): arrived[c, p + 1] = lax.ppermute(value, 'seq', pairs)]
    ppermute x12, waiting for transfers between devices: 12.3 us -> 3.7 us  [chain(): arrived[c, p + 1] = lax.ppermute(value, 'seq', pairs)]
    ppermute x2, starting transfers between devices: 3.22 us -> 0.63 us  [exchange(): received.append(lax.ppermute(sent, 'seq', swap))]
    ppermute x4, waiting for transfers between devices: 9.21 us -> 7.15 us  [chain(): theirs.append(lax.ppermute(send, 'seq', swap))]
    ppermute x4, starting transfers between devices: 3.66 us -> 5.18 us  [chain(): theirs.append(lax.ppermute(send, 'seq', swap))]
  transfers between devices with their start and end apart: 23 -> 23, of which waited for: 12 -> 9; matrix products, arithmetic and copies ran while one was open for 0% -> 0% of each run, Pallas kernels for 38% -> 35%
where the time goes in v4:
time: 115 us; the launch traced here: 114 us
  Pallas kernels  47.9 us (42%)
  starting transfers between devices  44.5 us (39%)
  waiting for transfers between devices  17.7 us (15%)
  local copies, waits for them, and re-layouts  3.02 us (3%)
    pallas_call x42, Pallas kernels, run(): pl.pallas_call(body, out_shape=[shape for shape, _ in outs], grid_spec=pl...  47.9 us
    ppermute x12, starting transfers between devices, chain(): arrived[c, p + 1] = lax.ppermute(value, 'seq', pairs)  32.5 us
    ppermute x4, waiting for transfers between devices, chain(): theirs.append(lax.ppermute(send, 'seq', swap))  7.15 us
    ppermute x4, starting transfers between devices, chain(): theirs.append(lax.ppermute(send, 'seq', swap))  5.18 us
    ppermute x2, starting transfers between devices, exchange(): received.append(lax.ppermute(sends[0], 'seq', swap))  4.5 us
    ppermute x12, waiting for transfers between devices, chain(): arrived[c, p + 1] = lax.ppermute(value, 'seq', pairs)  3.7 us
    unnamed x16, local copies, waits for them, and re-layouts  3.02 us
    ppermute x3, waiting for transfers between devices, on_device(): lax.ppermute(sums, 'head', [(i, (i + k) % head_count) for i in range(head...  2.96 us
  transfers between devices with their start and end apart: 23, of which 9 were waited for; matrix products, arithmetic and copies ran while one was open for 0% of the time, Pallas kernels for 35%

profile of v4, /device:TPU:0, one launch (start us, length us, event | category | flops | bytes accessed | tf_op | source)
XLA Modules:
  0.0 114.1 jit_solution(9697953176150286499)
XLA Ops:
  0.7 3.0 %shard_map.93 = (f32[520,128]{1,0:T(8,128)}, f32[16,512]{1,0:T(8,128)}) custom-call(s32[1]{0:T(128)} %bitcast.member_ref, s32[1]{0:T(128)} %bitcast.1.pair_ref, bf16[512,2048]{1,0:T(8,128)(2,1)} %refs_2_.31, bf16[512,2048]{1,0:T(8,128)(2,1)} %refs_3_.15, f32[16,512]{1,0:T(8,128)} %bitcast.12), custom_call_target="tpu_custom_call" | custom-call | flops 50000000 | bytes 125000 | tf_op jit(solution)/shard_map/pallas_call | solution.py:355
  3.6 3.0 %collective-permute-start = (f32[520,128]{1,0:T(8,128)}, f32[520,128]{1,0:T(8,128)S(1)}, u32[]{:S(2)}, u32[]{:S(2)}) collective-permute-start(f32[520,128]{1,0:T(8,128)} %get-tuple-element.58), channel_id=1, source_target_pairs={{0,4},{4,0},{8,12},{12,8},{16,20},{20,16},{24,28},{28,24},{1,5},{5... | collective-permute-start | bytes 798728 | tf_op jit(solution)/shard_map/ppermute | solution.py:415
  6.6 1.6 %copy-done.2 = bf16[512,2048]{1,0:T(8,128)(2,1)S(1)} copy-done((bf16[512,2048]{1,0:T(8,128)(2,1)S(1)}, bf16[512,2048]{1,0:T(8,128)(2,1)}, u32[]{:S(2)}) %copy-start.2) | copy-done | bytes 2097176
  11.4 2.7 %collective-permute-done.refs_1_ = f32[520,128]{1,0:T(8,128)S(1)} collective-permute-done((f32[520,128]{1,0:T(8,128)}, f32[520,128]{1,0:T(8,128)S(1)}, u32[]{:S(2)}, u32[]{:S(2)}) %collective-permute-start) | collective-permute-done | bytes 266272 | tf_op jit(solution)/shard_map/ppermute | solution.py:415
  14.1 4.1 %collective-permute-start.1 = (f32[512,128]{1,0:T(8,128)S(1)}, f32[512,128]{1,0:T(8,128)S(1)}, u32[]{:S(2)}, u32[]{:S(2)}) collective-permute-start(f32[512,128]{1,0:T(8,128)S(1)} %shard_map.97.refs_3_), channel_id=1, source_target_pairs={{0,8},{4,12},{8,0},{12,4},{16,16},{20,20},{24,24},{28,28},{1,9},{5... | collective-permute-start | bytes 786440 | tf_op jit(solution)/shard_map/ppermute | solution.py:450
  19.0 1.9 %shard_map.99.refs_2_.refs_0_ = f32[512,512]{1,0:T(8,128)S(1)} custom-call(s32[1]{0:T(128)} %bitcast.member_ref, s32[1]{0:T(128)} %bitcast.1.pair_ref, bf16[512,2048]{1,0:T(8,128)(2,1)S(1)} %copy-done, bf16[512,2048]{1,0:T(8,128)(2,1)S(1)} %copy-done.1, bf16[512,2048]{1,0:T(8,128)(2,1)S(1)} %copy-done.3, f32[16,512]{1,0:T(8,128)S(1)} %copy-done.5, ...), custom_call_target="tpu_custom_call" | custom-call | flops 100000000 | bytes 250000 | tf_op jit(solution)/shard_map/pallas_call | solution.py:355
  21.0 1.9 %collective-permute-start.4 = (f32[512,128]{1,0:T(8,128)S(1)}, f32[512,128]{1,0:T(8,128)S(1)}, u32[]{:S(2)}, u32[]{:S(2)}) collective-permute-start(f32[512,128]{1,0:T(8,128)S(1)} %shard_map.100.refs_3_), channel_id=1, source_target_pairs={{0,8},{4,12},{8,0},{12,4},{16,16},{20,20},{24,24},{28,28},{1,9},{5... | collective-permute-start | bytes 786440 | tf_op jit(solution)/shard_map/ppermute | solution.py:450
  23.7 1.9 %shard_map.102.refs_3_.refs_0_ = f32[512,512]{1,0:T(8,128)S(1)} custom-call(s32[1]{0:T(128)} %bitcast.member_ref, s32[1]{0:T(128)} %bitcast.1.pair_ref, bf16[512,2048]{1,0:T(8,128)(2,1)S(1)} %copy-done, bf16[512,2048]{1,0:T(8,128)(2,1)S(1)} %copy-done.1, bf16[512,2048]{1,0:T(8,128)(2,1)S(1)} %copy-done.3, f32[16,512]{1,0:T(8,128)S(1)} %copy-done.5, ...), custom_call_target="tpu_custom_call" | custom-call | flops 2200000000 | bytes 5500000 | tf_op jit(solution)/shard_map/pallas_call | solution.py:355
  25.6 3.7 %collective-permute-done.4.refs_2_ = f32[512,128]{1,0:T(8,128)S(1)} collective-permute-done((f32[512,128]{1,0:T(8,128)S(1)}, f32[512,128]{1,0:T(8,128)S(1)}, u32[]{:S(2)}, u32[]{:S(2)}) %collective-permute-start.4) | collective-permute-done | bytes 262176 | tf_op jit(solution)/shard_map/ppermute | solution.py:450
  30.7 1.9 %shard_map.105.refs_3_.refs_0_ = f32[512,512]{1,0:T(8,128)S(1)} custom-call(s32[1]{0:T(128)} %bitcast.member_ref, s32[1]{0:T(128)} %bitcast.1.pair_ref, bf16[512,2048]{1,0:T(8,128)(2,1)S(1)} %copy-done, bf16[512,2048]{1,0:T(8,128)(2,1)S(1)} %copy-done.1, bf16[512,2048]{1,0:T(8,128)(2,1)S(1)} %copy-done.3, f32[16,512]{1,0:T(8,128)S(1)} %copy-done.6, ...), custom_call_target="tpu_custom_call" | custom-call | flops 2200000000 | bytes 5500000 | tf_op jit(solution)/shard_map/pallas_call | solution.py:355
  33.4 1.9 %shard_map.107.refs_5_.refs_0_ = f32[512,512]{1,0:T(8,128)S(1)} custom-call(s32[1]{0:T(128)} %bitcast.member_ref, s32[1]{0:T(128)} %bitcast.1.pair_ref, bf16[512,2048]{1,0:T(8,128)(2,1)S(1)} %copy-done, bf16[512,2048]{1,0:T(8,128)(2,1)S(1)} %copy-done.1, bf16[512,2048]{1,0:T(8,128)(2,1)S(1)} %copy-done.3, f32[16,512]{1,0:T(8,128)S(1)} %copy-done.6, ...), custom_call_target="tpu_custom_call" | custom-call | flops 2200000000 | bytes 5500000 | tf_op jit(solution)/shard_map/pallas_call | solution.py:355
  35.4 1.6 %collective-permute-start.9 = (f32[512,128]{1,0:T(8,128)S(1)}, f32[512,128]{1,0:T(8,128)S(1)}, u32[]{:S(2)}, u32[]{:S(2)}) collective-permute-start(f32[512,128]{1,0:T(8,128)S(1)} %get-tuple-element.60.refs_7_), channel_id=1, source_target_pairs={{0,4},{4,0},{8,12},{12,8},{16,20},{20,16},{24,28},{28,24},{1,5},{5... | collective-permute-start | bytes 786440 | tf_op jit(solution)/shard_map/ppermute | solution.py:466
  40.8 2.1 %collective-permute-done.9.refs_5_ = f32[512,128]{1,0:T(8,128)S(1)} collective-permute-done((f32[512,128]{1,0:T(8,128)S(1)}, f32[512,128]{1,0:T(8,128)S(1)}, u32[]{:S(2)}, u32[]{:S(2)}) %collective-permute-start.9) | collective-permute-done | bytes 262176 | tf_op jit(solution)/shard_map/ppermute | solution.py:466
  44.0 1.7 %collective-permute-done.8.refs_5_ = f32[512,128]{1,0:T(8,128)S(1)} collective-permute-done((f32[512,128]{1,0:T(8,128)S(1)}, f32[512,128]{1,0:T(8,128)S(1)}, u32[]{:S(2)}, u32[]{:S(2)}) %collective-permute-start.8) | collective-permute-done | bytes 262176 | tf_op jit(solution)/shard_map/ppermute | solution.py:466
  48.5 2.1 %collective-permute-done.11.refs_7_ = f32[8,512]{1,0:T(8,128)S(1)} collective-permute-done((f32[8,512]{1,0:T(8,128)S(1)}, f32[8,512]{1,0:T(8,128)S(1)}, u32[]{:S(2)}, u32[]{:S(2)}) %collective-permute-start.11) | collective-permute-done | bytes 16416 | tf_op jit(solution)/shard_map/ppermute | solution.py:535
  51.5 1.7 %shard_map.114 = (bf16[512,2048]{1,0:T(8,128)(2,1)}, bf16[512,512]{1,0:T(8,128)(2,1)S(1)}, f32[520,128]{1,0:T(8,128)S(1)}) custom-call(s32[1]{0:T(128)} %bitcast.member_ref, s32[1]{0:T(128)} %bitcast.1.pair_ref, f32[512,512]{1,0:T(8,128)S(1)} %get-tuple-element.70.refs_0_, bf16[512,2048]{1,0:T(8,128)(2,1)S(1)} %copy-done.4, f32[1,2048]{1,0:T(1,128)S(1)} %bitcast.8, ...), custom_call_target="tpu_custom_call" | custom-call | flops 2000000000 | bytes 5000000 | tf_op jit(solution)/shard_map/pallas_call | solution.py:355
  53.2 1.5 %collective-permute-start.13 = (f32[520,128]{1,0:T(8,128)S(1)}, f32[520,128]{1,0:T(8,128)S(1)}, u32[]{:S(2)}, u32[]{:S(2)}) collective-permute-start(f32[520,128]{1,0:T(8,128)S(1)} %get-tuple-element.72.refs_10_), channel_id=1, source_target_pairs={{0,4},{4,0},{8,12},{12,8},{16,20},{20,16},{24,28},{28,24},{1,5},{5... | collective-permute-start | bytes 798728 | tf_op jit(solution)/shard_map/ppermute | solution.py:415
  54.7 1.7 %shard_map.115 = (bf16[512,2048]{1,0:T(8,128)(2,1)}, bf16[512,512]{1,0:T(8,128)(2,1)S(1)}, f32[520,128]{1,0:T(8,128)S(1)}) custom-call(s32[1]{0:T(128)} %bitcast.member_ref, s32[1]{0:T(128)} %bitcast.1.pair_ref, f32[512,512]{1,0:T(8,128)S(1)} %get-tuple-element.69.refs_0_, bf16[512,2048]{1,0:T(8,128)(2,1)S(1)} %copy-done.4, ...), custom_call_target="tpu_custom_call", output_to_operand_aliasing={{0}: (11, {})} | custom-call | flops 2000000000 | bytes 5000000 | tf_op jit(solution)/shard_map/pallas_call | solution.py:355
  56.5 1.7 %shard_map.116 = (bf16[512,2048]{1,0:T(8,128)(2,1)}, bf16[512,512]{1,0:T(8,128)(2,1)S(1)}, f32[520,128]{1,0:T(8,128)S(1)}) custom-call(s32[1]{0:T(128)} %bitcast.member_ref, s32[1]{0:T(128)} %bitcast.1.pair_ref, f32[512,512]{1,0:T(8,128)S(1)} %get-tuple-element.68.refs_0_, bf16[512,2048]{1,0:T(8,128)(2,1)S(1)} %copy-done.4, ...), custom_call_target="tpu_custom_call", output_to_operand_aliasing={{0}: (11, {})} | custom-call | flops 2000000000 | bytes 5000000 | tf_op jit(solution)/shard_map/pallas_call | solution.py:355
  58.2 1.7 %shard_map.117 = (bf16[512,2048]{1,0:T(8,128)(2,1)}, bf16[512,512]{1,0:T(8,128)(2,1)S(1)}, f32[520,128]{1,0:T(8,128)S(1)}) custom-call(s32[1]{0:T(128)} %bitcast.member_ref, s32[1]{0:T(128)} %bitcast.1.pair_ref, f32[512,512]{1,0:T(8,128)S(1)} %get-tuple-element.64.refs_0_, bf16[512,2048]{1,0:T(8,128)(2,1)S(1)} %copy-done.4, ...), custom_call_target="tpu_custom_call", output_to_operand_aliasing={{0}: (11, {})} | custom-call | flops 2000000000 | bytes 5000000 | tf_op jit(solution)/shard_map/pallas_call | solution.py:355
  61.3 4.0 %shard_map.120 = (bf16[512,2048]{1,0:T(8,128)(2,1)}, f32[512,512]{1,0:T(8,128)S(1)}, f32[512,512]{1,0:T(8,128)S(1)}) custom-call(s32[1]{0:T(128)} %bitcast.member_ref, s32[1]{0:T(128)} %bitcast.1.pair_ref, bf16[512,2048]{1,0:T(8,128)(2,1)S(1)} %copy-done, bf16[512,2048]{1,0:T(8,128)(2,1)S(1)} %copy-done.1, bf16[512,2048]{1,0:T(8,128)(2,1)S(1)} %copy-done.3, ...), custom_call_target="tpu_custom_call" | custom-call | flops 4300000256 | bytes 10750000 | tf_op jit(solution)/shard_map/pallas_call | solution.py:355
  67.9 4.0 %shard_map.123 = (bf16[512,2048]{1,0:T(8,128)(2,1)}, f32[512,512]{1,0:T(8,128)S(1)}, f32[512,512]{1,0:T(8,128)S(1)}) custom-call(s32[1]{0:T(128)} %bitcast.member_ref, s32[1]{0:T(128)} %bitcast.1.pair_ref, bf16[512,2048]{1,0:T(8,128)(2,1)S(1)} %copy-done, bf16[512,2048]{1,0:T(8,128)(2,1)S(1)} %copy-done.1, ...), custom_call_target="tpu_custom_call", output_to_operand_aliasing={{0}: (8, {})} | custom-call | flops 4300000256 | bytes 10750000 | tf_op jit(solution)/shard_map/pallas_call | solution.py:355
  72.6 18.6 %collective-permute-start.20 = (f32[512,128]{1,0:T(8,128)S(1)}, f32[512,128]{1,0:T(8,128)S(1)}, u32[]{:S(2)}, u32[]{:S(2)}) collective-permute-start(f32[512,128]{1,0:T(8,128)S(1)} %shard_map.125.refs_7_), channel_id=1, source_target_pairs={{24,24},{28,28},{16,16},{20,20},{8,0},{12,4},{0,8},{4,12},{25,25},... | collective-permute-start | bytes 786440 | tf_op jit(solution)/shard_map/ppermute | solution.py:450
  91.3 4.0 %shard_map.126 = (bf16[512,2048]{1,0:T(8,128)(2,1)}, f32[512,512]{1,0:T(8,128)S(1)}, f32[512,512]{1,0:T(8,128)S(1)}) custom-call(s32[1]{0:T(128)} %bitcast.member_ref, s32[1]{0:T(128)} %bitcast.1.pair_ref, bf16[512,2048]{1,0:T(8,128)(2,1)S(1)} %copy-done, bf16[512,2048]{1,0:T(8,128)(2,1)S(1)} %copy-done.1, ...), custom_call_target="tpu_custom_call", output_to_operand_aliasing={{0}: (8, {})} | custom-call | flops 4300000256 | bytes 10750000 | tf_op jit(solution)/shard_map/pallas_call | solution.py:355
  95.2 2.3 %collective-permute-start.19 = (f32[512,128]{1,0:T(8,128)S(1)}, f32[512,128]{1,0:T(8,128)S(1)}, u32[]{:S(2)}, u32[]{:S(2)}) collective-permute-start(f32[512,128]{1,0:T(8,128)S(1)} %shard_map.127.refs_7_), channel_id=1, source_target_pairs={{24,24},{28,28},{16,16},{20,20},{8,0},{12,4},{0,8},{4,12},{25,25},... | collective-permute-start | bytes 786440 | tf_op jit(solution)/shard_map/ppermute | solution.py:450
  97.5 4.0 %shard_map.128 = (bf16[512,2048]{1,0:T(8,128)(2,1)}, f32[512,512]{1,0:T(8,128)S(1)}, f32[512,512]{1,0:T(8,128)S(1)}) custom-call(s32[1]{0:T(128)} %bitcast.member_ref, s32[1]{0:T(128)} %bitcast.1.pair_ref, bf16[512,2048]{1,0:T(8,128)(2,1)S(1)} %copy-done, bf16[512,2048]{1,0:T(8,128)(2,1)S(1)} %copy-done.1, ...), custom_call_target="tpu_custom_call", output_to_operand_aliasing={{0}: (8, {})} | custom-call | flops 4300000256 | bytes 10750000 | tf_op jit(solution)/shard_map/pallas_call | solution.py:355
  101.6 1.6 %collective-permute-start.22 = (f32[512,128]{1,0:T(8,128)S(1)}, f32[512,128]{1,0:T(8,128)S(1)}, u32[]{:S(2)}, u32[]{:S(2)}) collective-permute-start(f32[512,128]{1,0:T(8,128)S(1)} %get-tuple-element.94.refs_6_), channel_id=1, source_target_pairs={{0,4},{4,0},{8,12},{12,8},{16,20},{20,16},{24,28},{28,24},{1,5},{5... | collective-permute-start | bytes 786440 | tf_op jit(solution)/shard_map/ppermute | solution.py:466
  103.2 1.8 %shard_map.130 = (bf16[512,2048]{1,0:T(8,128)(2,1)}, bf16[512,2048]{1,0:T(8,128)(2,1)}, f32[8,128]{1,0:T(8,128)S(1)}) custom-call(s32[1]{0:T(128)} %bitcast.member_ref, s32[1]{0:T(128)} %bitcast.1.pair_ref, f32[512,512]{1,0:T(8,128)S(1)} %get-tuple-element.84.refs_2_.refs_0_, f32[512,512]{1,0:T(8,128)S(1)} %get-tuple-element.92.refs_1_, ...), custom_call_target="tpu_custom_call" | custom-call | flops 2000000000 | bytes 5000000 | tf_op jit(solution)/shard_map/pallas_call | solution.py:355
  105.6 1.7 %shard_map.132 = (bf16[512,2048]{1,0:T(8,128)(2,1)}, bf16[512,2048]{1,0:T(8,128)(2,1)}, f32[8,128]{1,0:T(8,128)S(1)}) custom-call(s32[1]{0:T(128)} %bitcast.member_ref, s32[1]{0:T(128)} %bitcast.1.pair_ref, f32[512,512]{1,0:T(8,128)S(1)} %get-tuple-element.88.refs_3_.refs_0_, ...), custom_call_target="tpu_custom_call", output_to_operand_aliasing={{0}: (8, {}), {1}: (9, {})} | custom-call | flops 2000000000 | bytes 5000000 | tf_op jit(solution)/shard_map/pallas_call | solution.py:355
  107.3 2.3 %collective-permute-done.22.refs_5_ = f32[512,128]{1,0:T(8,128)S(1)} collective-permute-done((f32[512,128]{1,0:T(8,128)S(1)}, f32[512,128]{1,0:T(8,128)S(1)}, u32[]{:S(2)}, u32[]{:S(2)}) %collective-permute-start.22) | collective-permute-done | bytes 262176 | tf_op jit(solution)/shard_map/ppermute | solution.py:466
  109.6 1.7 %shard_map.133 = (bf16[512,2048]{1,0:T(8,128)(2,1)}, bf16[512,2048]{1,0:T(8,128)(2,1)}, f32[8,128]{1,0:T(8,128)S(1)}) custom-call(s32[1]{0:T(128)} %bitcast.member_ref, s32[1]{0:T(128)} %bitcast.1.pair_ref, f32[512,512]{1,0:T(8,128)S(1)} %get-tuple-element.86.refs_3_.refs_0_, ...), custom_call_target="tpu_custom_call", output_to_operand_aliasing={{0}: (8, {}), {1}: (9, {})} | custom-call | flops 2000000000 | bytes 5000000 | tf_op jit(solution)/shard_map/pallas_call | solution.py:355
  112.4 1.7 %shard_map.134 = (bf16[512,2048]{1,0:T(8,128)(2,1)}, bf16[512,2048]{1,0:T(8,128)(2,1)}, f32[8,128]{1,0:T(8,128)}) custom-call(s32[1]{0:T(128)} %bitcast.member_ref, s32[1]{0:T(128)} %bitcast.1.pair_ref, f32[512,512]{1,0:T(8,128)S(1)} %get-tuple-element.90.refs_5_.refs_0_, ...), custom_call_target="tpu_custom_call", output_to_operand_aliasing={{0}: (8, {}), {1}: (9, {})} | custom-call | flops 2000000000 | bytes 5000000 | tf_op jit(solution)/shard_map/pallas_call | solution.py:355
  (73 shorter events, 22.0 us)
Async XLA Ops:
  0.7 5.9 %copy-start.1 = (bf16[512,2048]{1,0:T(8,128)(2,1)S(1)}, bf16[512,2048]{1,0:T(8,128)(2,1)}, u32[]{:S(2)}) copy-start(bf16[512,2048]{1,0:T(8,128)(2,1)} %refs_2_.31) | copy-start | bytes 6291460
  3.6 10.4 %collective-permute-start = (f32[520,128]{1,0:T(8,128)}, f32[520,128]{1,0:T(8,128)S(1)}, u32[]{:S(2)}, u32[]{:S(2)}) collective-permute-start(f32[520,128]{1,0:T(8,128)} %get-tuple-element.58), channel_id=1, source_target_pairs={{0,4},{4,0},{8,12},{12,8},{16,20},{20,16},{24,28},{28,24},{1,5},{5... | collective-permute-start | bytes 798728 | tf_op jit(solution)/shard_map/ppermute | solution.py:415
  6.6 1.6 %copy-start.2 = (bf16[512,2048]{1,0:T(8,128)(2,1)S(1)}, bf16[512,2048]{1,0:T(8,128)(2,1)}, u32[]{:S(2)}) copy-start(bf16[512,2048]{1,0:T(8,128)(2,1)} %refs_3_.15) | copy-start | bytes 6291460
  8.2 0.8 copy-start.5
  8.9 1.6 %copy-start.3 = (bf16[512,2048]{1,0:T(8,128)(2,1)S(1)}, bf16[512,2048]{1,0:T(8,128)(2,1)}, u32[]{:S(2)}) copy-start(bf16[512,2048]{1,0:T(8,128)(2,1)} %refs_3_.15) | copy-start | bytes 6291460
  9.8 11.2 %collective-permute-start.2 = (f32[520,128]{1,0:T(8,128)S(1)}, f32[520,128]{1,0:T(8,128)S(1)}, u32[]{:S(2)}, u32[]{:S(2)}) collective-permute-start(f32[520,128]{1,0:T(8,128)S(1)} %shard_map.95.refs_3_), channel_id=1, source_target_pairs={{0,4},{4,0},{8,12},{12,8},{16,20},{20,16},{24,28},{28,24},{1,5},{5... | collective-permute-start | bytes 798728 | tf_op jit(solution)/shard_map/ppermute | solution.py:418
  14.1 5.0 %copy-start = (bf16[512,2048]{1,0:T(8,128)(2,1)S(1)}, bf16[512,2048]{1,0:T(8,128)(2,1)}, u32[]{:S(2)}) copy-start(bf16[512,2048]{1,0:T(8,128)(2,1)} %refs_0_.23) | copy-start | bytes 6291460
  14.1 8.9 %collective-permute-start.1 = (f32[512,128]{1,0:T(8,128)S(1)}, f32[512,128]{1,0:T(8,128)S(1)}, u32[]{:S(2)}, u32[]{:S(2)}) collective-permute-start(f32[512,128]{1,0:T(8,128)S(1)} %shard_map.97.refs_3_), channel_id=1, source_target_pairs={{0,8},{4,12},{8,0},{12,4},{16,16},{20,20},{24,24},{28,28},{1,9},{5... | collective-permute-start | bytes 786440 | tf_op jit(solution)/shard_map/ppermute | solution.py:450
  21.0 8.3 %collective-permute-start.4 = (f32[512,128]{1,0:T(8,128)S(1)}, f32[512,128]{1,0:T(8,128)S(1)}, u32[]{:S(2)}, u32[]{:S(2)}) collective-permute-start(f32[512,128]{1,0:T(8,128)S(1)} %shard_map.100.refs_3_), channel_id=1, source_target_pairs={{0,8},{4,12},{8,0},{12,4},{16,16},{20,20},{24,24},{28,28},{1,9},{5... | collective-permute-start | bytes 786440 | tf_op jit(solution)/shard_map/ppermute | solution.py:450
  23.0 7.0 %collective-permute-start.3 = (f32[512,128]{1,0:T(8,128)S(1)}, f32[512,128]{1,0:T(8,128)S(1)}, u32[]{:S(2)}, u32[]{:S(2)}) collective-permute-start(f32[512,128]{1,0:T(8,128)S(1)} %shard_map.101.refs_4_), channel_id=1, source_target_pairs={{0,0},{4,4},{8,16},{12,20},{16,8},{20,12},{24,24},{28,28},{1,1},{5... | collective-permute-start | bytes 786440 | tf_op jit(solution)/shard_map/ppermute | solution.py:450
  25.6 5.1 %copy-start.6 = (f32[16,512]{1,0:T(8,128)S(1)}, f32[16,512]{1,0:T(8,128)}, u32[]{:S(2)}) copy-start(f32[16,512]{1,0:T(8,128)} %get-tuple-element.57.refs_2_.refs_3_.refs_4_) | copy-start | bytes 98308
  29.3 3.3 %collective-permute-start.5 = (f32[512,128]{1,0:T(8,128)S(1)}, f32[512,128]{1,0:T(8,128)S(1)}, u32[]{:S(2)}, u32[]{:S(2)}) collective-permute-start(f32[512,128]{1,0:T(8,128)S(1)} %shard_map.103.refs_3_), channel_id=1, source_target_pairs={{0,0},{4,4},{8,16},{12,20},{16,8},{20,12},{24,24},{28,28},{1,1},{5... | collective-permute-start | bytes 786440 | tf_op jit(solution)/shard_map/ppermute | solution.py:450
  30.0 5.3 %collective-permute-start.7 = (f32[512,128]{1,0:T(8,128)S(1)}, f32[512,128]{1,0:T(8,128)S(1)}, u32[]{:S(2)}, u32[]{:S(2)}) collective-permute-start(f32[512,128]{1,0:T(8,128)S(1)} %shard_map.104.refs_4_), channel_id=1, source_target_pairs={{0,0},{4,4},{8,8},{12,12},{16,24},{20,28},{24,16},{28,20},{1,1},{5... | collective-permute-start | bytes 786440 | tf_op jit(solution)/shard_map/ppermute | solution.py:450
  32.7 5.5 %collective-permute-start.6 = (f32[512,128]{1,0:T(8,128)S(1)}, f32[512,128]{1,0:T(8,128)S(1)}, u32[]{:S(2)}, u32[]{:S(2)}) collective-permute-start(f32[512,128]{1,0:T(8,128)S(1)} %shard_map.106.refs_4_), channel_id=1, source_target_pairs={{0,0},{4,4},{8,8},{12,12},{16,24},{20,28},{24,16},{28,20},{1,1},{5... | collective-permute-start | bytes 786440 | tf_op jit(solution)/shard_map/ppermute | solution.py:450
  35.3 1.7 %copy-start.4 = (bf16[512,2048]{1,0:T(8,128)(2,1)S(1)}, bf16[512,2048]{1,0:T(8,128)(2,1)}, u32[]{:S(2)}) copy-start(bf16[512,2048]{1,0:T(8,128)(2,1)} %refs_1_.35) | copy-start | bytes 6291460
  35.3 1.7 %copy-start.7 = (f32[2048]{0:T(1024)S(1)}, f32[2048]{0:T(1024)}, u32[]{:S(2)}) copy-start(f32[2048]{0:T(1024)} %param.10) | copy-start | bytes 24580
  35.4 7.5 %collective-permute-start.9 = (f32[512,128]{1,0:T(8,128)S(1)}, f32[512,128]{1,0:T(8,128)S(1)}, u32[]{:S(2)}, u32[]{:S(2)}) collective-permute-start(f32[512,128]{1,0:T(8,128)S(1)} %get-tuple-element.60.refs_7_), channel_id=1, source_target_pairs={{0,4},{4,0},{8,12},{12,8},{16,20},{20,16},{24,28},{28,24},{1,5},{5... | collective-permute-start | bytes 786440 | tf_op jit(solution)/shard_map/ppermute | solution.py:466
  38.2 7.5 %collective-permute-start.8 = (f32[512,128]{1,0:T(8,128)S(1)}, f32[512,128]{1,0:T(8,128)S(1)}, u32[]{:S(2)}, u32[]{:S(2)}) collective-permute-start(f32[512,128]{1,0:T(8,128)S(1)} %get-tuple-element.63.refs_7_), channel_id=1, source_target_pairs={{0,4},{4,0},{8,12},{12,8},{16,20},{20,16},{24,28},{28,24},{1,5},{5... | collective-permute-start | bytes 786440 | tf_op jit(solution)/shard_map/ppermute | solution.py:466
  46.8 1.7 %collective-permute-start.12 = (f32[8,512]{1,0:T(8,128)S(1)}, f32[8,512]{1,0:T(8,128)S(1)}, u32[]{:S(2)}, u32[]{:S(2)}) collective-permute-start(f32[8,512]{1,0:T(8,128)S(1)} %get-tuple-element.67.refs_5_), channel_id=1, source_target_pairs={{0,3},{1,0},{2,1},{3,2},{4,7},{5,4},{6,5},{7,6},{8,11},{9,8},{10,9... | collective-permute-start | bytes 49160 | tf_op jit(solution)/shard_map/ppermute | solution.py:535
  46.8 3.8 %collective-permute-start.11 = (f32[8,512]{1,0:T(8,128)S(1)}, f32[8,512]{1,0:T(8,128)S(1)}, u32[]{:S(2)}, u32[]{:S(2)}) collective-permute-start(f32[8,512]{1,0:T(8,128)S(1)} %get-tuple-element.67.refs_5_), channel_id=1, source_target_pairs={{0,2},{1,3},{2,0},{3,1},{4,6},{5,7},{6,4},{7,5},{8,10},{9,11},{10,... | collective-permute-start | bytes 49160 | tf_op jit(solution)/shard_map/ppermute | solution.py:535
  48.3 3.2 %collective-permute-start.10 = (f32[8,512]{1,0:T(8,128)S(1)}, f32[8,512]{1,0:T(8,128)S(1)}, u32[]{:S(2)}, u32[]{:S(2)}) collective-permute-start(f32[8,512]{1,0:T(8,128)S(1)} %get-tuple-element.67.refs_5_), channel_id=1, source_target_pairs={{0,1},{1,2},{2,3},{3,0},{4,5},{5,6},{6,7},{7,4},{8,9},{9,10},{10,1... | collective-permute-start | bytes 49160 | tf_op jit(solution)/shard_map/ppermute | solution.py:535
  53.2 7.3 %collective-permute-start.13 = (f32[520,128]{1,0:T(8,128)S(1)}, f32[520,128]{1,0:T(8,128)S(1)}, u32[]{:S(2)}, u32[]{:S(2)}) collective-permute-start(f32[520,128]{1,0:T(8,128)S(1)} %get-tuple-element.72.refs_10_), channel_id=1, source_target_pairs={{0,4},{4,0},{8,12},{12,8},{16,20},{20,16},{24,28},{28,24},{1,5},{5... | collective-permute-start | bytes 798728 | tf_op jit(solution)/shard_map/ppermute | solution.py:415
  59.9 6.6 %collective-permute-start.15 = (f32[520,128]{1,0:T(8,128)S(1)}, f32[520,128]{1,0:T(8,128)S(1)}, u32[]{:S(2)}, u32[]{:S(2)}) collective-permute-start(f32[520,128]{1,0:T(8,128)S(1)} %shard_map.118.refs_2_), channel_id=1, source_target_pairs={{0,4},{4,0},{8,12},{12,8},{16,20},{20,16},{24,28},{28,24},{1,5},{5... | collective-permute-start | bytes 798728 | tf_op jit(solution)/shard_map/ppermute | solution.py:418
  60.5 6.7 %collective-permute-start.14 = (f32[512,128]{1,0:T(8,128)S(1)}, f32[512,128]{1,0:T(8,128)S(1)}, u32[]{:S(2)}, u32[]{:S(2)}) collective-permute-start(f32[512,128]{1,0:T(8,128)S(1)} %shard_map.119.refs_6_), channel_id=1, source_target_pairs={{24,16},{28,20},{16,24},{20,28},{8,8},{12,12},{0,0},{4,4},{25,17},... | collective-permute-start | bytes 786440 | tf_op jit(solution)/shard_map/ppermute | solution.py:450
  66.5 5.4 %collective-permute-start.17 = (f32[512,128]{1,0:T(8,128)S(1)}, f32[512,128]{1,0:T(8,128)S(1)}, u32[]{:S(2)}, u32[]{:S(2)}) collective-permute-start(f32[512,128]{1,0:T(8,128)S(1)} %shard_map.121.refs_3_), channel_id=1, source_target_pairs={{24,16},{28,20},{16,24},{20,28},{8,8},{12,12},{0,0},{4,4},{25,17},... | collective-permute-start | bytes 786440 | tf_op jit(solution)/shard_map/ppermute | solution.py:450
  67.2 5.3 %collective-permute-start.16 = (f32[512,128]{1,0:T(8,128)S(1)}, f32[512,128]{1,0:T(8,128)S(1)}, u32[]{:S(2)}, u32[]{:S(2)}) collective-permute-start(f32[512,128]{1,0:T(8,128)S(1)} %shard_map.122.refs_7_), channel_id=1, source_target_pairs={{24,24},{28,28},{16,8},{20,12},{8,16},{12,20},{0,0},{4,4},{25,25},... | collective-permute-start | bytes 786440 | tf_op jit(solution)/shard_map/ppermute | solution.py:450
  71.9 23.3 %collective-permute-start.18 = (f32[512,128]{1,0:T(8,128)S(1)}, f32[512,128]{1,0:T(8,128)S(1)}, u32[]{:S(2)}, u32[]{:S(2)}) collective-permute-start(f32[512,128]{1,0:T(8,128)S(1)} %shard_map.124.refs_3_), channel_id=1, source_target_pairs={{24,24},{28,28},{16,8},{20,12},{8,16},{12,20},{0,0},{4,4},{25,25},... | collective-permute-start | bytes 786440 | tf_op jit(solution)/shard_map/ppermute | solution.py:450
  72.6 28.9 %collective-permute-start.20 = (f32[512,128]{1,0:T(8,128)S(1)}, f32[512,128]{1,0:T(8,128)S(1)}, u32[]{:S(2)}, u32[]{:S(2)}) collective-permute-start(f32[512,128]{1,0:T(8,128)S(1)} %shard_map.125.refs_7_), channel_id=1, source_target_pairs={{24,24},{28,28},{16,16},{20,20},{8,0},{12,4},{0,8},{4,12},{25,25},... | collective-permute-start | bytes 786440 | tf_op jit(solution)/shard_map/ppermute | solution.py:450
  95.2 9.7 %collective-permute-start.19 = (f32[512,128]{1,0:T(8,128)S(1)}, f32[512,128]{1,0:T(8,128)S(1)}, u32[]{:S(2)}, u32[]{:S(2)}) collective-permute-start(f32[512,128]{1,0:T(8,128)S(1)} %shard_map.127.refs_7_), channel_id=1, source_target_pairs={{24,24},{28,28},{16,16},{20,20},{8,0},{12,4},{0,8},{4,12},{25,25},... | collective-permute-start | bytes 786440 | tf_op jit(solution)/shard_map/ppermute | solution.py:450
  101.6 8.0 %collective-permute-start.22 = (f32[512,128]{1,0:T(8,128)S(1)}, f32[512,128]{1,0:T(8,128)S(1)}, u32[]{:S(2)}, u32[]{:S(2)}) collective-permute-start(f32[512,128]{1,0:T(8,128)S(1)} %get-tuple-element.94.refs_6_), channel_id=1, source_target_pairs={{0,4},{4,0},{8,12},{12,8},{16,20},{20,16},{24,28},{28,24},{1,5},{5... | collective-permute-start | bytes 786440 | tf_op jit(solution)/shard_map/ppermute | solution.py:466
  105.0 7.4 %collective-permute-start.21 = (f32[512,128]{1,0:T(8,128)S(1)}, f32[512,128]{1,0:T(8,128)S(1)}, u32[]{:S(2)}, u32[]{:S(2)}) collective-permute-start(f32[512,128]{1,0:T(8,128)S(1)} %get-tuple-element.96.refs_8_), channel_id=1, source_target_pairs={{0,4},{4,0},{8,12},{12,8},{16,20},{20,16},{24,28},{28,24},{1,5},{5... | collective-permute-start | bytes 786440 | tf_op jit(solution)/shard_map/ppermute | solution.py:466

commit v5 on v4

--- a/solution.py
+++ b/solution.py
@@ -56,7 +56,7 @@
 
 
 def outer_sum(left, scale_row, right):
-    scaled = jnp.transpose(left.astype(f32)) * scale_row
+    scaled = jnp.transpose(left).astype(f32) * scale_row
     high, low = halves(scaled)
     return dot(high, right) + dot(low, right)
 
@@ -443,10 +443,7 @@
                     functools.partial(hop_kernel, count, p, position), 1, ins, [give(state)],
                     after=last, cost=0.3,
                 )
-                other = {p: p + 1, p + 1: p}
-                pairs = [
-                    (device(q, m), device(other.get(q, q), m)) for q in range(places) for m in (0, 1)
-                ]
+                pairs = [(device(p, m), device(p + 1, m)) for m in (0, 1)]
                 arrived[c, p + 1] = lax.ppermute(value, "seq", pairs)
                 last = (value,)
             last = exchange(last)

time: 115 us -> 106 us (0.922)
  starting transfers between devices: 44.5 us -> 24.8 us
  waiting for transfers between devices: 17.7 us -> 28.7 us
    ppermute x12, starting transfers between devices: 32.5 us -> 13.6 us  [chain(): arrived[c, p + 1] = lax.ppermute(value, 'seq', pairs)]
    ppermute x12, waiting for transfers between devices: 3.7 us -> 12.1 us  [chain(): arrived[c, p + 1] = lax.ppermute(value, 'seq', pairs)]
    ppermute x4, waiting for transfers between devices: 7.15 us -> 9.65 us  [chain(): theirs.append(lax.ppermute(send, 'seq', swap))]
  transfers between devices with their start and end apart: 23 -> 23, of which waited for: 9 -> 11; matrix products, arithmetic and copies ran while one was open for 0% -> 0% of each run, Pallas kernels for 35% -> 38%
where the time goes in v5:
time: 106 us
  Pallas kernels  47.9 us (45%)
  waiting for transfers between devices  28.7 us (27%)
  starting transfers between devices  24.8 us (23%)
  local copies, waits for them, and re-layouts  3.03 us (3%)
    pallas_call x42, Pallas kernels, run(): pl.pallas_call(body, out_shape=[shape for shape, _ in outs], grid_spec=pl...  47.9 us
    ppermute x12, starting transfers between devices, chain(): arrived[c, p + 1] = lax.ppermute(value, 'seq', pairs)  13.6 us
    ppermute x12, waiting for transfers between devices, chain(): arrived[c, p + 1] = lax.ppermute(value, 'seq', pairs)  12.1 us
    ppermute x4, waiting for transfers between devices, chain(): theirs.append(lax.ppermute(send, 'seq', swap))  9.65 us
    ppermute x2, starting transfers between devices, exchange(): received.append(lax.ppermute(sends[0], 'seq', swap))  4.48 us
    ppermute x4, starting transfers between devices, chain(): theirs.append(lax.ppermute(send, 'seq', swap))  4.31 us
    unnamed x16, local copies, waits for them, and re-layouts  3.03 us
    ppermute x3, waiting for transfers between devices, on_device(): lax.ppermute(sums, 'head', [(i, (i + k) % head_count) for i in range(head...  2.96 us
  transfers between devices with their start and end apart: 23, of which 11 were waited for; matrix products, arithmetic and copies ran while one was open for 0% of the time, Pallas kernels for 38%

profile of v5, /device:TPU:0, one launch (start us, length us, event | category | flops | bytes accessed | tf_op | source)
XLA Modules:
  0.0 105.6 jit_solution(2862032389041462487)
XLA Ops:
  0.7 3.0 %shard_map.93 = (f32[520,128]{1,0:T(8,128)}, f32[16,512]{1,0:T(8,128)}) custom-call(s32[1]{0:T(128)} %bitcast.member_ref, s32[1]{0:T(128)} %bitcast.1.pair_ref, bf16[512,2048]{1,0:T(8,128)(2,1)} %refs_2_.31, bf16[512,2048]{1,0:T(8,128)(2,1)} %refs_3_.15, f32[16,512]{1,0:T(8,128)} %bitcast.12), custom_call_target="tpu_custom_call" | custom-call | flops 50000000 | bytes 125000 | tf_op jit(solution)/shard_map/pallas_call | solution.py:355
  3.7 3.0 %collective-permute-start = (f32[520,128]{1,0:T(8,128)}, f32[520,128]{1,0:T(8,128)S(1)}, u32[]{:S(2)}, u32[]{:S(2)}) collective-permute-start(f32[520,128]{1,0:T(8,128)} %get-tuple-element.58), channel_id=1, source_target_pairs={{0,4},{4,0},{8,12},{12,8},{16,20},{20,16},{24,28},{28,24},{1,5},{5... | collective-permute-start | bytes 798728 | tf_op jit(solution)/shard_map/ppermute | solution.py:415
  6.6 1.6 %copy-done.2 = bf16[512,2048]{1,0:T(8,128)(2,1)S(1)} copy-done((bf16[512,2048]{1,0:T(8,128)(2,1)S(1)}, bf16[512,2048]{1,0:T(8,128)(2,1)}, u32[]{:S(2)}) %copy-start.2) | copy-done | bytes 2097176
  11.4 2.7 %collective-permute-done.refs_1_ = f32[520,128]{1,0:T(8,128)S(1)} collective-permute-done((f32[520,128]{1,0:T(8,128)}, f32[520,128]{1,0:T(8,128)S(1)}, u32[]{:S(2)}, u32[]{:S(2)}) %collective-permute-start) | collective-permute-done | bytes 266272 | tf_op jit(solution)/shard_map/ppermute | solution.py:415
  14.1 4.1 %collective-permute-start.1 = (f32[512,128]{1,0:T(8,128)S(1)}, f32[512,128]{1,0:T(8,128)S(1)}, u32[]{:S(2)}, u32[]{:S(2)}) collective-permute-start(f32[512,128]{1,0:T(8,128)S(1)} %shard_map.97.refs_3_), channel_id=1, source_target_pairs={{0,8},{4,12},{1,9},{5,13},{2,10},{6,14},{3,11},{7,15}} | collective-permute-start | bytes 786440 | tf_op jit(solution)/shard_map/ppermute | solution.py:447
  19.1 1.9 %shard_map.99.refs_2_.refs_0_ = f32[512,512]{1,0:T(8,128)S(1)} custom-call(s32[1]{0:T(128)} %bitcast.member_ref, s32[1]{0:T(128)} %bitcast.1.pair_ref, bf16[512,2048]{1,0:T(8,128)(2,1)S(1)} %copy-done, bf16[512,2048]{1,0:T(8,128)(2,1)S(1)} %copy-done.1, bf16[512,2048]{1,0:T(8,128)(2,1)S(1)} %copy-done.3, f32[16,512]{1,0:T(8,128)S(1)} %copy-done.5, ...), custom_call_target="tpu_custom_call" | custom-call | flops 100000000 | bytes 250000 | tf_op jit(solution)/shard_map/pallas_call | solution.py:355
  21.1 1.6 %collective-permute-start.4 = (f32[512,128]{1,0:T(8,128)S(1)}, f32[512,128]{1,0:T(8,128)S(1)}, u32[]{:S(2)}, u32[]{:S(2)}) collective-permute-start(f32[512,128]{1,0:T(8,128)S(1)} %shard_map.100.refs_3_), channel_id=1, source_target_pairs={{0,8},{4,12},{1,9},{5,13},{2,10},{6,14},{3,11},{7,15}} | collective-permute-start | bytes 786440 | tf_op jit(solution)/shard_map/ppermute | solution.py:447
  23.4 1.9 %shard_map.102.refs_3_.refs_0_ = f32[512,512]{1,0:T(8,128)S(1)} custom-call(s32[1]{0:T(128)} %bitcast.member_ref, s32[1]{0:T(128)} %bitcast.1.pair_ref, bf16[512,2048]{1,0:T(8,128)(2,1)S(1)} %copy-done, bf16[512,2048]{1,0:T(8,128)(2,1)S(1)} %copy-done.1, bf16[512,2048]{1,0:T(8,128)(2,1)S(1)} %copy-done.3, f32[16,512]{1,0:T(8,128)S(1)} %copy-done.5, ...), custom_call_target="tpu_custom_call" | custom-call | flops 2200000000 | bytes 5500000 | tf_op jit(solution)/shard_map/pallas_call | solution.py:355
  25.3 2.4 %collective-permute-done.4.refs_2_ = f32[512,128]{1,0:T(8,128)S(1)} collective-permute-done((f32[512,128]{1,0:T(8,128)S(1)}, f32[512,128]{1,0:T(8,128)S(1)}, u32[]{:S(2)}, u32[]{:S(2)}) %collective-permute-start.4) | collective-permute-done | bytes 262176 | tf_op jit(solution)/shard_map/ppermute | solution.py:447
  29.1 1.9 %shard_map.105.refs_3_.refs_0_ = f32[512,512]{1,0:T(8,128)S(1)} custom-call(s32[1]{0:T(128)} %bitcast.member_ref, s32[1]{0:T(128)} %bitcast.1.pair_ref, bf16[512,2048]{1,0:T(8,128)(2,1)S(1)} %copy-done, bf16[512,2048]{1,0:T(8,128)(2,1)S(1)} %copy-done.1, bf16[512,2048]{1,0:T(8,128)(2,1)S(1)} %copy-done.3, f32[16,512]{1,0:T(8,128)S(1)} %copy-done.6, ...), custom_call_target="tpu_custom_call" | custom-call | flops 2200000000 | bytes 5500000 | tf_op jit(solution)/shard_map/pallas_call | solution.py:355
  31.7 1.9 %shard_map.107.refs_5_.refs_0_ = f32[512,512]{1,0:T(8,128)S(1)} custom-call(s32[1]{0:T(128)} %bitcast.member_ref, s32[1]{0:T(128)} %bitcast.1.pair_ref, bf16[512,2048]{1,0:T(8,128)(2,1)S(1)} %copy-done, bf16[512,2048]{1,0:T(8,128)(2,1)S(1)} %copy-done.1, bf16[512,2048]{1,0:T(8,128)(2,1)S(1)} %copy-done.3, f32[16,512]{1,0:T(8,128)S(1)} %copy-done.6, ...), custom_call_target="tpu_custom_call" | custom-call | flops 2200000000 | bytes 5500000 | tf_op jit(solution)/shard_map/pallas_call | solution.py:355
  33.8 1.6 %collective-permute-start.9 = (f32[512,128]{1,0:T(8,128)S(1)}, f32[512,128]{1,0:T(8,128)S(1)}, u32[]{:S(2)}, u32[]{:S(2)}) collective-permute-start(f32[512,128]{1,0:T(8,128)S(1)} %get-tuple-element.60.refs_7_), channel_id=1, source_target_pairs={{0,4},{4,0},{8,12},{12,8},{16,20},{20,16},{24,28},{28,24},{1,5},{5... | collective-permute-start | bytes 786440 | tf_op jit(solution)/shard_map/ppermute | solution.py:463
  39.2 3.9 %collective-permute-done.9.refs_5_ = f32[512,128]{1,0:T(8,128)S(1)} collective-permute-done((f32[512,128]{1,0:T(8,128)S(1)}, f32[512,128]{1,0:T(8,128)S(1)}, u32[]{:S(2)}, u32[]{:S(2)}) %collective-permute-start.9) | collective-permute-done | bytes 262176 | tf_op jit(solution)/shard_map/ppermute | solution.py:463
  44.2 1.9 %collective-permute-done.8.refs_5_ = f32[512,128]{1,0:T(8,128)S(1)} collective-permute-done((f32[512,128]{1,0:T(8,128)S(1)}, f32[512,128]{1,0:T(8,128)S(1)}, u32[]{:S(2)}, u32[]{:S(2)}) %collective-permute-start.8) | collective-permute-done | bytes 262176 | tf_op jit(solution)/shard_map/ppermute | solution.py:463
  47.2 1.6 %collective-permute-start.11 = (f32[8,512]{1,0:T(8,128)S(1)}, f32[8,512]{1,0:T(8,128)S(1)}, u32[]{:S(2)}, u32[]{:S(2)}) collective-permute-start(f32[8,512]{1,0:T(8,128)S(1)} %get-tuple-element.67.refs_5_), channel_id=1, source_target_pairs={{0,2},{1,3},{2,0},{3,1},{4,6},{5,7},{6,4},{7,5},{8,10},{9,11},{10,... | collective-permute-start | bytes 49160 | tf_op jit(solution)/shard_map/ppermute | solution.py:532
  49.0 2.0 %collective-permute-done.11.refs_7_ = f32[8,512]{1,0:T(8,128)S(1)} collective-permute-done((f32[8,512]{1,0:T(8,128)S(1)}, f32[8,512]{1,0:T(8,128)S(1)}, u32[]{:S(2)}, u32[]{:S(2)}) %collective-permute-start.11) | collective-permute-done | bytes 16416 | tf_op jit(solution)/shard_map/ppermute | solution.py:532
  52.0 1.7 %shard_map.114 = (bf16[512,2048]{1,0:T(8,128)(2,1)}, bf16[512,512]{1,0:T(8,128)(2,1)S(1)}, f32[520,128]{1,0:T(8,128)S(1)}) custom-call(s32[1]{0:T(128)} %bitcast.member_ref, s32[1]{0:T(128)} %bitcast.1.pair_ref, f32[512,512]{1,0:T(8,128)S(1)} %get-tuple-element.70.refs_0_, bf16[512,2048]{1,0:T(8,128)(2,1)S(1)} %copy-done.4, f32[1,2048]{1,0:T(1,128)S(1)} %bitcast.8, ...), custom_call_target="tpu_custom_call" | custom-call | flops 2000000000 | bytes 5000000 | tf_op jit(solution)/shard_map/pallas_call | solution.py:355
  53.7 1.5 %collective-permute-start.13 = (f32[520,128]{1,0:T(8,128)S(1)}, f32[520,128]{1,0:T(8,128)S(1)}, u32[]{:S(2)}, u32[]{:S(2)}) collective-permute-start(f32[520,128]{1,0:T(8,128)S(1)} %get-tuple-element.72.refs_10_), channel_id=1, source_target_pairs={{0,4},{4,0},{8,12},{12,8},{16,20},{20,16},{24,28},{28,24},{1,5},{5... | collective-permute-start | bytes 798728 | tf_op jit(solution)/shard_map/ppermute | solution.py:415
  55.2 1.7 %shard_map.115 = (bf16[512,2048]{1,0:T(8,128)(2,1)}, bf16[512,512]{1,0:T(8,128)(2,1)S(1)}, f32[520,128]{1,0:T(8,128)S(1)}) custom-call(s32[1]{0:T(128)} %bitcast.member_ref, s32[1]{0:T(128)} %bitcast.1.pair_ref, f32[512,512]{1,0:T(8,128)S(1)} %get-tuple-element.69.refs_0_, bf16[512,2048]{1,0:T(8,128)(2,1)S(1)} %copy-done.4, ...), custom_call_target="tpu_custom_call", output_to_operand_aliasing={{0}: (11, {})} | custom-call | flops 2000000000 | bytes 5000000 | tf_op jit(solution)/shard_map/pallas_call | solution.py:355
  56.9 1.7 %shard_map.116 = (bf16[512,2048]{1,0:T(8,128)(2,1)}, bf16[512,512]{1,0:T(8,128)(2,1)S(1)}, f32[520,128]{1,0:T(8,128)S(1)}) custom-call(s32[1]{0:T(128)} %bitcast.member_ref, s32[1]{0:T(128)} %bitcast.1.pair_ref, f32[512,512]{1,0:T(8,128)S(1)} %get-tuple-element.68.refs_0_, bf16[512,2048]{1,0:T(8,128)(2,1)S(1)} %copy-done.4, ...), custom_call_target="tpu_custom_call", output_to_operand_aliasing={{0}: (11, {})} | custom-call | flops 2000000000 | bytes 5000000 | tf_op jit(solution)/shard_map/pallas_call | solution.py:355
  58.6 1.7 %shard_map.117 = (bf16[512,2048]{1,0:T(8,128)(2,1)}, bf16[512,512]{1,0:T(8,128)(2,1)S(1)}, f32[520,128]{1,0:T(8,128)S(1)}) custom-call(s32[1]{0:T(128)} %bitcast.member_ref, s32[1]{0:T(128)} %bitcast.1.pair_ref, f32[512,512]{1,0:T(8,128)S(1)} %get-tuple-element.64.refs_0_, bf16[512,2048]{1,0:T(8,128)(2,1)S(1)} %copy-done.4, ...), custom_call_target="tpu_custom_call", output_to_operand_aliasing={{0}: (11, {})} | custom-call | flops 2000000000 | bytes 5000000 | tf_op jit(solution)/shard_map/pallas_call | solution.py:355
  61.6 4.0 %shard_map.120 = (bf16[512,2048]{1,0:T(8,128)(2,1)}, f32[512,512]{1,0:T(8,128)S(1)}, f32[512,512]{1,0:T(8,128)S(1)}) custom-call(s32[1]{0:T(128)} %bitcast.member_ref, s32[1]{0:T(128)} %bitcast.1.pair_ref, bf16[512,2048]{1,0:T(8,128)(2,1)S(1)} %copy-done, bf16[512,2048]{1,0:T(8,128)(2,1)S(1)} %copy-done.1, bf16[512,2048]{1,0:T(8,128)(2,1)S(1)} %copy-done.3, ...), custom_call_target="tpu_custom_call" | custom-call | flops 4300000256 | bytes 10750000 | tf_op jit(solution)/shard_map/pallas_call | solution.py:355
  68.4 4.0 %shard_map.123 = (bf16[512,2048]{1,0:T(8,128)(2,1)}, f32[512,512]{1,0:T(8,128)S(1)}, f32[512,512]{1,0:T(8,128)S(1)}) custom-call(s32[1]{0:T(128)} %bitcast.member_ref, s32[1]{0:T(128)} %bitcast.1.pair_ref, bf16[512,2048]{1,0:T(8,128)(2,1)S(1)} %copy-done, bf16[512,2048]{1,0:T(8,128)(2,1)S(1)} %copy-done.1, ...), custom_call_target="tpu_custom_call", output_to_operand_aliasing={{0}: (8, {})} | custom-call | flops 4300000256 | bytes 10750000 | tf_op jit(solution)/shard_map/pallas_call | solution.py:355
  74.4 4.0 %shard_map.126 = (bf16[512,2048]{1,0:T(8,128)(2,1)}, f32[512,512]{1,0:T(8,128)S(1)}, f32[512,512]{1,0:T(8,128)S(1)}) custom-call(s32[1]{0:T(128)} %bitcast.member_ref, s32[1]{0:T(128)} %bitcast.1.pair_ref, bf16[512,2048]{1,0:T(8,128)(2,1)S(1)} %copy-done, bf16[512,2048]{1,0:T(8,128)(2,1)S(1)} %copy-done.1, ...), custom_call_target="tpu_custom_call", output_to_operand_aliasing={{0}: (8, {})} | custom-call | flops 4300000256 | bytes 10750000 | tf_op jit(solution)/shard_map/pallas_call | solution.py:355
  79.6 4.0 %shard_map.128 = (bf16[512,2048]{1,0:T(8,128)(2,1)}, f32[512,512]{1,0:T(8,128)S(1)}, f32[512,512]{1,0:T(8,128)S(1)}) custom-call(s32[1]{0:T(128)} %bitcast.member_ref, s32[1]{0:T(128)} %bitcast.1.pair_ref, bf16[512,2048]{1,0:T(8,128)(2,1)S(1)} %copy-done, bf16[512,2048]{1,0:T(8,128)(2,1)S(1)} %copy-done.1, ...), custom_call_target="tpu_custom_call", output_to_operand_aliasing={{0}: (8, {})} | custom-call | flops 4300000256 | bytes 10750000 | tf_op jit(solution)/shard_map/pallas_call | solution.py:355
  83.6 8.1 %collective-permute-done.20.refs_4_ = f32[512,128]{1,0:T(8,128)S(1)} collective-permute-done((f32[512,128]{1,0:T(8,128)S(1)}, f32[512,128]{1,0:T(8,128)S(1)}, u32[]{:S(2)}, u32[]{:S(2)}) %collective-permute-start.20) | collective-permute-done | bytes 262176 | tf_op jit(solution)/shard_map/ppermute | solution.py:447
  91.9 1.8 %shard_map.130 = (bf16[512,2048]{1,0:T(8,128)(2,1)}, bf16[512,2048]{1,0:T(8,128)(2,1)}, f32[8,128]{1,0:T(8,128)S(1)}) custom-call(s32[1]{0:T(128)} %bitcast.member_ref, s32[1]{0:T(128)} %bitcast.1.pair_ref, f32[512,512]{1,0:T(8,128)S(1)} %get-tuple-element.84.refs_2_.refs_0_, f32[512,512]{1,0:T(8,128)S(1)} %get-tuple-element.92.refs_1_, ...), custom_call_target="tpu_custom_call" | custom-call | flops 2000000000 | bytes 5000000 | tf_op jit(solution)/shard_map/pallas_call | solution.py:355
  93.6 1.6 %collective-permute-done.19.refs_4_ = f32[512,128]{1,0:T(8,128)S(1)} collective-permute-done((f32[512,128]{1,0:T(8,128)S(1)}, f32[512,128]{1,0:T(8,128)S(1)}, u32[]{:S(2)}, u32[]{:S(2)}) %collective-permute-start.19) | collective-permute-done | bytes 262176 | tf_op jit(solution)/shard_map/ppermute | solution.py:447
  96.5 1.7 %shard_map.132 = (bf16[512,2048]{1,0:T(8,128)(2,1)}, bf16[512,2048]{1,0:T(8,128)(2,1)}, f32[8,128]{1,0:T(8,128)S(1)}) custom-call(s32[1]{0:T(128)} %bitcast.member_ref, s32[1]{0:T(128)} %bitcast.1.pair_ref, f32[512,512]{1,0:T(8,128)S(1)} %get-tuple-element.88.refs_3_.refs_0_, ...), custom_call_target="tpu_custom_call", output_to_operand_aliasing={{0}: (8, {}), {1}: (9, {})} | custom-call | flops 2000000000 | bytes 5000000 | tf_op jit(solution)/shard_map/pallas_call | solution.py:355
  98.2 2.7 %collective-permute-done.22.refs_5_ = f32[512,128]{1,0:T(8,128)S(1)} collective-permute-done((f32[512,128]{1,0:T(8,128)S(1)}, f32[512,128]{1,0:T(8,128)S(1)}, u32[]{:S(2)}, u32[]{:S(2)}) %collective-permute-start.22) | collective-permute-done | bytes 262176 | tf_op jit(solution)/shard_map/ppermute | solution.py:463
  100.9 1.7 %shard_map.133 = (bf16[512,2048]{1,0:T(8,128)(2,1)}, bf16[512,2048]{1,0:T(8,128)(2,1)}, f32[8,128]{1,0:T(8,128)S(1)}) custom-call(s32[1]{0:T(128)} %bitcast.member_ref, s32[1]{0:T(128)} %bitcast.1.pair_ref, f32[512,512]{1,0:T(8,128)S(1)} %get-tuple-element.86.refs_3_.refs_0_, ...), custom_call_target="tpu_custom_call", output_to_operand_aliasing={{0}: (8, {}), {1}: (9, {})} | custom-call | flops 2000000000 | bytes 5000000 | tf_op jit(solution)/shard_map/pallas_call | solution.py:355
  103.8 1.7 %shard_map.134 = (bf16[512,2048]{1,0:T(8,128)(2,1)}, bf16[512,2048]{1,0:T(8,128)(2,1)}, f32[8,128]{1,0:T(8,128)}) custom-call(s32[1]{0:T(128)} %bitcast.member_ref, s32[1]{0:T(128)} %bitcast.1.pair_ref, f32[512,512]{1,0:T(8,128)S(1)} %get-tuple-element.90.refs_5_.refs_0_, ...), custom_call_target="tpu_custom_call", output_to_operand_aliasing={{0}: (8, {}), {1}: (9, {})} | custom-call | flops 2000000000 | bytes 5000000 | tf_op jit(solution)/shard_map/pallas_call | solution.py:355
  (73 shorter events, 24.0 us)
Async XLA Ops:
  0.7 6.0 %copy-start.1 = (bf16[512,2048]{1,0:T(8,128)(2,1)S(1)}, bf16[512,2048]{1,0:T(8,128)(2,1)}, u32[]{:S(2)}) copy-start(bf16[512,2048]{1,0:T(8,128)(2,1)} %refs_2_.31) | copy-start | bytes 6291460
  3.7 10.4 %collective-permute-start = (f32[520,128]{1,0:T(8,128)}, f32[520,128]{1,0:T(8,128)S(1)}, u32[]{:S(2)}, u32[]{:S(2)}) collective-permute-start(f32[520,128]{1,0:T(8,128)} %get-tuple-element.58), channel_id=1, source_target_pairs={{0,4},{4,0},{8,12},{12,8},{16,20},{20,16},{24,28},{28,24},{1,5},{5... | collective-permute-start | bytes 798728 | tf_op jit(solution)/shard_map/ppermute | solution.py:415
  6.6 1.6 %copy-start.2 = (bf16[512,2048]{1,0:T(8,128)(2,1)S(1)}, bf16[512,2048]{1,0:T(8,128)(2,1)}, u32[]{:S(2)}) copy-start(bf16[512,2048]{1,0:T(8,128)(2,1)} %refs_3_.15) | copy-start | bytes 6291460
  8.2 0.8 copy-start.5
  9.0 1.6 %copy-start.3 = (bf16[512,2048]{1,0:T(8,128)(2,1)S(1)}, bf16[512,2048]{1,0:T(8,128)(2,1)}, u32[]{:S(2)}) copy-start(bf16[512,2048]{1,0:T(8,128)(2,1)} %refs_3_.15) | copy-start | bytes 6291460
  9.8 11.2 %collective-permute-start.2 = (f32[520,128]{1,0:T(8,128)S(1)}, f32[520,128]{1,0:T(8,128)S(1)}, u32[]{:S(2)}, u32[]{:S(2)}) collective-permute-start(f32[520,128]{1,0:T(8,128)S(1)} %shard_map.95.refs_3_), channel_id=1, source_target_pairs={{0,4},{4,0},{8,12},{12,8},{16,20},{20,16},{24,28},{28,24},{1,5},{5... | collective-permute-start | bytes 798728 | tf_op jit(solution)/shard_map/ppermute | solution.py:418
  14.1 5.0 %copy-start = (bf16[512,2048]{1,0:T(8,128)(2,1)S(1)}, bf16[512,2048]{1,0:T(8,128)(2,1)}, u32[]{:S(2)}) copy-start(bf16[512,2048]{1,0:T(8,128)(2,1)} %refs_0_.23) | copy-start | bytes 6291460
  14.1 8.5 %collective-permute-start.1 = (f32[512,128]{1,0:T(8,128)S(1)}, f32[512,128]{1,0:T(8,128)S(1)}, u32[]{:S(2)}, u32[]{:S(2)}) collective-permute-start(f32[512,128]{1,0:T(8,128)S(1)} %shard_map.97.refs_3_), channel_id=1, source_target_pairs={{0,8},{4,12},{1,9},{5,13},{2,10},{6,14},{3,11},{7,15}} | collective-permute-start | bytes 786440 | tf_op jit(solution)/shard_map/ppermute | solution.py:447
  21.1 6.6 %collective-permute-start.4 = (f32[512,128]{1,0:T(8,128)S(1)}, f32[512,128]{1,0:T(8,128)S(1)}, u32[]{:S(2)}, u32[]{:S(2)}) collective-permute-start(f32[512,128]{1,0:T(8,128)S(1)} %shard_map.100.refs_3_), channel_id=1, source_target_pairs={{0,8},{4,12},{1,9},{5,13},{2,10},{6,14},{3,11},{7,15}} | collective-permute-start | bytes 786440 | tf_op jit(solution)/shard_map/ppermute | solution.py:447
  22.7 5.7 %collective-permute-start.3 = (f32[512,128]{1,0:T(8,128)S(1)}, f32[512,128]{1,0:T(8,128)S(1)}, u32[]{:S(2)}, u32[]{:S(2)}) collective-permute-start(f32[512,128]{1,0:T(8,128)S(1)} %shard_map.101.refs_4_), channel_id=1, source_target_pairs={{8,16},{12,20},{9,17},{13,21},{10,18},{14,22},{11,19},{15,23}} | collective-permute-start | bytes 786440 | tf_op jit(solution)/shard_map/ppermute | solution.py:447
  25.3 3.8 %copy-start.6 = (f32[16,512]{1,0:T(8,128)S(1)}, f32[16,512]{1,0:T(8,128)}, u32[]{:S(2)}) copy-start(f32[16,512]{1,0:T(8,128)} %get-tuple-element.57.refs_2_.refs_3_.refs_4_) | copy-start | bytes 98308
  27.7 3.3 %collective-permute-start.5 = (f32[512,128]{1,0:T(8,128)S(1)}, f32[512,128]{1,0:T(8,128)S(1)}, u32[]{:S(2)}, u32[]{:S(2)}) collective-permute-start(f32[512,128]{1,0:T(8,128)S(1)} %shard_map.103.refs_3_), channel_id=1, source_target_pairs={{8,16},{12,20},{9,17},{13,21},{10,18},{14,22},{11,19},{15,23}} | collective-permute-start | bytes 786440 | tf_op jit(solution)/shard_map/ppermute | solution.py:447
  28.4 5.3 %collective-permute-start.7 = (f32[512,128]{1,0:T(8,128)S(1)}, f32[512,128]{1,0:T(8,128)S(1)}, u32[]{:S(2)}, u32[]{:S(2)}) collective-permute-start(f32[512,128]{1,0:T(8,128)S(1)} %shard_map.104.refs_4_), channel_id=1, source_target_pairs={{16,24},{20,28},{17,25},{21,29},{18,26},{22,30},{19,27},{23,31}} | collective-permute-start | bytes 786440 | tf_op jit(solution)/shard_map/ppermute | solution.py:447
  31.1 5.5 %collective-permute-start.6 = (f32[512,128]{1,0:T(8,128)S(1)}, f32[512,128]{1,0:T(8,128)S(1)}, u32[]{:S(2)}, u32[]{:S(2)}) collective-permute-start(f32[512,128]{1,0:T(8,128)S(1)} %shard_map.106.refs_4_), channel_id=1, source_target_pairs={{16,24},{20,28},{17,25},{21,29},{18,26},{22,30},{19,27},{23,31}} | collective-permute-start | bytes 786440 | tf_op jit(solution)/shard_map/ppermute | solution.py:447
  33.7 1.7 %copy-start.4 = (bf16[512,2048]{1,0:T(8,128)(2,1)S(1)}, bf16[512,2048]{1,0:T(8,128)(2,1)}, u32[]{:S(2)}) copy-start(bf16[512,2048]{1,0:T(8,128)(2,1)} %refs_1_.35) | copy-start | bytes 6291460
  33.7 1.7 %copy-start.7 = (f32[2048]{0:T(1024)S(1)}, f32[2048]{0:T(1024)}, u32[]{:S(2)}) copy-start(f32[2048]{0:T(1024)} %param.10) | copy-start | bytes 24580
  33.8 9.3 %collective-permute-start.9 = (f32[512,128]{1,0:T(8,128)S(1)}, f32[512,128]{1,0:T(8,128)S(1)}, u32[]{:S(2)}, u32[]{:S(2)}) collective-permute-start(f32[512,128]{1,0:T(8,128)S(1)} %get-tuple-element.60.refs_7_), channel_id=1, source_target_pairs={{0,4},{4,0},{8,12},{12,8},{16,20},{20,16},{24,28},{28,24},{1,5},{5... | collective-permute-start | bytes 786440 | tf_op jit(solution)/shard_map/ppermute | solution.py:463
  36.6 9.5 %collective-permute-start.8 = (f32[512,128]{1,0:T(8,128)S(1)}, f32[512,128]{1,0:T(8,128)S(1)}, u32[]{:S(2)}, u32[]{:S(2)}) collective-permute-start(f32[512,128]{1,0:T(8,128)S(1)} %get-tuple-element.63.refs_7_), channel_id=1, source_target_pairs={{0,4},{4,0},{8,12},{12,8},{16,20},{20,16},{24,28},{28,24},{1,5},{5... | collective-permute-start | bytes 786440 | tf_op jit(solution)/shard_map/ppermute | solution.py:463
  47.2 1.8 %collective-permute-start.12 = (f32[8,512]{1,0:T(8,128)S(1)}, f32[8,512]{1,0:T(8,128)S(1)}, u32[]{:S(2)}, u32[]{:S(2)}) collective-permute-start(f32[8,512]{1,0:T(8,128)S(1)} %get-tuple-element.67.refs_5_), channel_id=1, source_target_pairs={{0,3},{1,0},{2,1},{3,2},{4,7},{5,4},{6,5},{7,6},{8,11},{9,8},{10,9... | collective-permute-start | bytes 49160 | tf_op jit(solution)/shard_map/ppermute | solution.py:532
  47.2 3.8 %collective-permute-start.11 = (f32[8,512]{1,0:T(8,128)S(1)}, f32[8,512]{1,0:T(8,128)S(1)}, u32[]{:S(2)}, u32[]{:S(2)}) collective-permute-start(f32[8,512]{1,0:T(8,128)S(1)} %get-tuple-element.67.refs_5_), channel_id=1, source_target_pairs={{0,2},{1,3},{2,0},{3,1},{4,6},{5,7},{6,4},{7,5},{8,10},{9,11},{10,... | collective-permute-start | bytes 49160 | tf_op jit(solution)/shard_map/ppermute | solution.py:532
  48.8 3.2 %collective-permute-start.10 = (f32[8,512]{1,0:T(8,128)S(1)}, f32[8,512]{1,0:T(8,128)S(1)}, u32[]{:S(2)}, u32[]{:S(2)}) collective-permute-start(f32[8,512]{1,0:T(8,128)S(1)} %get-tuple-element.67.refs_5_), channel_id=1, source_target_pairs={{0,1},{1,2},{2,3},{3,0},{4,5},{5,6},{6,7},{7,4},{8,9},{9,10},{10,1... | collective-permute-start | bytes 49160 | tf_op jit(solution)/shard_map/ppermute | solution.py:532
  53.7 7.3 %collective-permute-start.13 = (f32[520,128]{1,0:T(8,128)S(1)}, f32[520,128]{1,0:T(8,128)S(1)}, u32[]{:S(2)}, u32[]{:S(2)}) collective-permute-start(f32[520,128]{1,0:T(8,128)S(1)} %get-tuple-element.72.refs_10_), channel_id=1, source_target_pairs={{0,4},{4,0},{8,12},{12,8},{16,20},{20,16},{24,28},{28,24},{1,5},{5... | collective-permute-start | bytes 798728 | tf_op jit(solution)/shard_map/ppermute | solution.py:415
  60.4 6.6 %collective-permute-start.15 = (f32[520,128]{1,0:T(8,128)S(1)}, f32[520,128]{1,0:T(8,128)S(1)}, u32[]{:S(2)}, u32[]{:S(2)}) collective-permute-start(f32[520,128]{1,0:T(8,128)S(1)} %shard_map.118.refs_2_), channel_id=1, source_target_pairs={{0,4},{4,0},{8,12},{12,8},{16,20},{20,16},{24,28},{28,24},{1,5},{5... | collective-permute-start | bytes 798728 | tf_op jit(solution)/shard_map/ppermute | solution.py:418
  61.0 6.7 %collective-permute-start.14 = (f32[512,128]{1,0:T(8,128)S(1)}, f32[512,128]{1,0:T(8,128)S(1)}, u32[]{:S(2)}, u32[]{:S(2)}) collective-permute-start(f32[512,128]{1,0:T(8,128)S(1)} %shard_map.119.refs_6_), channel_id=1, source_target_pairs={{24,16},{28,20},{25,17},{29,21},{26,18},{30,22},{27,19},{31,23}} | collective-permute-start | bytes 786440 | tf_op jit(solution)/shard_map/ppermute | solution.py:447
  67.0 5.4 %collective-permute-start.17 = (f32[512,128]{1,0:T(8,128)S(1)}, f32[512,128]{1,0:T(8,128)S(1)}, u32[]{:S(2)}, u32[]{:S(2)}) collective-permute-start(f32[512,128]{1,0:T(8,128)S(1)} %shard_map.121.refs_3_), channel_id=1, source_target_pairs={{24,16},{28,20},{25,17},{29,21},{26,18},{30,22},{27,19},{31,23}} | collective-permute-start | bytes 786440 | tf_op jit(solution)/shard_map/ppermute | solution.py:447
  67.7 5.3 %collective-permute-start.16 = (f32[512,128]{1,0:T(8,128)S(1)}, f32[512,128]{1,0:T(8,128)S(1)}, u32[]{:S(2)}, u32[]{:S(2)}) collective-permute-start(f32[512,128]{1,0:T(8,128)S(1)} %shard_map.122.refs_7_), channel_id=1, source_target_pairs={{16,8},{20,12},{17,9},{21,13},{18,10},{22,14},{19,11},{23,15}} | collective-permute-start | bytes 786440 | tf_op jit(solution)/shard_map/ppermute | solution.py:447
  72.3 6.0 %collective-permute-start.18 = (f32[512,128]{1,0:T(8,128)S(1)}, f32[512,128]{1,0:T(8,128)S(1)}, u32[]{:S(2)}, u32[]{:S(2)}) collective-permute-start(f32[512,128]{1,0:T(8,128)S(1)} %shard_map.124.refs_3_), channel_id=1, source_target_pairs={{16,8},{20,12},{17,9},{21,13},{18,10},{22,14},{19,11},{23,15}} | collective-permute-start | bytes 786440 | tf_op jit(solution)/shard_map/ppermute | solution.py:447
  73.1 18.6 %collective-permute-start.20 = (f32[512,128]{1,0:T(8,128)S(1)}, f32[512,128]{1,0:T(8,128)S(1)}, u32[]{:S(2)}, u32[]{:S(2)}) collective-permute-start(f32[512,128]{1,0:T(8,128)S(1)} %shard_map.125.refs_7_), channel_id=1, source_target_pairs={{8,0},{12,4},{9,1},{13,5},{10,2},{14,6},{11,3},{15,7}} | collective-permute-start | bytes 786440 | tf_op jit(solution)/shard_map/ppermute | solution.py:447
  78.3 16.9 %collective-permute-start.19 = (f32[512,128]{1,0:T(8,128)S(1)}, f32[512,128]{1,0:T(8,128)S(1)}, u32[]{:S(2)}, u32[]{:S(2)}) collective-permute-start(f32[512,128]{1,0:T(8,128)S(1)} %shard_map.127.refs_7_), channel_id=1, source_target_pairs={{8,0},{12,4},{9,1},{13,5},{10,2},{14,6},{11,3},{15,7}} | collective-permute-start | bytes 786440 | tf_op jit(solution)/shard_map/ppermute | solution.py:447
  91.8 9.2 %collective-permute-start.22 = (f32[512,128]{1,0:T(8,128)S(1)}, f32[512,128]{1,0:T(8,128)S(1)}, u32[]{:S(2)}, u32[]{:S(2)}) collective-permute-start(f32[512,128]{1,0:T(8,128)S(1)} %get-tuple-element.94.refs_6_), channel_id=1, source_target_pairs={{0,4},{4,0},{8,12},{12,8},{16,20},{20,16},{24,28},{28,24},{1,5},{5... | collective-permute-start | bytes 786440 | tf_op jit(solution)/shard_map/ppermute | solution.py:463
  95.3 8.5 %collective-permute-start.21 = (f32[512,128]{1,0:T(8,128)S(1)}, f32[512,128]{1,0:T(8,128)S(1)}, u32[]{:S(2)}, u32[]{:S(2)}) collective-permute-start(f32[512,128]{1,0:T(8,128)S(1)} %get-tuple-element.96.refs_8_), channel_id=1, source_target_pairs={{0,4},{4,0},{8,12},{12,8},{16,20},{20,16},{24,28},{28,24},{1,5},{5... | collective-permute-start | bytes 786440 | tf_op jit(solution)/shard_map/ppermute | solution.py:463

commit v6 on v0

--- a/solution.py
+++ b/solution.py
@@ -420,14 +420,10 @@
             sends.append(make_piece(part, last))
             last = () if forward and len(sends) == 1 else (sends[-1],)
         last = exchange(last)
-        if forward:
-            last = exchange(last)
-        rest = [functools.partial(make_piece, part) for part in my_parts]
-        for make in rest[:1] if forward else rest:
-            keeps.append(make(last))
+        for part in my_parts:
+            keeps.append(make_piece(part, last))
             last = (keeps[-1],)
-        if not forward:
-            last = exchange(last)
+        last = exchange(last)
         arrived, mine, theirs, late = {}, [], [], []
         for step in range(chunks + places - 1):
             for p in range(places - 1):
@@ -445,9 +441,6 @@
                 arrived[c, p + 1] = lax.ppermute(value, "seq", pairs)
                 last = (value,)
             last = exchange(last)
-            while len(keeps) < chunks:
-                keeps.append(rest[len(keeps)](last))
-                last = (keeps[-1],)
             c = step + 1 - places
             if c >= 0:
                 ins = [plain(keeps[c]), plain(received[c])]

time: 104 us -> 103 us (level)
  waiting for transfers between devices: 26.7 us -> 24.8 us
  starting transfers between devices: 25 us -> 26.2 us
    ppermute x12, waiting for transfers between devices: 14.5 us -> 12.5 us  [chain(): arrived[c, p + 1] = lax.ppermute(value, 'seq', pairs)]
    ppermute x12, starting transfers between devices: 13.8 us -> 15 us  [chain(): arrived[c, p + 1] = lax.ppermute(value, 'seq', pairs)]
  transfers between devices with their start and end apart: 23 -> 23, of which waited for: 9 -> 10; matrix products, arithmetic and copies ran while one was open for 0% -> 0% of each run, Pallas kernels for 39% -> 39%
where the time goes in v6:
time: 103 us; the launch traced here: 102 us
  Pallas kernels  47.8 us (46%)
  starting transfers between devices  26.2 us (25%)
  waiting for transfers between devices  24.8 us (24%)
  local copies, waits for them, and re-layouts  2.39 us (2%)
  between operations  1.06 us (1%)
    pallas_call x42, Pallas kernels, run(): pl.pallas_call(body, out_shape=[shape for shape, _ in outs], grid_spec=pl...  47.8 us
    ppermute x12, starting transfers between devices, chain(): arrived[c, p + 1] = lax.ppermute(value, 'seq', pairs)  15 us
    ppermute x12, waiting for transfers between devices, chain(): arrived[c, p + 1] = lax.ppermute(value, 'seq', pairs)  12.5 us
    ppermute x4, waiting for transfers between devices, chain(): theirs.append(lax.ppermute(send, 'seq', swap))  5.5 us
    ppermute x2, starting transfers between devices, exchange(): received.append(lax.ppermute(sends[0], 'seq', swap))  4.7 us
    ppermute x4, starting transfers between devices, chain(): theirs.append(lax.ppermute(send, 'seq', swap))  4.33 us
    ppermute x3, waiting for transfers between devices, on_device(): lax.ppermute(sums, 'head', [(i, (i + k) % head_count) for i in range(head...  2.96 us
    unnamed x16, local copies, waits for them, and re-layouts  2.38 us
  transfers between devices with their start and end apart: 23, of which 10 were waited for; matrix products, arithmetic and copies ran while one was open for 0% of the time, Pallas kernels for 39%

profile of v6, /device:TPU:0, one launch (start us, length us, event | category | flops | bytes accessed | tf_op | source)
XLA Modules:
  0.0 102.3 jit_solution(16207152823634559630)
XLA Ops:
  0.7 3.0 %shard_map.93 = (f32[520,128]{1,0:T(8,128)}, f32[16,512]{1,0:T(8,128)}) custom-call(s32[1]{0:T(128)} %bitcast.member_ref, s32[1]{0:T(128)} %bitcast.1.pair_ref, bf16[512,2048]{1,0:T(8,128)(2,1)} %refs_2_.31, bf16[512,2048]{1,0:T(8,128)(2,1)} %refs_3_.15, f32[16,512]{1,0:T(8,128)} %bitcast.12), custom_call_target="tpu_custom_call" | custom-call | flops 50000000 | bytes 125000 | tf_op jit(solution)/shard_map/pallas_call | solution.py:353
  3.6 3.0 %collective-permute-start = (f32[520,128]{1,0:T(8,128)}, f32[520,128]{1,0:T(8,128)S(1)}, u32[]{:S(2)}, u32[]{:S(2)}) collective-permute-start(f32[520,128]{1,0:T(8,128)} %get-tuple-element.55), channel_id=1, source_target_pairs={{0,4},{4,0},{8,12},{12,8},{16,20},{20,16},{24,28},{28,24},{1,5},{5... | collective-permute-start | bytes 798728 | tf_op jit(solution)/shard_map/ppermute | solution.py:413
  6.6 1.6 %copy-done.2 = bf16[512,2048]{1,0:T(8,128)(2,1)S(1)} copy-done((bf16[512,2048]{1,0:T(8,128)(2,1)S(1)}, bf16[512,2048]{1,0:T(8,128)(2,1)}, u32[]{:S(2)}) %copy-start.2) | copy-done | bytes 2097176
  11.6 1.8 %collective-permute-done.refs_1_ = f32[520,128]{1,0:T(8,128)S(1)} collective-permute-done((f32[520,128]{1,0:T(8,128)}, f32[520,128]{1,0:T(8,128)S(1)}, u32[]{:S(2)}, u32[]{:S(2)}) %collective-permute-start) | collective-permute-done | bytes 266272 | tf_op jit(solution)/shard_map/ppermute | solution.py:413
  13.5 3.5 %collective-permute-start.1 = (f32[512,128]{1,0:T(8,128)S(1)}, f32[512,128]{1,0:T(8,128)S(1)}, u32[]{:S(2)}, u32[]{:S(2)}) collective-permute-start(f32[512,128]{1,0:T(8,128)S(1)} %shard_map.98.refs_4_), channel_id=1, source_target_pairs={{0,8},{4,12},{1,9},{5,13},{2,10},{6,14},{3,11},{7,15}} | collective-permute-start | bytes 786440 | tf_op jit(solution)/shard_map/ppermute | solution.py:441
  16.9 1.9 %shard_map.99.refs_2_.refs_0_ = f32[512,512]{1,0:T(8,128)S(1)} custom-call(s32[1]{0:T(128)} %bitcast.member_ref, s32[1]{0:T(128)} %bitcast.1.pair_ref, bf16[512,2048]{1,0:T(8,128)(2,1)S(1)} %copy-done, bf16[512,2048]{1,0:T(8,128)(2,1)S(1)} %copy-done.1, bf16[512,2048]{1,0:T(8,128)(2,1)S(1)} %copy-done.3, f32[16,512]{1,0:T(8,128)S(1)} %copy-done.5, ...), custom_call_target="tpu_custom_call" | custom-call | flops 100000000 | bytes 250000 | tf_op jit(solution)/shard_map/pallas_call | solution.py:353
  19.5 3.4 %collective-permute-start.4 = (f32[512,128]{1,0:T(8,128)S(1)}, f32[512,128]{1,0:T(8,128)S(1)}, u32[]{:S(2)}, u32[]{:S(2)}) collective-permute-start(f32[512,128]{1,0:T(8,128)S(1)} %shard_map.100.refs_3_), channel_id=1, source_target_pairs={{0,8},{4,12},{1,9},{5,13},{2,10},{6,14},{3,11},{7,15}} | collective-permute-start | bytes 786440 | tf_op jit(solution)/shard_map/ppermute | solution.py:441
  23.7 1.9 %shard_map.102.refs_3_.refs_0_ = f32[512,512]{1,0:T(8,128)S(1)} custom-call(s32[1]{0:T(128)} %bitcast.member_ref, s32[1]{0:T(128)} %bitcast.1.pair_ref, bf16[512,2048]{1,0:T(8,128)(2,1)S(1)} %copy-done, bf16[512,2048]{1,0:T(8,128)(2,1)S(1)} %copy-done.1, bf16[512,2048]{1,0:T(8,128)(2,1)S(1)} %copy-done.3, f32[16,512]{1,0:T(8,128)S(1)} %copy-done.5, ...), custom_call_target="tpu_custom_call" | custom-call | flops 2200000000 | bytes 5500000 | tf_op jit(solution)/shard_map/pallas_call | solution.py:353
  25.6 1.7 %collective-permute-done.4.refs_2_ = f32[512,128]{1,0:T(8,128)S(1)} collective-permute-done((f32[512,128]{1,0:T(8,128)S(1)}, f32[512,128]{1,0:T(8,128)S(1)}, u32[]{:S(2)}, u32[]{:S(2)}) %collective-permute-start.4) | collective-permute-done | bytes 262176 | tf_op jit(solution)/shard_map/ppermute | solution.py:441
  28.7 1.9 %shard_map.105.refs_3_.refs_0_ = f32[512,512]{1,0:T(8,128)S(1)} custom-call(s32[1]{0:T(128)} %bitcast.member_ref, s32[1]{0:T(128)} %bitcast.1.pair_ref, bf16[512,2048]{1,0:T(8,128)(2,1)S(1)} %copy-done, bf16[512,2048]{1,0:T(8,128)(2,1)S(1)} %copy-done.1, bf16[512,2048]{1,0:T(8,128)(2,1)S(1)} %copy-done.3, f32[16,512]{1,0:T(8,128)S(1)} %copy-done.6, ...), custom_call_target="tpu_custom_call" | custom-call | flops 2200000000 | bytes 5500000 | tf_op jit(solution)/shard_map/pallas_call | solution.py:353
  31.5 1.9 %collective-permute-start.9 = (f32[512,128]{1,0:T(8,128)S(1)}, f32[512,128]{1,0:T(8,128)S(1)}, u32[]{:S(2)}, u32[]{:S(2)}) collective-permute-start(f32[512,128]{1,0:T(8,128)S(1)} %get-tuple-element.57.refs_4_), channel_id=1, source_target_pairs={{0,4},{4,0},{8,12},{12,8},{16,20},{20,16},{24,28},{28,24},{1,5},{5... | collective-permute-start | bytes 786440 | tf_op jit(solution)/shard_map/ppermute | solution.py:452
  33.4 1.9 %shard_map.108.refs_7_.refs_0_ = f32[512,512]{1,0:T(8,128)S(1)} custom-call(s32[1]{0:T(128)} %bitcast.member_ref, s32[1]{0:T(128)} %bitcast.1.pair_ref, bf16[512,2048]{1,0:T(8,128)(2,1)S(1)} %copy-done, bf16[512,2048]{1,0:T(8,128)(2,1)S(1)} %copy-done.1, bf16[512,2048]{1,0:T(8,128)(2,1)S(1)} %copy-done.3, f32[16,512]{1,0:T(8,128)S(1)} %copy-done.6, ...), custom_call_target="tpu_custom_call" | custom-call | flops 2200000000 | bytes 5500000 | tf_op jit(solution)/shard_map/pallas_call | solution.py:353
  37.9 2.0 %collective-permute-done.9.refs_5_ = f32[512,128]{1,0:T(8,128)S(1)} collective-permute-done((f32[512,128]{1,0:T(8,128)S(1)}, f32[512,128]{1,0:T(8,128)S(1)}, u32[]{:S(2)}, u32[]{:S(2)}) %collective-permute-start.9) | collective-permute-done | bytes 262176 | tf_op jit(solution)/shard_map/ppermute | solution.py:452
  41.0 2.9 %collective-permute-done.8.refs_5_ = f32[512,128]{1,0:T(8,128)S(1)} collective-permute-done((f32[512,128]{1,0:T(8,128)S(1)}, f32[512,128]{1,0:T(8,128)S(1)}, u32[]{:S(2)}, u32[]{:S(2)}) %collective-permute-start.8) | collective-permute-done | bytes 262176 | tf_op jit(solution)/shard_map/ppermute | solution.py:452
  45.0 1.5 %collective-permute-start.11 = (f32[8,512]{1,0:T(8,128)S(1)}, f32[8,512]{1,0:T(8,128)S(1)}, u32[]{:S(2)}, u32[]{:S(2)}) collective-permute-start(f32[8,512]{1,0:T(8,128)S(1)} %get-tuple-element.64.refs_5_), channel_id=1, source_target_pairs={{0,2},{1,3},{2,0},{3,1},{4,6},{5,7},{6,4},{7,5},{8,10},{9,11},{10,... | collective-permute-start | bytes 49160 | tf_op jit(solution)/shard_map/ppermute | solution.py:524
  46.8 2.0 %collective-permute-done.11.refs_7_ = f32[8,512]{1,0:T(8,128)S(1)} collective-permute-done((f32[8,512]{1,0:T(8,128)S(1)}, f32[8,512]{1,0:T(8,128)S(1)}, u32[]{:S(2)}, u32[]{:S(2)}) %collective-permute-start.11) | collective-permute-done | bytes 16416 | tf_op jit(solution)/shard_map/ppermute | solution.py:524
  49.7 1.7 %shard_map.114 = (bf16[512,2048]{1,0:T(8,128)(2,1)}, bf16[512,512]{1,0:T(8,128)(2,1)S(1)}, f32[520,128]{1,0:T(8,128)S(1)}) custom-call(s32[1]{0:T(128)} %bitcast.member_ref, s32[1]{0:T(128)} %bitcast.1.pair_ref, f32[512,512]{1,0:T(8,128)S(1)} %get-tuple-element.67.refs_0_, bf16[512,2048]{1,0:T(8,128)(2,1)S(1)} %copy-done.4, f32[1,2048]{1,0:T(1,128)S(1)} %bitcast.8, ...), custom_call_target="tpu_custom_call" | custom-call | flops 2000000000 | bytes 5000000 | tf_op jit(solution)/shard_map/pallas_call | solution.py:353
  51.5 1.7 %collective-permute-start.13 = (f32[520,128]{1,0:T(8,128)S(1)}, f32[520,128]{1,0:T(8,128)S(1)}, u32[]{:S(2)}, u32[]{:S(2)}) collective-permute-start(f32[520,128]{1,0:T(8,128)S(1)} %get-tuple-element.69.refs_10_), channel_id=1, source_target_pairs={{0,4},{4,0},{8,12},{12,8},{16,20},{20,16},{24,28},{28,24},{1,5},{5... | collective-permute-start | bytes 798728 | tf_op jit(solution)/shard_map/ppermute | solution.py:413
  53.2 1.7 %shard_map.115 = (bf16[512,2048]{1,0:T(8,128)(2,1)}, bf16[512,512]{1,0:T(8,128)(2,1)S(1)}, f32[520,128]{1,0:T(8,128)S(1)}) custom-call(s32[1]{0:T(128)} %bitcast.member_ref, s32[1]{0:T(128)} %bitcast.1.pair_ref, f32[512,512]{1,0:T(8,128)S(1)} %get-tuple-element.66.refs_0_, bf16[512,2048]{1,0:T(8,128)(2,1)S(1)} %copy-done.4, ...), custom_call_target="tpu_custom_call", output_to_operand_aliasing={{0}: (11, {})} | custom-call | flops 2000000000 | bytes 5000000 | tf_op jit(solution)/shard_map/pallas_call | solution.py:353
  54.9 1.7 %shard_map.116 = (bf16[512,2048]{1,0:T(8,128)(2,1)}, bf16[512,512]{1,0:T(8,128)(2,1)S(1)}, f32[520,128]{1,0:T(8,128)S(1)}) custom-call(s32[1]{0:T(128)} %bitcast.member_ref, s32[1]{0:T(128)} %bitcast.1.pair_ref, f32[512,512]{1,0:T(8,128)S(1)} %get-tuple-element.65.refs_0_, bf16[512,2048]{1,0:T(8,128)(2,1)S(1)} %copy-done.4, ...), custom_call_target="tpu_custom_call", output_to_operand_aliasing={{0}: (11, {})} | custom-call | flops 2000000000 | bytes 5000000 | tf_op jit(solution)/shard_map/pallas_call | solution.py:353
  56.6 1.7 %shard_map.117 = (bf16[512,2048]{1,0:T(8,128)(2,1)}, bf16[512,512]{1,0:T(8,128)(2,1)S(1)}, f32[520,128]{1,0:T(8,128)S(1)}) custom-call(s32[1]{0:T(128)} %bitcast.member_ref, s32[1]{0:T(128)} %bitcast.1.pair_ref, f32[512,512]{1,0:T(8,128)S(1)} %get-tuple-element.61.refs_0_, bf16[512,2048]{1,0:T(8,128)(2,1)S(1)} %copy-done.4, ...), custom_call_target="tpu_custom_call", output_to_operand_aliasing={{0}: (11, {})} | custom-call | flops 2000000000 | bytes 5000000 | tf_op jit(solution)/shard_map/pallas_call | solution.py:353
  59.6 4.0 %shard_map.120 = (bf16[512,2048]{1,0:T(8,128)(2,1)}, f32[512,512]{1,0:T(8,128)S(1)}, f32[512,512]{1,0:T(8,128)S(1)}) custom-call(s32[1]{0:T(128)} %bitcast.member_ref, s32[1]{0:T(128)} %bitcast.1.pair_ref, bf16[512,2048]{1,0:T(8,128)(2,1)S(1)} %copy-done, bf16[512,2048]{1,0:T(8,128)(2,1)S(1)} %copy-done.1, bf16[512,2048]{1,0:T(8,128)(2,1)S(1)} %copy-done.3, ...), custom_call_target="tpu_custom_call" | custom-call | flops 4300000256 | bytes 10750000 | tf_op jit(solution)/shard_map/pallas_call | solution.py:353
  63.5 1.4 %collective-permute-done.15.refs_1_ = f32[520,128]{1,0:T(8,128)S(1)} collective-permute-done((f32[520,128]{1,0:T(8,128)S(1)}, f32[520,128]{1,0:T(8,128)S(1)}, u32[]{:S(2)}, u32[]{:S(2)}) %collective-permute-start.15) | collective-permute-done | bytes 266272 | tf_op jit(solution)/shard_map/ppermute | solution.py:416
  66.4 4.0 %shard_map.123 = (bf16[512,2048]{1,0:T(8,128)(2,1)}, f32[512,512]{1,0:T(8,128)S(1)}, f32[512,512]{1,0:T(8,128)S(1)}) custom-call(s32[1]{0:T(128)} %bitcast.member_ref, s32[1]{0:T(128)} %bitcast.1.pair_ref, bf16[512,2048]{1,0:T(8,128)(2,1)S(1)} %copy-done, bf16[512,2048]{1,0:T(8,128)(2,1)S(1)} %copy-done.1, ...), custom_call_target="tpu_custom_call", output_to_operand_aliasing={{0}: (8, {})} | custom-call | flops 4300000256 | bytes 10750000 | tf_op jit(solution)/shard_map/pallas_call | solution.py:353
  72.3 4.0 %shard_map.126 = (bf16[512,2048]{1,0:T(8,128)(2,1)}, f32[512,512]{1,0:T(8,128)S(1)}, f32[512,512]{1,0:T(8,128)S(1)}) custom-call(s32[1]{0:T(128)} %bitcast.member_ref, s32[1]{0:T(128)} %bitcast.1.pair_ref, bf16[512,2048]{1,0:T(8,128)(2,1)S(1)} %copy-done, bf16[512,2048]{1,0:T(8,128)(2,1)S(1)} %copy-done.1, ...), custom_call_target="tpu_custom_call", output_to_operand_aliasing={{0}: (8, {})} | custom-call | flops 4300000256 | bytes 10750000 | tf_op jit(solution)/shard_map/pallas_call | solution.py:353
  77.6 10.8 %collective-permute-done.18.refs_4_ = f32[512,128]{1,0:T(8,128)S(1)} collective-permute-done((f32[512,128]{1,0:T(8,128)S(1)}, f32[512,128]{1,0:T(8,128)S(1)}, u32[]{:S(2)}, u32[]{:S(2)}) %collective-permute-start.18) | collective-permute-done | bytes 262176 | tf_op jit(solution)/shard_map/ppermute | solution.py:441
  88.5 1.6 %collective-permute-start.22 = (f32[512,128]{1,0:T(8,128)S(1)}, f32[512,128]{1,0:T(8,128)S(1)}, u32[]{:S(2)}, u32[]{:S(2)}) collective-permute-start(f32[512,128]{1,0:T(8,128)S(1)} %get-tuple-element.86.refs_7_), channel_id=1, source_target_pairs={{0,4},{4,0},{8,12},{12,8},{16,20},{20,16},{24,28},{28,24},{1,5},{5... | collective-permute-start | bytes 786440 | tf_op jit(solution)/shard_map/ppermute | solution.py:452
  90.1 3.9 %shard_map.129 = (bf16[512,2048]{1,0:T(8,128)(2,1)}, f32[512,512]{1,0:T(8,128)S(1)}, f32[512,512]{1,0:T(8,128)S(1)}) custom-call(s32[1]{0:T(128)} %bitcast.member_ref, s32[1]{0:T(128)} %bitcast.1.pair_ref, bf16[512,2048]{1,0:T(8,128)(2,1)S(1)} %copy-done, bf16[512,2048]{1,0:T(8,128)(2,1)S(1)} %copy-done.1, ...), custom_call_target="tpu_custom_call", output_to_operand_aliasing={{0}: (8, {})} | custom-call | flops 4300000256 | bytes 10750000 | tf_op jit(solution)/shard_map/pallas_call | solution.py:353
  94.7 1.8 %shard_map.131 = (bf16[512,2048]{1,0:T(8,128)(2,1)}, bf16[512,2048]{1,0:T(8,128)(2,1)}) custom-call(s32[1]{0:T(128)} %bitcast.member_ref, s32[1]{0:T(128)} %bitcast.1.pair_ref, f32[512,512]{1,0:T(8,128)S(1)} %get-tuple-element.81.refs_2_.refs_0_, f32[512,512]{1,0:T(8,128)S(1)} %get-tuple-element.94.refs_1_, bf16[512,2048]{1,0:T(8,128)(2,1)S(1)} %copy-done.1, ...), custom_call_target="tpu_custom_call" | custom-call | flops 2000000000 | bytes 5000000 | tf_op jit(solution)/shard_map/pallas_call | solution.py:353
  96.4 1.7 %shard_map.132 = (bf16[512,2048]{1,0:T(8,128)(2,1)}, bf16[512,2048]{1,0:T(8,128)(2,1)}) custom-call(s32[1]{0:T(128)} %bitcast.member_ref, s32[1]{0:T(128)} %bitcast.1.pair_ref, f32[512,512]{1,0:T(8,128)S(1)} %get-tuple-element.85.refs_3_.refs_0_, f32[512,512]{1,0:T(8,128)S(1)} %get-tuple-element.92.refs_1_, ...), custom_call_target="tpu_custom_call", output_to_operand_aliasing={{0}: (8, {}), {1}: (9, {})} | custom-call | flops 2000000000 | bytes 5000000 | tf_op jit(solution)/shard_map/pallas_call | solution.py:353
  98.1 1.7 %shard_map.133 = (bf16[512,2048]{1,0:T(8,128)(2,1)}, bf16[512,2048]{1,0:T(8,128)(2,1)}) custom-call(s32[1]{0:T(128)} %bitcast.member_ref, s32[1]{0:T(128)} %bitcast.1.pair_ref, f32[512,512]{1,0:T(8,128)S(1)} %get-tuple-element.83.refs_3_.refs_0_, f32[512,512]{1,0:T(8,128)S(1)} %get-tuple-element.91.refs_1_, ...), custom_call_target="tpu_custom_call", output_to_operand_aliasing={{0}: (8, {}), {1}: (9, {})} | custom-call | flops 2000000000 | bytes 5000000 | tf_op jit(solution)/shard_map/pallas_call | solution.py:353
  100.5 1.7 %shard_map.134 = (bf16[512,2048]{1,0:T(8,128)(2,1)}, bf16[512,2048]{1,0:T(8,128)(2,1)}) custom-call(s32[1]{0:T(128)} %bitcast.member_ref, s32[1]{0:T(128)} %bitcast.1.pair_ref, f32[512,512]{1,0:T(8,128)S(1)} %get-tuple-element.88.refs_5_.refs_0_, f32[512,512]{1,0:T(8,128)S(1)} %get-tuple-element.89.refs_1_, ...), custom_call_target="tpu_custom_call", output_to_operand_aliasing={{0}: (8, {}), {1}: (9, {})} | custom-call | flops 2000000000 | bytes 5000000 | tf_op jit(solution)/shard_map/pallas_call | solution.py:353
  (73 shorter events, 20.1 us)
Async XLA Ops:
  0.7 5.9 %copy-start.1 = (bf16[512,2048]{1,0:T(8,128)(2,1)S(1)}, bf16[512,2048]{1,0:T(8,128)(2,1)}, u32[]{:S(2)}) copy-start(bf16[512,2048]{1,0:T(8,128)(2,1)} %refs_2_.31) | copy-start | bytes 6291460
  3.6 9.8 %collective-permute-start = (f32[520,128]{1,0:T(8,128)}, f32[520,128]{1,0:T(8,128)S(1)}, u32[]{:S(2)}, u32[]{:S(2)}) collective-permute-start(f32[520,128]{1,0:T(8,128)} %get-tuple-element.55), channel_id=1, source_target_pairs={{0,4},{4,0},{8,12},{12,8},{16,20},{20,16},{24,28},{28,24},{1,5},{5... | collective-permute-start | bytes 798728 | tf_op jit(solution)/shard_map/ppermute | solution.py:413
  6.6 1.6 %copy-start.2 = (bf16[512,2048]{1,0:T(8,128)(2,1)S(1)}, bf16[512,2048]{1,0:T(8,128)(2,1)}, u32[]{:S(2)}) copy-start(bf16[512,2048]{1,0:T(8,128)(2,1)} %refs_3_.15) | copy-start | bytes 6291460
  8.2 0.8 copy-start.5
  10.6 6.3 %copy-start = (bf16[512,2048]{1,0:T(8,128)(2,1)S(1)}, bf16[512,2048]{1,0:T(8,128)(2,1)}, u32[]{:S(2)}) copy-start(bf16[512,2048]{1,0:T(8,128)(2,1)} %refs_0_.23) | copy-start | bytes 6291460
  10.6 6.3 %copy-start.3 = (bf16[512,2048]{1,0:T(8,128)(2,1)S(1)}, bf16[512,2048]{1,0:T(8,128)(2,1)}, u32[]{:S(2)}) copy-start(bf16[512,2048]{1,0:T(8,128)(2,1)} %refs_3_.15) | copy-start | bytes 6291460
  11.5 7.9 %collective-permute-start.2 = (f32[520,128]{1,0:T(8,128)S(1)}, f32[520,128]{1,0:T(8,128)S(1)}, u32[]{:S(2)}, u32[]{:S(2)}) collective-permute-start(f32[520,128]{1,0:T(8,128)S(1)} %shard_map.97.refs_2_), channel_id=1, source_target_pairs={{0,4},{4,0},{8,12},{12,8},{16,20},{20,16},{24,28},{28,24},{1,5},{5... | collective-permute-start | bytes 798728 | tf_op jit(solution)/shard_map/ppermute | solution.py:416
  13.5 9.5 %collective-permute-start.1 = (f32[512,128]{1,0:T(8,128)S(1)}, f32[512,128]{1,0:T(8,128)S(1)}, u32[]{:S(2)}, u32[]{:S(2)}) collective-permute-start(f32[512,128]{1,0:T(8,128)S(1)} %shard_map.98.refs_4_), channel_id=1, source_target_pairs={{0,8},{4,12},{1,9},{5,13},{2,10},{6,14},{3,11},{7,15}} | collective-permute-start | bytes 786440 | tf_op jit(solution)/shard_map/ppermute | solution.py:441
  19.5 7.8 %collective-permute-start.4 = (f32[512,128]{1,0:T(8,128)S(1)}, f32[512,128]{1,0:T(8,128)S(1)}, u32[]{:S(2)}, u32[]{:S(2)}) collective-permute-start(f32[512,128]{1,0:T(8,128)S(1)} %shard_map.100.refs_3_), channel_id=1, source_target_pairs={{0,8},{4,12},{1,9},{5,13},{2,10},{6,14},{3,11},{7,15}} | collective-permute-start | bytes 786440 | tf_op jit(solution)/shard_map/ppermute | solution.py:441
  23.0 5.0 %collective-permute-start.3 = (f32[512,128]{1,0:T(8,128)S(1)}, f32[512,128]{1,0:T(8,128)S(1)}, u32[]{:S(2)}, u32[]{:S(2)}) collective-permute-start(f32[512,128]{1,0:T(8,128)S(1)} %shard_map.101.refs_4_), channel_id=1, source_target_pairs={{8,16},{12,20},{9,17},{13,21},{10,18},{14,22},{11,19},{15,23}} | collective-permute-start | bytes 786440 | tf_op jit(solution)/shard_map/ppermute | solution.py:441
  25.6 3.1 %copy-start.6 = (f32[16,512]{1,0:T(8,128)S(1)}, f32[16,512]{1,0:T(8,128)}, u32[]{:S(2)}) copy-start(f32[16,512]{1,0:T(8,128)} %get-tuple-element.54.refs_2_.refs_3_.refs_4_) | copy-start | bytes 98308
  27.3 3.3 %collective-permute-start.5 = (f32[512,128]{1,0:T(8,128)S(1)}, f32[512,128]{1,0:T(8,128)S(1)}, u32[]{:S(2)}, u32[]{:S(2)}) collective-permute-start(f32[512,128]{1,0:T(8,128)S(1)} %shard_map.103.refs_3_), channel_id=1, source_target_pairs={{8,16},{12,20},{9,17},{13,21},{10,18},{14,22},{11,19},{15,23}} | collective-permute-start | bytes 786440 | tf_op jit(solution)/shard_map/ppermute | solution.py:441
  28.0 3.4 %collective-permute-start.7 = (f32[512,128]{1,0:T(8,128)S(1)}, f32[512,128]{1,0:T(8,128)S(1)}, u32[]{:S(2)}, u32[]{:S(2)}) collective-permute-start(f32[512,128]{1,0:T(8,128)S(1)} %shard_map.104.refs_4_), channel_id=1, source_target_pairs={{16,24},{20,28},{17,25},{21,29},{18,26},{22,30},{19,27},{23,31}} | collective-permute-start | bytes 786440 | tf_op jit(solution)/shard_map/ppermute | solution.py:441
  30.7 5.8 %collective-permute-start.6 = (f32[512,128]{1,0:T(8,128)S(1)}, f32[512,128]{1,0:T(8,128)S(1)}, u32[]{:S(2)}, u32[]{:S(2)}) collective-permute-start(f32[512,128]{1,0:T(8,128)S(1)} %shard_map.106.refs_5_), channel_id=1, source_target_pairs={{16,24},{20,28},{17,25},{21,29},{18,26},{22,30},{19,27},{23,31}} | collective-permute-start | bytes 786440 | tf_op jit(solution)/shard_map/ppermute | solution.py:441
  31.5 3.8 %copy-start.4 = (bf16[512,2048]{1,0:T(8,128)(2,1)S(1)}, bf16[512,2048]{1,0:T(8,128)(2,1)}, u32[]{:S(2)}) copy-start(bf16[512,2048]{1,0:T(8,128)(2,1)} %refs_1_.35) | copy-start | bytes 6291460
  31.5 3.8 %copy-start.7 = (f32[2048]{0:T(1024)S(1)}, f32[2048]{0:T(1024)}, u32[]{:S(2)}) copy-start(f32[2048]{0:T(1024)} %param.10) | copy-start | bytes 24580
  31.5 8.4 %collective-permute-start.9 = (f32[512,128]{1,0:T(8,128)S(1)}, f32[512,128]{1,0:T(8,128)S(1)}, u32[]{:S(2)}, u32[]{:S(2)}) collective-permute-start(f32[512,128]{1,0:T(8,128)S(1)} %get-tuple-element.57.refs_4_), channel_id=1, source_target_pairs={{0,4},{4,0},{8,12},{12,8},{16,20},{20,16},{24,28},{28,24},{1,5},{5... | collective-permute-start | bytes 786440 | tf_op jit(solution)/shard_map/ppermute | solution.py:452
  36.6 7.3 %collective-permute-start.8 = (f32[512,128]{1,0:T(8,128)S(1)}, f32[512,128]{1,0:T(8,128)S(1)}, u32[]{:S(2)}, u32[]{:S(2)}) collective-permute-start(f32[512,128]{1,0:T(8,128)S(1)} %get-tuple-element.60.refs_7_), channel_id=1, source_target_pairs={{0,4},{4,0},{8,12},{12,8},{16,20},{20,16},{24,28},{28,24},{1,5},{5... | collective-permute-start | bytes 786440 | tf_op jit(solution)/shard_map/ppermute | solution.py:452
  45.0 1.8 %collective-permute-start.12 = (f32[8,512]{1,0:T(8,128)S(1)}, f32[8,512]{1,0:T(8,128)S(1)}, u32[]{:S(2)}, u32[]{:S(2)}) collective-permute-start(f32[8,512]{1,0:T(8,128)S(1)} %get-tuple-element.64.refs_5_), channel_id=1, source_target_pairs={{0,3},{1,0},{2,1},{3,2},{4,7},{5,4},{6,5},{7,6},{8,11},{9,8},{10,9... | collective-permute-start | bytes 49160 | tf_op jit(solution)/shard_map/ppermute | solution.py:524
  45.0 3.8 %collective-permute-start.11 = (f32[8,512]{1,0:T(8,128)S(1)}, f32[8,512]{1,0:T(8,128)S(1)}, u32[]{:S(2)}, u32[]{:S(2)}) collective-permute-start(f32[8,512]{1,0:T(8,128)S(1)} %get-tuple-element.64.refs_5_), channel_id=1, source_target_pairs={{0,2},{1,3},{2,0},{3,1},{4,6},{5,7},{6,4},{7,5},{8,10},{9,11},{10,... | collective-permute-start | bytes 49160 | tf_op jit(solution)/shard_map/ppermute | solution.py:524
  46.6 3.2 %collective-permute-start.10 = (f32[8,512]{1,0:T(8,128)S(1)}, f32[8,512]{1,0:T(8,128)S(1)}, u32[]{:S(2)}, u32[]{:S(2)}) collective-permute-start(f32[8,512]{1,0:T(8,128)S(1)} %get-tuple-element.64.refs_5_), channel_id=1, source_target_pairs={{0,1},{1,2},{2,3},{3,0},{4,5},{5,6},{6,7},{7,4},{8,9},{9,10},{10,1... | collective-permute-start | bytes 49160 | tf_op jit(solution)/shard_map/ppermute | solution.py:524
  51.5 7.3 %collective-permute-start.13 = (f32[520,128]{1,0:T(8,128)S(1)}, f32[520,128]{1,0:T(8,128)S(1)}, u32[]{:S(2)}, u32[]{:S(2)}) collective-permute-start(f32[520,128]{1,0:T(8,128)S(1)} %get-tuple-element.69.refs_10_), channel_id=1, source_target_pairs={{0,4},{4,0},{8,12},{12,8},{16,20},{20,16},{24,28},{28,24},{1,5},{5... | collective-permute-start | bytes 798728 | tf_op jit(solution)/shard_map/ppermute | solution.py:413
  58.4 6.6 %collective-permute-start.15 = (f32[520,128]{1,0:T(8,128)S(1)}, f32[520,128]{1,0:T(8,128)S(1)}, u32[]{:S(2)}, u32[]{:S(2)}) collective-permute-start(f32[520,128]{1,0:T(8,128)S(1)} %shard_map.118.refs_2_), channel_id=1, source_target_pairs={{0,4},{4,0},{8,12},{12,8},{16,20},{20,16},{24,28},{28,24},{1,5},{5... | collective-permute-start | bytes 798728 | tf_op jit(solution)/shard_map/ppermute | solution.py:416
  58.7 6.9 %collective-permute-start.14 = (f32[512,128]{1,0:T(8,128)S(1)}, f32[512,128]{1,0:T(8,128)S(1)}, u32[]{:S(2)}, u32[]{:S(2)}) collective-permute-start(f32[512,128]{1,0:T(8,128)S(1)} %shard_map.119.refs_6_), channel_id=1, source_target_pairs={{24,16},{28,20},{25,17},{29,21},{26,18},{30,22},{27,19},{31,23}} | collective-permute-start | bytes 786440 | tf_op jit(solution)/shard_map/ppermute | solution.py:441
  65.0 5.4 %collective-permute-start.17 = (f32[512,128]{1,0:T(8,128)S(1)}, f32[512,128]{1,0:T(8,128)S(1)}, u32[]{:S(2)}, u32[]{:S(2)}) collective-permute-start(f32[512,128]{1,0:T(8,128)S(1)} %shard_map.121.refs_3_), channel_id=1, source_target_pairs={{24,16},{28,20},{25,17},{29,21},{26,18},{30,22},{27,19},{31,23}} | collective-permute-start | bytes 786440 | tf_op jit(solution)/shard_map/ppermute | solution.py:441
  65.7 5.3 %collective-permute-start.16 = (f32[512,128]{1,0:T(8,128)S(1)}, f32[512,128]{1,0:T(8,128)S(1)}, u32[]{:S(2)}, u32[]{:S(2)}) collective-permute-start(f32[512,128]{1,0:T(8,128)S(1)} %shard_map.122.refs_7_), channel_id=1, source_target_pairs={{16,8},{20,12},{17,9},{21,13},{18,10},{22,14},{19,11},{23,15}} | collective-permute-start | bytes 786440 | tf_op jit(solution)/shard_map/ppermute | solution.py:441
  70.3 6.0 %collective-permute-start.19 = (f32[512,128]{1,0:T(8,128)S(1)}, f32[512,128]{1,0:T(8,128)S(1)}, u32[]{:S(2)}, u32[]{:S(2)}) collective-permute-start(f32[512,128]{1,0:T(8,128)S(1)} %shard_map.124.refs_3_), channel_id=1, source_target_pairs={{16,8},{20,12},{17,9},{21,13},{18,10},{22,14},{19,11},{23,15}} | collective-permute-start | bytes 786440 | tf_op jit(solution)/shard_map/ppermute | solution.py:441
  71.0 17.4 %collective-permute-start.18 = (f32[512,128]{1,0:T(8,128)S(1)}, f32[512,128]{1,0:T(8,128)S(1)}, u32[]{:S(2)}, u32[]{:S(2)}) collective-permute-start(f32[512,128]{1,0:T(8,128)S(1)} %shard_map.125.refs_7_), channel_id=1, source_target_pairs={{8,0},{12,4},{9,1},{13,5},{10,2},{14,6},{11,3},{15,7}} | collective-permute-start | bytes 786440 | tf_op jit(solution)/shard_map/ppermute | solution.py:441
  76.3 17.7 %collective-permute-start.20 = (f32[512,128]{1,0:T(8,128)S(1)}, f32[512,128]{1,0:T(8,128)S(1)}, u32[]{:S(2)}, u32[]{:S(2)}) collective-permute-start(f32[512,128]{1,0:T(8,128)S(1)} %shard_map.127.refs_5_), channel_id=1, source_target_pairs={{8,0},{12,4},{9,1},{13,5},{10,2},{14,6},{11,3},{15,7}} | collective-permute-start | bytes 786440 | tf_op jit(solution)/shard_map/ppermute | solution.py:441
  88.5 9.7 %collective-permute-start.22 = (f32[512,128]{1,0:T(8,128)S(1)}, f32[512,128]{1,0:T(8,128)S(1)}, u32[]{:S(2)}, u32[]{:S(2)}) collective-permute-start(f32[512,128]{1,0:T(8,128)S(1)} %get-tuple-element.86.refs_7_), channel_id=1, source_target_pairs={{0,4},{4,0},{8,12},{12,8},{16,20},{20,16},{24,28},{28,24},{1,5},{5... | collective-permute-start | bytes 786440 | tf_op jit(solution)/shard_map/ppermute | solution.py:452
  94.1 6.4 %collective-permute-start.21 = (f32[512,128]{1,0:T(8,128)S(1)}, f32[512,128]{1,0:T(8,128)S(1)}, u32[]{:S(2)}, u32[]{:S(2)}) collective-permute-start(f32[512,128]{1,0:T(8,128)S(1)} %get-tuple-element.90.refs_6_), channel_id=1, source_target_pairs={{0,4},{4,0},{8,12},{12,8},{16,20},{20,16},{24,28},{28,24},{1,5},{5... | collective-permute-start | bytes 786440 | tf_op jit(solution)/shard_map/ppermute | solution.py:452

commit v7 on v6

--- a/solution.py
+++ b/solution.py
@@ -39,16 +39,16 @@
 
 
 def cumulative(decay):
-    length = decay.shape[1]
-    first = decay.astype(bf16)
-    rest = decay - first.astype(f32)
-    second = rest.astype(bf16)
-    third = (rest - second.astype(f32)).astype(bf16)
+    heads, length = decay.shape
+    first = decay.astype(bf16).astype(f32)
+    rest = decay - first
+    second = rest.astype(bf16).astype(f32)
+    parts = jnp.concatenate([first, second, rest - second], axis=0).astype(bf16)
     upto = lax.broadcasted_iota(jnp.int32, (length, length), 0) <= lax.broadcasted_iota(
         jnp.int32, (length, length), 1
     )
-    upto = jnp.where(upto, 1.0, 0.0).astype(bf16)
-    return dot(first, upto) + dot(second, upto) + dot(third, upto)
+    sums = dot(parts, jnp.where(upto, 1.0, 0.0).astype(bf16))
+    return sums[:heads] + sums[heads:2 * heads] + sums[2 * heads:]
 
 
 def trail_row(row):
@@ -189,13 +189,18 @@
 
 def grad_kernel(features, part, held, info, *refs):
     outs, (cot_ref, gain_ref, query_ref, cumul_ref, *refs) = refs[:held], refs[held:]
-    shares, (attended_ref, grad_ref, piece_ref) = refs[:-3], refs[-3:]
-    sums = shares[0][...]
-    for share in shares[1:]:
-        sums = sums + share[...]
-    inverse = lax.rsqrt(sums[0:1] / features + epsilon)
-    mean_term = inverse * sums[1:2] / features
-    inverse_col, mean_col = column(inverse), column(mean_term)
+    shares, (attended_ref, grad_ref, piece_ref, inverse_ref, mean_ref) = refs[:-5], refs[-5:]
+
+    @pl.when(pl.program_id(0) == 0)
+    def _():
+        sums = shares[0][...]
+        for share in shares[1:]:
+            sums = sums + share[...]
+        inverse = lax.rsqrt(sums[0:1] / features + epsilon)
+        inverse_ref[...] = column(inverse)
+        mean_ref[...] = column(inverse * sums[1:2] / features)
+
+    inverse_col, mean_col = inverse_ref[...], mean_ref[...]
 
     def head(o, j):
         at = part.wide_cols(info, o)
@@ -544,6 +549,7 @@
             functools.partial(grad_kernel, features, part, per_back), part.steps, ins,
             [(whole, part.full_spec()), give(local_of(part.count, bf16)),
              give(states_of(part.count, 8))],
+            scratch=[pltpu.VMEM((tokens, HEAD_DIM), f32)] * 2,
             after=before + tuple(after), aliases={2 + len(ins): 0} if before else None, cost=2.0,
         )
         attended.append(whole_out)

time: 103 us -> 103 us (level)
  no operation moved by 1% of the time
where the time goes in v7:
time: 103 us
  Pallas kernels  48.1 us (47%)
  starting transfers between devices  26.2 us (25%)
  waiting for transfers between devices  24.9 us (24%)
  local copies, waits for them, and re-layouts  2.39 us (2%)
  between operations  1.06 us (1%)
    pallas_call x42, Pallas kernels, run(): pl.pallas_call(body, out_shape=[shape for shape, _ in outs], grid_spec=pl...  48.1 us
    ppermute x12, starting transfers between devices, chain(): arrived[c, p + 1] = lax.ppermute(value, 'seq', pairs)  14.8 us
    ppermute x12, waiting for transfers between devices, chain(): arrived[c, p + 1] = lax.ppermute(value, 'seq', pairs)  12.5 us
    ppermute x4, waiting for transfers between devices, chain(): theirs.append(lax.ppermute(send, 'seq', swap))  5.46 us
    ppermute x2, starting transfers between devices, exchange(): received.append(lax.ppermute(sends[0], 'seq', swap))  4.7 us
    ppermute x4, starting transfers between devices, chain(): theirs.append(lax.ppermute(send, 'seq', swap))  4.49 us
    ppermute x3, waiting for transfers between devices, on_device(): lax.ppermute(sums, 'head', [(i, (i + k) % head_count) for i in range(head...  2.96 us
    unnamed x16, local copies, waits for them, and re-layouts  2.38 us
  transfers between devices with their start and end apart: 23, of which 10 were waited for; matrix products, arithmetic and copies ran while one was open for 0% of the time, Pallas kernels for 39%

profile of v7, /device:TPU:0, one launch (start us, length us, event | category | flops | bytes accessed | tf_op | source)
XLA Modules:
  0.0 102.7 jit_solution(12270589352350366217)
XLA Ops:
  0.7 2.9 %shard_map.93 = (f32[520,128]{1,0:T(8,128)}, f32[16,512]{1,0:T(8,128)}) custom-call(s32[1]{0:T(128)} %bitcast.member_ref, s32[1]{0:T(128)} %bitcast.1.pair_ref, bf16[512,2048]{1,0:T(8,128)(2,1)} %refs_2_.31, bf16[512,2048]{1,0:T(8,128)(2,1)} %refs_3_.15, f32[16,512]{1,0:T(8,128)} %bitcast.12), custom_call_target="tpu_custom_call" | custom-call | flops 50000000 | bytes 125000 | tf_op jit(solution)/shard_map/pallas_call | solution.py:358
  3.5 3.0 %collective-permute-start = (f32[520,128]{1,0:T(8,128)}, f32[520,128]{1,0:T(8,128)S(1)}, u32[]{:S(2)}, u32[]{:S(2)}) collective-permute-start(f32[520,128]{1,0:T(8,128)} %get-tuple-element.55), channel_id=1, source_target_pairs={{0,4},{4,0},{8,12},{12,8},{16,20},{20,16},{24,28},{28,24},{1,5},{5... | collective-permute-start | bytes 798728 | tf_op jit(solution)/shard_map/ppermute | solution.py:418
  6.5 1.6 %copy-done.2 = bf16[512,2048]{1,0:T(8,128)(2,1)S(1)} copy-done((bf16[512,2048]{1,0:T(8,128)(2,1)S(1)}, bf16[512,2048]{1,0:T(8,128)(2,1)}, u32[]{:S(2)}) %copy-start.2) | copy-done | bytes 2097176
  11.5 1.8 %collective-permute-done.refs_1_ = f32[520,128]{1,0:T(8,128)S(1)} collective-permute-done((f32[520,128]{1,0:T(8,128)}, f32[520,128]{1,0:T(8,128)S(1)}, u32[]{:S(2)}, u32[]{:S(2)}) %collective-permute-start) | collective-permute-done | bytes 266272 | tf_op jit(solution)/shard_map/ppermute | solution.py:418
  13.4 3.5 %collective-permute-start.1 = (f32[512,128]{1,0:T(8,128)S(1)}, f32[512,128]{1,0:T(8,128)S(1)}, u32[]{:S(2)}, u32[]{:S(2)}) collective-permute-start(f32[512,128]{1,0:T(8,128)S(1)} %shard_map.98.refs_4_), channel_id=1, source_target_pairs={{0,8},{4,12},{1,9},{5,13},{2,10},{6,14},{3,11},{7,15}} | collective-permute-start | bytes 786440 | tf_op jit(solution)/shard_map/ppermute | solution.py:446
  16.8 1.9 %shard_map.99.refs_2_.refs_0_ = f32[512,512]{1,0:T(8,128)S(1)} custom-call(s32[1]{0:T(128)} %bitcast.member_ref, s32[1]{0:T(128)} %bitcast.1.pair_ref, bf16[512,2048]{1,0:T(8,128)(2,1)S(1)} %copy-done, bf16[512,2048]{1,0:T(8,128)(2,1)S(1)} %copy-done.1, bf16[512,2048]{1,0:T(8,128)(2,1)S(1)} %copy-done.3, f32[16,512]{1,0:T(8,128)S(1)} %copy-done.5, ...), custom_call_target="tpu_custom_call" | custom-call | flops 100000000 | bytes 250000 | tf_op jit(solution)/shard_map/pallas_call | solution.py:358
  19.4 3.4 %collective-permute-start.4 = (f32[512,128]{1,0:T(8,128)S(1)}, f32[512,128]{1,0:T(8,128)S(1)}, u32[]{:S(2)}, u32[]{:S(2)}) collective-permute-start(f32[512,128]{1,0:T(8,128)S(1)} %shard_map.100.refs_3_), channel_id=1, source_target_pairs={{0,8},{4,12},{1,9},{5,13},{2,10},{6,14},{3,11},{7,15}} | collective-permute-start | bytes 786440 | tf_op jit(solution)/shard_map/ppermute | solution.py:446
  23.6 1.9 %shard_map.102.refs_3_.refs_0_ = f32[512,512]{1,0:T(8,128)S(1)} custom-call(s32[1]{0:T(128)} %bitcast.member_ref, s32[1]{0:T(128)} %bitcast.1.pair_ref, bf16[512,2048]{1,0:T(8,128)(2,1)S(1)} %copy-done, bf16[512,2048]{1,0:T(8,128)(2,1)S(1)} %copy-done.1, bf16[512,2048]{1,0:T(8,128)(2,1)S(1)} %copy-done.3, f32[16,512]{1,0:T(8,128)S(1)} %copy-done.5, ...), custom_call_target="tpu_custom_call" | custom-call | flops 2200000000 | bytes 5500000 | tf_op jit(solution)/shard_map/pallas_call | solution.py:358
  25.5 1.7 %collective-permute-done.4.refs_2_ = f32[512,128]{1,0:T(8,128)S(1)} collective-permute-done((f32[512,128]{1,0:T(8,128)S(1)}, f32[512,128]{1,0:T(8,128)S(1)}, u32[]{:S(2)}, u32[]{:S(2)}) %collective-permute-start.4) | collective-permute-done | bytes 262176 | tf_op jit(solution)/shard_map/ppermute | solution.py:446
  28.6 1.9 %shard_map.105.refs_3_.refs_0_ = f32[512,512]{1,0:T(8,128)S(1)} custom-call(s32[1]{0:T(128)} %bitcast.member_ref, s32[1]{0:T(128)} %bitcast.1.pair_ref, bf16[512,2048]{1,0:T(8,128)(2,1)S(1)} %copy-done, bf16[512,2048]{1,0:T(8,128)(2,1)S(1)} %copy-done.1, bf16[512,2048]{1,0:T(8,128)(2,1)S(1)} %copy-done.3, f32[16,512]{1,0:T(8,128)S(1)} %copy-done.6, ...), custom_call_target="tpu_custom_call" | custom-call | flops 2200000000 | bytes 5500000 | tf_op jit(solution)/shard_map/pallas_call | solution.py:358
  31.4 1.9 %collective-permute-start.9 = (f32[512,128]{1,0:T(8,128)S(1)}, f32[512,128]{1,0:T(8,128)S(1)}, u32[]{:S(2)}, u32[]{:S(2)}) collective-permute-start(f32[512,128]{1,0:T(8,128)S(1)} %get-tuple-element.57.refs_4_), channel_id=1, source_target_pairs={{0,4},{4,0},{8,12},{12,8},{16,20},{20,16},{24,28},{28,24},{1,5},{5... | collective-permute-start | bytes 786440 | tf_op jit(solution)/shard_map/ppermute | solution.py:457
  33.3 1.9 %shard_map.108.refs_7_.refs_0_ = f32[512,512]{1,0:T(8,128)S(1)} custom-call(s32[1]{0:T(128)} %bitcast.member_ref, s32[1]{0:T(128)} %bitcast.1.pair_ref, bf16[512,2048]{1,0:T(8,128)(2,1)S(1)} %copy-done, bf16[512,2048]{1,0:T(8,128)(2,1)S(1)} %copy-done.1, bf16[512,2048]{1,0:T(8,128)(2,1)S(1)} %copy-done.3, f32[16,512]{1,0:T(8,128)S(1)} %copy-done.6, ...), custom_call_target="tpu_custom_call" | custom-call | flops 2200000000 | bytes 5500000 | tf_op jit(solution)/shard_map/pallas_call | solution.py:358
  37.8 2.0 %collective-permute-done.9.refs_5_ = f32[512,128]{1,0:T(8,128)S(1)} collective-permute-done((f32[512,128]{1,0:T(8,128)S(1)}, f32[512,128]{1,0:T(8,128)S(1)}, u32[]{:S(2)}, u32[]{:S(2)}) %collective-permute-start.9) | collective-permute-done | bytes 262176 | tf_op jit(solution)/shard_map/ppermute | solution.py:457
  40.9 2.9 %collective-permute-done.8.refs_5_ = f32[512,128]{1,0:T(8,128)S(1)} collective-permute-done((f32[512,128]{1,0:T(8,128)S(1)}, f32[512,128]{1,0:T(8,128)S(1)}, u32[]{:S(2)}, u32[]{:S(2)}) %collective-permute-start.8) | collective-permute-done | bytes 262176 | tf_op jit(solution)/shard_map/ppermute | solution.py:457
  44.9 1.5 %collective-permute-start.11 = (f32[8,512]{1,0:T(8,128)S(1)}, f32[8,512]{1,0:T(8,128)S(1)}, u32[]{:S(2)}, u32[]{:S(2)}) collective-permute-start(f32[8,512]{1,0:T(8,128)S(1)} %get-tuple-element.64.refs_5_), channel_id=1, source_target_pairs={{0,2},{1,3},{2,0},{3,1},{4,6},{5,7},{6,4},{7,5},{8,10},{9,11},{10,... | collective-permute-start | bytes 49160 | tf_op jit(solution)/shard_map/ppermute | solution.py:529
  46.7 2.0 %collective-permute-done.11.refs_7_ = f32[8,512]{1,0:T(8,128)S(1)} collective-permute-done((f32[8,512]{1,0:T(8,128)S(1)}, f32[8,512]{1,0:T(8,128)S(1)}, u32[]{:S(2)}, u32[]{:S(2)}) %collective-permute-start.11) | collective-permute-done | bytes 16416 | tf_op jit(solution)/shard_map/ppermute | solution.py:529
  49.6 1.8 %shard_map.114 = (bf16[512,2048]{1,0:T(8,128)(2,1)}, bf16[512,512]{1,0:T(8,128)(2,1)S(1)}, f32[520,128]{1,0:T(8,128)S(1)}) custom-call(s32[1]{0:T(128)} %bitcast.member_ref, s32[1]{0:T(128)} %bitcast.1.pair_ref, f32[512,512]{1,0:T(8,128)S(1)} %get-tuple-element.67.refs_0_, bf16[512,2048]{1,0:T(8,128)(2,1)S(1)} %copy-done.4, f32[1,2048]{1,0:T(1,128)S(1)} %bitcast.8, ...), custom_call_target="tpu_custom_call" | custom-call | flops 2000000000 | bytes 5000000 | tf_op jit(solution)/shard_map/pallas_call | solution.py:358
  51.4 1.7 %collective-permute-start.13 = (f32[520,128]{1,0:T(8,128)S(1)}, f32[520,128]{1,0:T(8,128)S(1)}, u32[]{:S(2)}, u32[]{:S(2)}) collective-permute-start(f32[520,128]{1,0:T(8,128)S(1)} %get-tuple-element.69.refs_10_), channel_id=1, source_target_pairs={{0,4},{4,0},{8,12},{12,8},{16,20},{20,16},{24,28},{28,24},{1,5},{5... | collective-permute-start | bytes 798728 | tf_op jit(solution)/shard_map/ppermute | solution.py:418
  53.2 1.8 %shard_map.115 = (bf16[512,2048]{1,0:T(8,128)(2,1)}, bf16[512,512]{1,0:T(8,128)(2,1)S(1)}, f32[520,128]{1,0:T(8,128)S(1)}) custom-call(s32[1]{0:T(128)} %bitcast.member_ref, s32[1]{0:T(128)} %bitcast.1.pair_ref, f32[512,512]{1,0:T(8,128)S(1)} %get-tuple-element.66.refs_0_, bf16[512,2048]{1,0:T(8,128)(2,1)S(1)} %copy-done.4, ...), custom_call_target="tpu_custom_call", output_to_operand_aliasing={{0}: (11, {})} | custom-call | flops 2000000000 | bytes 5000000 | tf_op jit(solution)/shard_map/pallas_call | solution.py:358
  55.0 1.8 %shard_map.116 = (bf16[512,2048]{1,0:T(8,128)(2,1)}, bf16[512,512]{1,0:T(8,128)(2,1)S(1)}, f32[520,128]{1,0:T(8,128)S(1)}) custom-call(s32[1]{0:T(128)} %bitcast.member_ref, s32[1]{0:T(128)} %bitcast.1.pair_ref, f32[512,512]{1,0:T(8,128)S(1)} %get-tuple-element.65.refs_0_, bf16[512,2048]{1,0:T(8,128)(2,1)S(1)} %copy-done.4, ...), custom_call_target="tpu_custom_call", output_to_operand_aliasing={{0}: (11, {})} | custom-call | flops 2000000000 | bytes 5000000 | tf_op jit(solution)/shard_map/pallas_call | solution.py:358
  56.8 1.8 %shard_map.117 = (bf16[512,2048]{1,0:T(8,128)(2,1)}, bf16[512,512]{1,0:T(8,128)(2,1)S(1)}, f32[520,128]{1,0:T(8,128)S(1)}) custom-call(s32[1]{0:T(128)} %bitcast.member_ref, s32[1]{0:T(128)} %bitcast.1.pair_ref, f32[512,512]{1,0:T(8,128)S(1)} %get-tuple-element.61.refs_0_, bf16[512,2048]{1,0:T(8,128)(2,1)S(1)} %copy-done.4, ...), custom_call_target="tpu_custom_call", output_to_operand_aliasing={{0}: (11, {})} | custom-call | flops 2000000000 | bytes 5000000 | tf_op jit(solution)/shard_map/pallas_call | solution.py:358
  59.7 4.0 %shard_map.120 = (bf16[512,2048]{1,0:T(8,128)(2,1)}, f32[512,512]{1,0:T(8,128)S(1)}, f32[512,512]{1,0:T(8,128)S(1)}) custom-call(s32[1]{0:T(128)} %bitcast.member_ref, s32[1]{0:T(128)} %bitcast.1.pair_ref, bf16[512,2048]{1,0:T(8,128)(2,1)S(1)} %copy-done, bf16[512,2048]{1,0:T(8,128)(2,1)S(1)} %copy-done.1, bf16[512,2048]{1,0:T(8,128)(2,1)S(1)} %copy-done.3, ...), custom_call_target="tpu_custom_call" | custom-call | flops 4300000256 | bytes 10750000 | tf_op jit(solution)/shard_map/pallas_call | solution.py:358
  63.6 1.6 %collective-permute-done.15.refs_1_ = f32[520,128]{1,0:T(8,128)S(1)} collective-permute-done((f32[520,128]{1,0:T(8,128)S(1)}, f32[520,128]{1,0:T(8,128)S(1)}, u32[]{:S(2)}, u32[]{:S(2)}) %collective-permute-start.15) | collective-permute-done | bytes 266272 | tf_op jit(solution)/shard_map/ppermute | solution.py:421
  66.6 4.0 %shard_map.123 = (bf16[512,2048]{1,0:T(8,128)(2,1)}, f32[512,512]{1,0:T(8,128)S(1)}, f32[512,512]{1,0:T(8,128)S(1)}) custom-call(s32[1]{0:T(128)} %bitcast.member_ref, s32[1]{0:T(128)} %bitcast.1.pair_ref, bf16[512,2048]{1,0:T(8,128)(2,1)S(1)} %copy-done, bf16[512,2048]{1,0:T(8,128)(2,1)S(1)} %copy-done.1, ...), custom_call_target="tpu_custom_call", output_to_operand_aliasing={{0}: (8, {})} | custom-call | flops 4300000256 | bytes 10750000 | tf_op jit(solution)/shard_map/pallas_call | solution.py:358
  72.6 4.0 %shard_map.126 = (bf16[512,2048]{1,0:T(8,128)(2,1)}, f32[512,512]{1,0:T(8,128)S(1)}, f32[512,512]{1,0:T(8,128)S(1)}) custom-call(s32[1]{0:T(128)} %bitcast.member_ref, s32[1]{0:T(128)} %bitcast.1.pair_ref, bf16[512,2048]{1,0:T(8,128)(2,1)S(1)} %copy-done, bf16[512,2048]{1,0:T(8,128)(2,1)S(1)} %copy-done.1, ...), custom_call_target="tpu_custom_call", output_to_operand_aliasing={{0}: (8, {})} | custom-call | flops 4300000256 | bytes 10750000 | tf_op jit(solution)/shard_map/pallas_call | solution.py:358
  77.8 10.8 %collective-permute-done.18.refs_4_ = f32[512,128]{1,0:T(8,128)S(1)} collective-permute-done((f32[512,128]{1,0:T(8,128)S(1)}, f32[512,128]{1,0:T(8,128)S(1)}, u32[]{:S(2)}, u32[]{:S(2)}) %collective-permute-start.18) | collective-permute-done | bytes 262176 | tf_op jit(solution)/shard_map/ppermute | solution.py:446
  88.8 1.8 %collective-permute-start.22 = (f32[512,128]{1,0:T(8,128)S(1)}, f32[512,128]{1,0:T(8,128)S(1)}, u32[]{:S(2)}, u32[]{:S(2)}) collective-permute-start(f32[512,128]{1,0:T(8,128)S(1)} %get-tuple-element.86.refs_7_), channel_id=1, source_target_pairs={{0,4},{4,0},{8,12},{12,8},{16,20},{20,16},{24,28},{28,24},{1,5},{5... | collective-permute-start | bytes 786440 | tf_op jit(solution)/shard_map/ppermute | solution.py:457
  90.5 3.9 %shard_map.129 = (bf16[512,2048]{1,0:T(8,128)(2,1)}, f32[512,512]{1,0:T(8,128)S(1)}, f32[512,512]{1,0:T(8,128)S(1)}) custom-call(s32[1]{0:T(128)} %bitcast.member_ref, s32[1]{0:T(128)} %bitcast.1.pair_ref, bf16[512,2048]{1,0:T(8,128)(2,1)S(1)} %copy-done, bf16[512,2048]{1,0:T(8,128)(2,1)S(1)} %copy-done.1, ...), custom_call_target="tpu_custom_call", output_to_operand_aliasing={{0}: (8, {})} | custom-call | flops 4300000256 | bytes 10750000 | tf_op jit(solution)/shard_map/pallas_call | solution.py:358
  95.1 1.8 %shard_map.131 = (bf16[512,2048]{1,0:T(8,128)(2,1)}, bf16[512,2048]{1,0:T(8,128)(2,1)}) custom-call(s32[1]{0:T(128)} %bitcast.member_ref, s32[1]{0:T(128)} %bitcast.1.pair_ref, f32[512,512]{1,0:T(8,128)S(1)} %get-tuple-element.81.refs_2_.refs_0_, f32[512,512]{1,0:T(8,128)S(1)} %get-tuple-element.94.refs_1_, bf16[512,2048]{1,0:T(8,128)(2,1)S(1)} %copy-done.1, ...), custom_call_target="tpu_custom_call" | custom-call | flops 2000000000 | bytes 5000000 | tf_op jit(solution)/shard_map/pallas_call | solution.py:358
  96.9 1.7 %shard_map.132 = (bf16[512,2048]{1,0:T(8,128)(2,1)}, bf16[512,2048]{1,0:T(8,128)(2,1)}) custom-call(s32[1]{0:T(128)} %bitcast.member_ref, s32[1]{0:T(128)} %bitcast.1.pair_ref, f32[512,512]{1,0:T(8,128)S(1)} %get-tuple-element.85.refs_3_.refs_0_, f32[512,512]{1,0:T(8,128)S(1)} %get-tuple-element.92.refs_1_, ...), custom_call_target="tpu_custom_call", output_to_operand_aliasing={{0}: (8, {}), {1}: (9, {})} | custom-call | flops 2000000000 | bytes 5000000 | tf_op jit(solution)/shard_map/pallas_call | solution.py:358
  98.6 1.7 %shard_map.133 = (bf16[512,2048]{1,0:T(8,128)(2,1)}, bf16[512,2048]{1,0:T(8,128)(2,1)}) custom-call(s32[1]{0:T(128)} %bitcast.member_ref, s32[1]{0:T(128)} %bitcast.1.pair_ref, f32[512,512]{1,0:T(8,128)S(1)} %get-tuple-element.83.refs_3_.refs_0_, f32[512,512]{1,0:T(8,128)S(1)} %get-tuple-element.91.refs_1_, ...), custom_call_target="tpu_custom_call", output_to_operand_aliasing={{0}: (8, {}), {1}: (9, {})} | custom-call | flops 2000000000 | bytes 5000000 | tf_op jit(solution)/shard_map/pallas_call | solution.py:358
  101.0 1.7 %shard_map.134 = (bf16[512,2048]{1,0:T(8,128)(2,1)}, bf16[512,2048]{1,0:T(8,128)(2,1)}) custom-call(s32[1]{0:T(128)} %bitcast.member_ref, s32[1]{0:T(128)} %bitcast.1.pair_ref, f32[512,512]{1,0:T(8,128)S(1)} %get-tuple-element.88.refs_5_.refs_0_, f32[512,512]{1,0:T(8,128)S(1)} %get-tuple-element.89.refs_1_, ...), custom_call_target="tpu_custom_call", output_to_operand_aliasing={{0}: (8, {}), {1}: (9, {})} | custom-call | flops 2000000000 | bytes 5000000 | tf_op jit(solution)/shard_map/pallas_call | solution.py:358
  (73 shorter events, 19.9 us)
Async XLA Ops:
  0.7 5.9 %copy-start.1 = (bf16[512,2048]{1,0:T(8,128)(2,1)S(1)}, bf16[512,2048]{1,0:T(8,128)(2,1)}, u32[]{:S(2)}) copy-start(bf16[512,2048]{1,0:T(8,128)(2,1)} %refs_2_.31) | copy-start | bytes 6291460
  3.5 9.8 %collective-permute-start = (f32[520,128]{1,0:T(8,128)}, f32[520,128]{1,0:T(8,128)S(1)}, u32[]{:S(2)}, u32[]{:S(2)}) collective-permute-start(f32[520,128]{1,0:T(8,128)} %get-tuple-element.55), channel_id=1, source_target_pairs={{0,4},{4,0},{8,12},{12,8},{16,20},{20,16},{24,28},{28,24},{1,5},{5... | collective-permute-start | bytes 798728 | tf_op jit(solution)/shard_map/ppermute | solution.py:418
  6.5 1.6 %copy-start.2 = (bf16[512,2048]{1,0:T(8,128)(2,1)S(1)}, bf16[512,2048]{1,0:T(8,128)(2,1)}, u32[]{:S(2)}) copy-start(bf16[512,2048]{1,0:T(8,128)(2,1)} %refs_3_.15) | copy-start | bytes 6291460
  8.1 0.8 copy-start.5
  10.5 6.3 %copy-start = (bf16[512,2048]{1,0:T(8,128)(2,1)S(1)}, bf16[512,2048]{1,0:T(8,128)(2,1)}, u32[]{:S(2)}) copy-start(bf16[512,2048]{1,0:T(8,128)(2,1)} %refs_0_.23) | copy-start | bytes 6291460
  10.6 6.3 %copy-start.3 = (bf16[512,2048]{1,0:T(8,128)(2,1)S(1)}, bf16[512,2048]{1,0:T(8,128)(2,1)}, u32[]{:S(2)}) copy-start(bf16[512,2048]{1,0:T(8,128)(2,1)} %refs_3_.15) | copy-start | bytes 6291460
  11.5 7.9 %collective-permute-start.2 = (f32[520,128]{1,0:T(8,128)S(1)}, f32[520,128]{1,0:T(8,128)S(1)}, u32[]{:S(2)}, u32[]{:S(2)}) collective-permute-start(f32[520,128]{1,0:T(8,128)S(1)} %shard_map.97.refs_2_), channel_id=1, source_target_pairs={{0,4},{4,0},{8,12},{12,8},{16,20},{20,16},{24,28},{28,24},{1,5},{5... | collective-permute-start | bytes 798728 | tf_op jit(solution)/shard_map/ppermute | solution.py:421
  13.4 9.5 %collective-permute-start.1 = (f32[512,128]{1,0:T(8,128)S(1)}, f32[512,128]{1,0:T(8,128)S(1)}, u32[]{:S(2)}, u32[]{:S(2)}) collective-permute-start(f32[512,128]{1,0:T(8,128)S(1)} %shard_map.98.refs_4_), channel_id=1, source_target_pairs={{0,8},{4,12},{1,9},{5,13},{2,10},{6,14},{3,11},{7,15}} | collective-permute-start | bytes 786440 | tf_op jit(solution)/shard_map/ppermute | solution.py:446
  19.4 7.8 %collective-permute-start.4 = (f32[512,128]{1,0:T(8,128)S(1)}, f32[512,128]{1,0:T(8,128)S(1)}, u32[]{:S(2)}, u32[]{:S(2)}) collective-permute-start(f32[512,128]{1,0:T(8,128)S(1)} %shard_map.100.refs_3_), channel_id=1, source_target_pairs={{0,8},{4,12},{1,9},{5,13},{2,10},{6,14},{3,11},{7,15}} | collective-permute-start | bytes 786440 | tf_op jit(solution)/shard_map/ppermute | solution.py:446
  22.9 5.0 %collective-permute-start.3 = (f32[512,128]{1,0:T(8,128)S(1)}, f32[512,128]{1,0:T(8,128)S(1)}, u32[]{:S(2)}, u32[]{:S(2)}) collective-permute-start(f32[512,128]{1,0:T(8,128)S(1)} %shard_map.101.refs_4_), channel_id=1, source_target_pairs={{8,16},{12,20},{9,17},{13,21},{10,18},{14,22},{11,19},{15,23}} | collective-permute-start | bytes 786440 | tf_op jit(solution)/shard_map/ppermute | solution.py:446
  25.5 3.1 %copy-start.6 = (f32[16,512]{1,0:T(8,128)S(1)}, f32[16,512]{1,0:T(8,128)}, u32[]{:S(2)}) copy-start(f32[16,512]{1,0:T(8,128)} %get-tuple-element.54.refs_2_.refs_3_.refs_4_) | copy-start | bytes 98308
  27.2 3.3 %collective-permute-start.5 = (f32[512,128]{1,0:T(8,128)S(1)}, f32[512,128]{1,0:T(8,128)S(1)}, u32[]{:S(2)}, u32[]{:S(2)}) collective-permute-start(f32[512,128]{1,0:T(8,128)S(1)} %shard_map.103.refs_3_), channel_id=1, source_target_pairs={{8,16},{12,20},{9,17},{13,21},{10,18},{14,22},{11,19},{15,23}} | collective-permute-start | bytes 786440 | tf_op jit(solution)/shard_map/ppermute | solution.py:446
  27.9 3.3 %collective-permute-start.7 = (f32[512,128]{1,0:T(8,128)S(1)}, f32[512,128]{1,0:T(8,128)S(1)}, u32[]{:S(2)}, u32[]{:S(2)}) collective-permute-start(f32[512,128]{1,0:T(8,128)S(1)} %shard_map.104.refs_4_), channel_id=1, source_target_pairs={{16,24},{20,28},{17,25},{21,29},{18,26},{22,30},{19,27},{23,31}} | collective-permute-start | bytes 786440 | tf_op jit(solution)/shard_map/ppermute | solution.py:446
  30.6 5.8 %collective-permute-start.6 = (f32[512,128]{1,0:T(8,128)S(1)}, f32[512,128]{1,0:T(8,128)S(1)}, u32[]{:S(2)}, u32[]{:S(2)}) collective-permute-start(f32[512,128]{1,0:T(8,128)S(1)} %shard_map.106.refs_5_), channel_id=1, source_target_pairs={{16,24},{20,28},{17,25},{21,29},{18,26},{22,30},{19,27},{23,31}} | collective-permute-start | bytes 786440 | tf_op jit(solution)/shard_map/ppermute | solution.py:446
  31.4 3.9 %copy-start.4 = (bf16[512,2048]{1,0:T(8,128)(2,1)S(1)}, bf16[512,2048]{1,0:T(8,128)(2,1)}, u32[]{:S(2)}) copy-start(bf16[512,2048]{1,0:T(8,128)(2,1)} %refs_1_.35) | copy-start | bytes 6291460
  31.4 3.8 %copy-start.7 = (f32[2048]{0:T(1024)S(1)}, f32[2048]{0:T(1024)}, u32[]{:S(2)}) copy-start(f32[2048]{0:T(1024)} %param.10) | copy-start | bytes 24580
  31.4 8.4 %collective-permute-start.9 = (f32[512,128]{1,0:T(8,128)S(1)}, f32[512,128]{1,0:T(8,128)S(1)}, u32[]{:S(2)}, u32[]{:S(2)}) collective-permute-start(f32[512,128]{1,0:T(8,128)S(1)} %get-tuple-element.57.refs_4_), channel_id=1, source_target_pairs={{0,4},{4,0},{8,12},{12,8},{16,20},{20,16},{24,28},{28,24},{1,5},{5... | collective-permute-start | bytes 786440 | tf_op jit(solution)/shard_map/ppermute | solution.py:457
  36.5 7.3 %collective-permute-start.8 = (f32[512,128]{1,0:T(8,128)S(1)}, f32[512,128]{1,0:T(8,128)S(1)}, u32[]{:S(2)}, u32[]{:S(2)}) collective-permute-start(f32[512,128]{1,0:T(8,128)S(1)} %get-tuple-element.60.refs_7_), channel_id=1, source_target_pairs={{0,4},{4,0},{8,12},{12,8},{16,20},{20,16},{24,28},{28,24},{1,5},{5... | collective-permute-start | bytes 786440 | tf_op jit(solution)/shard_map/ppermute | solution.py:457
  44.9 1.7 %collective-permute-start.12 = (f32[8,512]{1,0:T(8,128)S(1)}, f32[8,512]{1,0:T(8,128)S(1)}, u32[]{:S(2)}, u32[]{:S(2)}) collective-permute-start(f32[8,512]{1,0:T(8,128)S(1)} %get-tuple-element.64.refs_5_), channel_id=1, source_target_pairs={{0,3},{1,0},{2,1},{3,2},{4,7},{5,4},{6,5},{7,6},{8,11},{9,8},{10,9... | collective-permute-start | bytes 49160 | tf_op jit(solution)/shard_map/ppermute | solution.py:529
  44.9 3.8 %collective-permute-start.11 = (f32[8,512]{1,0:T(8,128)S(1)}, f32[8,512]{1,0:T(8,128)S(1)}, u32[]{:S(2)}, u32[]{:S(2)}) collective-permute-start(f32[8,512]{1,0:T(8,128)S(1)} %get-tuple-element.64.refs_5_), channel_id=1, source_target_pairs={{0,2},{1,3},{2,0},{3,1},{4,6},{5,7},{6,4},{7,5},{8,10},{9,11},{10,... | collective-permute-start | bytes 49160 | tf_op jit(solution)/shard_map/ppermute | solution.py:529
  46.5 3.2 %collective-permute-start.10 = (f32[8,512]{1,0:T(8,128)S(1)}, f32[8,512]{1,0:T(8,128)S(1)}, u32[]{:S(2)}, u32[]{:S(2)}) collective-permute-start(f32[8,512]{1,0:T(8,128)S(1)} %get-tuple-element.64.refs_5_), channel_id=1, source_target_pairs={{0,1},{1,2},{2,3},{3,0},{4,5},{5,6},{6,7},{7,4},{8,9},{9,10},{10,1... | collective-permute-start | bytes 49160 | tf_op jit(solution)/shard_map/ppermute | solution.py:529
  51.4 7.5 %collective-permute-start.13 = (f32[520,128]{1,0:T(8,128)S(1)}, f32[520,128]{1,0:T(8,128)S(1)}, u32[]{:S(2)}, u32[]{:S(2)}) collective-permute-start(f32[520,128]{1,0:T(8,128)S(1)} %get-tuple-element.69.refs_10_), channel_id=1, source_target_pairs={{0,4},{4,0},{8,12},{12,8},{16,20},{20,16},{24,28},{28,24},{1,5},{5... | collective-permute-start | bytes 798728 | tf_op jit(solution)/shard_map/ppermute | solution.py:418
  58.6 6.6 %collective-permute-start.15 = (f32[520,128]{1,0:T(8,128)S(1)}, f32[520,128]{1,0:T(8,128)S(1)}, u32[]{:S(2)}, u32[]{:S(2)}) collective-permute-start(f32[520,128]{1,0:T(8,128)S(1)} %shard_map.118.refs_2_), channel_id=1, source_target_pairs={{0,4},{4,0},{8,12},{12,8},{16,20},{20,16},{24,28},{28,24},{1,5},{5... | collective-permute-start | bytes 798728 | tf_op jit(solution)/shard_map/ppermute | solution.py:421
  59.0 6.9 %collective-permute-start.14 = (f32[512,128]{1,0:T(8,128)S(1)}, f32[512,128]{1,0:T(8,128)S(1)}, u32[]{:S(2)}, u32[]{:S(2)}) collective-permute-start(f32[512,128]{1,0:T(8,128)S(1)} %shard_map.119.refs_6_), channel_id=1, source_target_pairs={{24,16},{28,20},{25,17},{29,21},{26,18},{30,22},{27,19},{31,23}} | collective-permute-start | bytes 786440 | tf_op jit(solution)/shard_map/ppermute | solution.py:446
  65.2 5.4 %collective-permute-start.17 = (f32[512,128]{1,0:T(8,128)S(1)}, f32[512,128]{1,0:T(8,128)S(1)}, u32[]{:S(2)}, u32[]{:S(2)}) collective-permute-start(f32[512,128]{1,0:T(8,128)S(1)} %shard_map.121.refs_3_), channel_id=1, source_target_pairs={{24,16},{28,20},{25,17},{29,21},{26,18},{30,22},{27,19},{31,23}} | collective-permute-start | bytes 786440 | tf_op jit(solution)/shard_map/ppermute | solution.py:446
  65.9 5.3 %collective-permute-start.16 = (f32[512,128]{1,0:T(8,128)S(1)}, f32[512,128]{1,0:T(8,128)S(1)}, u32[]{:S(2)}, u32[]{:S(2)}) collective-permute-start(f32[512,128]{1,0:T(8,128)S(1)} %shard_map.122.refs_7_), channel_id=1, source_target_pairs={{16,8},{20,12},{17,9},{21,13},{18,10},{22,14},{19,11},{23,15}} | collective-permute-start | bytes 786440 | tf_op jit(solution)/shard_map/ppermute | solution.py:446
  70.6 6.0 %collective-permute-start.19 = (f32[512,128]{1,0:T(8,128)S(1)}, f32[512,128]{1,0:T(8,128)S(1)}, u32[]{:S(2)}, u32[]{:S(2)}) collective-permute-start(f32[512,128]{1,0:T(8,128)S(1)} %shard_map.124.refs_3_), channel_id=1, source_target_pairs={{16,8},{20,12},{17,9},{21,13},{18,10},{22,14},{19,11},{23,15}} | collective-permute-start | bytes 786440 | tf_op jit(solution)/shard_map/ppermute | solution.py:446
  71.3 17.4 %collective-permute-start.18 = (f32[512,128]{1,0:T(8,128)S(1)}, f32[512,128]{1,0:T(8,128)S(1)}, u32[]{:S(2)}, u32[]{:S(2)}) collective-permute-start(f32[512,128]{1,0:T(8,128)S(1)} %shard_map.125.refs_7_), channel_id=1, source_target_pairs={{8,0},{12,4},{9,1},{13,5},{10,2},{14,6},{11,3},{15,7}} | collective-permute-start | bytes 786440 | tf_op jit(solution)/shard_map/ppermute | solution.py:446
  76.5 17.9 %collective-permute-start.20 = (f32[512,128]{1,0:T(8,128)S(1)}, f32[512,128]{1,0:T(8,128)S(1)}, u32[]{:S(2)}, u32[]{:S(2)}) collective-permute-start(f32[512,128]{1,0:T(8,128)S(1)} %shard_map.127.refs_5_), channel_id=1, source_target_pairs={{8,0},{12,4},{9,1},{13,5},{10,2},{14,6},{11,3},{15,7}} | collective-permute-start | bytes 786440 | tf_op jit(solution)/shard_map/ppermute | solution.py:446
  88.8 9.9 %collective-permute-start.22 = (f32[512,128]{1,0:T(8,128)S(1)}, f32[512,128]{1,0:T(8,128)S(1)}, u32[]{:S(2)}, u32[]{:S(2)}) collective-permute-start(f32[512,128]{1,0:T(8,128)S(1)} %get-tuple-element.86.refs_7_), channel_id=1, source_target_pairs={{0,4},{4,0},{8,12},{12,8},{16,20},{20,16},{24,28},{28,24},{1,5},{5... | collective-permute-start | bytes 786440 | tf_op jit(solution)/shard_map/ppermute | solution.py:457
  94.5 6.4 %collective-permute-start.21 = (f32[512,128]{1,0:T(8,128)S(1)}, f32[512,128]{1,0:T(8,128)S(1)}, u32[]{:S(2)}, u32[]{:S(2)}) collective-permute-start(f32[512,128]{1,0:T(8,128)S(1)} %get-tuple-element.90.refs_6_), channel_id=1, source_target_pairs={{0,4},{4,0},{8,12},{12,8},{16,20},{20,16},{24,28},{28,24},{1,5},{5... | collective-permute-start | bytes 786440 | tf_op jit(solution)/shard_map/ppermute | solution.py:457

commit v8 on v6

--- a/solution.py
+++ b/solution.py
@@ -66,9 +66,9 @@
 
 
 class Part:
-    def __init__(self, first, count, slot, group_heads):
+    def __init__(self, first, count, slot, group_heads, per_step=0):
         self.first, self.count, self.slot, self.group_heads = first, count, slot, group_heads
-        self.steps = 2 if count % 4 == 0 else 1
+        self.steps = count // per_step if per_step else 2 if count % 4 == 0 else 1
         self.per_step = count // self.steps
 
     def group(self, info):
@@ -389,9 +389,9 @@
         def call(self, kernel, ins, outs, **options):
             return run(functools.partial(kernel, self), self.steps, ins, outs, **options)
 
-    def parts_of(chunks, slot):
+    def parts_of(chunks, slot, per_step=0):
         count = group_heads // chunks
-        return [Calls(c * count, count, slot, group_heads) for c in range(chunks)]
+        return [Calls(c * count, count, slot, group_heads, per_step) for c in range(chunks)]
 
     swap = [(2 * p + m, 2 * p + 1 - m) for p in range(places) for m in (0, 1)]
 
@@ -470,7 +470,7 @@
     front_count = group_heads // FORWARD_CHUNKS
     per_back = back_count // front_count
     back_parts = {slot: parts_of(BACKWARD_CHUNKS, slot) for slot in ("mine", "theirs")}
-    front_parts = {slot: parts_of(FORWARD_CHUNKS, slot) for slot in ("mine", "theirs")}
+    front_parts = {slot: parts_of(FORWARD_CHUNKS, slot, front_count) for slot in ("mine", "theirs")}
 
     def cumul_in():
         return plain(held_cumul[0])

time: 103 us -> 103 us (level)
  no operation moved by 1% of the time
where the time goes in v8:
time: 103 us; the launch traced here: 102 us
  Pallas kernels  46.9 us (46%)
  starting transfers between devices  26.2 us (25%)
  waiting for transfers between devices  25.6 us (25%)
  local copies, waits for them, and re-layouts  2.39 us (2%)
  between operations  1.06 us (1%)
    pallas_call x42, Pallas kernels, run(): pl.pallas_call(body, out_shape=[shape for shape, _ in outs], grid_spec=pl...  46.9 us
    ppermute x12, starting transfers between devices, chain(): arrived[c, p + 1] = lax.ppermute(value, 'seq', pairs)  14.8 us
    ppermute x12, waiting for transfers between devices, chain(): arrived[c, p + 1] = lax.ppermute(value, 'seq', pairs)  12.5 us
    ppermute x4, waiting for transfers between devices, chain(): theirs.append(lax.ppermute(send, 'seq', swap))  6.13 us
    ppermute x2, starting transfers between devices, exchange(): received.append(lax.ppermute(sends[0], 'seq', swap))  4.7 us
    ppermute x4, starting transfers between devices, chain(): theirs.append(lax.ppermute(send, 'seq', swap))  4.43 us
    ppermute x3, waiting for transfers between devices, on_device(): lax.ppermute(sums, 'head', [(i, (i + k) % head_count) for i in range(head...  2.95 us
    unnamed x16, local copies, waits for them, and re-layouts  2.38 us
  transfers between devices with their start and end apart: 23, of which 10 were waited for; matrix products, arithmetic and copies ran while one was open for 0% of the time, Pallas kernels for 39%

profile of v8, /device:TPU:0, one launch (start us, length us, event | category | flops | bytes accessed | tf_op | source)
XLA Modules:
  0.0 102.1 jit_solution(11397355995316358227)
XLA Ops:
  0.7 3.0 %shard_map.93 = (f32[520,128]{1,0:T(8,128)}, f32[16,512]{1,0:T(8,128)}) custom-call(s32[1]{0:T(128)} %bitcast.member_ref, s32[1]{0:T(128)} %bitcast.1.pair_ref, bf16[512,2048]{1,0:T(8,128)(2,1)} %refs_2_.31, bf16[512,2048]{1,0:T(8,128)(2,1)} %refs_3_.15, f32[16,512]{1,0:T(8,128)} %bitcast.12), custom_call_target="tpu_custom_call" | custom-call | flops 50000000 | bytes 125000 | tf_op jit(solution)/shard_map/pallas_call | solution.py:353
  3.6 3.0 %collective-permute-start = (f32[520,128]{1,0:T(8,128)}, f32[520,128]{1,0:T(8,128)S(1)}, u32[]{:S(2)}, u32[]{:S(2)}) collective-permute-start(f32[520,128]{1,0:T(8,128)} %get-tuple-element.55), channel_id=1, source_target_pairs={{0,4},{4,0},{8,12},{12,8},{16,20},{20,16},{24,28},{28,24},{1,5},{5... | collective-permute-start | bytes 798728 | tf_op jit(solution)/shard_map/ppermute | solution.py:413
  6.6 1.6 %copy-done.2 = bf16[512,2048]{1,0:T(8,128)(2,1)S(1)} copy-done((bf16[512,2048]{1,0:T(8,128)(2,1)S(1)}, bf16[512,2048]{1,0:T(8,128)(2,1)}, u32[]{:S(2)}) %copy-start.2) | copy-done | bytes 2097176
  11.6 1.8 %collective-permute-done.refs_1_ = f32[520,128]{1,0:T(8,128)S(1)} collective-permute-done((f32[520,128]{1,0:T(8,128)}, f32[520,128]{1,0:T(8,128)S(1)}, u32[]{:S(2)}, u32[]{:S(2)}) %collective-permute-start) | collective-permute-done | bytes 266272 | tf_op jit(solution)/shard_map/ppermute | solution.py:413
  13.5 3.5 %collective-permute-start.1 = (f32[512,128]{1,0:T(8,128)S(1)}, f32[512,128]{1,0:T(8,128)S(1)}, u32[]{:S(2)}, u32[]{:S(2)}) collective-permute-start(f32[512,128]{1,0:T(8,128)S(1)} %shard_map.98.refs_4_), channel_id=1, source_target_pairs={{0,8},{4,12},{1,9},{5,13},{2,10},{6,14},{3,11},{7,15}} | collective-permute-start | bytes 786440 | tf_op jit(solution)/shard_map/ppermute | solution.py:441
  16.9 1.9 %shard_map.99.refs_2_.refs_0_ = f32[512,512]{1,0:T(8,128)S(1)} custom-call(s32[1]{0:T(128)} %bitcast.member_ref, s32[1]{0:T(128)} %bitcast.1.pair_ref, bf16[512,2048]{1,0:T(8,128)(2,1)S(1)} %copy-done, bf16[512,2048]{1,0:T(8,128)(2,1)S(1)} %copy-done.1, bf16[512,2048]{1,0:T(8,128)(2,1)S(1)} %copy-done.3, f32[16,512]{1,0:T(8,128)S(1)} %copy-done.5, ...), custom_call_target="tpu_custom_call" | custom-call | flops 100000000 | bytes 250000 | tf_op jit(solution)/shard_map/pallas_call | solution.py:353
  19.5 3.4 %collective-permute-start.4 = (f32[512,128]{1,0:T(8,128)S(1)}, f32[512,128]{1,0:T(8,128)S(1)}, u32[]{:S(2)}, u32[]{:S(2)}) collective-permute-start(f32[512,128]{1,0:T(8,128)S(1)} %shard_map.100.refs_3_), channel_id=1, source_target_pairs={{0,8},{4,12},{1,9},{5,13},{2,10},{6,14},{3,11},{7,15}} | collective-permute-start | bytes 786440 | tf_op jit(solution)/shard_map/ppermute | solution.py:441
  23.7 1.9 %shard_map.102.refs_3_.refs_0_ = f32[512,512]{1,0:T(8,128)S(1)} custom-call(s32[1]{0:T(128)} %bitcast.member_ref, s32[1]{0:T(128)} %bitcast.1.pair_ref, bf16[512,2048]{1,0:T(8,128)(2,1)S(1)} %copy-done, bf16[512,2048]{1,0:T(8,128)(2,1)S(1)} %copy-done.1, bf16[512,2048]{1,0:T(8,128)(2,1)S(1)} %copy-done.3, f32[16,512]{1,0:T(8,128)S(1)} %copy-done.5, ...), custom_call_target="tpu_custom_call" | custom-call | flops 2200000000 | bytes 5500000 | tf_op jit(solution)/shard_map/pallas_call | solution.py:353
  25.6 1.7 %collective-permute-done.4.refs_2_ = f32[512,128]{1,0:T(8,128)S(1)} collective-permute-done((f32[512,128]{1,0:T(8,128)S(1)}, f32[512,128]{1,0:T(8,128)S(1)}, u32[]{:S(2)}, u32[]{:S(2)}) %collective-permute-start.4) | collective-permute-done | bytes 262176 | tf_op jit(solution)/shard_map/ppermute | solution.py:441
  28.7 1.9 %shard_map.105.refs_3_.refs_0_ = f32[512,512]{1,0:T(8,128)S(1)} custom-call(s32[1]{0:T(128)} %bitcast.member_ref, s32[1]{0:T(128)} %bitcast.1.pair_ref, bf16[512,2048]{1,0:T(8,128)(2,1)S(1)} %copy-done, bf16[512,2048]{1,0:T(8,128)(2,1)S(1)} %copy-done.1, bf16[512,2048]{1,0:T(8,128)(2,1)S(1)} %copy-done.3, f32[16,512]{1,0:T(8,128)S(1)} %copy-done.6, ...), custom_call_target="tpu_custom_call" | custom-call | flops 2200000000 | bytes 5500000 | tf_op jit(solution)/shard_map/pallas_call | solution.py:353
  31.5 1.9 %collective-permute-start.9 = (f32[512,128]{1,0:T(8,128)S(1)}, f32[512,128]{1,0:T(8,128)S(1)}, u32[]{:S(2)}, u32[]{:S(2)}) collective-permute-start(f32[512,128]{1,0:T(8,128)S(1)} %get-tuple-element.57.refs_4_), channel_id=1, source_target_pairs={{0,4},{4,0},{8,12},{12,8},{16,20},{20,16},{24,28},{28,24},{1,5},{5... | collective-permute-start | bytes 786440 | tf_op jit(solution)/shard_map/ppermute | solution.py:452
  33.4 1.9 %shard_map.108.refs_7_.refs_0_ = f32[512,512]{1,0:T(8,128)S(1)} custom-call(s32[1]{0:T(128)} %bitcast.member_ref, s32[1]{0:T(128)} %bitcast.1.pair_ref, bf16[512,2048]{1,0:T(8,128)(2,1)S(1)} %copy-done, bf16[512,2048]{1,0:T(8,128)(2,1)S(1)} %copy-done.1, bf16[512,2048]{1,0:T(8,128)(2,1)S(1)} %copy-done.3, f32[16,512]{1,0:T(8,128)S(1)} %copy-done.6, ...), custom_call_target="tpu_custom_call" | custom-call | flops 2200000000 | bytes 5500000 | tf_op jit(solution)/shard_map/pallas_call | solution.py:353
  37.5 2.6 %collective-permute-done.9.refs_5_ = f32[512,128]{1,0:T(8,128)S(1)} collective-permute-done((f32[512,128]{1,0:T(8,128)S(1)}, f32[512,128]{1,0:T(8,128)S(1)}, u32[]{:S(2)}, u32[]{:S(2)}) %collective-permute-start.9) | collective-permute-done | bytes 262176 | tf_op jit(solution)/shard_map/ppermute | solution.py:452
  41.0 2.9 %collective-permute-done.8.refs_5_ = f32[512,128]{1,0:T(8,128)S(1)} collective-permute-done((f32[512,128]{1,0:T(8,128)S(1)}, f32[512,128]{1,0:T(8,128)S(1)}, u32[]{:S(2)}, u32[]{:S(2)}) %collective-permute-start.8) | collective-permute-done | bytes 262176 | tf_op jit(solution)/shard_map/ppermute | solution.py:452
  44.8 1.5 %collective-permute-start.11 = (f32[8,512]{1,0:T(8,128)S(1)}, f32[8,512]{1,0:T(8,128)S(1)}, u32[]{:S(2)}, u32[]{:S(2)}) collective-permute-start(f32[8,512]{1,0:T(8,128)S(1)} %get-tuple-element.64.refs_5_), channel_id=1, source_target_pairs={{0,2},{1,3},{2,0},{3,1},{4,6},{5,7},{6,4},{7,5},{8,10},{9,11},{10,... | collective-permute-start | bytes 49160 | tf_op jit(solution)/shard_map/ppermute | solution.py:524
  46.5 2.0 %collective-permute-done.11.refs_7_ = f32[8,512]{1,0:T(8,128)S(1)} collective-permute-done((f32[8,512]{1,0:T(8,128)S(1)}, f32[8,512]{1,0:T(8,128)S(1)}, u32[]{:S(2)}, u32[]{:S(2)}) %collective-permute-start.11) | collective-permute-done | bytes 16416 | tf_op jit(solution)/shard_map/ppermute | solution.py:524
  49.5 1.7 %shard_map.114 = (bf16[512,2048]{1,0:T(8,128)(2,1)}, bf16[512,512]{1,0:T(8,128)(2,1)S(1)}, f32[520,128]{1,0:T(8,128)S(1)}) custom-call(s32[1]{0:T(128)} %bitcast.member_ref, s32[1]{0:T(128)} %bitcast.1.pair_ref, f32[512,512]{1,0:T(8,128)S(1)} %get-tuple-element.67.refs_0_, bf16[512,2048]{1,0:T(8,128)(2,1)S(1)} %copy-done.4, f32[1,2048]{1,0:T(1,128)S(1)} %bitcast.8, ...), custom_call_target="tpu_custom_call" | custom-call | flops 2000000000 | bytes 5000000 | tf_op jit(solution)/shard_map/pallas_call | solution.py:353
  51.2 1.7 %collective-permute-start.13 = (f32[520,128]{1,0:T(8,128)S(1)}, f32[520,128]{1,0:T(8,128)S(1)}, u32[]{:S(2)}, u32[]{:S(2)}) collective-permute-start(f32[520,128]{1,0:T(8,128)S(1)} %get-tuple-element.69.refs_10_), channel_id=1, source_target_pairs={{0,4},{4,0},{8,12},{12,8},{16,20},{20,16},{24,28},{28,24},{1,5},{5... | collective-permute-start | bytes 798728 | tf_op jit(solution)/shard_map/ppermute | solution.py:413
  53.0 1.7 %shard_map.115 = (bf16[512,2048]{1,0:T(8,128)(2,1)}, bf16[512,512]{1,0:T(8,128)(2,1)S(1)}, f32[520,128]{1,0:T(8,128)S(1)}) custom-call(s32[1]{0:T(128)} %bitcast.member_ref, s32[1]{0:T(128)} %bitcast.1.pair_ref, f32[512,512]{1,0:T(8,128)S(1)} %get-tuple-element.66.refs_0_, bf16[512,2048]{1,0:T(8,128)(2,1)S(1)} %copy-done.4, ...), custom_call_target="tpu_custom_call", output_to_operand_aliasing={{0}: (11, {})} | custom-call | flops 2000000000 | bytes 5000000 | tf_op jit(solution)/shard_map/pallas_call | solution.py:353
  54.7 1.7 %shard_map.116 = (bf16[512,2048]{1,0:T(8,128)(2,1)}, bf16[512,512]{1,0:T(8,128)(2,1)S(1)}, f32[520,128]{1,0:T(8,128)S(1)}) custom-call(s32[1]{0:T(128)} %bitcast.member_ref, s32[1]{0:T(128)} %bitcast.1.pair_ref, f32[512,512]{1,0:T(8,128)S(1)} %get-tuple-element.65.refs_0_, bf16[512,2048]{1,0:T(8,128)(2,1)S(1)} %copy-done.4, ...), custom_call_target="tpu_custom_call", output_to_operand_aliasing={{0}: (11, {})} | custom-call | flops 2000000000 | bytes 5000000 | tf_op jit(solution)/shard_map/pallas_call | solution.py:353
  56.4 1.7 %shard_map.117 = (bf16[512,2048]{1,0:T(8,128)(2,1)}, bf16[512,512]{1,0:T(8,128)(2,1)S(1)}, f32[520,128]{1,0:T(8,128)S(1)}) custom-call(s32[1]{0:T(128)} %bitcast.member_ref, s32[1]{0:T(128)} %bitcast.1.pair_ref, f32[512,512]{1,0:T(8,128)S(1)} %get-tuple-element.61.refs_0_, bf16[512,2048]{1,0:T(8,128)(2,1)S(1)} %copy-done.4, ...), custom_call_target="tpu_custom_call", output_to_operand_aliasing={{0}: (11, {})} | custom-call | flops 2000000000 | bytes 5000000 | tf_op jit(solution)/shard_map/pallas_call | solution.py:353
  59.2 4.0 %shard_map.120 = (bf16[512,2048]{1,0:T(8,128)(2,1)}, f32[512,512]{1,0:T(8,128)S(1)}, f32[512,512]{1,0:T(8,128)S(1)}) custom-call(s32[1]{0:T(128)} %bitcast.member_ref, s32[1]{0:T(128)} %bitcast.1.pair_ref, bf16[512,2048]{1,0:T(8,128)(2,1)S(1)} %copy-done, bf16[512,2048]{1,0:T(8,128)(2,1)S(1)} %copy-done.1, bf16[512,2048]{1,0:T(8,128)(2,1)S(1)} %copy-done.3, ...), custom_call_target="tpu_custom_call" | custom-call | flops 4300000256 | bytes 10750000 | tf_op jit(solution)/shard_map/pallas_call | solution.py:353
  63.1 1.6 %collective-permute-done.15.refs_1_ = f32[520,128]{1,0:T(8,128)S(1)} collective-permute-done((f32[520,128]{1,0:T(8,128)S(1)}, f32[520,128]{1,0:T(8,128)S(1)}, u32[]{:S(2)}, u32[]{:S(2)}) %collective-permute-start.15) | collective-permute-done | bytes 266272 | tf_op jit(solution)/shard_map/ppermute | solution.py:416
  66.1 4.0 %shard_map.123 = (bf16[512,2048]{1,0:T(8,128)(2,1)}, f32[512,512]{1,0:T(8,128)S(1)}, f32[512,512]{1,0:T(8,128)S(1)}) custom-call(s32[1]{0:T(128)} %bitcast.member_ref, s32[1]{0:T(128)} %bitcast.1.pair_ref, bf16[512,2048]{1,0:T(8,128)(2,1)S(1)} %copy-done, bf16[512,2048]{1,0:T(8,128)(2,1)S(1)} %copy-done.1, ...), custom_call_target="tpu_custom_call", output_to_operand_aliasing={{0}: (8, {})} | custom-call | flops 4300000256 | bytes 10750000 | tf_op jit(solution)/shard_map/pallas_call | solution.py:353
  72.1 4.0 %shard_map.126 = (bf16[512,2048]{1,0:T(8,128)(2,1)}, f32[512,512]{1,0:T(8,128)S(1)}, f32[512,512]{1,0:T(8,128)S(1)}) custom-call(s32[1]{0:T(128)} %bitcast.member_ref, s32[1]{0:T(128)} %bitcast.1.pair_ref, bf16[512,2048]{1,0:T(8,128)(2,1)S(1)} %copy-done, bf16[512,2048]{1,0:T(8,128)(2,1)S(1)} %copy-done.1, ...), custom_call_target="tpu_custom_call", output_to_operand_aliasing={{0}: (8, {})} | custom-call | flops 4300000256 | bytes 10750000 | tf_op jit(solution)/shard_map/pallas_call | solution.py:353
  77.4 10.8 %collective-permute-done.18.refs_4_ = f32[512,128]{1,0:T(8,128)S(1)} collective-permute-done((f32[512,128]{1,0:T(8,128)S(1)}, f32[512,128]{1,0:T(8,128)S(1)}, u32[]{:S(2)}, u32[]{:S(2)}) %collective-permute-start.18) | collective-permute-done | bytes 262176 | tf_op jit(solution)/shard_map/ppermute | solution.py:441
  88.3 1.6 %collective-permute-start.22 = (f32[512,128]{1,0:T(8,128)S(1)}, f32[512,128]{1,0:T(8,128)S(1)}, u32[]{:S(2)}, u32[]{:S(2)}) collective-permute-start(f32[512,128]{1,0:T(8,128)S(1)} %get-tuple-element.86.refs_7_), channel_id=1, source_target_pairs={{0,4},{4,0},{8,12},{12,8},{16,20},{20,16},{24,28},{28,24},{1,5},{5... | collective-permute-start | bytes 786440 | tf_op jit(solution)/shard_map/ppermute | solution.py:452
  89.9 3.9 %shard_map.129 = (bf16[512,2048]{1,0:T(8,128)(2,1)}, f32[512,512]{1,0:T(8,128)S(1)}, f32[512,512]{1,0:T(8,128)S(1)}) custom-call(s32[1]{0:T(128)} %bitcast.member_ref, s32[1]{0:T(128)} %bitcast.1.pair_ref, bf16[512,2048]{1,0:T(8,128)(2,1)S(1)} %copy-done, bf16[512,2048]{1,0:T(8,128)(2,1)S(1)} %copy-done.1, ...), custom_call_target="tpu_custom_call", output_to_operand_aliasing={{0}: (8, {})} | custom-call | flops 4300000256 | bytes 10750000 | tf_op jit(solution)/shard_map/pallas_call | solution.py:353
  94.5 1.8 %shard_map.131 = (bf16[512,2048]{1,0:T(8,128)(2,1)}, bf16[512,2048]{1,0:T(8,128)(2,1)}) custom-call(s32[1]{0:T(128)} %bitcast.member_ref, s32[1]{0:T(128)} %bitcast.1.pair_ref, f32[512,512]{1,0:T(8,128)S(1)} %get-tuple-element.81.refs_2_.refs_0_, f32[512,512]{1,0:T(8,128)S(1)} %get-tuple-element.94.refs_1_, bf16[512,2048]{1,0:T(8,128)(2,1)S(1)} %copy-done.1, ...), custom_call_target="tpu_custom_call" | custom-call | flops 2000000000 | bytes 5000000 | tf_op jit(solution)/shard_map/pallas_call | solution.py:353
  96.3 1.7 %shard_map.132 = (bf16[512,2048]{1,0:T(8,128)(2,1)}, bf16[512,2048]{1,0:T(8,128)(2,1)}) custom-call(s32[1]{0:T(128)} %bitcast.member_ref, s32[1]{0:T(128)} %bitcast.1.pair_ref, f32[512,512]{1,0:T(8,128)S(1)} %get-tuple-element.85.refs_3_.refs_0_, f32[512,512]{1,0:T(8,128)S(1)} %get-tuple-element.92.refs_1_, ...), custom_call_target="tpu_custom_call", output_to_operand_aliasing={{0}: (8, {}), {1}: (9, {})} | custom-call | flops 2000000000 | bytes 5000000 | tf_op jit(solution)/shard_map/pallas_call | solution.py:353
  98.0 1.7 %shard_map.133 = (bf16[512,2048]{1,0:T(8,128)(2,1)}, bf16[512,2048]{1,0:T(8,128)(2,1)}) custom-call(s32[1]{0:T(128)} %bitcast.member_ref, s32[1]{0:T(128)} %bitcast.1.pair_ref, f32[512,512]{1,0:T(8,128)S(1)} %get-tuple-element.83.refs_3_.refs_0_, f32[512,512]{1,0:T(8,128)S(1)} %get-tuple-element.91.refs_1_, ...), custom_call_target="tpu_custom_call", output_to_operand_aliasing={{0}: (8, {}), {1}: (9, {})} | custom-call | flops 2000000000 | bytes 5000000 | tf_op jit(solution)/shard_map/pallas_call | solution.py:353
  100.4 1.7 %shard_map.134 = (bf16[512,2048]{1,0:T(8,128)(2,1)}, bf16[512,2048]{1,0:T(8,128)(2,1)}) custom-call(s32[1]{0:T(128)} %bitcast.member_ref, s32[1]{0:T(128)} %bitcast.1.pair_ref, f32[512,512]{1,0:T(8,128)S(1)} %get-tuple-element.88.refs_5_.refs_0_, f32[512,512]{1,0:T(8,128)S(1)} %get-tuple-element.89.refs_1_, ...), custom_call_target="tpu_custom_call", output_to_operand_aliasing={{0}: (8, {}), {1}: (9, {})} | custom-call | flops 2000000000 | bytes 5000000 | tf_op jit(solution)/shard_map/pallas_call | solution.py:353
  (73 shorter events, 19.0 us)
Async XLA Ops:
  0.7 5.9 %copy-start.1 = (bf16[512,2048]{1,0:T(8,128)(2,1)S(1)}, bf16[512,2048]{1,0:T(8,128)(2,1)}, u32[]{:S(2)}) copy-start(bf16[512,2048]{1,0:T(8,128)(2,1)} %refs_2_.31) | copy-start | bytes 6291460
  3.6 9.8 %collective-permute-start = (f32[520,128]{1,0:T(8,128)}, f32[520,128]{1,0:T(8,128)S(1)}, u32[]{:S(2)}, u32[]{:S(2)}) collective-permute-start(f32[520,128]{1,0:T(8,128)} %get-tuple-element.55), channel_id=1, source_target_pairs={{0,4},{4,0},{8,12},{12,8},{16,20},{20,16},{24,28},{28,24},{1,5},{5... | collective-permute-start | bytes 798728 | tf_op jit(solution)/shard_map/ppermute | solution.py:413
  6.6 1.6 %copy-start.2 = (bf16[512,2048]{1,0:T(8,128)(2,1)S(1)}, bf16[512,2048]{1,0:T(8,128)(2,1)}, u32[]{:S(2)}) copy-start(bf16[512,2048]{1,0:T(8,128)(2,1)} %refs_3_.15) | copy-start | bytes 6291460
  8.2 0.8 copy-start.5
  10.6 6.3 %copy-start = (bf16[512,2048]{1,0:T(8,128)(2,1)S(1)}, bf16[512,2048]{1,0:T(8,128)(2,1)}, u32[]{:S(2)}) copy-start(bf16[512,2048]{1,0:T(8,128)(2,1)} %refs_0_.23) | copy-start | bytes 6291460
  10.6 6.3 %copy-start.3 = (bf16[512,2048]{1,0:T(8,128)(2,1)S(1)}, bf16[512,2048]{1,0:T(8,128)(2,1)}, u32[]{:S(2)}) copy-start(bf16[512,2048]{1,0:T(8,128)(2,1)} %refs_3_.15) | copy-start | bytes 6291460
  11.5 7.9 %collective-permute-start.2 = (f32[520,128]{1,0:T(8,128)S(1)}, f32[520,128]{1,0:T(8,128)S(1)}, u32[]{:S(2)}, u32[]{:S(2)}) collective-permute-start(f32[520,128]{1,0:T(8,128)S(1)} %shard_map.97.refs_2_), channel_id=1, source_target_pairs={{0,4},{4,0},{8,12},{12,8},{16,20},{20,16},{24,28},{28,24},{1,5},{5... | collective-permute-start | bytes 798728 | tf_op jit(solution)/shard_map/ppermute | solution.py:416
  13.5 9.5 %collective-permute-start.1 = (f32[512,128]{1,0:T(8,128)S(1)}, f32[512,128]{1,0:T(8,128)S(1)}, u32[]{:S(2)}, u32[]{:S(2)}) collective-permute-start(f32[512,128]{1,0:T(8,128)S(1)} %shard_map.98.refs_4_), channel_id=1, source_target_pairs={{0,8},{4,12},{1,9},{5,13},{2,10},{6,14},{3,11},{7,15}} | collective-permute-start | bytes 786440 | tf_op jit(solution)/shard_map/ppermute | solution.py:441
  19.5 7.8 %collective-permute-start.4 = (f32[512,128]{1,0:T(8,128)S(1)}, f32[512,128]{1,0:T(8,128)S(1)}, u32[]{:S(2)}, u32[]{:S(2)}) collective-permute-start(f32[512,128]{1,0:T(8,128)S(1)} %shard_map.100.refs_3_), channel_id=1, source_target_pairs={{0,8},{4,12},{1,9},{5,13},{2,10},{6,14},{3,11},{7,15}} | collective-permute-start | bytes 786440 | tf_op jit(solution)/shard_map/ppermute | solution.py:441
  23.0 5.0 %collective-permute-start.3 = (f32[512,128]{1,0:T(8,128)S(1)}, f32[512,128]{1,0:T(8,128)S(1)}, u32[]{:S(2)}, u32[]{:S(2)}) collective-permute-start(f32[512,128]{1,0:T(8,128)S(1)} %shard_map.101.refs_4_), channel_id=1, source_target_pairs={{8,16},{12,20},{9,17},{13,21},{10,18},{14,22},{11,19},{15,23}} | collective-permute-start | bytes 786440 | tf_op jit(solution)/shard_map/ppermute | solution.py:441
  25.6 3.1 %copy-start.6 = (f32[16,512]{1,0:T(8,128)S(1)}, f32[16,512]{1,0:T(8,128)}, u32[]{:S(2)}) copy-start(f32[16,512]{1,0:T(8,128)} %get-tuple-element.54.refs_2_.refs_3_.refs_4_) | copy-start | bytes 98308
  27.3 3.3 %collective-permute-start.5 = (f32[512,128]{1,0:T(8,128)S(1)}, f32[512,128]{1,0:T(8,128)S(1)}, u32[]{:S(2)}, u32[]{:S(2)}) collective-permute-start(f32[512,128]{1,0:T(8,128)S(1)} %shard_map.103.refs_3_), channel_id=1, source_target_pairs={{8,16},{12,20},{9,17},{13,21},{10,18},{14,22},{11,19},{15,23}} | collective-permute-start | bytes 786440 | tf_op jit(solution)/shard_map/ppermute | solution.py:441
  28.0 3.4 %collective-permute-start.7 = (f32[512,128]{1,0:T(8,128)S(1)}, f32[512,128]{1,0:T(8,128)S(1)}, u32[]{:S(2)}, u32[]{:S(2)}) collective-permute-start(f32[512,128]{1,0:T(8,128)S(1)} %shard_map.104.refs_4_), channel_id=1, source_target_pairs={{16,24},{20,28},{17,25},{21,29},{18,26},{22,30},{19,27},{23,31}} | collective-permute-start | bytes 786440 | tf_op jit(solution)/shard_map/ppermute | solution.py:441
  30.7 5.6 %collective-permute-start.6 = (f32[512,128]{1,0:T(8,128)S(1)}, f32[512,128]{1,0:T(8,128)S(1)}, u32[]{:S(2)}, u32[]{:S(2)}) collective-permute-start(f32[512,128]{1,0:T(8,128)S(1)} %shard_map.106.refs_5_), channel_id=1, source_target_pairs={{16,24},{20,28},{17,25},{21,29},{18,26},{22,30},{19,27},{23,31}} | collective-permute-start | bytes 786440 | tf_op jit(solution)/shard_map/ppermute | solution.py:441
  31.5 3.8 %copy-start.4 = (bf16[512,2048]{1,0:T(8,128)(2,1)S(1)}, bf16[512,2048]{1,0:T(8,128)(2,1)}, u32[]{:S(2)}) copy-start(bf16[512,2048]{1,0:T(8,128)(2,1)} %refs_1_.35) | copy-start | bytes 6291460
  31.5 3.8 %copy-start.7 = (f32[2048]{0:T(1024)S(1)}, f32[2048]{0:T(1024)}, u32[]{:S(2)}) copy-start(f32[2048]{0:T(1024)} %param.10) | copy-start | bytes 24580
  31.5 8.6 %collective-permute-start.9 = (f32[512,128]{1,0:T(8,128)S(1)}, f32[512,128]{1,0:T(8,128)S(1)}, u32[]{:S(2)}, u32[]{:S(2)}) collective-permute-start(f32[512,128]{1,0:T(8,128)S(1)} %get-tuple-element.57.refs_4_), channel_id=1, source_target_pairs={{0,4},{4,0},{8,12},{12,8},{16,20},{20,16},{24,28},{28,24},{1,5},{5... | collective-permute-start | bytes 786440 | tf_op jit(solution)/shard_map/ppermute | solution.py:452
  36.3 7.6 %collective-permute-start.8 = (f32[512,128]{1,0:T(8,128)S(1)}, f32[512,128]{1,0:T(8,128)S(1)}, u32[]{:S(2)}, u32[]{:S(2)}) collective-permute-start(f32[512,128]{1,0:T(8,128)S(1)} %get-tuple-element.60.refs_7_), channel_id=1, source_target_pairs={{0,4},{4,0},{8,12},{12,8},{16,20},{20,16},{24,28},{28,24},{1,5},{5... | collective-permute-start | bytes 786440 | tf_op jit(solution)/shard_map/ppermute | solution.py:452
  44.8 1.8 %collective-permute-start.12 = (f32[8,512]{1,0:T(8,128)S(1)}, f32[8,512]{1,0:T(8,128)S(1)}, u32[]{:S(2)}, u32[]{:S(2)}) collective-permute-start(f32[8,512]{1,0:T(8,128)S(1)} %get-tuple-element.64.refs_5_), channel_id=1, source_target_pairs={{0,3},{1,0},{2,1},{3,2},{4,7},{5,4},{6,5},{7,6},{8,11},{9,8},{10,9... | collective-permute-start | bytes 49160 | tf_op jit(solution)/shard_map/ppermute | solution.py:524
  44.8 3.8 %collective-permute-start.11 = (f32[8,512]{1,0:T(8,128)S(1)}, f32[8,512]{1,0:T(8,128)S(1)}, u32[]{:S(2)}, u32[]{:S(2)}) collective-permute-start(f32[8,512]{1,0:T(8,128)S(1)} %get-tuple-element.64.refs_5_), channel_id=1, source_target_pairs={{0,2},{1,3},{2,0},{3,1},{4,6},{5,7},{6,4},{7,5},{8,10},{9,11},{10,... | collective-permute-start | bytes 49160 | tf_op jit(solution)/shard_map/ppermute | solution.py:524
  46.3 3.2 %collective-permute-start.10 = (f32[8,512]{1,0:T(8,128)S(1)}, f32[8,512]{1,0:T(8,128)S(1)}, u32[]{:S(2)}, u32[]{:S(2)}) collective-permute-start(f32[8,512]{1,0:T(8,128)S(1)} %get-tuple-element.64.refs_5_), channel_id=1, source_target_pairs={{0,1},{1,2},{2,3},{3,0},{4,5},{5,6},{6,7},{7,4},{8,9},{9,10},{10,1... | collective-permute-start | bytes 49160 | tf_op jit(solution)/shard_map/ppermute | solution.py:524
  51.2 7.3 %collective-permute-start.13 = (f32[520,128]{1,0:T(8,128)S(1)}, f32[520,128]{1,0:T(8,128)S(1)}, u32[]{:S(2)}, u32[]{:S(2)}) collective-permute-start(f32[520,128]{1,0:T(8,128)S(1)} %get-tuple-element.69.refs_10_), channel_id=1, source_target_pairs={{0,4},{4,0},{8,12},{12,8},{16,20},{20,16},{24,28},{28,24},{1,5},{5... | collective-permute-start | bytes 798728 | tf_op jit(solution)/shard_map/ppermute | solution.py:413
  58.1 6.6 %collective-permute-start.15 = (f32[520,128]{1,0:T(8,128)S(1)}, f32[520,128]{1,0:T(8,128)S(1)}, u32[]{:S(2)}, u32[]{:S(2)}) collective-permute-start(f32[520,128]{1,0:T(8,128)S(1)} %shard_map.118.refs_2_), channel_id=1, source_target_pairs={{0,4},{4,0},{8,12},{12,8},{16,20},{20,16},{24,28},{28,24},{1,5},{5... | collective-permute-start | bytes 798728 | tf_op jit(solution)/shard_map/ppermute | solution.py:416
  58.5 6.9 %collective-permute-start.14 = (f32[512,128]{1,0:T(8,128)S(1)}, f32[512,128]{1,0:T(8,128)S(1)}, u32[]{:S(2)}, u32[]{:S(2)}) collective-permute-start(f32[512,128]{1,0:T(8,128)S(1)} %shard_map.119.refs_6_), channel_id=1, source_target_pairs={{24,16},{28,20},{25,17},{29,21},{26,18},{30,22},{27,19},{31,23}} | collective-permute-start | bytes 786440 | tf_op jit(solution)/shard_map/ppermute | solution.py:441
  64.7 5.4 %collective-permute-start.17 = (f32[512,128]{1,0:T(8,128)S(1)}, f32[512,128]{1,0:T(8,128)S(1)}, u32[]{:S(2)}, u32[]{:S(2)}) collective-permute-start(f32[512,128]{1,0:T(8,128)S(1)} %shard_map.121.refs_3_), channel_id=1, source_target_pairs={{24,16},{28,20},{25,17},{29,21},{26,18},{30,22},{27,19},{31,23}} | collective-permute-start | bytes 786440 | tf_op jit(solution)/shard_map/ppermute | solution.py:441
  65.4 5.3 %collective-permute-start.16 = (f32[512,128]{1,0:T(8,128)S(1)}, f32[512,128]{1,0:T(8,128)S(1)}, u32[]{:S(2)}, u32[]{:S(2)}) collective-permute-start(f32[512,128]{1,0:T(8,128)S(1)} %shard_map.122.refs_7_), channel_id=1, source_target_pairs={{16,8},{20,12},{17,9},{21,13},{18,10},{22,14},{19,11},{23,15}} | collective-permute-start | bytes 786440 | tf_op jit(solution)/shard_map/ppermute | solution.py:441
  70.1 6.0 %collective-permute-start.19 = (f32[512,128]{1,0:T(8,128)S(1)}, f32[512,128]{1,0:T(8,128)S(1)}, u32[]{:S(2)}, u32[]{:S(2)}) collective-permute-start(f32[512,128]{1,0:T(8,128)S(1)} %shard_map.124.refs_3_), channel_id=1, source_target_pairs={{16,8},{20,12},{17,9},{21,13},{18,10},{22,14},{19,11},{23,15}} | collective-permute-start | bytes 786440 | tf_op jit(solution)/shard_map/ppermute | solution.py:441
  70.8 17.4 %collective-permute-start.18 = (f32[512,128]{1,0:T(8,128)S(1)}, f32[512,128]{1,0:T(8,128)S(1)}, u32[]{:S(2)}, u32[]{:S(2)}) collective-permute-start(f32[512,128]{1,0:T(8,128)S(1)} %shard_map.125.refs_7_), channel_id=1, source_target_pairs={{8,0},{12,4},{9,1},{13,5},{10,2},{14,6},{11,3},{15,7}} | collective-permute-start | bytes 786440 | tf_op jit(solution)/shard_map/ppermute | solution.py:441
  76.1 17.8 %collective-permute-start.20 = (f32[512,128]{1,0:T(8,128)S(1)}, f32[512,128]{1,0:T(8,128)S(1)}, u32[]{:S(2)}, u32[]{:S(2)}) collective-permute-start(f32[512,128]{1,0:T(8,128)S(1)} %shard_map.127.refs_5_), channel_id=1, source_target_pairs={{8,0},{12,4},{9,1},{13,5},{10,2},{14,6},{11,3},{15,7}} | collective-permute-start | bytes 786440 | tf_op jit(solution)/shard_map/ppermute | solution.py:441
  88.3 9.8 %collective-permute-start.22 = (f32[512,128]{1,0:T(8,128)S(1)}, f32[512,128]{1,0:T(8,128)S(1)}, u32[]{:S(2)}, u32[]{:S(2)}) collective-permute-start(f32[512,128]{1,0:T(8,128)S(1)} %get-tuple-element.86.refs_7_), channel_id=1, source_target_pairs={{0,4},{4,0},{8,12},{12,8},{16,20},{20,16},{24,28},{28,24},{1,5},{5... | collective-permute-start | bytes 786440 | tf_op jit(solution)/shard_map/ppermute | solution.py:452
  93.9 6.4 %collective-permute-start.21 = (f32[512,128]{1,0:T(8,128)S(1)}, f32[512,128]{1,0:T(8,128)S(1)}, u32[]{:S(2)}, u32[]{:S(2)}) collective-permute-start(f32[512,128]{1,0:T(8,128)S(1)} %get-tuple-element.90.refs_6_), channel_id=1, source_target_pairs={{0,4},{4,0},{8,12},{12,8},{16,20},{20,16},{24,28},{28,24},{1,5},{5... | collective-permute-start | bytes 786440 | tf_op jit(solution)/shard_map/ppermute | solution.py:452

commit v9 on v8

--- a/solution.py
+++ b/solution.py
@@ -485,6 +485,7 @@
             )
             held_cumul.append(cumul)
             return piece
+        part = Calls(part.first, part.count, part.slot, group_heads, part.count)
         return part.call(
             pieces_kernel, [plain(key_vecs), plain(value_vecs), cumul_in()],
             [give(states_of(part.count, 8))], after=after, cost=0.05,

time: 103 us -> 102 us (level)
  transfers between devices with their start and end apart: 23 -> 23, of which waited for: 10 -> 9; matrix products, arithmetic and copies ran while one was open for 0% -> 0% of each run, Pallas kernels for 39% -> 38%
where the time goes in v9:
time: 102 us
  Pallas kernels  46.3 us (45%)
  starting transfers between devices  26.1 us (26%)
  waiting for transfers between devices  26 us (25%)
  local copies, waits for them, and re-layouts  2.39 us (2%)
  between operations  1.06 us (1%)
    pallas_call x42, Pallas kernels, run(): pl.pallas_call(body, out_shape=[shape for shape, _ in outs], grid_spec=pl...  46.3 us
    ppermute x12, starting transfers between devices, chain(): arrived[c, p + 1] = lax.ppermute(value, 'seq', pairs)  14.8 us
    ppermute x12, waiting for transfers between devices, chain(): arrived[c, p + 1] = lax.ppermute(value, 'seq', pairs)  12.7 us
    ppermute x4, waiting for transfers between devices, chain(): theirs.append(lax.ppermute(send, 'seq', swap))  6.05 us
    ppermute x2, starting transfers between devices, exchange(): received.append(lax.ppermute(sends[0], 'seq', swap))  4.71 us
    ppermute x4, starting transfers between devices, chain(): theirs.append(lax.ppermute(send, 'seq', swap))  4.48 us
    ppermute x3, waiting for transfers between devices, on_device(): lax.ppermute(sums, 'head', [(i, (i + k) % head_count) for i in range(head...  2.95 us
    ppermute x2, waiting for transfers between devices, exchange(): received.append(lax.ppermute(sends[0], 'seq', swap))  2.68 us
  transfers between devices with their start and end apart: 23, of which 9 were waited for; matrix products, arithmetic and copies ran while one was open for 0% of the time, Pallas kernels for 38%

profile of v9, /device:TPU:0, one launch (start us, length us, event | category | flops | bytes accessed | tf_op | source)
XLA Modules:
  0.0 101.9 jit_solution(929628407748688476)
XLA Ops:
  0.7 3.0 %shard_map.93 = (f32[520,128]{1,0:T(8,128)}, f32[16,512]{1,0:T(8,128)}) custom-call(s32[1]{0:T(128)} %bitcast.member_ref, s32[1]{0:T(128)} %bitcast.1.pair_ref, bf16[512,2048]{1,0:T(8,128)(2,1)} %refs_2_.31, bf16[512,2048]{1,0:T(8,128)(2,1)} %refs_3_.15, f32[16,512]{1,0:T(8,128)} %bitcast.12), custom_call_target="tpu_custom_call" | custom-call | flops 50000000 | bytes 125000 | tf_op jit(solution)/shard_map/pallas_call | solution.py:353
  3.6 3.0 %collective-permute-start = (f32[520,128]{1,0:T(8,128)}, f32[520,128]{1,0:T(8,128)S(1)}, u32[]{:S(2)}, u32[]{:S(2)}) collective-permute-start(f32[520,128]{1,0:T(8,128)} %get-tuple-element.55), channel_id=1, source_target_pairs={{0,4},{4,0},{8,12},{12,8},{16,20},{20,16},{24,28},{28,24},{1,5},{5... | collective-permute-start | bytes 798728 | tf_op jit(solution)/shard_map/ppermute | solution.py:413
  6.6 1.6 %copy-done.2 = bf16[512,2048]{1,0:T(8,128)(2,1)S(1)} copy-done((bf16[512,2048]{1,0:T(8,128)(2,1)S(1)}, bf16[512,2048]{1,0:T(8,128)(2,1)}, u32[]{:S(2)}) %copy-start.2) | copy-done | bytes 2097176
  11.0 2.7 %collective-permute-done.refs_1_ = f32[520,128]{1,0:T(8,128)S(1)} collective-permute-done((f32[520,128]{1,0:T(8,128)}, f32[520,128]{1,0:T(8,128)S(1)}, u32[]{:S(2)}, u32[]{:S(2)}) %collective-permute-start) | collective-permute-done | bytes 266272 | tf_op jit(solution)/shard_map/ppermute | solution.py:413
  13.8 3.4 %collective-permute-start.1 = (f32[512,128]{1,0:T(8,128)S(1)}, f32[512,128]{1,0:T(8,128)S(1)}, u32[]{:S(2)}, u32[]{:S(2)}) collective-permute-start(f32[512,128]{1,0:T(8,128)S(1)} %shard_map.98.refs_4_), channel_id=1, source_target_pairs={{0,8},{4,12},{1,9},{5,13},{2,10},{6,14},{3,11},{7,15}} | collective-permute-start | bytes 786440 | tf_op jit(solution)/shard_map/ppermute | solution.py:441
  17.2 1.9 %shard_map.99.refs_2_.refs_0_ = f32[512,512]{1,0:T(8,128)S(1)} custom-call(s32[1]{0:T(128)} %bitcast.member_ref, s32[1]{0:T(128)} %bitcast.1.pair_ref, bf16[512,2048]{1,0:T(8,128)(2,1)S(1)} %copy-done, bf16[512,2048]{1,0:T(8,128)(2,1)S(1)} %copy-done.1, bf16[512,2048]{1,0:T(8,128)(2,1)S(1)} %copy-done.3, f32[16,512]{1,0:T(8,128)S(1)} %copy-done.5, ...), custom_call_target="tpu_custom_call" | custom-call | flops 100000000 | bytes 250000 | tf_op jit(solution)/shard_map/pallas_call | solution.py:353
  19.2 3.4 %collective-permute-start.4 = (f32[512,128]{1,0:T(8,128)S(1)}, f32[512,128]{1,0:T(8,128)S(1)}, u32[]{:S(2)}, u32[]{:S(2)}) collective-permute-start(f32[512,128]{1,0:T(8,128)S(1)} %shard_map.100.refs_3_), channel_id=1, source_target_pairs={{0,8},{4,12},{1,9},{5,13},{2,10},{6,14},{3,11},{7,15}} | collective-permute-start | bytes 786440 | tf_op jit(solution)/shard_map/ppermute | solution.py:441
  23.3 1.9 %shard_map.102.refs_3_.refs_0_ = f32[512,512]{1,0:T(8,128)S(1)} custom-call(s32[1]{0:T(128)} %bitcast.member_ref, s32[1]{0:T(128)} %bitcast.1.pair_ref, bf16[512,2048]{1,0:T(8,128)(2,1)S(1)} %copy-done, bf16[512,2048]{1,0:T(8,128)(2,1)S(1)} %copy-done.1, bf16[512,2048]{1,0:T(8,128)(2,1)S(1)} %copy-done.3, f32[16,512]{1,0:T(8,128)S(1)} %copy-done.5, ...), custom_call_target="tpu_custom_call" | custom-call | flops 2200000000 | bytes 5500000 | tf_op jit(solution)/shard_map/pallas_call | solution.py:353
  25.3 1.9 %collective-permute-done.4.refs_2_ = f32[512,128]{1,0:T(8,128)S(1)} collective-permute-done((f32[512,128]{1,0:T(8,128)S(1)}, f32[512,128]{1,0:T(8,128)S(1)}, u32[]{:S(2)}, u32[]{:S(2)}) %collective-permute-start.4) | collective-permute-done | bytes 262176 | tf_op jit(solution)/shard_map/ppermute | solution.py:441
  28.6 1.9 %shard_map.105.refs_3_.refs_0_ = f32[512,512]{1,0:T(8,128)S(1)} custom-call(s32[1]{0:T(128)} %bitcast.member_ref, s32[1]{0:T(128)} %bitcast.1.pair_ref, bf16[512,2048]{1,0:T(8,128)(2,1)S(1)} %copy-done, bf16[512,2048]{1,0:T(8,128)(2,1)S(1)} %copy-done.1, bf16[512,2048]{1,0:T(8,128)(2,1)S(1)} %copy-done.3, f32[16,512]{1,0:T(8,128)S(1)} %copy-done.6, ...), custom_call_target="tpu_custom_call" | custom-call | flops 2200000000 | bytes 5500000 | tf_op jit(solution)/shard_map/pallas_call | solution.py:353
  31.4 1.9 %collective-permute-start.9 = (f32[512,128]{1,0:T(8,128)S(1)}, f32[512,128]{1,0:T(8,128)S(1)}, u32[]{:S(2)}, u32[]{:S(2)}) collective-permute-start(f32[512,128]{1,0:T(8,128)S(1)} %get-tuple-element.57.refs_4_), channel_id=1, source_target_pairs={{0,4},{4,0},{8,12},{12,8},{16,20},{20,16},{24,28},{28,24},{1,5},{5... | collective-permute-start | bytes 786440 | tf_op jit(solution)/shard_map/ppermute | solution.py:452
  33.3 1.9 %shard_map.108.refs_7_.refs_0_ = f32[512,512]{1,0:T(8,128)S(1)} custom-call(s32[1]{0:T(128)} %bitcast.member_ref, s32[1]{0:T(128)} %bitcast.1.pair_ref, bf16[512,2048]{1,0:T(8,128)(2,1)S(1)} %copy-done, bf16[512,2048]{1,0:T(8,128)(2,1)S(1)} %copy-done.1, bf16[512,2048]{1,0:T(8,128)(2,1)S(1)} %copy-done.3, f32[16,512]{1,0:T(8,128)S(1)} %copy-done.6, ...), custom_call_target="tpu_custom_call" | custom-call | flops 2200000000 | bytes 5500000 | tf_op jit(solution)/shard_map/pallas_call | solution.py:353
  37.4 2.5 %collective-permute-done.9.refs_5_ = f32[512,128]{1,0:T(8,128)S(1)} collective-permute-done((f32[512,128]{1,0:T(8,128)S(1)}, f32[512,128]{1,0:T(8,128)S(1)}, u32[]{:S(2)}, u32[]{:S(2)}) %collective-permute-start.9) | collective-permute-done | bytes 262176 | tf_op jit(solution)/shard_map/ppermute | solution.py:452
  40.8 2.9 %collective-permute-done.8.refs_5_ = f32[512,128]{1,0:T(8,128)S(1)} collective-permute-done((f32[512,128]{1,0:T(8,128)S(1)}, f32[512,128]{1,0:T(8,128)S(1)}, u32[]{:S(2)}, u32[]{:S(2)}) %collective-permute-start.8) | collective-permute-done | bytes 262176 | tf_op jit(solution)/shard_map/ppermute | solution.py:452
  44.6 1.5 %collective-permute-start.11 = (f32[8,512]{1,0:T(8,128)S(1)}, f32[8,512]{1,0:T(8,128)S(1)}, u32[]{:S(2)}, u32[]{:S(2)}) collective-permute-start(f32[8,512]{1,0:T(8,128)S(1)} %get-tuple-element.64.refs_5_), channel_id=1, source_target_pairs={{0,2},{1,3},{2,0},{3,1},{4,6},{5,7},{6,4},{7,5},{8,10},{9,11},{10,... | collective-permute-start | bytes 49160 | tf_op jit(solution)/shard_map/ppermute | solution.py:525
  46.3 2.0 %collective-permute-done.11.refs_7_ = f32[8,512]{1,0:T(8,128)S(1)} collective-permute-done((f32[8,512]{1,0:T(8,128)S(1)}, f32[8,512]{1,0:T(8,128)S(1)}, u32[]{:S(2)}, u32[]{:S(2)}) %collective-permute-start.11) | collective-permute-done | bytes 16416 | tf_op jit(solution)/shard_map/ppermute | solution.py:525
  49.3 1.7 %shard_map.114 = (bf16[512,2048]{1,0:T(8,128)(2,1)}, bf16[512,512]{1,0:T(8,128)(2,1)S(1)}, f32[520,128]{1,0:T(8,128)S(1)}) custom-call(s32[1]{0:T(128)} %bitcast.member_ref, s32[1]{0:T(128)} %bitcast.1.pair_ref, f32[512,512]{1,0:T(8,128)S(1)} %get-tuple-element.67.refs_0_, bf16[512,2048]{1,0:T(8,128)(2,1)S(1)} %copy-done.4, f32[1,2048]{1,0:T(1,128)S(1)} %bitcast.8, ...), custom_call_target="tpu_custom_call" | custom-call | flops 2000000000 | bytes 5000000 | tf_op jit(solution)/shard_map/pallas_call | solution.py:353
  51.0 1.7 %collective-permute-start.13 = (f32[520,128]{1,0:T(8,128)S(1)}, f32[520,128]{1,0:T(8,128)S(1)}, u32[]{:S(2)}, u32[]{:S(2)}) collective-permute-start(f32[520,128]{1,0:T(8,128)S(1)} %get-tuple-element.69.refs_10_), channel_id=1, source_target_pairs={{0,4},{4,0},{8,12},{12,8},{16,20},{20,16},{24,28},{28,24},{1,5},{5... | collective-permute-start | bytes 798728 | tf_op jit(solution)/shard_map/ppermute | solution.py:413
  52.7 1.7 %shard_map.115 = (bf16[512,2048]{1,0:T(8,128)(2,1)}, bf16[512,512]{1,0:T(8,128)(2,1)S(1)}, f32[520,128]{1,0:T(8,128)S(1)}) custom-call(s32[1]{0:T(128)} %bitcast.member_ref, s32[1]{0:T(128)} %bitcast.1.pair_ref, f32[512,512]{1,0:T(8,128)S(1)} %get-tuple-element.66.refs_0_, bf16[512,2048]{1,0:T(8,128)(2,1)S(1)} %copy-done.4, ...), custom_call_target="tpu_custom_call", output_to_operand_aliasing={{0}: (11, {})} | custom-call | flops 2000000000 | bytes 5000000 | tf_op jit(solution)/shard_map/pallas_call | solution.py:353
  54.5 1.7 %shard_map.116 = (bf16[512,2048]{1,0:T(8,128)(2,1)}, bf16[512,512]{1,0:T(8,128)(2,1)S(1)}, f32[520,128]{1,0:T(8,128)S(1)}) custom-call(s32[1]{0:T(128)} %bitcast.member_ref, s32[1]{0:T(128)} %bitcast.1.pair_ref, f32[512,512]{1,0:T(8,128)S(1)} %get-tuple-element.65.refs_0_, bf16[512,2048]{1,0:T(8,128)(2,1)S(1)} %copy-done.4, ...), custom_call_target="tpu_custom_call", output_to_operand_aliasing={{0}: (11, {})} | custom-call | flops 2000000000 | bytes 5000000 | tf_op jit(solution)/shard_map/pallas_call | solution.py:353
  56.2 1.7 %shard_map.117 = (bf16[512,2048]{1,0:T(8,128)(2,1)}, bf16[512,512]{1,0:T(8,128)(2,1)S(1)}, f32[520,128]{1,0:T(8,128)S(1)}) custom-call(s32[1]{0:T(128)} %bitcast.member_ref, s32[1]{0:T(128)} %bitcast.1.pair_ref, f32[512,512]{1,0:T(8,128)S(1)} %get-tuple-element.61.refs_0_, bf16[512,2048]{1,0:T(8,128)(2,1)S(1)} %copy-done.4, ...), custom_call_target="tpu_custom_call", output_to_operand_aliasing={{0}: (11, {})} | custom-call | flops 2000000000 | bytes 5000000 | tf_op jit(solution)/shard_map/pallas_call | solution.py:353
  58.9 4.0 %shard_map.120 = (bf16[512,2048]{1,0:T(8,128)(2,1)}, f32[512,512]{1,0:T(8,128)S(1)}, f32[512,512]{1,0:T(8,128)S(1)}) custom-call(s32[1]{0:T(128)} %bitcast.member_ref, s32[1]{0:T(128)} %bitcast.1.pair_ref, bf16[512,2048]{1,0:T(8,128)(2,1)S(1)} %copy-done, bf16[512,2048]{1,0:T(8,128)(2,1)S(1)} %copy-done.1, bf16[512,2048]{1,0:T(8,128)(2,1)S(1)} %copy-done.3, ...), custom_call_target="tpu_custom_call" | custom-call | flops 4300000256 | bytes 10750000 | tf_op jit(solution)/shard_map/pallas_call | solution.py:353
  62.9 1.6 %collective-permute-done.15.refs_1_ = f32[520,128]{1,0:T(8,128)S(1)} collective-permute-done((f32[520,128]{1,0:T(8,128)S(1)}, f32[520,128]{1,0:T(8,128)S(1)}, u32[]{:S(2)}, u32[]{:S(2)}) %collective-permute-start.15) | collective-permute-done | bytes 266272 | tf_op jit(solution)/shard_map/ppermute | solution.py:416
  65.9 4.0 %shard_map.123 = (bf16[512,2048]{1,0:T(8,128)(2,1)}, f32[512,512]{1,0:T(8,128)S(1)}, f32[512,512]{1,0:T(8,128)S(1)}) custom-call(s32[1]{0:T(128)} %bitcast.member_ref, s32[1]{0:T(128)} %bitcast.1.pair_ref, bf16[512,2048]{1,0:T(8,128)(2,1)S(1)} %copy-done, bf16[512,2048]{1,0:T(8,128)(2,1)S(1)} %copy-done.1, ...), custom_call_target="tpu_custom_call", output_to_operand_aliasing={{0}: (8, {})} | custom-call | flops 4300000256 | bytes 10750000 | tf_op jit(solution)/shard_map/pallas_call | solution.py:353
  71.9 4.0 %shard_map.126 = (bf16[512,2048]{1,0:T(8,128)(2,1)}, f32[512,512]{1,0:T(8,128)S(1)}, f32[512,512]{1,0:T(8,128)S(1)}) custom-call(s32[1]{0:T(128)} %bitcast.member_ref, s32[1]{0:T(128)} %bitcast.1.pair_ref, bf16[512,2048]{1,0:T(8,128)(2,1)S(1)} %copy-done, bf16[512,2048]{1,0:T(8,128)(2,1)S(1)} %copy-done.1, ...), custom_call_target="tpu_custom_call", output_to_operand_aliasing={{0}: (8, {})} | custom-call | flops 4300000256 | bytes 10750000 | tf_op jit(solution)/shard_map/pallas_call | solution.py:353
  77.2 10.8 %collective-permute-done.18.refs_4_ = f32[512,128]{1,0:T(8,128)S(1)} collective-permute-done((f32[512,128]{1,0:T(8,128)S(1)}, f32[512,128]{1,0:T(8,128)S(1)}, u32[]{:S(2)}, u32[]{:S(2)}) %collective-permute-start.18) | collective-permute-done | bytes 262176 | tf_op jit(solution)/shard_map/ppermute | solution.py:441
  88.0 1.7 %collective-permute-start.22 = (f32[512,128]{1,0:T(8,128)S(1)}, f32[512,128]{1,0:T(8,128)S(1)}, u32[]{:S(2)}, u32[]{:S(2)}) collective-permute-start(f32[512,128]{1,0:T(8,128)S(1)} %get-tuple-element.86.refs_7_), channel_id=1, source_target_pairs={{0,4},{4,0},{8,12},{12,8},{16,20},{20,16},{24,28},{28,24},{1,5},{5... | collective-permute-start | bytes 786440 | tf_op jit(solution)/shard_map/ppermute | solution.py:452
  89.7 3.9 %shard_map.129 = (bf16[512,2048]{1,0:T(8,128)(2,1)}, f32[512,512]{1,0:T(8,128)S(1)}, f32[512,512]{1,0:T(8,128)S(1)}) custom-call(s32[1]{0:T(128)} %bitcast.member_ref, s32[1]{0:T(128)} %bitcast.1.pair_ref, bf16[512,2048]{1,0:T(8,128)(2,1)S(1)} %copy-done, bf16[512,2048]{1,0:T(8,128)(2,1)S(1)} %copy-done.1, ...), custom_call_target="tpu_custom_call", output_to_operand_aliasing={{0}: (8, {})} | custom-call | flops 4300000256 | bytes 10750000 | tf_op jit(solution)/shard_map/pallas_call | solution.py:353
  94.3 1.8 %shard_map.131 = (bf16[512,2048]{1,0:T(8,128)(2,1)}, bf16[512,2048]{1,0:T(8,128)(2,1)}) custom-call(s32[1]{0:T(128)} %bitcast.member_ref, s32[1]{0:T(128)} %bitcast.1.pair_ref, f32[512,512]{1,0:T(8,128)S(1)} %get-tuple-element.81.refs_2_.refs_0_, f32[512,512]{1,0:T(8,128)S(1)} %get-tuple-element.94.refs_1_, bf16[512,2048]{1,0:T(8,128)(2,1)S(1)} %copy-done.1, ...), custom_call_target="tpu_custom_call" | custom-call | flops 2000000000 | bytes 5000000 | tf_op jit(solution)/shard_map/pallas_call | solution.py:353
  96.1 1.7 %shard_map.132 = (bf16[512,2048]{1,0:T(8,128)(2,1)}, bf16[512,2048]{1,0:T(8,128)(2,1)}) custom-call(s32[1]{0:T(128)} %bitcast.member_ref, s32[1]{0:T(128)} %bitcast.1.pair_ref, f32[512,512]{1,0:T(8,128)S(1)} %get-tuple-element.85.refs_3_.refs_0_, f32[512,512]{1,0:T(8,128)S(1)} %get-tuple-element.92.refs_1_, ...), custom_call_target="tpu_custom_call", output_to_operand_aliasing={{0}: (8, {}), {1}: (9, {})} | custom-call | flops 2000000000 | bytes 5000000 | tf_op jit(solution)/shard_map/pallas_call | solution.py:353
  97.8 1.8 %shard_map.133 = (bf16[512,2048]{1,0:T(8,128)(2,1)}, bf16[512,2048]{1,0:T(8,128)(2,1)}) custom-call(s32[1]{0:T(128)} %bitcast.member_ref, s32[1]{0:T(128)} %bitcast.1.pair_ref, f32[512,512]{1,0:T(8,128)S(1)} %get-tuple-element.83.refs_3_.refs_0_, f32[512,512]{1,0:T(8,128)S(1)} %get-tuple-element.91.refs_1_, ...), custom_call_target="tpu_custom_call", output_to_operand_aliasing={{0}: (8, {}), {1}: (9, {})} | custom-call | flops 2000000000 | bytes 5000000 | tf_op jit(solution)/shard_map/pallas_call | solution.py:353
  100.2 1.7 %shard_map.134 = (bf16[512,2048]{1,0:T(8,128)(2,1)}, bf16[512,2048]{1,0:T(8,128)(2,1)}) custom-call(s32[1]{0:T(128)} %bitcast.member_ref, s32[1]{0:T(128)} %bitcast.1.pair_ref, f32[512,512]{1,0:T(8,128)S(1)} %get-tuple-element.88.refs_5_.refs_0_, f32[512,512]{1,0:T(8,128)S(1)} %get-tuple-element.89.refs_1_, ...), custom_call_target="tpu_custom_call", output_to_operand_aliasing={{0}: (8, {}), {1}: (9, {})} | custom-call | flops 2000000000 | bytes 5000000 | tf_op jit(solution)/shard_map/pallas_call | solution.py:353
  (73 shorter events, 17.8 us)
Async XLA Ops:
  0.7 5.9 %copy-start.1 = (bf16[512,2048]{1,0:T(8,128)(2,1)S(1)}, bf16[512,2048]{1,0:T(8,128)(2,1)}, u32[]{:S(2)}) copy-start(bf16[512,2048]{1,0:T(8,128)(2,1)} %refs_2_.31) | copy-start | bytes 6291460
  3.6 10.1 %collective-permute-start = (f32[520,128]{1,0:T(8,128)}, f32[520,128]{1,0:T(8,128)S(1)}, u32[]{:S(2)}, u32[]{:S(2)}) collective-permute-start(f32[520,128]{1,0:T(8,128)} %get-tuple-element.55), channel_id=1, source_target_pairs={{0,4},{4,0},{8,12},{12,8},{16,20},{20,16},{24,28},{28,24},{1,5},{5... | collective-permute-start | bytes 798728 | tf_op jit(solution)/shard_map/ppermute | solution.py:413
  6.6 1.6 %copy-start.2 = (bf16[512,2048]{1,0:T(8,128)(2,1)S(1)}, bf16[512,2048]{1,0:T(8,128)(2,1)}, u32[]{:S(2)}) copy-start(bf16[512,2048]{1,0:T(8,128)(2,1)} %refs_3_.15) | copy-start | bytes 6291460
  8.2 0.8 copy-start.5
  10.2 7.0 %copy-start = (bf16[512,2048]{1,0:T(8,128)(2,1)S(1)}, bf16[512,2048]{1,0:T(8,128)(2,1)}, u32[]{:S(2)}) copy-start(bf16[512,2048]{1,0:T(8,128)(2,1)} %refs_0_.23) | copy-start | bytes 6291460
  10.3 7.0 %copy-start.3 = (bf16[512,2048]{1,0:T(8,128)(2,1)S(1)}, bf16[512,2048]{1,0:T(8,128)(2,1)}, u32[]{:S(2)}) copy-start(bf16[512,2048]{1,0:T(8,128)(2,1)} %refs_3_.15) | copy-start | bytes 6291460
  11.0 8.2 %collective-permute-start.2 = (f32[520,128]{1,0:T(8,128)S(1)}, f32[520,128]{1,0:T(8,128)S(1)}, u32[]{:S(2)}, u32[]{:S(2)}) collective-permute-start(f32[520,128]{1,0:T(8,128)S(1)} %shard_map.97.refs_2_), channel_id=1, source_target_pairs={{0,4},{4,0},{8,12},{12,8},{16,20},{20,16},{24,28},{28,24},{1,5},{5... | collective-permute-start | bytes 798728 | tf_op jit(solution)/shard_map/ppermute | solution.py:416
  13.8 8.8 %collective-permute-start.1 = (f32[512,128]{1,0:T(8,128)S(1)}, f32[512,128]{1,0:T(8,128)S(1)}, u32[]{:S(2)}, u32[]{:S(2)}) collective-permute-start(f32[512,128]{1,0:T(8,128)S(1)} %shard_map.98.refs_4_), channel_id=1, source_target_pairs={{0,8},{4,12},{1,9},{5,13},{2,10},{6,14},{3,11},{7,15}} | collective-permute-start | bytes 786440 | tf_op jit(solution)/shard_map/ppermute | solution.py:441
  19.2 8.0 %collective-permute-start.4 = (f32[512,128]{1,0:T(8,128)S(1)}, f32[512,128]{1,0:T(8,128)S(1)}, u32[]{:S(2)}, u32[]{:S(2)}) collective-permute-start(f32[512,128]{1,0:T(8,128)S(1)} %shard_map.100.refs_3_), channel_id=1, source_target_pairs={{0,8},{4,12},{1,9},{5,13},{2,10},{6,14},{3,11},{7,15}} | collective-permute-start | bytes 786440 | tf_op jit(solution)/shard_map/ppermute | solution.py:441
  22.6 5.2 %collective-permute-start.3 = (f32[512,128]{1,0:T(8,128)S(1)}, f32[512,128]{1,0:T(8,128)S(1)}, u32[]{:S(2)}, u32[]{:S(2)}) collective-permute-start(f32[512,128]{1,0:T(8,128)S(1)} %shard_map.101.refs_4_), channel_id=1, source_target_pairs={{8,16},{12,20},{9,17},{13,21},{10,18},{14,22},{11,19},{15,23}} | collective-permute-start | bytes 786440 | tf_op jit(solution)/shard_map/ppermute | solution.py:441
  25.3 3.3 %copy-start.6 = (f32[16,512]{1,0:T(8,128)S(1)}, f32[16,512]{1,0:T(8,128)}, u32[]{:S(2)}) copy-start(f32[16,512]{1,0:T(8,128)} %get-tuple-element.54.refs_2_.refs_3_.refs_4_) | copy-start | bytes 98308
  27.2 3.3 %collective-permute-start.5 = (f32[512,128]{1,0:T(8,128)S(1)}, f32[512,128]{1,0:T(8,128)S(1)}, u32[]{:S(2)}, u32[]{:S(2)}) collective-permute-start(f32[512,128]{1,0:T(8,128)S(1)} %shard_map.103.refs_3_), channel_id=1, source_target_pairs={{8,16},{12,20},{9,17},{13,21},{10,18},{14,22},{11,19},{15,23}} | collective-permute-start | bytes 786440 | tf_op jit(solution)/shard_map/ppermute | solution.py:441
  27.9 3.3 %collective-permute-start.7 = (f32[512,128]{1,0:T(8,128)S(1)}, f32[512,128]{1,0:T(8,128)S(1)}, u32[]{:S(2)}, u32[]{:S(2)}) collective-permute-start(f32[512,128]{1,0:T(8,128)S(1)} %shard_map.104.refs_4_), channel_id=1, source_target_pairs={{16,24},{20,28},{17,25},{21,29},{18,26},{22,30},{19,27},{23,31}} | collective-permute-start | bytes 786440 | tf_op jit(solution)/shard_map/ppermute | solution.py:441
  30.6 5.6 %collective-permute-start.6 = (f32[512,128]{1,0:T(8,128)S(1)}, f32[512,128]{1,0:T(8,128)S(1)}, u32[]{:S(2)}, u32[]{:S(2)}) collective-permute-start(f32[512,128]{1,0:T(8,128)S(1)} %shard_map.106.refs_5_), channel_id=1, source_target_pairs={{16,24},{20,28},{17,25},{21,29},{18,26},{22,30},{19,27},{23,31}} | collective-permute-start | bytes 786440 | tf_op jit(solution)/shard_map/ppermute | solution.py:441
  31.4 3.8 %copy-start.4 = (bf16[512,2048]{1,0:T(8,128)(2,1)S(1)}, bf16[512,2048]{1,0:T(8,128)(2,1)}, u32[]{:S(2)}) copy-start(bf16[512,2048]{1,0:T(8,128)(2,1)} %refs_1_.35) | copy-start | bytes 6291460
  31.4 3.8 %copy-start.7 = (f32[2048]{0:T(1024)S(1)}, f32[2048]{0:T(1024)}, u32[]{:S(2)}) copy-start(f32[2048]{0:T(1024)} %param.10) | copy-start | bytes 24580
  31.4 8.5 %collective-permute-start.9 = (f32[512,128]{1,0:T(8,128)S(1)}, f32[512,128]{1,0:T(8,128)S(1)}, u32[]{:S(2)}, u32[]{:S(2)}) collective-permute-start(f32[512,128]{1,0:T(8,128)S(1)} %get-tuple-element.57.refs_4_), channel_id=1, source_target_pairs={{0,4},{4,0},{8,12},{12,8},{16,20},{20,16},{24,28},{28,24},{1,5},{5... | collective-permute-start | bytes 786440 | tf_op jit(solution)/shard_map/ppermute | solution.py:452
  36.2 7.4 %collective-permute-start.8 = (f32[512,128]{1,0:T(8,128)S(1)}, f32[512,128]{1,0:T(8,128)S(1)}, u32[]{:S(2)}, u32[]{:S(2)}) collective-permute-start(f32[512,128]{1,0:T(8,128)S(1)} %get-tuple-element.60.refs_7_), channel_id=1, source_target_pairs={{0,4},{4,0},{8,12},{12,8},{16,20},{20,16},{24,28},{28,24},{1,5},{5... | collective-permute-start | bytes 786440 | tf_op jit(solution)/shard_map/ppermute | solution.py:452
  44.6 1.8 %collective-permute-start.12 = (f32[8,512]{1,0:T(8,128)S(1)}, f32[8,512]{1,0:T(8,128)S(1)}, u32[]{:S(2)}, u32[]{:S(2)}) collective-permute-start(f32[8,512]{1,0:T(8,128)S(1)} %get-tuple-element.64.refs_5_), channel_id=1, source_target_pairs={{0,3},{1,0},{2,1},{3,2},{4,7},{5,4},{6,5},{7,6},{8,11},{9,8},{10,9... | collective-permute-start | bytes 49160 | tf_op jit(solution)/shard_map/ppermute | solution.py:525
  44.6 3.8 %collective-permute-start.11 = (f32[8,512]{1,0:T(8,128)S(1)}, f32[8,512]{1,0:T(8,128)S(1)}, u32[]{:S(2)}, u32[]{:S(2)}) collective-permute-start(f32[8,512]{1,0:T(8,128)S(1)} %get-tuple-element.64.refs_5_), channel_id=1, source_target_pairs={{0,2},{1,3},{2,0},{3,1},{4,6},{5,7},{6,4},{7,5},{8,10},{9,11},{10,... | collective-permute-start | bytes 49160 | tf_op jit(solution)/shard_map/ppermute | solution.py:525
  46.1 3.2 %collective-permute-start.10 = (f32[8,512]{1,0:T(8,128)S(1)}, f32[8,512]{1,0:T(8,128)S(1)}, u32[]{:S(2)}, u32[]{:S(2)}) collective-permute-start(f32[8,512]{1,0:T(8,128)S(1)} %get-tuple-element.64.refs_5_), channel_id=1, source_target_pairs={{0,1},{1,2},{2,3},{3,0},{4,5},{5,6},{6,7},{7,4},{8,9},{9,10},{10,1... | collective-permute-start | bytes 49160 | tf_op jit(solution)/shard_map/ppermute | solution.py:525
  51.0 7.3 %collective-permute-start.13 = (f32[520,128]{1,0:T(8,128)S(1)}, f32[520,128]{1,0:T(8,128)S(1)}, u32[]{:S(2)}, u32[]{:S(2)}) collective-permute-start(f32[520,128]{1,0:T(8,128)S(1)} %get-tuple-element.69.refs_10_), channel_id=1, source_target_pairs={{0,4},{4,0},{8,12},{12,8},{16,20},{20,16},{24,28},{28,24},{1,5},{5... | collective-permute-start | bytes 798728 | tf_op jit(solution)/shard_map/ppermute | solution.py:413
  57.9 6.6 %collective-permute-start.15 = (f32[520,128]{1,0:T(8,128)S(1)}, f32[520,128]{1,0:T(8,128)S(1)}, u32[]{:S(2)}, u32[]{:S(2)}) collective-permute-start(f32[520,128]{1,0:T(8,128)S(1)} %shard_map.118.refs_2_), channel_id=1, source_target_pairs={{0,4},{4,0},{8,12},{12,8},{16,20},{20,16},{24,28},{28,24},{1,5},{5... | collective-permute-start | bytes 798728 | tf_op jit(solution)/shard_map/ppermute | solution.py:416
  58.3 6.9 %collective-permute-start.14 = (f32[512,128]{1,0:T(8,128)S(1)}, f32[512,128]{1,0:T(8,128)S(1)}, u32[]{:S(2)}, u32[]{:S(2)}) collective-permute-start(f32[512,128]{1,0:T(8,128)S(1)} %shard_map.119.refs_6_), channel_id=1, source_target_pairs={{24,16},{28,20},{25,17},{29,21},{26,18},{30,22},{27,19},{31,23}} | collective-permute-start | bytes 786440 | tf_op jit(solution)/shard_map/ppermute | solution.py:441
  64.5 5.4 %collective-permute-start.17 = (f32[512,128]{1,0:T(8,128)S(1)}, f32[512,128]{1,0:T(8,128)S(1)}, u32[]{:S(2)}, u32[]{:S(2)}) collective-permute-start(f32[512,128]{1,0:T(8,128)S(1)} %shard_map.121.refs_3_), channel_id=1, source_target_pairs={{24,16},{28,20},{25,17},{29,21},{26,18},{30,22},{27,19},{31,23}} | collective-permute-start | bytes 786440 | tf_op jit(solution)/shard_map/ppermute | solution.py:441
  65.2 5.3 %collective-permute-start.16 = (f32[512,128]{1,0:T(8,128)S(1)}, f32[512,128]{1,0:T(8,128)S(1)}, u32[]{:S(2)}, u32[]{:S(2)}) collective-permute-start(f32[512,128]{1,0:T(8,128)S(1)} %shard_map.122.refs_7_), channel_id=1, source_target_pairs={{16,8},{20,12},{17,9},{21,13},{18,10},{22,14},{19,11},{23,15}} | collective-permute-start | bytes 786440 | tf_op jit(solution)/shard_map/ppermute | solution.py:441
  69.9 6.0 %collective-permute-start.19 = (f32[512,128]{1,0:T(8,128)S(1)}, f32[512,128]{1,0:T(8,128)S(1)}, u32[]{:S(2)}, u32[]{:S(2)}) collective-permute-start(f32[512,128]{1,0:T(8,128)S(1)} %shard_map.124.refs_3_), channel_id=1, source_target_pairs={{16,8},{20,12},{17,9},{21,13},{18,10},{22,14},{19,11},{23,15}} | collective-permute-start | bytes 786440 | tf_op jit(solution)/shard_map/ppermute | solution.py:441
  70.6 17.3 %collective-permute-start.18 = (f32[512,128]{1,0:T(8,128)S(1)}, f32[512,128]{1,0:T(8,128)S(1)}, u32[]{:S(2)}, u32[]{:S(2)}) collective-permute-start(f32[512,128]{1,0:T(8,128)S(1)} %shard_map.125.refs_7_), channel_id=1, source_target_pairs={{8,0},{12,4},{9,1},{13,5},{10,2},{14,6},{11,3},{15,7}} | collective-permute-start | bytes 786440 | tf_op jit(solution)/shard_map/ppermute | solution.py:441
  75.9 17.8 %collective-permute-start.20 = (f32[512,128]{1,0:T(8,128)S(1)}, f32[512,128]{1,0:T(8,128)S(1)}, u32[]{:S(2)}, u32[]{:S(2)}) collective-permute-start(f32[512,128]{1,0:T(8,128)S(1)} %shard_map.127.refs_5_), channel_id=1, source_target_pairs={{8,0},{12,4},{9,1},{13,5},{10,2},{14,6},{11,3},{15,7}} | collective-permute-start | bytes 786440 | tf_op jit(solution)/shard_map/ppermute | solution.py:441
  88.0 9.8 %collective-permute-start.22 = (f32[512,128]{1,0:T(8,128)S(1)}, f32[512,128]{1,0:T(8,128)S(1)}, u32[]{:S(2)}, u32[]{:S(2)}) collective-permute-start(f32[512,128]{1,0:T(8,128)S(1)} %get-tuple-element.86.refs_7_), channel_id=1, source_target_pairs={{0,4},{4,0},{8,12},{12,8},{16,20},{20,16},{24,28},{28,24},{1,5},{5... | collective-permute-start | bytes 786440 | tf_op jit(solution)/shard_map/ppermute | solution.py:452
  93.7 6.4 %collective-permute-start.21 = (f32[512,128]{1,0:T(8,128)S(1)}, f32[512,128]{1,0:T(8,128)S(1)}, u32[]{:S(2)}, u32[]{:S(2)}) collective-permute-start(f32[512,128]{1,0:T(8,128)S(1)} %get-tuple-element.90.refs_6_), channel_id=1, source_target_pairs={{0,4},{4,0},{8,12},{12,8},{16,20},{20,16},{24,28},{28,24},{1,5},{5... | collective-permute-start | bytes 786440 | tf_op jit(solution)/shard_map/ppermute | solution.py:452
